TPU v7x, 32 devices: a whole 2x2x4 slice. The times are simulated.
32 devices in a mesh: grp: 2 (over x), sec: 16 (over z, y, core).
Axes of the slice: x: 2, y: 2, z: 4, core: 2. Of those that a mesh axis runs over, the one named last changes fastest.
Arguments:
- psi: bfloat16 [32, 1024, 512], P(('grp', 'sec')), parts along dimension 0, may hold values from -6 to 6
- left_env: bfloat16 [32, 4, 1024, 1024], P(('grp', 'sec')), parts along dimension 0, may hold values from -1 to 2, as said below
- right_env: bfloat16 [32, 4, 512, 512], P(('grp', 'sec')), parts along dimension 0, may hold values from -1 to 2, as said below
- row_sizes: int32 [32], P(('grp', 'sec')), parts along dimension 0, may hold values from 64 to 1024, as said below
- col_sizes: int32 [32], P(('grp', 'sec')), parts along dimension 0, may hold values from 64 to 512, as said below
Outputs:
- sigma: bfloat16 [32, 1024, 512], P(('grp', 'sec')), parts along dimension 0
- energy: float32 [2], P('grp'), parts along dimension 0
There are 2 independent parts, one for each index of `grp`. A program takes and returns all parts, laid end to end along the dimension named above; each array names one. Nothing has to cross between parts.
Inputs may be any that keep to these rules, and one draw needn't show every extreme that they name: `row_sizes`: every sector's left width is at least 64, and some sector's is exactly 1024. `col_sizes`: every sector's right width is at least 64, and some sector's is exactly 512. `left_env`: the blocks of term group 0 have a positive diagonal. `right_env`: the blocks of term group 0 have a positive diagonal.
All inputs are finite; a program needn't handle non-finite values.
Results may differ from a plain program's by a relative error of at most 0.0049.
Values sent between devices are 32-bit elements; how exact they have to be, the bound alone decides.
No kernel may reach another device: no remote copies, remote signals or barrier semaphores. Data moves between devices by JAX's collectives and lax.ppermute only.
A program may use at most 64 MiB of HBM per device.

v0:
```python
import jax
import jax.numpy as jnp
from jax import lax
from jax.sharding import PartitionSpec as P


def shifted(value, axis, steps):
    count = lax.axis_size(axis)
    initial, last = (max(0, -steps), min(count, count - steps))
    return lax.ppermute(value, axis, [(source, source + steps) for source in range(initial, last)])


def term_block(psi_live, left_env, right_env, term):
    left = jnp.dot(left_env[0, term], psi_live, preferred_element_type=jnp.float32).astype(
        jnp.bfloat16
    )
    return jnp.dot(left, right_env[0, term], preferred_element_type=jnp.float32)


def on_device(psi, left_env, right_env, row_sizes, col_sizes):
    rows = jnp.arange(psi.shape[1], dtype=jnp.int32)[:, None] < row_sizes[0]
    cols = jnp.arange(psi.shape[2], dtype=jnp.int32)[None, :] < col_sizes[0]
    live = jnp.logical_and(rows, cols)
    psi_live = jnp.where(live, psi[0], jnp.zeros_like(psi[0]))
    carried = term_block(psi_live, left_env, right_env, 2)
    for term in (1, 0):
        moved = shifted(carried, "sec", 1)
        carried = moved + term_block(psi_live, left_env, right_env, term)
    lowered = term_block(psi_live, left_env, right_env, 3)
    total = carried + shifted(lowered, "sec", -1)
    total = jnp.where(live, total, jnp.zeros_like(total))
    sigma = total.astype(jnp.bfloat16)
    local_part = jnp.sum(psi_live.astype(jnp.float32) * total)
    energy = lax.psum(local_part, "sec")
    return (sigma[None], jnp.reshape(energy, (1,)))


def solution(mesh):
    return jax.shard_map(
        on_device,
        mesh=mesh,
        in_specs=(
            P(("grp", "sec"), None, None),
            P(("grp", "sec"), None, None, None),
            P(("grp", "sec"), None, None, None),
            P(("grp", "sec")),
            P(("grp", "sec")),
        ),
        out_specs=(P(("grp", "sec"), None, None), P("grp")),
        check_vma=False,
    )
```

profile of v0, /device:TPU:0, one launch (start us, length us, event | category | flops | bytes accessed | tf_op | source)
XLA Modules:
  0.0 126.3 jit_solution(11348946042983286096)
XLA Ops:
  1.9 0.0 copy-start
  2.0 5.5 %fusion.31 = f32[1024,512]{1,0:T(8,128)} fusion(bf16[1,4,1024,1024]{3,2,1,0:T(8,128)(2,1)} %param.6, bf16[1,4,512,512]{3,2,1,0:T(8,128)(2,1)} %param.7, bf16[1,1024,512]{2,1,0:T(8,128)(2,1)} %param.5, pred[512]{0:T(512)(128)(4,1)S(1)} %iota_compare_fusion.1, pred[1024]{0:T(1024)(128)(4,1)S(1)} %iota_compare_fusion), kind=kOutput, calls=%fused_computation.23 | convolution fusion | flops 1612185600 | bytes 5768704 | tf_op jit(solution)/shard_map/dot_general | solution.py:17
  7.5 3.7 %collective-permute-start = (f32[1024,512]{1,0:T(8,128)}, f32[1024,512]{1,0:T(8,128)}, u32[]{:S(2)}, u32[]{:S(2)}) collective-permute-start(f32[1024,512]{1,0:T(8,128)} %fusion.31), channel_id=1, source_target_pairs={{0,1},{1,2},{2,3},{3,4},{4,5},{5,6},{6,7},{7,8},{8,9},{9,10},{10,1... | collective-permute-start | bytes 6291464 | tf_op jit(solution)/shard_map/ppermute | solution.py:10
  11.1 0.0 copy-done
  11.1 5.2 %fusion.25 = f32[1024,512]{1,0:T(8,128)} fusion(bf16[1,4,1024,1024]{3,2,1,0:T(8,128)(2,1)} %param.6, bf16[1,4,512,512]{3,2,1,0:T(8,128)(2,1)} %param.7, bf16[1,1024,512]{2,1,0:T(8,128)(2,1)S(1)} %copy-done, pred[512]{0:T(512)(128)(4,1)S(1)} %iota_compare_fusion.1, pred[1024]{0:T(1024)(128)(4,1)S(1)} %iota_compare_fusion), kind=kOutput, calls=%fused_computation.21 | convolution fusion | flops 1612185600 | bytes 5768704 | tf_op jit(solution)/shard_map/dot_general | solution.py:17
  16.3 1.3 %collective-permute-start.2 = (f32[1024,512]{1,0:T(8,128)}, f32[1024,512]{1,0:T(8,128)S(1)}, u32[]{:S(2)}, u32[]{:S(2)}) collective-permute-start(f32[1024,512]{1,0:T(8,128)} %fusion.25), channel_id=1, source_target_pairs={{1,0},{2,1},{3,2},{4,3},{5,4},{6,5},{7,6},{8,7},{9,8},{10,9},{11,1... | collective-permute-start | bytes 6291464 | tf_op jit(solution)/shard_map/ppermute | solution.py:10
  17.6 0.0 collective-permute-done
  17.6 5.8 %convolution_add_fusion = f32[1024,512]{1,0:T(8,128)} fusion(f32[1024,512]{1,0:T(8,128)} %collective-permute-done, bf16[1,4,1024,1024]{3,2,1,0:T(8,128)(2,1)} %param.6, bf16[1,4,512,512]{3,2,1,0:T(8,128)(2,1)} %param.7, bf16[1,1024,512]{2,1,0:T(8,128)(2,1)S(1)} %copy-done, pred[512]{0:T(512)(128)(4,1)S(1)} %iota_compare_fusion.1, ...), kind=kOutput, calls=%fused_computation.16 | convolution fusion | flops 1612709888 | bytes 7865856 | tf_op jit(solution)/shard_map/dot_general | solution.py:17
  23.4 43.8 %collective-permute-start.1 = (f32[1024,512]{1,0:T(8,128)}, f32[1024,512]{1,0:T(8,128)}, u32[]{:S(2)}, u32[]{:S(2)}) collective-permute-start(f32[1024,512]{1,0:T(8,128)} %convolution_add_fusion), channel_id=1, source_target_pairs={{0,1},{1,2},{2,3},{3,4},{4,5},{5,6},{6,7},{7,8},{8,9},{9,10},{10,1... | collective-permute-start | bytes 6291464 | tf_op jit(solution)/shard_map/ppermute | solution.py:10
  67.3 5.2 %fusion.28 = f32[1024,512]{1,0:T(8,128)} fusion(bf16[1,4,1024,1024]{3,2,1,0:T(8,128)(2,1)} %param.6, bf16[1,4,512,512]{3,2,1,0:T(8,128)(2,1)} %param.7, bf16[1,1024,512]{2,1,0:T(8,128)(2,1)S(1)} %copy-done, pred[512]{0:T(512)(128)(4,1)S(1)} %iota_compare_fusion.1, pred[1024]{0:T(1024)(128)(4,1)S(1)} %iota_compare_fusion), kind=kOutput, calls=%fused_computation.22 | convolution fusion | flops 1612185600 | bytes 5768704 | tf_op jit(solution)/shard_map/dot_general | solution.py:17
  72.4 0.0 collective-permute-done.2
  72.4 0.0 collective-permute-done.1
  72.4 4.6 %multiply_reduce_fusion = (f32[]{:T(128)}, bf16[1,1024,512]{2,1,0:T(8,128)(2,1)}) fusion(bf16[1,1024,512]{2,1,0:T(8,128)(2,1)S(1)} %copy-done, pred[512]{0:T(512)(128)(4,1)S(1)} %iota_compare_fusion.1, pred[1024]{0:T(1024)(128)(4,1)S(1)} %iota_compare_fusion, f32[1024,512]{1,0:T(8,128)S(1)} %collective-permute-done.2, ...), kind=kLoop, calls=%fused_computation.10 | loop fusion | flops 4718591 | bytes 8390148 | tf_op jit(solution)/shard_map/reduce_sum | solution.py:33
  77.0 49.4 %psum.7 = f32[1]{0:T(128)} all-reduce(f32[1]{0:T(128)} %bitcast.13), channel_id=1, replica_groups=mesh['grp'=2,'sec'=16] {'sec'}, use_global_device_ids=true, to_apply=%region_1.2 | all-reduce | flops 1 | bytes 8 | tf_op jit(solution)/shard_map/psum | solution.py:34
  (2 shorter events, 0.0 us)
Async XLA Ops:
  1.9 9.2 %copy-start = (bf16[1,1024,512]{2,1,0:T(8,128)(2,1)S(1)}, bf16[1,1024,512]{2,1,0:T(8,128)(2,1)}, u32[]{:S(2)}) copy-start(bf16[1,1024,512]{2,1,0:T(8,128)(2,1)} %param.5) | copy-start | bytes 3145732
  7.5 10.1 %collective-permute-start = (f32[1024,512]{1,0:T(8,128)}, f32[1024,512]{1,0:T(8,128)}, u32[]{:S(2)}, u32[]{:S(2)}) collective-permute-start(f32[1024,512]{1,0:T(8,128)} %fusion.31), channel_id=1, source_target_pairs={{0,1},{1,2},{2,3},{3,4},{4,5},{5,6},{6,7},{7,8},{8,9},{9,10},{10,1... | collective-permute-start | bytes 6291464 | tf_op jit(solution)/shard_map/ppermute | solution.py:10
  16.3 56.1 %collective-permute-start.2 = (f32[1024,512]{1,0:T(8,128)}, f32[1024,512]{1,0:T(8,128)S(1)}, u32[]{:S(2)}, u32[]{:S(2)}) collective-permute-start(f32[1024,512]{1,0:T(8,128)} %fusion.25), channel_id=1, source_target_pairs={{1,0},{2,1},{3,2},{4,3},{5,4},{6,5},{7,6},{8,7},{9,8},{10,9},{11,1... | collective-permute-start | bytes 6291464 | tf_op jit(solution)/shard_map/ppermute | solution.py:10
  23.4 49.0 %collective-permute-start.1 = (f32[1024,512]{1,0:T(8,128)}, f32[1024,512]{1,0:T(8,128)}, u32[]{:S(2)}, u32[]{:S(2)}) collective-permute-start(f32[1024,512]{1,0:T(8,128)} %convolution_add_fusion), channel_id=1, source_target_pairs={{0,1},{1,2},{2,3},{3,4},{4,5},{5,6},{6,7},{7,8},{8,9},{9,10},{10,1... | collective-permute-start | bytes 6291464 | tf_op jit(solution)/shard_map/ppermute | solution.py:10
where the time goes:
time: 127 us; the launch traced here: 126 us
  blocking collectives  49.4 us (39%)
  starting transfers between devices  48.8 us (38%)
  matrix products  21.7 us (17%)
  other arithmetic  4.57 us (4%)
  between operations  1.97 us (2%)
    psum x1, blocking collectives, on_device(): energy = lax.psum(local_part, 'sec')  49.4 us
    ppermute x3, starting transfers between devices, shifted(): lax.ppermute(value, axis, [(source, source + steps) for source in range(i...  48.8 us
    dot_general x4, matrix products, term_block(): return jnp.dot(left, right_env[0, term], preferred_element_type=jnp.float32)  21.7 us
    reduce_sum x1, other arithmetic, on_device(): local_part = jnp.sum(psi_live.astype(jnp.float32) * total)  4.56 us
  transfers between devices with their start and end apart: 3, of which 0 were waited for; matrix products, arithmetic and copies ran while one was open for 13% of the time, Pallas kernels for 0%

commit v1 on v0

v1 whole, which is shorter than its diff:
```python
import functools

import jax
import jax.numpy as jnp
from jax import lax
from jax.experimental import pallas as pl
from jax.experimental.pallas import tpu as pltpu
from jax.sharding import PartitionSpec as P

PARTS = 2
VMEM = 48 * 1024 * 1024


def params():
    return pltpu.CompilerParams(vmem_limit_bytes=VMEM, dimension_semantics=("arbitrary",))


def mask_kernel(size_ref, psi_ref, out_ref):
    rows = lax.broadcasted_iota(jnp.int32, psi_ref.shape, 0) < size_ref[0]
    cols = lax.broadcasted_iota(jnp.int32, psi_ref.shape, 1) < size_ref[1]
    values = psi_ref[...].astype(jnp.float32)
    out_ref[...] = jnp.where(jnp.logical_and(rows, cols), values, 0.0).astype(out_ref.dtype)


def masked(psi, sizes):
    return pl.pallas_call(
        mask_kernel,
        out_shape=jax.ShapeDtypeStruct(psi.shape, psi.dtype),
        in_specs=[
            pl.BlockSpec(memory_space=pltpu.SMEM),
            pl.BlockSpec(memory_space=pltpu.VMEM),
        ],
        out_specs=pl.BlockSpec(memory_space=pltpu.VMEM),
        compiler_params=pltpu.CompilerParams(vmem_limit_bytes=VMEM),
        name="mask_psi",
    )(sizes, psi)


def term_kernel(added, term_ref, live_ref, left_ref, right_ref, *refs):
    out_ref = refs[-1]
    left = jnp.dot(left_ref[0, 0], live_ref[...], preferred_element_type=jnp.float32)
    value = jnp.dot(
        left.astype(jnp.bfloat16), right_ref[0, 0], preferred_element_type=jnp.float32
    )
    if added:
        value = value + refs[0][...]
    out_ref[...] = value


def term_rows(term, live, left_env, right_env, first, count, added=None):
    width, cols = live.shape
    block = min(256, count)
    in_specs = [
        pl.BlockSpec((width, cols), lambda i, t: (0, 0)),
        pl.BlockSpec((1, 1, block, width), lambda i, t: (0, t[0], first // block + i, 0)),
        pl.BlockSpec((1, 1, cols, cols), lambda i, t: (0, t[0], 0, 0)),
    ]
    operands = [live, left_env, right_env]
    if added is not None:
        in_specs.append(pl.BlockSpec((block, cols), lambda i, t: (i, 0)))
        operands.append(added)
    return pl.pallas_call(
        functools.partial(term_kernel, added is not None),
        out_shape=jax.ShapeDtypeStruct((count, cols), jnp.float32),
        grid_spec=pltpu.PrefetchScalarGridSpec(
            num_scalar_prefetch=1,
            grid=(count // block,),
            in_specs=in_specs,
            out_specs=pl.BlockSpec((block, cols), lambda i, t: (i, 0)),
        ),
        compiler_params=params(),
        cost_estimate=pl.CostEstimate(
            flops=2 * count * cols * (width + cols),
            bytes_accessed=2 * (width * cols + count * width + cols * cols) + 4 * count * cols,
            transcendentals=0,
        ),
        name="term_rows",
    )(jnp.reshape(term, (1,)), *operands)


def finish_kernel(first, steps, info_ref, *refs):
    live_ref, own_ref, a_ref, b_ref, c_ref, before_ref = refs[:6]
    sigma_ref, energy_ref, sum_ref = refs[-3:]
    step = pl.program_id(0)
    block, cols = own_ref.shape
    which = info_ref[2]
    arrived = jnp.where(
        which == 0, a_ref[...], jnp.where(which == 1, b_ref[...], c_ref[...])
    )
    total = own_ref[...] + arrived
    row = lax.broadcasted_iota(jnp.int32, (block, cols), 0) + (first + step * block)
    col = lax.broadcasted_iota(jnp.int32, (block, cols), 1)
    inside = jnp.logical_and(row < info_ref[0], col < info_ref[1])
    total = jnp.where(inside, total, 0.0)
    sigma_ref[0] = total.astype(sigma_ref.dtype)
    part = jnp.sum(
        jnp.reshape(live_ref[...].astype(jnp.float32) * total, (block // 8, 8, cols)), axis=0
    )

    @pl.when(step == 0)
    def _():
        sum_ref[...] = jnp.zeros_like(sum_ref)

    sum_ref[...] += part

    @pl.when(step == steps - 1)
    def _():
        energy_ref[0] = before_ref[0] + jnp.sum(sum_ref[...])


def finish(info, live, own, arrivals, before, sigma, first):
    count, cols = own.shape
    block = min(256, count)
    base = first // block

    def arrival(which):
        return pl.BlockSpec((block, cols), lambda i, n: (jnp.where(n[2] == which, i, 0), 0))

    in_specs = [
        pl.BlockSpec((block, cols), lambda i, n: (base + i, 0)),
        pl.BlockSpec((block, cols), lambda i, n: (i, 0)),
        arrival(0),
        arrival(1),
        arrival(2),
        pl.BlockSpec(memory_space=pltpu.SMEM),
    ]
    operands = [live, own, *arrivals, before]
    aliases = {}
    if sigma is not None:
        in_specs.append(pl.BlockSpec(memory_space=pl.ANY))
        operands.append(sigma)
        aliases = {len(operands): 0}
    steps = count // block
    return pl.pallas_call(
        functools.partial(finish_kernel, first, steps),
        out_shape=(
            jax.ShapeDtypeStruct((1, *live.shape), jnp.bfloat16),
            jax.ShapeDtypeStruct((1,), jnp.float32),
        ),
        grid_spec=pltpu.PrefetchScalarGridSpec(
            num_scalar_prefetch=1,
            grid=(steps,),
            in_specs=in_specs,
            out_specs=[
                pl.BlockSpec((1, block, cols), lambda i, n: (0, base + i, 0)),
                pl.BlockSpec(memory_space=pltpu.SMEM),
            ],
            scratch_shapes=[pltpu.VMEM((8, cols), jnp.float32)],
        ),
        input_output_aliases=aliases,
        compiler_params=params(),
        cost_estimate=pl.CostEstimate(
            flops=4 * count * cols, bytes_accessed=12 * count * cols, transcendentals=0
        ),
        name="finish_rows",
    )(info, *operands)


def on_device(psi, left_env, right_env, row_sizes, col_sizes):
    sectors = lax.axis_size("sec")
    sector = lax.axis_index("sec")
    even = sector % 2 == 0
    place = sector % 4

    def send(value, *hops):
        pairs = [
            (s, s + steps)
            for at, steps in hops
            for s in range(at, sectors, 4)
            if 0 <= s + steps < sectors
        ]
        return lax.ppermute(value, "sec", pairs)

    rows = psi.shape[1]
    part = rows // PARTS
    sizes = jnp.concatenate([row_sizes, col_sizes])
    live = masked(psi[0], sizes)
    one = jnp.where(even, 2, 1).astype(jnp.int32)
    two = jnp.where(even, 3, 2).astype(jnp.int32)
    three = jnp.where(even, 1, 3).astype(jnp.int32)

    first_blocks, second_blocks = [], []
    for p in range(PARTS):
        first_blocks.append(term_rows(one, live, left_env, right_env, p * part, part))
    for p in range(PARTS):
        second_blocks.append(term_rows(two, live, left_env, right_env, p * part, part))

    raised, relayed = [], []
    for p in range(PARTS):
        pair = send(first_blocks[p], (0, 1), (2, 1))
        both = first_blocks[p] + pair
        pairs_up = [(s, s + 1) for s in range(1, sectors, 4) if s + 1 < sectors]
        pairs_up += [(s, s - 3) for s in range(3, sectors, 4) if s + 1 < sectors]
        raised.append(lax.ppermute(both, "sec", pairs_up))
    crossed = []
    for p in range(PARTS):
        along = send(second_blocks[p], (3, 3), (0, -3))
        crossed.append(send(second_blocks[p] + along, (1, 2), (2, -1)))
    for p in range(PARTS):
        relayed.append(send(raised[p], (0, 4)))

    swapped, own = [], []
    for p in range(PARTS):
        third = term_rows(three, live, left_env, right_env, p * part, part)
        swapped.append(send(third, (0, 1), (1, -1), (2, 1), (3, -1)))
    for p in range(PARTS):
        own.append(
            term_rows(jnp.int32(0), live, left_env, right_env, p * part, part, swapped[p])
        )

    which = jnp.where(place == 0, 1, jnp.where(place == 2, 0, 2)).astype(jnp.int32)
    info = jnp.concatenate([sizes, jnp.reshape(which, (1,))])
    energy, sigma = jnp.zeros((1,), jnp.float32), None
    for p in range(PARTS):
        sigma, energy = finish(
            info, live, own[p], (raised[p], relayed[p], crossed[p]), energy, sigma, p * part
        )
    return sigma, lax.psum(energy, "sec")


def solution(mesh):
    return jax.shard_map(
        on_device,
        mesh=mesh,
        in_specs=(
            P(("grp", "sec"), None, None),
            P(("grp", "sec"), None, None, None),
            P(("grp", "sec"), None, None, None),
            P(("grp", "sec")),
            P(("grp", "sec")),
        ),
        out_specs=(P(("grp", "sec"), None, None), P("grp")),
        check_vma=False,
    )
```

time: 127 us -> 118 us (0.929)
  Pallas kernels: 0 us -> 30.9 us
  matrix products: 21.7 us -> 0 us
  starting transfers between devices: 48.8 us -> 32.6 us
  blocking collectives: 49.4 us -> 33.5 us
  local copies, waits for them, and re-layouts: 0.01 us -> 5.02 us
  other arithmetic: 4.57 us -> 9.19 us
  waiting for transfers between devices: 0.01 us -> 3.76 us
    pallas_call x0 -> x11, Pallas kernels: none -> 30.9 us  [the longest x8 23.1 us: term_rows(): pl.pallas_call(functools.partial(term_kernel, added is not None), out_sha...]
    dot_general x4 -> x0, matrix products: 21.7 us -> none  [term_block(): return jnp.dot(left, right_env[0, term], preferred_element_type=jnp.float32)]
    ppermute x3 -> x12, starting transfers between devices: 48.8 us -> 32.6 us  [the longest x10 30 us: send(): return lax.ppermute(value, 'sec', pairs)]
    psum x1, blocking collectives: 49.4 us -> 33.5 us  [on_device(): return (sigma, lax.psum(energy, 'sec'))]
    add x0 -> x4, other arithmetic: none -> 9.03 us  [the longest x2 5.54 us: on_device(): crossed.append(send(second_blocks[p] + along, (1, 2), (2, -1)))]
    unnamed x2 -> x10, local copies, waits for them, and re-layouts: 0.01 us -> 5.02 us
    reduce_sum x1 -> x0, other arithmetic: 4.56 us -> none  [on_device(): local_part = jnp.sum(psi_live.astype(jnp.float32) * total)]
    ppermute x3 -> x12, waiting for transfers between devices: 0.01 us -> 3.76 us  [the longest x10 2.25 us: send(): return lax.ppermute(value, 'sec', pairs)]
  transfers between devices with their start and end apart: 3 -> 12, of which waited for: 0 -> 2; matrix products, arithmetic and copies ran while one was open for 13% -> 8% of each run, Pallas kernels for 0% -> 20%
where the time goes in v1:
time: 118 us; the launch traced here: 117 us
  blocking collectives  33.5 us (28%)
  starting transfers between devices  32.6 us (28%)
  Pallas kernels  30.9 us (26%)
  other arithmetic  9.19 us (8%)
  local copies, waits for them, and re-layouts  5.02 us (4%)
  waiting for transfers between devices  3.76 us (3%)
  between operations  2.04 us (2%)
    psum x1, blocking collectives, on_device(): return (sigma, lax.psum(energy, 'sec'))  33.5 us
    ppermute x10, starting transfers between devices, send(): return lax.ppermute(value, 'sec', pairs)  30 us
    pallas_call x8, Pallas kernels, term_rows(): pl.pallas_call(functools.partial(term_kernel, added is not None), out_sha...  23.1 us
    pallas_call x2, Pallas kernels, finish(): pl.pallas_call(functools.partial(finish_kernel, first, steps), out_shape=...  6.93 us
    add x2, other arithmetic, on_device(): crossed.append(send(second_blocks[p] + along, (1, 2), (2, -1)))  5.54 us
    unnamed x10, local copies, waits for them, and re-layouts  5.02 us
    add x2, other arithmetic, on_device(): both = first_blocks[p] + pair  3.5 us
    ppermute x2, starting transfers between devices, on_device(): raised.append(lax.ppermute(both, 'sec', pairs_up))  2.58 us
  transfers between devices with their start and end apart: 12, of which 2 were waited for; matrix products, arithmetic and copies ran while one was open for 8% of the time, Pallas kernels for 20%

profile of v1, /device:TPU:0, one launch (start us, length us, event | category | flops | bytes accessed | tf_op | source)
XLA Modules:
  0.0 117.0 jit_solution(576452578886140818)
XLA Ops:
  5.7 3.2 %term_rows.14 = f32[512,512]{1,0:T(8,128)} custom-call(s32[1]{0:T(128)} %bitcast.3.term_ref, bf16[1024,512]{1,0:T(8,128)(2,1)S(1)} %mask_psi.1.live_ref.refs_0_, bf16[1,4,1024,1024]{3,2,1,0:T(8,128)(2,1)} %left_ref.15, bf16[1,4,512,512]{3,2,1,0:T(8,128)(2,1)S(1)} %copy-done), custom_call_target="tpu_custom_call" | custom-call | flops 805306368 | bytes 3670016 | tf_op jit(solution)/shard_map/term_rows/pallas_call | solution.py:62
  8.8 3.5 %collective-permute-start.7 = (f32[512,512]{1,0:T(8,128)}, f32[512,512]{1,0:T(8,128)}, u32[]{:S(2)}, u32[]{:S(2)}) collective-permute-start(f32[512,512]{1,0:T(8,128)} %term_rows.14), channel_id=1, source_target_pairs={{0,1},{4,5},{8,9},{12,13},{2,3},{6,7},{10,11},{14,15},{16,17},{20,... | collective-permute-start | bytes 3145736 | tf_op jit(solution)/shard_map/ppermute | solution.py:172
  12.3 3.1 %term_rows.10 = f32[512,512]{1,0:T(8,128)} custom-call(s32[1]{0:T(128)} %bitcast.3.term_ref, bf16[1024,512]{1,0:T(8,128)(2,1)S(1)} %mask_psi.1.live_ref.refs_0_, bf16[1,4,1024,1024]{3,2,1,0:T(8,128)(2,1)} %left_ref.15, bf16[1,4,512,512]{3,2,1,0:T(8,128)(2,1)S(1)} %copy-done), custom_call_target="tpu_custom_call" | custom-call | flops 805306368 | bytes 3670016 | tf_op jit(solution)/shard_map/term_rows/pallas_call | solution.py:62
  15.5 2.3 %collective-permute-start.1 = (f32[512,512]{1,0:T(8,128)}, f32[512,512]{1,0:T(8,128)}, u32[]{:S(2)}, u32[]{:S(2)}) collective-permute-start(f32[512,512]{1,0:T(8,128)} %term_rows.10), channel_id=1, source_target_pairs={{0,1},{4,5},{8,9},{12,13},{2,3},{6,7},{10,11},{14,15},{16,17},{20,... | collective-permute-start | bytes 3145736 | tf_op jit(solution)/shard_map/ppermute | solution.py:172
  17.7 3.2 %term_rows.15 = f32[512,512]{1,0:T(8,128)} custom-call(s32[1]{0:T(128)} %bitcast.4.term_ref, bf16[1024,512]{1,0:T(8,128)(2,1)S(1)} %mask_psi.1.live_ref.refs_0_, bf16[1,4,1024,1024]{3,2,1,0:T(8,128)(2,1)} %left_ref.15, bf16[1,4,512,512]{3,2,1,0:T(8,128)(2,1)S(1)} %copy-done.1), custom_call_target="tpu_custom_call" | custom-call | flops 805306368 | bytes 3670016 | tf_op jit(solution)/shard_map/term_rows/pallas_call | solution.py:62
  20.9 1.7 %collective-permute-start.10 = (f32[512,512]{1,0:T(8,128)}, f32[512,512]{1,0:T(8,128)}, u32[]{:S(2)}, u32[]{:S(2)}) collective-permute-start(f32[512,512]{1,0:T(8,128)} %term_rows.15), channel_id=1, source_target_pairs={{3,6},{7,10},{11,14},{4,1},{8,5},{12,9},{19,22},{23,26},{27,30},{2... | collective-permute-start | bytes 3145736 | tf_op jit(solution)/shard_map/ppermute | solution.py:172
  22.6 3.2 %term_rows.11 = f32[512,512]{1,0:T(8,128)} custom-call(s32[1]{0:T(128)} %bitcast.4.term_ref, bf16[1024,512]{1,0:T(8,128)(2,1)S(1)} %mask_psi.1.live_ref.refs_0_, bf16[1,4,1024,1024]{3,2,1,0:T(8,128)(2,1)} %left_ref.15, bf16[1,4,512,512]{3,2,1,0:T(8,128)(2,1)S(1)} %copy-done.1), custom_call_target="tpu_custom_call" | custom-call | flops 805306368 | bytes 3670016 | tf_op jit(solution)/shard_map/term_rows/pallas_call | solution.py:62
  27.4 1.7 %add.25 = f32[512,512]{1,0:T(8,128)S(1)} add(f32[512,512]{1,0:T(8,128)} %term_rows.14, f32[512,512]{1,0:T(8,128)} %collective-permute-done.7) | non-fusion elementwise | flops 262144 | bytes 3145728 | tf_op jit(solution)/shard_map/add | solution.py:191
  30.4 2.4 %term_rows.12 = f32[512,512]{1,0:T(8,128)S(1)} custom-call(s32[1]{0:T(128)} %bitcast.2.term_ref, bf16[1024,512]{1,0:T(8,128)(2,1)S(1)} %mask_psi.1.live_ref.refs_0_, bf16[1,4,1024,1024]{3,2,1,0:T(8,128)(2,1)} %left_ref.15, bf16[1,4,512,512]{3,2,1,0:T(8,128)(2,1)S(1)} %copy-done.1), custom_call_target="tpu_custom_call" | custom-call | flops 805306368 | bytes 3670016 | tf_op jit(solution)/shard_map/term_rows/pallas_call | solution.py:62
  32.8 4.1 %collective-permute-start.6 = (f32[512,512]{1,0:T(8,128)S(1)}, f32[512,512]{1,0:T(8,128)S(1)}, u32[]{:S(2)}, u32[]{:S(2)}) collective-permute-start(f32[512,512]{1,0:T(8,128)S(1)} %term_rows.12), channel_id=1, source_target_pairs={{0,1},{4,5},{8,9},{12,13},{1,0},{5,4},{9,8},{13,12},{2,3},{6,7},{1... | collective-permute-start | bytes 3145736 | tf_op jit(solution)/shard_map/ppermute | solution.py:172
  36.9 1.7 %add.23 = f32[512,512]{1,0:T(8,128)S(1)} add(f32[512,512]{1,0:T(8,128)} %term_rows.10, f32[512,512]{1,0:T(8,128)} %collective-permute-done.1) | non-fusion elementwise | flops 262144 | bytes 3145728 | tf_op jit(solution)/shard_map/add | solution.py:191
  40.0 3.2 %term_rows.8 = f32[512,512]{1,0:T(8,128)} custom-call(s32[1]{0:T(128)} %bitcast.2.term_ref, bf16[1024,512]{1,0:T(8,128)(2,1)S(1)} %mask_psi.1.live_ref.refs_0_, bf16[1,4,1024,1024]{3,2,1,0:T(8,128)(2,1)} %left_ref.15, bf16[1,4,512,512]{3,2,1,0:T(8,128)(2,1)S(1)} %copy-done.1), custom_call_target="tpu_custom_call" | custom-call | flops 805306368 | bytes 3670016 | tf_op jit(solution)/shard_map/term_rows/pallas_call | solution.py:62
  43.2 4.5 %collective-permute-start = (f32[512,512]{1,0:T(8,128)}, f32[512,512]{1,0:T(8,128)}, u32[]{:S(2)}, u32[]{:S(2)}) collective-permute-start(f32[512,512]{1,0:T(8,128)} %term_rows.8), channel_id=1, source_target_pairs={{0,1},{4,5},{8,9},{12,13},{1,0},{5,4},{9,8},{13,12},{2,3},{6,7},{1... | collective-permute-start | bytes 3145736 | tf_op jit(solution)/shard_map/ppermute | solution.py:172
  47.7 2.8 %add.26 = f32[512,512]{1,0:T(8,128)} add(f32[512,512]{1,0:T(8,128)} %term_rows.15, f32[512,512]{1,0:T(8,128)} %collective-permute-done.10) | non-fusion elementwise | flops 262144 | bytes 3145728 | tf_op jit(solution)/shard_map/add | solution.py:198
  52.2 4.5 %collective-permute-start.9 = (f32[512,512]{1,0:T(8,128)}, f32[512,512]{1,0:T(8,128)}, u32[]{:S(2)}, u32[]{:S(2)}) collective-permute-start(f32[512,512]{1,0:T(8,128)} %collective-permute-done.8.refs_2_), channel_id=1, source_target_pairs={{0,4},{4,8},{8,12},{16,20},{20,24},{24,28}} | collective-permute-start | bytes 3145736 | tf_op jit(solution)/shard_map/ppermute | solution.py:172
  56.6 2.7 %add.24 = f32[512,512]{1,0:T(8,128)} add(f32[512,512]{1,0:T(8,128)} %term_rows.11, f32[512,512]{1,0:T(8,128)} %collective-permute-done.4) | non-fusion elementwise | flops 262144 | bytes 3145728 | tf_op jit(solution)/shard_map/add | solution.py:198
  60.4 1.7 %collective-permute-start.5 = (f32[512,512]{1,0:T(8,128)}, f32[512,512]{1,0:T(8,128)}, u32[]{:S(2)}, u32[]{:S(2)}) collective-permute-start(f32[512,512]{1,0:T(8,128)} %add.24), channel_id=1, source_target_pairs={{1,3},{5,7},{9,11},{13,15},{2,1},{6,5},{10,9},{14,13},{17,19},{21,... | collective-permute-start | bytes 3145736 | tf_op jit(solution)/shard_map/ppermute | solution.py:172
  63.6 4.4 %collective-permute-start.3 = (f32[512,512]{1,0:T(8,128)}, f32[512,512]{1,0:T(8,128)}, u32[]{:S(2)}, u32[]{:S(2)}) collective-permute-start(f32[512,512]{1,0:T(8,128)} %collective-permute-done.2.refs_2_), channel_id=1, source_target_pairs={{0,4},{4,8},{8,12},{16,20},{20,24},{24,28}} | collective-permute-start | bytes 3145736 | tf_op jit(solution)/shard_map/ppermute | solution.py:172
  69.3 2.4 %term_rows.13.refs_1_ = f32[512,512]{1,0:T(8,128)S(1)} custom-call(s32[1]{0:T(128)} %constant.32.clone.1.term_ref, bf16[1024,512]{1,0:T(8,128)(2,1)S(1)} %mask_psi.1.live_ref.refs_0_, bf16[1,4,1024,1024]{3,2,1,0:T(8,128)(2,1)} %left_ref.15, bf16[1,4,512,512]{3,2,1,0:T(8,128)(2,1)S(1)} %copy-done.1, f32[512,512]{1,0:T(8,128)S(1)} %copy-done.4), custom_call_target="tpu_custom_call" | custom-call | flops 805306368 | bytes 3670016 | tf_op jit(solution)/shard_map/term_rows/pallas_call | solution.py:62
  71.7 2.6 %term_rows.9.refs_1_ = f32[512,512]{1,0:T(8,128)S(1)} custom-call(s32[1]{0:T(128)} %constant.32.clone.1.term_ref, bf16[1024,512]{1,0:T(8,128)(2,1)S(1)} %mask_psi.1.live_ref.refs_0_, bf16[1,4,1024,1024]{3,2,1,0:T(8,128)(2,1)} %left_ref.15, bf16[1,4,512,512]{3,2,1,0:T(8,128)(2,1)S(1)} %copy-done.1, f32[512,512]{1,0:T(8,128)} %collective-permute-done.refs_0_), custom_call_target="tpu_custom_call" | custom-call | flops 805306368 | bytes 3670016 | tf_op jit(solution)/shard_map/term_rows/pallas_call | solution.py:62
  74.3 3.1 %finish_rows.2 = (bf16[1,1024,512]{2,1,0:T(8,128)(2,1)}, f32[1]{0:T(128)}) custom-call(s32[3]{0:T(128)S(1)} %pad_add_fusion.info_ref, bf16[1024,512]{1,0:T(8,128)(2,1)S(1)} %mask_psi.1.live_ref.refs_0_, f32[512,512]{1,0:T(8,128)S(1)} %term_rows.13.refs_1_, f32[512,512]{1,0:T(8,128)} %collective-permute-done.8.refs_2_, ...), custom_call_target="tpu_custom_call" | custom-call | flops 1048576 | bytes 3145728 | tf_op jit(solution)/shard_map/finish_rows/pallas_call | solution.py:134
  77.4 2.2 %collective-permute-done.3.refs_3_ = f32[512,512]{1,0:T(8,128)} collective-permute-done((f32[512,512]{1,0:T(8,128)}, f32[512,512]{1,0:T(8,128)}, u32[]{:S(2)}, u32[]{:S(2)}) %collective-permute-start.3) | collective-permute-done | bytes 1048608 | tf_op jit(solution)/shard_map/ppermute | solution.py:172
  79.7 3.8 %finish_rows.3 = (bf16[1,1024,512]{2,1,0:T(8,128)(2,1)}, f32[1]{0:T(128)}) custom-call(s32[3]{0:T(128)S(1)} %pad_add_fusion.info_ref, bf16[1024,512]{1,0:T(8,128)(2,1)S(1)} %mask_psi.1.live_ref.refs_0_, f32[512,512]{1,0:T(8,128)S(1)} %term_rows.9.refs_1_, f32[512,512]{1,0:T(8,128)} %collective-permute-done.2.refs_2_, ...), custom_call_target="tpu_custom_call", output_to_operand_aliasing={{0}: (7, {})} | custom-call | flops 1048576 | bytes 3145728 | tf_op jit(solution)/shard_map/finish_rows/pallas_call | solution.py:134
  83.5 33.5 %psum.7 = f32[1]{0:T(128)} all-reduce(f32[1]{0:T(128)} %get-tuple-element.9), channel_id=1, replica_groups=mesh['grp'=2,'sec'=16] {'sec'}, use_global_device_ids=true, to_apply=%region_0.1 | all-reduce | flops 1 | bytes 8 | tf_op jit(solution)/shard_map/psum | solution.py:218
  (28 shorter events, 13.4 us)
Async XLA Ops:
  2.0 1.2 %copy-start.2 = (bf16[1,1024,512]{2,1,0:T(8,128)(2,1)S(1)}, bf16[1,1024,512]{2,1,0:T(8,128)(2,1)}, u32[]{:S(2)}) copy-start(bf16[1,1024,512]{2,1,0:T(8,128)(2,1)} %param.5) | copy-start | bytes 3145732
  4.1 1.6 %copy-start = (bf16[1,4,512,512]{3,2,1,0:T(8,128)(2,1)S(1)}, bf16[1,4,512,512]{3,2,1,0:T(8,128)(2,1)}, u32[]{:S(2)}) copy-start(bf16[1,4,512,512]{3,2,1,0:T(8,128)(2,1)} %right_ref.15) | copy-start | bytes 6291460
  8.8 8.9 %copy-start.1 = (bf16[1,4,512,512]{3,2,1,0:T(8,128)(2,1)S(1)}, bf16[1,4,512,512]{3,2,1,0:T(8,128)(2,1)}, u32[]{:S(2)}) copy-start(bf16[1,4,512,512]{3,2,1,0:T(8,128)(2,1)} %right_ref.15) | copy-start | bytes 6291460
  8.8 18.5 %collective-permute-start.7 = (f32[512,512]{1,0:T(8,128)}, f32[512,512]{1,0:T(8,128)}, u32[]{:S(2)}, u32[]{:S(2)}) collective-permute-start(f32[512,512]{1,0:T(8,128)} %term_rows.14), channel_id=1, source_target_pairs={{0,1},{4,5},{8,9},{12,13},{2,3},{6,7},{10,11},{14,15},{16,17},{20,... | collective-permute-start | bytes 3145736 | tf_op jit(solution)/shard_map/ppermute | solution.py:172
  15.5 21.5 %collective-permute-start.1 = (f32[512,512]{1,0:T(8,128)}, f32[512,512]{1,0:T(8,128)}, u32[]{:S(2)}, u32[]{:S(2)}) collective-permute-start(f32[512,512]{1,0:T(8,128)} %term_rows.10), channel_id=1, source_target_pairs={{0,1},{4,5},{8,9},{12,13},{2,3},{6,7},{10,11},{14,15},{16,17},{20,... | collective-permute-start | bytes 3145736 | tf_op jit(solution)/shard_map/ppermute | solution.py:172
  20.9 22.2 %collective-permute-start.10 = (f32[512,512]{1,0:T(8,128)}, f32[512,512]{1,0:T(8,128)}, u32[]{:S(2)}, u32[]{:S(2)}) collective-permute-start(f32[512,512]{1,0:T(8,128)} %term_rows.15), channel_id=1, source_target_pairs={{3,6},{7,10},{11,14},{4,1},{8,5},{12,9},{19,22},{23,26},{27,30},{2... | collective-permute-start | bytes 3145736 | tf_op jit(solution)/shard_map/ppermute | solution.py:172
  25.8 24.7 %collective-permute-start.4 = (f32[512,512]{1,0:T(8,128)}, f32[512,512]{1,0:T(8,128)}, u32[]{:S(2)}, u32[]{:S(2)}) collective-permute-start(f32[512,512]{1,0:T(8,128)} %term_rows.11), channel_id=1, source_target_pairs={{3,6},{7,10},{11,14},{4,1},{8,5},{12,9},{19,22},{23,26},{27,30},{2... | collective-permute-start | bytes 3145736 | tf_op jit(solution)/shard_map/ppermute | solution.py:172
  29.1 23.0 %collective-permute-start.8 = (f32[512,512]{1,0:T(8,128)S(1)}, f32[512,512]{1,0:T(8,128)}, u32[]{:S(2)}, u32[]{:S(2)}) collective-permute-start(f32[512,512]{1,0:T(8,128)S(1)} %add.25), channel_id=1, source_target_pairs={{1,2},{5,6},{9,10},{13,14},{3,0},{7,4},{11,8},{17,18},{21,22},{25,... | collective-permute-start | bytes 3145736 | tf_op jit(solution)/shard_map/ppermute | solution.py:194
  32.8 26.6 %collective-permute-start.6 = (f32[512,512]{1,0:T(8,128)S(1)}, f32[512,512]{1,0:T(8,128)S(1)}, u32[]{:S(2)}, u32[]{:S(2)}) collective-permute-start(f32[512,512]{1,0:T(8,128)S(1)} %term_rows.12), channel_id=1, source_target_pairs={{0,1},{4,5},{8,9},{12,13},{1,0},{5,4},{9,8},{13,12},{2,3},{6,7},{1... | collective-permute-start | bytes 3145736 | tf_op jit(solution)/shard_map/ppermute | solution.py:172
  38.7 24.9 %collective-permute-start.2 = (f32[512,512]{1,0:T(8,128)S(1)}, f32[512,512]{1,0:T(8,128)}, u32[]{:S(2)}, u32[]{:S(2)}) collective-permute-start(f32[512,512]{1,0:T(8,128)S(1)} %add.23), channel_id=1, source_target_pairs={{1,2},{5,6},{9,10},{13,14},{3,0},{7,4},{11,8},{17,18},{21,22},{25,... | collective-permute-start | bytes 3145736 | tf_op jit(solution)/shard_map/ppermute | solution.py:194
  43.2 28.5 %collective-permute-start = (f32[512,512]{1,0:T(8,128)}, f32[512,512]{1,0:T(8,128)}, u32[]{:S(2)}, u32[]{:S(2)}) collective-permute-start(f32[512,512]{1,0:T(8,128)} %term_rows.8), channel_id=1, source_target_pairs={{0,1},{4,5},{8,9},{12,13},{1,0},{5,4},{9,8},{13,12},{2,3},{6,7},{1... | collective-permute-start | bytes 3145736 | tf_op jit(solution)/shard_map/ppermute | solution.py:172
  50.5 23.8 %collective-permute-start.11 = (f32[512,512]{1,0:T(8,128)}, f32[512,512]{1,0:T(8,128)}, u32[]{:S(2)}, u32[]{:S(2)}) collective-permute-start(f32[512,512]{1,0:T(8,128)} %add.26), channel_id=1, source_target_pairs={{1,3},{5,7},{9,11},{13,15},{2,1},{6,5},{10,9},{14,13},{17,19},{21,... | collective-permute-start | bytes 3145736 | tf_op jit(solution)/shard_map/ppermute | solution.py:172
  52.2 22.1 %collective-permute-start.9 = (f32[512,512]{1,0:T(8,128)}, f32[512,512]{1,0:T(8,128)}, u32[]{:S(2)}, u32[]{:S(2)}) collective-permute-start(f32[512,512]{1,0:T(8,128)} %collective-permute-done.8.refs_2_), channel_id=1, source_target_pairs={{0,4},{4,8},{8,12},{16,20},{20,24},{24,28}} | collective-permute-start | bytes 3145736 | tf_op jit(solution)/shard_map/ppermute | solution.py:172
  59.4 1.0 copy-start.3
  60.4 17.1 %collective-permute-start.5 = (f32[512,512]{1,0:T(8,128)}, f32[512,512]{1,0:T(8,128)}, u32[]{:S(2)}, u32[]{:S(2)}) collective-permute-start(f32[512,512]{1,0:T(8,128)} %add.24), channel_id=1, source_target_pairs={{1,3},{5,7},{9,11},{13,15},{2,1},{6,5},{10,9},{14,13},{17,19},{21,... | collective-permute-start | bytes 3145736 | tf_op jit(solution)/shard_map/ppermute | solution.py:172
  63.6 16.1 %collective-permute-start.3 = (f32[512,512]{1,0:T(8,128)}, f32[512,512]{1,0:T(8,128)}, u32[]{:S(2)}, u32[]{:S(2)}) collective-permute-start(f32[512,512]{1,0:T(8,128)} %collective-permute-done.2.refs_2_), channel_id=1, source_target_pairs={{0,4},{4,8},{8,12},{16,20},{20,24},{24,28}} | collective-permute-start | bytes 3145736 | tf_op jit(solution)/shard_map/ppermute | solution.py:172
  68.1 1.2 %copy-start.4 = (f32[512,512]{1,0:T(8,128)S(1)}, f32[512,512]{1,0:T(8,128)}, u32[]{:S(2)}) copy-start(f32[512,512]{1,0:T(8,128)} %copy-done.3) | copy-start | bytes 3145732

commit v2 on v0

v2 whole, which is shorter than its diff:
```python
import functools

import jax
import jax.numpy as jnp
from jax import lax
from jax.experimental import pallas as pl
from jax.experimental.pallas import tpu as pltpu
from jax.sharding import PartitionSpec as P

PARTS = 2
MIB = 1024 * 1024

ANY = pl.BlockSpec(memory_space=pl.ANY)
HBM = pl.BlockSpec(memory_space=pltpu.HBM)
SMEM = pl.BlockSpec(memory_space=pltpu.SMEM)
WHOLE = pl.BlockSpec(memory_space=pltpu.VMEM)


def params(mib=8):
    return pltpu.CompilerParams(vmem_limit_bytes=mib * MIB)


def term_kernel(slot, first, blocks, masks, adds, tokens, *refs):
    refs = list(refs)
    info_ref, live_ref, left_hbm, right_hbm = refs[:4]
    refs = refs[4:]
    add_ref = refs.pop(0) if adds else None
    refs = refs[tokens:]
    out_ref = refs.pop(0)
    live_out = refs.pop(0) if masks else None
    left_buf, right_buf = refs[:2]
    sems = refs[-1]
    psi_buf = refs[2] if masks else None
    block = left_buf.shape[1]
    term = info_ref[slot]
    copies = []
    if masks:
        psi_copy = pltpu.make_async_copy(live_ref, psi_buf, sems.at[blocks + 1])
        psi_copy.start()
    for i in range(blocks):
        copy = pltpu.make_async_copy(
            left_hbm.at[0, term, pl.ds(first + i * block, block), :], left_buf.at[i], sems.at[i]
        )
        copy.start()
        copies.append(copy)
        if i == 0:
            right_copy = pltpu.make_async_copy(
                right_hbm.at[0, term], right_buf, sems.at[blocks]
            )
            right_copy.start()
    if masks:
        psi_copy.wait()
        rows, cols = psi_buf.shape
        step = 128
        col = lax.broadcasted_iota(jnp.int32, (step, cols), 1) < info_ref[5]
        row = lax.broadcasted_iota(jnp.int32, (step, cols), 0)
        for r in range(0, rows, step):
            inside = jnp.logical_and(row < info_ref[4] - r, col)
            values = psi_buf[r : r + step, :].astype(jnp.float32)
            live_out[r : r + step, :] = jnp.where(inside, values, 0.0).astype(jnp.bfloat16)
        live_ref = live_out
    for i in range(blocks):
        copies[i].wait()
        left = jnp.dot(left_buf[i], live_ref[...], preferred_element_type=jnp.float32)
        if i == 0:
            right_copy.wait()
        value = jnp.dot(
            left.astype(jnp.bfloat16), right_buf[...], preferred_element_type=jnp.float32
        )
        span = pl.ds(i * block, block)
        if adds:
            value = value + add_ref[span, :]
        out_ref[span, :] = value


def term_rows(
    info, slot, live, left_env, right_env, first, count, block, masks=False, added=None, tokens=()
):
    width, cols = live.shape[-2:]
    blocks = count // block
    in_specs = [SMEM, HBM if masks else WHOLE, HBM, HBM]
    operands = [info, live, left_env, right_env]
    if added is not None:
        in_specs.append(WHOLE)
        operands.append(added)
    in_specs += [ANY] * len(tokens)
    operands += tokens
    out_shape = [jax.ShapeDtypeStruct((count, cols), jnp.float32)]
    scratch = [
        pltpu.VMEM((blocks, block, width), jnp.bfloat16),
        pltpu.VMEM((cols, cols), jnp.bfloat16),
    ]
    if masks:
        out_shape.append(jax.ShapeDtypeStruct((width, cols), jnp.bfloat16))
        scratch.append(pltpu.VMEM((width, cols), jnp.bfloat16))
    scratch.append(pltpu.SemaphoreType.DMA((blocks + 2,)))
    out = pl.pallas_call(
        functools.partial(
            term_kernel, slot, first, blocks, masks, added is not None, len(tokens)
        ),
        out_shape=out_shape,
        in_specs=in_specs,
        out_specs=[WHOLE] * len(out_shape),
        scratch_shapes=scratch,
        compiler_params=params(50),
        cost_estimate=pl.CostEstimate(
            flops=2 * count * cols * (width + cols),
            bytes_accessed=2 * (count * width + cols * cols) + 4 * count * cols,
            transcendentals=0,
        ),
        name=f"term_slot{slot}",
    )(*operands)
    return out if masks else out[0]


def add_kernel(a_ref, b_ref, out_ref):
    rows = a_ref.shape[0]
    step = 64

    def body(i, _):
        span = pl.ds(pl.multiple_of(i * step, step), step)
        out_ref[span, :] = a_ref[span, :] + b_ref[span, :]
        return _

    lax.fori_loop(0, rows // step, body, 0)


def add(a, b):
    return pl.pallas_call(
        add_kernel,
        out_shape=jax.ShapeDtypeStruct(a.shape, a.dtype),
        in_specs=[WHOLE, WHOLE],
        out_specs=WHOLE,
        compiler_params=params(),
        cost_estimate=pl.CostEstimate(flops=a.size, bytes_accessed=12 * a.size, transcendentals=0),
        name="add_blocks",
    )(a, b)


def finish_kernel(first, steps, info_ref, live_ref, own_ref, a_ref, b_ref, c_ref, *refs):
    before_ref = refs[0]
    sigma_ref, energy_ref, sum_ref = refs[-3:]
    step = pl.program_id(0)
    block, cols = sigma_ref.shape[1:]
    span = pl.ds(pl.multiple_of(step * block, block), block)
    row = lax.broadcasted_iota(jnp.int32, (block, cols), 0) + (first + step * block)
    col = lax.broadcasted_iota(jnp.int32, (block, cols), 1)
    inside = jnp.logical_and(row < info_ref[4], col < info_ref[5])

    @pl.when(step == 0)
    def _():
        sum_ref[...] = jnp.zeros_like(sum_ref)

    def work(arrival):
        total = jnp.where(inside, own_ref[span, :] + arrival[span, :], 0.0)
        sigma_ref[0] = total.astype(sigma_ref.dtype)
        here = pl.ds(pl.multiple_of(first + step * block, block), block)
        product = live_ref[here, :].astype(jnp.float32) * total
        sum_ref[...] += jnp.sum(jnp.reshape(product, (block // 8, 8, cols)), axis=0)

    for n, arrival in enumerate((a_ref, b_ref, c_ref)):
        pl.when(info_ref[6] == n)(functools.partial(work, arrival))

    @pl.when(step == steps - 1)
    def _():
        energy_ref[0] = before_ref[0] + jnp.sum(sum_ref[...])


def finish(info, live, own, arrivals, before, sigma, first):
    count, cols = own.shape
    block = 128
    base = first // block
    steps = count // block
    in_specs = [SMEM] + [WHOLE] * 5 + [SMEM]
    operands = [info, live, own, *arrivals, before]
    aliases = {}
    if sigma is not None:
        in_specs.append(ANY)
        aliases = {len(operands): 0}
        operands.append(sigma)
    return pl.pallas_call(
        functools.partial(finish_kernel, first, steps),
        out_shape=(
            jax.ShapeDtypeStruct((1, *live.shape), jnp.bfloat16),
            jax.ShapeDtypeStruct((1,), jnp.float32),
        ),
        grid=(steps,),
        in_specs=in_specs,
        out_specs=[pl.BlockSpec((1, block, cols), lambda i: (0, base + i, 0)), SMEM],
        scratch_shapes=[pltpu.VMEM((8, cols), jnp.float32)],
        input_output_aliases=aliases,
        compiler_params=params(),
        cost_estimate=pl.CostEstimate(
            flops=4 * count * cols, bytes_accessed=12 * count * cols, transcendentals=0
        ),
        name="finish_rows",
    )(*operands)


def sum_over_sectors(value, sectors):
    if sectors & (sectors - 1):
        return lax.psum(value, "sec")
    stride = 1
    while stride < sectors:
        radix = min(4, sectors // stride)
        arrived = [
            lax.ppermute(value, "sec", [(s, s ^ (n * stride)) for s in range(sectors)])
            for n in range(1, radix)
        ]
        if radix == 4:
            value = (value + arrived[0]) + (arrived[1] + arrived[2])
        else:
            value = value + arrived[0]
        stride *= radix
    return value


def on_device(psi, left_env, right_env, row_sizes, col_sizes):
    sectors = lax.axis_size("sec")
    sector = lax.axis_index("sec")
    even = sector % 2 == 0
    place = sector % 4

    def send(value, *hops):
        pairs = [
            (s, s + steps)
            for at, steps in hops
            for s in range(at, sectors, 4)
            if 0 <= s + steps < sectors
        ]
        return lax.ppermute(value, "sec", pairs)

    rows = psi.shape[1]
    part = rows // PARTS
    which = jnp.where(place == 0, 1, jnp.where(place == 2, 0, 2))
    orders = [jnp.where(even, 2, 1), jnp.where(even, 3, 2), jnp.where(even, 1, 3), 0]
    info = jnp.stack([*orders, row_sizes[0], col_sizes[0], which]).astype(jnp.int32)

    first_blocks, raised, both = [], [], []
    block, live = term_rows(info, 0, psi[0], left_env, right_env, 0, part, part, masks=True)
    first_blocks.append(block)
    for p in range(1, PARTS):
        first_blocks.append(term_rows(info, 0, live, left_env, right_env, p * part, part, part))
    pairs_up = [(s, s + 1) for s in range(1, sectors, 4) if s + 1 < sectors]
    pairs_up += [(s, s - 3) for s in range(3, sectors, 4) if s + 1 < sectors]
    for p in range(PARTS):
        both.append(add(first_blocks[p], send(first_blocks[p], (0, 1), (2, 1))))
        raised.append(lax.ppermute(both[p], "sec", pairs_up))

    crossed = []
    for p in range(PARTS):
        block = term_rows(
            info, 1, live, left_env, right_env, p * part, part, 256, tokens=(both[p],)
        )
        along = send(block, (3, 3), (0, -3))
        crossed.append(send(add(block, along), (1, 2), (2, -1)))

    swapped, own, relayed = [], [], []
    for p in range(PARTS):
        third = term_rows(
            info, 2, live, left_env, right_env, p * part, part, 128, tokens=(both[-1],)
        )
        swapped.append(send(third, (0, 1), (1, -1), (2, 1), (3, -1)))
    for p in range(PARTS):
        own.append(
            term_rows(
                info, 3, live, left_env, right_env, p * part, part, 64, added=swapped[p]
            )
        )
    for p in range(PARTS):
        relayed.append(send(raised[p], (0, 4)))

    energy, sigma = jnp.zeros((1,), jnp.float32), None
    for p in range(PARTS):
        sigma, energy = finish(
            info, live, own[p], (raised[p], relayed[p], crossed[p]), energy, sigma, p * part
        )
    return sigma, sum_over_sectors(energy, sectors)


def solution(mesh):
    return jax.shard_map(
        on_device,
        mesh=mesh,
        in_specs=(
            P(("grp", "sec"), None, None),
            P(("grp", "sec"), None, None, None),
            P(("grp", "sec"), None, None, None),
            P(("grp", "sec")),
            P(("grp", "sec")),
        ),
        out_specs=(P(("grp", "sec"), None, None), P("grp")),
        check_vma=False,
    )
```

time: 127 us -> 96.7 us (0.76)
  blocking collectives: 49.4 us -> 0 us
  Pallas kernels: 0 us -> 37.4 us
  matrix products: 21.7 us -> 0 us
  waiting for transfers between devices: 0.01 us -> 8.5 us
  starting transfers between devices: 48.8 us -> 41.1 us
  between operations: 1.97 us -> 7.76 us
  other arithmetic: 4.57 us -> 0 us
  local copies, waits for them, and re-layouts: 0.01 us -> 1.31 us
    psum x1 -> x0, blocking collectives: 49.4 us -> none  [on_device(): energy = lax.psum(local_part, 'sec')]
    pallas_call x0 -> x14, Pallas kernels: none -> 37.4 us  [the longest x8 31.4 us: term_rows(): pl.pallas_call(functools.partial(term_kernel, slot, first, blocks, masks,...]
    dot_general x4 -> x0, matrix products: 21.7 us -> none  [term_block(): return jnp.dot(left, right_env[0, term], preferred_element_type=jnp.float32)]
    ppermute x3 -> x18, waiting for transfers between devices: 0.01 us -> 8.5 us  [the longest x10 5.36 us: send(): return lax.ppermute(value, 'sec', pairs)]
    ppermute x3 -> x18, starting transfers between devices: 48.8 us -> 41.1 us  [the longest x10 27.3 us: send(): return lax.ppermute(value, 'sec', pairs)]
    reduce_sum x1 -> x0, other arithmetic: 4.56 us -> none  [on_device(): local_part = jnp.sum(psi_live.astype(jnp.float32) * total)]
  transfers between devices with their start and end apart: 3 -> 18, of which waited for: 0 -> 3; matrix products, arithmetic and copies ran while one was open for 13% -> 0% of each run, Pallas kernels for 0% -> 33%
where the time goes in v2:
time: 96.7 us; the launch traced here: 96.1 us
  starting transfers between devices  41.1 us (43%)
  Pallas kernels  37.4 us (39%)
  waiting for transfers between devices  8.5 us (9%)
  between operations  7.76 us (8%)
  local copies, waits for them, and re-layouts  1.31 us (1%)
    pallas_call x8, Pallas kernels, term_rows(): pl.pallas_call(functools.partial(term_kernel, slot, first, blocks, masks,...  31.4 us
    ppermute x10, starting transfers between devices, send(): return lax.ppermute(value, 'sec', pairs)  27.3 us
    ppermute x6, starting transfers between devices, sum_over_sectors(): lax.ppermute(value, 'sec', [(s, s ^ n * stride) for s in range(sectors)])  11.2 us
    pallas_call x2, Pallas kernels, finish(): pl.pallas_call(functools.partial(finish_kernel, first, steps), out_shape=...  5.46 us
    ppermute x10, waiting for transfers between devices, send(): return lax.ppermute(value, 'sec', pairs)  5.36 us
    ppermute x6, waiting for transfers between devices, sum_over_sectors(): lax.ppermute(value, 'sec', [(s, s ^ n * stride) for s in range(sectors)])  3.13 us
    ppermute x2, starting transfers between devices, on_device(): raised.append(lax.ppermute(both[p], 'sec', pairs_up))  2.57 us
  transfers between devices with their start and end apart: 18, of which 3 were waited for; matrix products, arithmetic and copies ran while one was open for 0% of the time, Pallas kernels for 33%

profile of v2, /device:TPU:0, one launch (start us, length us, event | category | flops | bytes accessed | tf_op | source)
XLA Modules:
  0.0 96.1 jit_solution(7963464619137218731)
XLA Ops:
  3.3 3.0 %term_slot0.2 = (f32[512,512]{1,0:T(8,128)S(1)}, bf16[1024,512]{1,0:T(8,128)(2,1)S(1)}) custom-call(s32[7]{0:T(128)S(1)} %stack.19.refs_0_.info_ref, bf16[1024,512]{1,0:T(8,128)(2,1)S(1)} %bitcast.5, bf16[1,4,1024,1024]{3,2,1,0:T(8,128)(2,1)} %refs_2_.15, bf16[1,4,512,512]{3,2,1,0:T(8,128)(2,1)} %refs_3_.15), custom_call_target="tpu_custom_call" | custom-call | flops 805306368 | bytes 2621440 | tf_op jit(solution)/shard_map/term_slot0/pallas_call | solution.py:97
  6.3 2.4 %collective-permute-start.7 = (f32[512,512]{1,0:T(8,128)S(1)}, f32[512,512]{1,0:T(8,128)S(1)}, u32[]{:S(2)}, u32[]{:S(2)}) collective-permute-start(f32[512,512]{1,0:T(8,128)S(1)} %get-tuple-element.9.a_ref), channel_id=1, source_target_pairs={{0,1},{4,5},{8,9},{12,13},{2,3},{6,7},{10,11},{14,15},{16,17},{20,... | collective-permute-start | bytes 3145736 | tf_op jit(solution)/shard_map/ppermute | solution.py:231
  8.7 3.0 %term_slot0.3.a_ref = f32[512,512]{1,0:T(8,128)S(1)} custom-call(s32[7]{0:T(128)S(1)} %stack.19.refs_0_.info_ref, bf16[1024,512]{1,0:T(8,128)(2,1)S(1)} %get-tuple-element.8.refs_1_.live_ref, bf16[1,4,1024,1024]{3,2,1,0:T(8,128)(2,1)} %refs_2_.15, bf16[1,4,512,512]{3,2,1,0:T(8,128)(2,1)} %refs_3_.15), custom_call_target="tpu_custom_call" | custom-call | flops 805306368 | bytes 2621440 | tf_op jit(solution)/shard_map/term_slot0/pallas_call | solution.py:97
  11.7 1.4 %collective-permute-start = (f32[512,512]{1,0:T(8,128)S(1)}, f32[512,512]{1,0:T(8,128)S(1)}, u32[]{:S(2)}, u32[]{:S(2)}) collective-permute-start(f32[512,512]{1,0:T(8,128)S(1)} %term_slot0.3.a_ref), channel_id=1, source_target_pairs={{0,1},{4,5},{8,9},{12,13},{2,3},{6,7},{10,11},{14,15},{16,17},{20,... | collective-permute-start | bytes 3145736 | tf_op jit(solution)/shard_map/ppermute | solution.py:231
  13.2 1.3 %collective-permute-start.8 = (f32[512,512]{1,0:T(8,128)S(1)}, f32[512,512]{1,0:T(8,128)S(1)}, u32[]{:S(2)}, u32[]{:S(2)}) collective-permute-start(f32[512,512]{1,0:T(8,128)S(1)} %add_blocks.6.refs_4_), channel_id=1, source_target_pairs={{1,2},{5,6},{9,10},{13,14},{3,0},{7,4},{11,8},{17,18},{21,22},{25,... | collective-permute-start | bytes 3145736 | tf_op jit(solution)/shard_map/ppermute | solution.py:248
  14.5 3.0 %term_slot1.3.a_ref = f32[512,512]{1,0:T(8,128)S(1)} custom-call(s32[7]{0:T(128)S(1)} %stack.19.refs_0_.info_ref, bf16[1024,512]{1,0:T(8,128)(2,1)S(1)} %get-tuple-element.8.refs_1_.live_ref, bf16[1,4,1024,1024]{3,2,1,0:T(8,128)(2,1)} %refs_2_.15, bf16[1,4,512,512]{3,2,1,0:T(8,128)(2,1)} %refs_3_.15, f32[512,512]{1,0:T(8,128)S(1)} %add_blocks.6.refs_4_), custom_call_target="tpu_custom_call" | custom-call | flops 805306368 | bytes 2621440 | tf_op jit(solution)/shard_map/term_slot1/pallas_call | solution.py:97
  18.4 3.0 %term_slot1.2.a_ref = f32[512,512]{1,0:T(8,128)S(1)} custom-call(s32[7]{0:T(128)S(1)} %stack.19.refs_0_.info_ref, bf16[1024,512]{1,0:T(8,128)(2,1)S(1)} %get-tuple-element.8.refs_1_.live_ref, bf16[1,4,1024,1024]{3,2,1,0:T(8,128)(2,1)} %refs_2_.15, bf16[1,4,512,512]{3,2,1,0:T(8,128)(2,1)} %refs_3_.15, f32[512,512]{1,0:T(8,128)S(1)} %add_blocks.4.refs_4_), custom_call_target="tpu_custom_call" | custom-call | flops 805306368 | bytes 2621440 | tf_op jit(solution)/shard_map/term_slot1/pallas_call | solution.py:97
  22.2 3.6 %term_slot2.3 = f32[512,512]{1,0:T(8,128)S(1)} custom-call(s32[7]{0:T(128)S(1)} %stack.19.refs_0_.info_ref, bf16[1024,512]{1,0:T(8,128)(2,1)S(1)} %get-tuple-element.8.refs_1_.live_ref, bf16[1,4,1024,1024]{3,2,1,0:T(8,128)(2,1)} %refs_2_.15, bf16[1,4,512,512]{3,2,1,0:T(8,128)(2,1)} %refs_3_.15, f32[512,512]{1,0:T(8,128)S(1)} %add_blocks.4.refs_4_), custom_call_target="tpu_custom_call" | custom-call | flops 805306368 | bytes 2621440 | tf_op jit(solution)/shard_map/term_slot2/pallas_call | solution.py:97
  25.8 4.3 %collective-permute-start.6 = (f32[512,512]{1,0:T(8,128)S(1)}, f32[512,512]{1,0:T(8,128)S(1)}, u32[]{:S(2)}, u32[]{:S(2)}) collective-permute-start(f32[512,512]{1,0:T(8,128)S(1)} %term_slot2.3), channel_id=1, source_target_pairs={{0,1},{4,5},{8,9},{12,13},{1,0},{5,4},{9,8},{13,12},{2,3},{6,7},{1... | collective-permute-start | bytes 3145736 | tf_op jit(solution)/shard_map/ppermute | solution.py:231
  30.1 1.3 %collective-permute-start.2 = (f32[512,512]{1,0:T(8,128)S(1)}, f32[512,512]{1,0:T(8,128)S(1)}, u32[]{:S(2)}, u32[]{:S(2)}) collective-permute-start(f32[512,512]{1,0:T(8,128)S(1)} %add_blocks.4.refs_4_), channel_id=1, source_target_pairs={{1,2},{5,6},{9,10},{13,14},{3,0},{7,4},{11,8},{17,18},{21,22},{25,... | collective-permute-start | bytes 3145736 | tf_op jit(solution)/shard_map/ppermute | solution.py:248
  31.4 4.6 %term_slot2.2 = f32[512,512]{1,0:T(8,128)} custom-call(s32[7]{0:T(128)S(1)} %stack.19.refs_0_.info_ref, bf16[1024,512]{1,0:T(8,128)(2,1)S(1)} %get-tuple-element.8.refs_1_.live_ref, bf16[1,4,1024,1024]{3,2,1,0:T(8,128)(2,1)} %refs_2_.15, bf16[1,4,512,512]{3,2,1,0:T(8,128)(2,1)} %refs_3_.15, f32[512,512]{1,0:T(8,128)S(1)} %add_blocks.4.refs_4_), custom_call_target="tpu_custom_call" | custom-call | flops 805306368 | bytes 2621440 | tf_op jit(solution)/shard_map/term_slot2/pallas_call | solution.py:97
  36.0 2.5 %collective-permute-start.1 = (f32[512,512]{1,0:T(8,128)}, f32[512,512]{1,0:T(8,128)}, u32[]{:S(2)}, u32[]{:S(2)}) collective-permute-start(f32[512,512]{1,0:T(8,128)} %term_slot2.2), channel_id=1, source_target_pairs={{0,1},{4,5},{8,9},{12,13},{1,0},{5,4},{9,8},{13,12},{2,3},{6,7},{1... | collective-permute-start | bytes 3145736 | tf_op jit(solution)/shard_map/ppermute | solution.py:231
  39.4 10.3 %collective-permute-start.9 = (f32[512,512]{1,0:T(8,128)S(1)}, f32[512,512]{1,0:T(8,128)S(1)}, u32[]{:S(2)}, u32[]{:S(2)}) collective-permute-start(f32[512,512]{1,0:T(8,128)S(1)} %collective-permute-done.8.a_ref), channel_id=1, source_target_pairs={{0,4},{4,8},{8,12},{16,20},{20,24},{24,28}} | collective-permute-start | bytes 3145736 | tf_op jit(solution)/shard_map/ppermute | solution.py:231
  50.6 3.5 %collective-permute-start.3 = (f32[512,512]{1,0:T(8,128)S(1)}, f32[512,512]{1,0:T(8,128)S(1)}, u32[]{:S(2)}, u32[]{:S(2)}) collective-permute-start(f32[512,512]{1,0:T(8,128)S(1)} %collective-permute-done.2.a_ref), channel_id=1, source_target_pairs={{0,4},{4,8},{8,12},{16,20},{20,24},{24,28}} | collective-permute-start | bytes 3145736 | tf_op jit(solution)/shard_map/ppermute | solution.py:231
  54.1 5.3 %term_slot3.3.own_ref = f32[512,512]{1,0:T(8,128)S(1)} custom-call(s32[7]{0:T(128)S(1)} %stack.19.refs_0_.info_ref, bf16[1024,512]{1,0:T(8,128)(2,1)S(1)} %get-tuple-element.8.refs_1_.live_ref, bf16[1,4,1024,1024]{3,2,1,0:T(8,128)(2,1)} %refs_2_.15, bf16[1,4,512,512]{3,2,1,0:T(8,128)(2,1)} %refs_3_.15, f32[512,512]{1,0:T(8,128)S(1)} %collective-permute-done.6.refs_4_), custom_call_target="tpu_custom_call" | custom-call | flops 805306368 | bytes 2621440 | tf_op jit(solution)/shard_map/term_slot3/pallas_call | solution.py:97
  59.4 6.0 %term_slot3.2.own_ref = f32[512,512]{1,0:T(8,128)S(1)} custom-call(s32[7]{0:T(128)S(1)} %stack.19.refs_0_.info_ref, bf16[1024,512]{1,0:T(8,128)(2,1)S(1)} %get-tuple-element.8.refs_1_.live_ref, bf16[1,4,1024,1024]{3,2,1,0:T(8,128)(2,1)} %refs_2_.15, bf16[1,4,512,512]{3,2,1,0:T(8,128)(2,1)} %refs_3_.15, f32[512,512]{1,0:T(8,128)} %collective-permute-done.1.refs_4_), custom_call_target="tpu_custom_call" | custom-call | flops 805306368 | bytes 2621440 | tf_op jit(solution)/shard_map/term_slot3/pallas_call | solution.py:97
  65.4 2.4 %finish_rows.2 = (bf16[1,1024,512]{2,1,0:T(8,128)(2,1)}, f32[1]{0:T(128)}) custom-call(s32[7]{0:T(128)S(1)} %stack.19.refs_0_.info_ref, bf16[1024,512]{1,0:T(8,128)(2,1)S(1)} %get-tuple-element.8.refs_1_.live_ref, f32[512,512]{1,0:T(8,128)S(1)} %term_slot3.3.own_ref, f32[512,512]{1,0:T(8,128)S(1)} %collective-permute-done.8.a_ref, ...), custom_call_target="tpu_custom_call" | custom-call | flops 1048576 | bytes 3145728 | tf_op jit(solution)/shard_map/finish_rows/pallas_call | solution.py:181
  67.8 5.3 %collective-permute-done.3.b_ref = f32[512,512]{1,0:T(8,128)S(1)} collective-permute-done((f32[512,512]{1,0:T(8,128)S(1)}, f32[512,512]{1,0:T(8,128)S(1)}, u32[]{:S(2)}, u32[]{:S(2)}) %collective-permute-start.3) | collective-permute-done | bytes 1048608 | tf_op jit(solution)/shard_map/ppermute | solution.py:231
  73.2 3.1 %finish_rows.3 = (bf16[1,1024,512]{2,1,0:T(8,128)(2,1)}, f32[1]{0:T(128)}) custom-call(s32[7]{0:T(128)S(1)} %stack.19.refs_0_.info_ref, bf16[1024,512]{1,0:T(8,128)(2,1)S(1)} %get-tuple-element.8.refs_1_.live_ref, f32[512,512]{1,0:T(8,128)S(1)} %term_slot3.2.own_ref, f32[512,512]{1,0:T(8,128)S(1)} %collective-permute-done.2.a_ref, ...), custom_call_target="tpu_custom_call", output_to_operand_aliasing={{0}: (7, {})} | custom-call | flops 1048576 | bytes 3145728 | tf_op jit(solution)/shard_map/finish_rows/pallas_call | solution.py:181
  76.3 2.1 %collective-permute-start.12 = (f32[1]{0:T(128)}, f32[1]{0:T(128)}, u32[]{:S(2)}, u32[]{:S(2)}) collective-permute-start(f32[1]{0:T(128)} %get-tuple-element.13), channel_id=1, source_target_pairs={{0,1},{1,0},{2,3},{3,2},{4,5},{5,4},{6,7},{7,6},{8,9},{9,8},{10,11... | collective-permute-start | bytes 20 | tf_op jit(solution)/shard_map/ppermute | solution.py:207
  82.1 4.9 %collective-permute-start.16 = (f32[1]{0:T(128)}, f32[1]{0:T(128)}, u32[]{:S(2)}, u32[]{:S(2)}) collective-permute-start(f32[1]{0:T(128)} %add.29), channel_id=1, source_target_pairs={{0,8},{1,9},{2,10},{3,11},{4,12},{5,13},{6,14},{7,15},{8,0},{9,1},... | collective-permute-start | bytes 20 | tf_op jit(solution)/shard_map/ppermute | solution.py:207
  86.9 2.6 %collective-permute-start.17 = (f32[1]{0:T(128)}, f32[1]{0:T(128)}, u32[]{:S(2)}, u32[]{:S(2)}) collective-permute-start(f32[1]{0:T(128)} %add.29), channel_id=1, source_target_pairs={{0,12},{1,13},{2,14},{3,15},{4,8},{5,9},{6,10},{7,11},{8,4},{9,5},... | collective-permute-start | bytes 20 | tf_op jit(solution)/shard_map/ppermute | solution.py:207
  89.6 1.5 %collective-permute-start.15 = (f32[1]{0:T(128)}, f32[1]{0:T(128)}, u32[]{:S(2)}, u32[]{:S(2)}) collective-permute-start(f32[1]{0:T(128)} %add.29), channel_id=1, source_target_pairs={{0,4},{1,5},{2,6},{3,7},{4,0},{5,1},{6,2},{7,3},{8,12},{9,13},{10,... | collective-permute-start | bytes 20 | tf_op jit(solution)/shard_map/ppermute | solution.py:207
  91.1 2.0 %collective-permute-done.15 = f32[1]{0:T(128)} collective-permute-done((f32[1]{0:T(128)}, f32[1]{0:T(128)}, u32[]{:S(2)}, u32[]{:S(2)}) %collective-permute-start.15) | collective-permute-done | bytes 36 | tf_op jit(solution)/shard_map/ppermute | solution.py:207
  (29 shorter events, 6.0 us)
Async XLA Ops:
  2.0 1.2 %copy-start = (bf16[1,1024,512]{2,1,0:T(8,128)(2,1)S(1)}, bf16[1,1024,512]{2,1,0:T(8,128)(2,1)}, u32[]{:S(2)}) copy-start(bf16[1,1024,512]{2,1,0:T(8,128)(2,1)} %param.5) | copy-start | bytes 3145732
  6.3 6.8 %collective-permute-start.7 = (f32[512,512]{1,0:T(8,128)S(1)}, f32[512,512]{1,0:T(8,128)S(1)}, u32[]{:S(2)}, u32[]{:S(2)}) collective-permute-start(f32[512,512]{1,0:T(8,128)S(1)} %get-tuple-element.9.a_ref), channel_id=1, source_target_pairs={{0,1},{4,5},{8,9},{12,13},{2,3},{6,7},{10,11},{14,15},{16,17},{20,... | collective-permute-start | bytes 3145736 | tf_op jit(solution)/shard_map/ppermute | solution.py:231
  11.7 6.6 %collective-permute-start = (f32[512,512]{1,0:T(8,128)S(1)}, f32[512,512]{1,0:T(8,128)S(1)}, u32[]{:S(2)}, u32[]{:S(2)}) collective-permute-start(f32[512,512]{1,0:T(8,128)S(1)} %term_slot0.3.a_ref), channel_id=1, source_target_pairs={{0,1},{4,5},{8,9},{12,13},{2,3},{6,7},{10,11},{14,15},{16,17},{20,... | collective-permute-start | bytes 3145736 | tf_op jit(solution)/shard_map/ppermute | solution.py:231
  13.2 25.4 %collective-permute-start.8 = (f32[512,512]{1,0:T(8,128)S(1)}, f32[512,512]{1,0:T(8,128)S(1)}, u32[]{:S(2)}, u32[]{:S(2)}) collective-permute-start(f32[512,512]{1,0:T(8,128)S(1)} %add_blocks.6.refs_4_), channel_id=1, source_target_pairs={{1,2},{5,6},{9,10},{13,14},{3,0},{7,4},{11,8},{17,18},{21,22},{25,... | collective-permute-start | bytes 3145736 | tf_op jit(solution)/shard_map/ppermute | solution.py:248
  17.5 18.4 %collective-permute-start.10 = (f32[512,512]{1,0:T(8,128)S(1)}, f32[512,512]{1,0:T(8,128)S(1)}, u32[]{:S(2)}, u32[]{:S(2)}) collective-permute-start(f32[512,512]{1,0:T(8,128)S(1)} %term_slot1.3.a_ref), channel_id=1, source_target_pairs={{3,6},{7,10},{11,14},{4,1},{8,5},{12,9},{19,22},{23,26},{27,30},{2... | collective-permute-start | bytes 3145736 | tf_op jit(solution)/shard_map/ppermute | solution.py:231
  21.5 17.9 %collective-permute-start.4 = (f32[512,512]{1,0:T(8,128)S(1)}, f32[512,512]{1,0:T(8,128)S(1)}, u32[]{:S(2)}, u32[]{:S(2)}) collective-permute-start(f32[512,512]{1,0:T(8,128)S(1)} %term_slot1.2.a_ref), channel_id=1, source_target_pairs={{3,6},{7,10},{11,14},{4,1},{8,5},{12,9},{19,22},{23,26},{27,30},{2... | collective-permute-start | bytes 3145736 | tf_op jit(solution)/shard_map/ppermute | solution.py:231
  25.8 24.1 %collective-permute-start.6 = (f32[512,512]{1,0:T(8,128)S(1)}, f32[512,512]{1,0:T(8,128)S(1)}, u32[]{:S(2)}, u32[]{:S(2)}) collective-permute-start(f32[512,512]{1,0:T(8,128)S(1)} %term_slot2.3), channel_id=1, source_target_pairs={{0,1},{4,5},{8,9},{12,13},{1,0},{5,4},{9,8},{13,12},{2,3},{6,7},{1... | collective-permute-start | bytes 3145736 | tf_op jit(solution)/shard_map/ppermute | solution.py:231
  30.1 20.5 %collective-permute-start.2 = (f32[512,512]{1,0:T(8,128)S(1)}, f32[512,512]{1,0:T(8,128)S(1)}, u32[]{:S(2)}, u32[]{:S(2)}) collective-permute-start(f32[512,512]{1,0:T(8,128)S(1)} %add_blocks.4.refs_4_), channel_id=1, source_target_pairs={{1,2},{5,6},{9,10},{13,14},{3,0},{7,4},{11,8},{17,18},{21,22},{25,... | collective-permute-start | bytes 3145736 | tf_op jit(solution)/shard_map/ppermute | solution.py:248
  36.0 23.4 %collective-permute-start.1 = (f32[512,512]{1,0:T(8,128)}, f32[512,512]{1,0:T(8,128)}, u32[]{:S(2)}, u32[]{:S(2)}) collective-permute-start(f32[512,512]{1,0:T(8,128)} %term_slot2.2), channel_id=1, source_target_pairs={{0,1},{4,5},{8,9},{12,13},{1,0},{5,4},{9,8},{13,12},{2,3},{6,7},{1... | collective-permute-start | bytes 3145736 | tf_op jit(solution)/shard_map/ppermute | solution.py:231
  38.6 26.8 %collective-permute-start.11 = (f32[512,512]{1,0:T(8,128)S(1)}, f32[512,512]{1,0:T(8,128)S(1)}, u32[]{:S(2)}, u32[]{:S(2)}) collective-permute-start(f32[512,512]{1,0:T(8,128)S(1)} %add_blocks.7), channel_id=1, source_target_pairs={{1,3},{5,7},{9,11},{13,15},{2,1},{6,5},{10,9},{14,13},{17,19},{21,... | collective-permute-start | bytes 3145736 | tf_op jit(solution)/shard_map/ppermute | solution.py:231
  39.4 26.0 %collective-permute-start.9 = (f32[512,512]{1,0:T(8,128)S(1)}, f32[512,512]{1,0:T(8,128)S(1)}, u32[]{:S(2)}, u32[]{:S(2)}) collective-permute-start(f32[512,512]{1,0:T(8,128)S(1)} %collective-permute-done.8.a_ref), channel_id=1, source_target_pairs={{0,4},{4,8},{8,12},{16,20},{20,24},{24,28}} | collective-permute-start | bytes 3145736 | tf_op jit(solution)/shard_map/ppermute | solution.py:231
  49.9 18.0 %collective-permute-start.5 = (f32[512,512]{1,0:T(8,128)S(1)}, f32[512,512]{1,0:T(8,128)S(1)}, u32[]{:S(2)}, u32[]{:S(2)}) collective-permute-start(f32[512,512]{1,0:T(8,128)S(1)} %add_blocks.5), channel_id=1, source_target_pairs={{1,3},{5,7},{9,11},{13,15},{2,1},{6,5},{10,9},{14,13},{17,19},{21,... | collective-permute-start | bytes 3145736 | tf_op jit(solution)/shard_map/ppermute | solution.py:231
  50.6 22.6 %collective-permute-start.3 = (f32[512,512]{1,0:T(8,128)S(1)}, f32[512,512]{1,0:T(8,128)S(1)}, u32[]{:S(2)}, u32[]{:S(2)}) collective-permute-start(f32[512,512]{1,0:T(8,128)S(1)} %collective-permute-done.2.a_ref), channel_id=1, source_target_pairs={{0,4},{4,8},{8,12},{16,20},{20,24},{24,28}} | collective-permute-start | bytes 3145736 | tf_op jit(solution)/shard_map/ppermute | solution.py:231
  76.2 4.6 %collective-permute-start.13 = (f32[1]{0:T(128)}, f32[1]{0:T(128)}, u32[]{:S(2)}, u32[]{:S(2)}) collective-permute-start(f32[1]{0:T(128)} %get-tuple-element.13), channel_id=1, source_target_pairs={{0,2},{1,3},{2,0},{3,1},{4,6},{5,7},{6,4},{7,5},{8,10},{9,11},{10,... | collective-permute-start | bytes 20 | tf_op jit(solution)/shard_map/ppermute | solution.py:207
  76.2 4.6 %collective-permute-start.14 = (f32[1]{0:T(128)}, f32[1]{0:T(128)}, u32[]{:S(2)}, u32[]{:S(2)}) collective-permute-start(f32[1]{0:T(128)} %get-tuple-element.13), channel_id=1, source_target_pairs={{0,3},{1,2},{2,1},{3,0},{4,7},{5,6},{6,5},{7,4},{8,11},{9,10},{10,... | collective-permute-start | bytes 20 | tf_op jit(solution)/shard_map/ppermute | solution.py:207
  76.3 3.3 %collective-permute-start.12 = (f32[1]{0:T(128)}, f32[1]{0:T(128)}, u32[]{:S(2)}, u32[]{:S(2)}) collective-permute-start(f32[1]{0:T(128)} %get-tuple-element.13), channel_id=1, source_target_pairs={{0,1},{1,0},{2,3},{3,2},{4,5},{5,4},{6,7},{7,6},{8,9},{9,8},{10,11... | collective-permute-start | bytes 20 | tf_op jit(solution)/shard_map/ppermute | solution.py:207
  82.1 11.6 %collective-permute-start.16 = (f32[1]{0:T(128)}, f32[1]{0:T(128)}, u32[]{:S(2)}, u32[]{:S(2)}) collective-permute-start(f32[1]{0:T(128)} %add.29), channel_id=1, source_target_pairs={{0,8},{1,9},{2,10},{3,11},{4,12},{5,13},{6,14},{7,15},{8,0},{9,1},... | collective-permute-start | bytes 20 | tf_op jit(solution)/shard_map/ppermute | solution.py:207
  86.9 6.8 %collective-permute-start.17 = (f32[1]{0:T(128)}, f32[1]{0:T(128)}, u32[]{:S(2)}, u32[]{:S(2)}) collective-permute-start(f32[1]{0:T(128)} %add.29), channel_id=1, source_target_pairs={{0,12},{1,13},{2,14},{3,15},{4,8},{5,9},{6,10},{7,11},{8,4},{9,5},... | collective-permute-start | bytes 20 | tf_op jit(solution)/shard_map/ppermute | solution.py:207
  89.6 3.5 %collective-permute-start.15 = (f32[1]{0:T(128)}, f32[1]{0:T(128)}, u32[]{:S(2)}, u32[]{:S(2)}) collective-permute-start(f32[1]{0:T(128)} %add.29), channel_id=1, source_target_pairs={{0,4},{1,5},{2,6},{3,7},{4,0},{5,1},{6,2},{7,3},{8,12},{9,13},{10,... | collective-permute-start | bytes 20 | tf_op jit(solution)/shard_map/ppermute | solution.py:207

commit v3 on v2

v3 whole, which is shorter than its diff:
```python
import functools

import jax
import jax.numpy as jnp
from jax import lax
from jax.experimental import pallas as pl
from jax.experimental.pallas import tpu as pltpu
from jax.sharding import PartitionSpec as P

MIB = 1024 * 1024

ANY = pl.BlockSpec(memory_space=pl.ANY)
HBM = pl.BlockSpec(memory_space=pltpu.HBM)
SMEM = pl.BlockSpec(memory_space=pltpu.SMEM)
WHOLE = pl.BlockSpec(memory_space=pltpu.VMEM)
TOKEN = jax.ShapeDtypeStruct((8, 128), jnp.float32)
SMALL = pl.CostEstimate(flops=200000000, bytes_accessed=1000000, transcendentals=0)


def params(mib=8):
    return pltpu.CompilerParams(vmem_limit_bytes=mib * MIB)


def term_kernel(slot, first, blocks, masks, adds, tokens, *refs):
    refs = list(refs)
    info_ref, live_ref, left_hbm, right_hbm = refs[:4]
    refs = refs[4:]
    add_ref = refs.pop(0) if adds else None
    refs = refs[tokens:]
    out_ref, _ = refs[:2]
    refs = refs[2:]
    live_out = refs.pop(0) if masks else None
    left_buf, right_buf = refs[:2]
    sems = refs[-1]
    psi_buf = refs[2] if masks else None
    block = left_buf.shape[1]
    term = info_ref[slot]
    copies = []
    if masks:
        psi_copy = pltpu.make_async_copy(live_ref, psi_buf, sems.at[blocks + 1])
        psi_copy.start()
    for i in range(blocks):
        copy = pltpu.make_async_copy(
            left_hbm.at[0, term, pl.ds(first + i * block, block), :], left_buf.at[i], sems.at[i]
        )
        copy.start()
        copies.append(copy)
        if i == 0:
            right_copy = pltpu.make_async_copy(
                right_hbm.at[0, term], right_buf, sems.at[blocks]
            )
            right_copy.start()
    if masks:
        psi_copy.wait()
        rows, cols = psi_buf.shape
        step = 128
        col = lax.broadcasted_iota(jnp.int32, (step, cols), 1) < info_ref[5]
        row = lax.broadcasted_iota(jnp.int32, (step, cols), 0)
        for r in range(0, rows, step):
            inside = jnp.logical_and(row < info_ref[4] - r, col)
            values = psi_buf[r : r + step, :].astype(jnp.float32)
            live_out[r : r + step, :] = jnp.where(inside, values, 0.0).astype(jnp.bfloat16)
        live_ref = live_out
    for i in range(blocks):
        copies[i].wait()
        left = jnp.dot(left_buf[i], live_ref[...], preferred_element_type=jnp.float32)
        if i == 0:
            right_copy.wait()
        value = jnp.dot(
            left.astype(jnp.bfloat16), right_buf[...], preferred_element_type=jnp.float32
        )
        span = pl.ds(i * block, block)
        if adds:
            value = value + add_ref[span, :]
        out_ref[span, :] = value


def term_rows(
    info, slot, live, left_env, right_env, first, count, block, masks=False, added=None, tokens=()
):
    width, cols = live.shape[-2:]
    blocks = count // block
    in_specs = [SMEM, HBM if masks else WHOLE, HBM, HBM]
    operands = [info, live, left_env, right_env]
    if added is not None:
        in_specs.append(WHOLE)
        operands.append(added)
    in_specs += [ANY] * len(tokens)
    operands += tokens
    out_shape = [jax.ShapeDtypeStruct((count, cols), jnp.float32), TOKEN]
    scratch = [
        pltpu.VMEM((blocks, block, width), jnp.bfloat16),
        pltpu.VMEM((cols, cols), jnp.bfloat16),
    ]
    if masks:
        out_shape.append(jax.ShapeDtypeStruct((width, cols), jnp.bfloat16))
        scratch.append(pltpu.VMEM((width, cols), jnp.bfloat16))
    scratch.append(pltpu.SemaphoreType.DMA((blocks + 2,)))
    out = pl.pallas_call(
        functools.partial(
            term_kernel, slot, first, blocks, masks, added is not None, len(tokens)
        ),
        out_shape=out_shape,
        in_specs=in_specs,
        out_specs=[WHOLE, ANY] + [WHOLE] * (len(out_shape) - 2),
        scratch_shapes=scratch,
        compiler_params=params(50),
        cost_estimate=SMALL,
        name=f"term_slot{slot}",
    )(*operands)
    return out


def add_kernel(a_ref, b_ref, *refs):
    out_ref = refs[-2]
    rows = a_ref.shape[0]
    step = 64

    def body(i, _):
        span = pl.ds(pl.multiple_of(i * step, step), step)
        out_ref[span, :] = a_ref[span, :] + b_ref[span, :]
        return _

    lax.fori_loop(0, rows // step, body, 0)


def add(a, b, *tokens):
    return pl.pallas_call(
        add_kernel,
        out_shape=(jax.ShapeDtypeStruct(a.shape, a.dtype), TOKEN),
        in_specs=[WHOLE, WHOLE] + [ANY] * len(tokens),
        out_specs=(WHOLE, ANY),
        compiler_params=params(),
        cost_estimate=SMALL,
        name="add_blocks",
    )(a, b, *tokens)


def touch(*values):
    return pl.pallas_call(
        lambda *refs: None,
        out_shape=TOKEN,
        in_specs=[ANY] * len(values),
        out_specs=ANY,
        compiler_params=params(),
        cost_estimate=SMALL,
        name="touch",
    )(*values)


def finish_kernel(first, info_ref, live_ref, own_ref, a_ref, b_ref, c_ref, before_ref, *refs):
    sigma_hbm, energy_ref, sigma_buf, sems = refs[-4:]
    count, cols = own_ref.shape
    step = 64
    piece = count // sems.shape[0]
    col = lax.broadcasted_iota(jnp.int32, (step, cols), 1) < info_ref[5]
    row = lax.broadcasted_iota(jnp.int32, (step, cols), 0)

    def copy(i):
        span = pl.ds(i * piece, piece)
        return pltpu.make_async_copy(
            sigma_buf.at[span, :], sigma_hbm.at[0, pl.ds(first + i * piece, piece), :], sems.at[i]
        )

    def work(arrival):
        energy = jnp.zeros((8, cols), jnp.float32)
        for i in range(count // piece):

            def body(n, energy):
                start = pl.multiple_of(i * piece + n * step, step)
                span = pl.ds(start, step)
                inside = jnp.logical_and(row < info_ref[4] - first - start, col)
                total = jnp.where(inside, own_ref[span, :] + arrival[span, :], 0.0)
                sigma_buf[span, :] = total.astype(sigma_buf.dtype)
                here = pl.ds(pl.multiple_of(first + start, step), step)
                product = live_ref[here, :].astype(jnp.float32) * total
                return energy + jnp.sum(jnp.reshape(product, (step // 8, 8, cols)), axis=0)

            energy = lax.fori_loop(0, piece // step, body, energy)
            copy(i).start()
        energy_ref[...] = before_ref[...] + jnp.sum(energy)

    for n, arrival in enumerate((a_ref, b_ref, c_ref)):
        pl.when(info_ref[6] == n)(functools.partial(work, arrival))
    for i in range(count // piece):
        copy(i).wait()


def finish(info, live, own, arrivals, before, sigma, first):
    count, cols = own.shape
    in_specs = [SMEM] + [WHOLE] * 6
    operands = [info, live, own, *arrivals, before]
    aliases = {}
    if sigma is not None:
        in_specs.append(ANY)
        aliases = {len(operands): 0}
        operands.append(sigma)
    return pl.pallas_call(
        functools.partial(finish_kernel, first),
        out_shape=(
            jax.ShapeDtypeStruct((1, *live.shape), jnp.bfloat16),
            jax.ShapeDtypeStruct(before.shape, jnp.float32),
        ),
        in_specs=in_specs,
        out_specs=(ANY, WHOLE),
        scratch_shapes=[pltpu.VMEM((count, cols), jnp.bfloat16), pltpu.SemaphoreType.DMA((4,))],
        input_output_aliases=aliases,
        compiler_params=params(),
        cost_estimate=SMALL,
        name="finish_rows",
    )(*operands)


def sum_kernel(in_ref, out_ref):
    out_ref[0] = jnp.sum(in_ref[:, :1])


def sum_over_sectors(value):
    arrived = lax.all_to_all(value, "sec", 0, 0, tiled=True)
    return pl.pallas_call(
        sum_kernel,
        out_shape=jax.ShapeDtypeStruct((1,), jnp.float32),
        in_specs=[WHOLE],
        out_specs=SMEM,
        compiler_params=params(),
        cost_estimate=SMALL,
        name="sum_energy",
    )(arrived)


def on_device(psi, left_env, right_env, row_sizes, col_sizes):
    sectors = lax.axis_size("sec")
    sector = lax.axis_index("sec")
    even = sector % 2 == 0
    place = sector % 4

    def send(value, *hops):
        pairs = [
            (s, s + steps)
            for at, steps in hops
            for s in range(at, sectors, 4)
            if 0 <= s + steps < sectors
        ]
        return lax.ppermute(value, "sec", pairs)

    rows = psi.shape[1]
    part = rows // 2
    which = jnp.where(place == 0, 1, jnp.where(place == 2, 0, 2))
    orders = [jnp.where(even, 2, 1), jnp.where(even, 3, 2), jnp.where(even, 1, 3), 0]
    info = jnp.stack([*orders, row_sizes[0], col_sizes[0], which]).astype(jnp.int32)

    def rows_of(slot, p, *tokens, added=None):
        return term_rows(
            info, slot, live, left_env, right_env, p * part, part, 512, added=added, tokens=tokens
        )

    pairs_up = [(s, s + 1) for s in range(1, sectors, 4) if s + 1 < sectors]
    pairs_up += [(s, s - 3) for s in range(3, sectors, 4) if s + 1 < sectors]

    def raise_one(value):
        return lax.ppermute(value, "sec", pairs_up)

    def up_chip(value):
        return send(value, (0, 1), (2, 1))

    def along(value):
        return send(value, (3, 3), (0, -3))

    def across(value):
        return send(value, (1, 2), (2, -1))

    def swap(value):
        return send(value, (0, 1), (1, -1), (2, 1), (3, -1))

    def relay(value):
        return send(value, (0, 4))

    first0, token, live = term_rows(
        info, 0, psi[0], left_env, right_env, 0, part, 512, masks=True
    )
    paired0 = up_chip(first0)
    first1, token = rows_of(0, 1, token)
    paired1 = up_chip(first1)
    both0, token = add(first0, paired0, token)
    raised0 = raise_one(both0)
    second0, token = rows_of(1, 0, token)
    moved0 = along(second0)
    both1, token = add(first1, paired1, token)
    raised1 = raise_one(both1)
    second1, token = rows_of(1, 1, token)
    moved1 = along(second1)
    third0, token = rows_of(2, 0, token)
    swapped0 = swap(third0)
    token = touch(raised0, token)
    relayed0 = relay(raised0)
    third1, token = rows_of(2, 1, token)
    swapped1 = swap(third1)
    summed0, token = add(second0, moved0, token)
    crossed0 = across(summed0)
    own0, token = rows_of(3, 0, token, added=swapped0)
    token = touch(raised1, token)
    relayed1 = relay(raised1)
    summed1, token = add(second1, moved1, token)
    crossed1 = across(summed1)
    token = touch(relayed0, token)
    own1, token = rows_of(3, 1, token, added=swapped1)

    energy = jnp.zeros((sectors, 128), jnp.float32)
    sigma, energy = finish(info, live, own0, (raised0, relayed0, crossed0), energy, None, 0)
    sigma, energy = finish(info, live, own1, (raised1, relayed1, crossed1), energy, sigma, part)
    return sigma, sum_over_sectors(energy)


def solution(mesh):
    return jax.shard_map(
        on_device,
        mesh=mesh,
        in_specs=(
            P(("grp", "sec"), None, None),
            P(("grp", "sec"), None, None, None),
            P(("grp", "sec"), None, None, None),
            P(("grp", "sec")),
            P(("grp", "sec")),
        ),
        out_specs=(P(("grp", "sec"), None, None), P("grp")),
        check_vma=False,
    )
```

time: 96.7 us -> 81 us (0.84)
  starting transfers between devices: 41.1 us -> 25.4 us
  blocking collectives: 0 us -> 12.1 us
  Pallas kernels: 37.4 us -> 28.9 us
  between operations: 7.76 us -> 2.23 us
  waiting for transfers between devices: 8.5 us -> 10.5 us
    all_to_all x0 -> x1, blocking collectives: none -> 12.1 us  [sum_over_sectors(): arrived = lax.all_to_all(value, 'sec', 0, 0, tiled=True)]
    ppermute x8 -> x2, starting transfers between devices: 13.7 us -> 2.57 us  [raise_one(): return lax.ppermute(value, 'sec', pairs_up)]
    pallas_call x8, Pallas kernels: 31.4 us -> 24.7 us  [term_rows(): pl.pallas_call(functools.partial(term_kernel, slot, first, blocks, masks,...]
    ppermute x10, starting transfers between devices: 27.3 us -> 22.8 us  [send(): return lax.ppermute(value, 'sec', pairs)]
    ppermute x10, waiting for transfers between devices: 5.36 us -> 7.7 us  [send(): return lax.ppermute(value, 'sec', pairs)]
    pallas_call x6 -> x10, Pallas kernels: 6 us -> 4.27 us  [the longest x2 3.09 us: finish(): pl.pallas_call(functools.partial(finish_kernel, first), out_shape=(jax.Sh...]
    ppermute x8 -> x2, waiting for transfers between devices: 3.14 us -> 2.78 us  [raise_one(): return lax.ppermute(value, 'sec', pairs_up)]
  transfers between devices with their start and end apart: 18 -> 12, of which waited for: 3 -> 3; matrix products, arithmetic and copies ran while one was open for 0% -> 0% of each run, Pallas kernels for 33% -> 30%
where the time goes in v3:
time: 81 us; the launch traced here: 80.4 us
  Pallas kernels  28.9 us (36%)
  starting transfers between devices  25.4 us (31%)
  blocking collectives  12.1 us (15%)
  waiting for transfers between devices  10.5 us (13%)
  between operations  2.23 us (3%)
  local copies, waits for them, and re-layouts  1.31 us (2%)
    pallas_call x8, Pallas kernels, term_rows(): pl.pallas_call(functools.partial(term_kernel, slot, first, blocks, masks,...  24.7 us
    ppermute x10, starting transfers between devices, send(): return lax.ppermute(value, 'sec', pairs)  22.8 us
    all_to_all x1, blocking collectives, sum_over_sectors(): arrived = lax.all_to_all(value, 'sec', 0, 0, tiled=True)  12.1 us
    ppermute x10, waiting for transfers between devices, send(): return lax.ppermute(value, 'sec', pairs)  7.7 us
    pallas_call x2, Pallas kernels, finish(): pl.pallas_call(functools.partial(finish_kernel, first), out_shape=(jax.Sh...  3.09 us
    ppermute x2, waiting for transfers between devices, raise_one(): return lax.ppermute(value, 'sec', pairs_up)  2.78 us
    ppermute x2, starting transfers between devices, raise_one(): return lax.ppermute(value, 'sec', pairs_up)  2.57 us
  transfers between devices with their start and end apart: 12, of which 3 were waited for; matrix products, arithmetic and copies ran while one was open for 0% of the time, Pallas kernels for 30%

profile of v3, /device:TPU:0, one launch (start us, length us, event | category | flops | bytes accessed | tf_op | source)
XLA Modules:
  0.0 80.4 jit_solution(18439988326641768682)
XLA Ops:
  2.0 1.2 %copy-done = bf16[1,1024,512]{2,1,0:T(8,128)(2,1)S(1)} copy-done((bf16[1,1024,512]{2,1,0:T(8,128)(2,1)S(1)}, bf16[1,1024,512]{2,1,0:T(8,128)(2,1)}, u32[]{:S(2)}) %copy-start) | copy-done | bytes 1048600
  3.3 3.0 %term_slot0.2 = (f32[512,512]{1,0:T(8,128)S(1)}, f32[8,128]{1,0:T(8,128)S(1)}, bf16[1024,512]{1,0:T(8,128)(2,1)S(1)}) custom-call(s32[7]{0:T(128)S(1)} %stack.19.refs_0_.info_ref, bf16[1024,512]{1,0:T(8,128)(2,1)S(1)} %bitcast.9, bf16[1,4,1024,1024]{3,2,1,0:T(8,128)(2,1)} %refs_2_.15, bf16[1,4,512,512]{3,2,1,0:T(8,128)(2,1)} %refs_3_.15), custom_call_target="tpu_custom_call" | custom-call | flops 200000000 | bytes 1000000 | tf_op jit(solution)/shard_map/term_slot0/pallas_call | solution.py:99
  6.3 2.4 %collective-permute-start = (f32[512,512]{1,0:T(8,128)S(1)}, f32[512,512]{1,0:T(8,128)S(1)}, u32[]{:S(2)}, u32[]{:S(2)}) collective-permute-start(f32[512,512]{1,0:T(8,128)S(1)} %get-tuple-element.31.a_ref), channel_id=1, source_target_pairs={{0,1},{4,5},{8,9},{12,13},{2,3},{6,7},{10,11},{14,15},{16,17},{20,... | collective-permute-start | bytes 3145736 | tf_op jit(solution)/shard_map/ppermute | solution.py:244
  8.7 3.0 %term_slot0.3 = (f32[512,512]{1,0:T(8,128)S(1)}, f32[8,128]{1,0:T(8,128)S(1)}) custom-call(s32[7]{0:T(128)S(1)} %stack.19.refs_0_.info_ref, bf16[1024,512]{1,0:T(8,128)(2,1)S(1)} %get-tuple-element.30.refs_1_.live_ref, bf16[1,4,1024,1024]{3,2,1,0:T(8,128)(2,1)} %refs_2_.15, bf16[1,4,512,512]{3,2,1,0:T(8,128)(2,1)} %refs_3_.15, ...), custom_call_target="tpu_custom_call" | custom-call | flops 200000000 | bytes 1000000 | tf_op jit(solution)/shard_map/term_slot0/pallas_call | solution.py:99
  11.7 1.4 %collective-permute-start.2 = (f32[512,512]{1,0:T(8,128)S(1)}, f32[512,512]{1,0:T(8,128)S(1)}, u32[]{:S(2)}, u32[]{:S(2)}) collective-permute-start(f32[512,512]{1,0:T(8,128)S(1)} %get-tuple-element.35.a_ref), channel_id=1, source_target_pairs={{0,1},{4,5},{8,9},{12,13},{2,3},{6,7},{10,11},{14,15},{16,17},{20,... | collective-permute-start | bytes 3145736 | tf_op jit(solution)/shard_map/ppermute | solution.py:244
  13.2 1.3 %collective-permute-start.1 = (f32[512,512]{1,0:T(8,128)S(1)}, f32[512,512]{1,0:T(8,128)S(1)}, u32[]{:S(2)}, u32[]{:S(2)}) collective-permute-start(f32[512,512]{1,0:T(8,128)S(1)} %get-tuple-element.34), channel_id=1, source_target_pairs={{1,2},{5,6},{9,10},{13,14},{3,0},{7,4},{11,8},{17,18},{21,22},{25,... | collective-permute-start | bytes 3145736 | tf_op jit(solution)/shard_map/ppermute | solution.py:261
  14.5 3.0 %term_slot1.2 = (f32[512,512]{1,0:T(8,128)S(1)}, f32[8,128]{1,0:T(8,128)S(1)}) custom-call(s32[7]{0:T(128)S(1)} %stack.19.refs_0_.info_ref, bf16[1024,512]{1,0:T(8,128)(2,1)S(1)} %get-tuple-element.30.refs_1_.live_ref, bf16[1,4,1024,1024]{3,2,1,0:T(8,128)(2,1)} %refs_2_.15, bf16[1,4,512,512]{3,2,1,0:T(8,128)(2,1)} %refs_3_.15, ...), custom_call_target="tpu_custom_call" | custom-call | flops 200000000 | bytes 1000000 | tf_op jit(solution)/shard_map/term_slot1/pallas_call | solution.py:99
  17.5 0.7 collective-permute-start.8
  18.4 3.0 %term_slot1.3 = (f32[512,512]{1,0:T(8,128)S(1)}, f32[8,128]{1,0:T(8,128)S(1)}) custom-call(s32[7]{0:T(128)S(1)} %stack.19.refs_0_.info_ref, bf16[1024,512]{1,0:T(8,128)(2,1)S(1)} %get-tuple-element.30.refs_1_.live_ref, bf16[1,4,1024,1024]{3,2,1,0:T(8,128)(2,1)} %refs_2_.15, bf16[1,4,512,512]{3,2,1,0:T(8,128)(2,1)} %refs_3_.15, ...), custom_call_target="tpu_custom_call" | custom-call | flops 200000000 | bytes 1000000 | tf_op jit(solution)/shard_map/term_slot1/pallas_call | solution.py:99
  21.3 3.9 %term_slot2.2 = (f32[512,512]{1,0:T(8,128)}, f32[8,128]{1,0:T(8,128)S(1)}) custom-call(s32[7]{0:T(128)S(1)} %stack.19.refs_0_.info_ref, bf16[1024,512]{1,0:T(8,128)(2,1)S(1)} %get-tuple-element.30.refs_1_.live_ref, bf16[1,4,1024,1024]{3,2,1,0:T(8,128)(2,1)} %refs_2_.15, bf16[1,4,512,512]{3,2,1,0:T(8,128)(2,1)} %refs_3_.15, ...), custom_call_target="tpu_custom_call" | custom-call | flops 200000000 | bytes 1000000 | tf_op jit(solution)/shard_map/term_slot2/pallas_call | solution.py:99
  25.3 3.8 %collective-permute-start.7 = (f32[512,512]{1,0:T(8,128)}, f32[512,512]{1,0:T(8,128)S(1)}, u32[]{:S(2)}, u32[]{:S(2)}) collective-permute-start(f32[512,512]{1,0:T(8,128)} %get-tuple-element.44), channel_id=1, source_target_pairs={{0,1},{4,5},{8,9},{12,13},{1,0},{5,4},{9,8},{13,12},{2,3},{6,7},{1... | collective-permute-start | bytes 3145736 | tf_op jit(solution)/shard_map/ppermute | solution.py:244
  29.0 1.3 %collective-permute-start.6 = (f32[512,512]{1,0:T(8,128)S(1)}, f32[512,512]{1,0:T(8,128)S(1)}, u32[]{:S(2)}, u32[]{:S(2)}) collective-permute-start(f32[512,512]{1,0:T(8,128)S(1)} %get-tuple-element.43), channel_id=1, source_target_pairs={{1,2},{5,6},{9,10},{13,14},{3,0},{7,4},{11,8},{17,18},{21,22},{25,... | collective-permute-start | bytes 3145736 | tf_op jit(solution)/shard_map/ppermute | solution.py:261
  30.3 0.7 collective-permute-start.5
  31.1 3.0 %term_slot2.3 = (f32[512,512]{1,0:T(8,128)S(1)}, f32[8,128]{1,0:T(8,128)S(1)}) custom-call(s32[7]{0:T(128)S(1)} %stack.19.refs_0_.info_ref, bf16[1024,512]{1,0:T(8,128)(2,1)S(1)} %get-tuple-element.30.refs_1_.live_ref, bf16[1,4,1024,1024]{3,2,1,0:T(8,128)(2,1)} %refs_2_.15, bf16[1,4,512,512]{3,2,1,0:T(8,128)(2,1)} %refs_3_.15, f32[8,128]{1,0:T(8,128)S(1)} %touch.3.refs_4_), custom_call_target="tpu_custom_call" | custom-call | flops 200000000 | bytes 1000000 | tf_op jit(solution)/shard_map/term_slot2/pallas_call | solution.py:99
  34.9 7.2 %collective-permute-start.4 = (f32[512,512]{1,0:T(8,128)S(1)}, f32[512,512]{1,0:T(8,128)S(1)}, u32[]{:S(2)}, u32[]{:S(2)}) collective-permute-start(f32[512,512]{1,0:T(8,128)S(1)} %collective-permute-done.1.refs_0_.a_ref), channel_id=1, source_target_pairs={{0,4},{4,8},{8,12},{16,20},{20,24},{24,28}} | collective-permute-start | bytes 3145736 | tf_op jit(solution)/shard_map/ppermute | solution.py:244
  42.2 3.0 %term_slot3.2 = (f32[512,512]{1,0:T(8,128)S(1)}, f32[8,128]{1,0:T(8,128)S(1)}) custom-call(s32[7]{0:T(128)S(1)} %stack.19.refs_0_.info_ref, bf16[1024,512]{1,0:T(8,128)(2,1)S(1)} %get-tuple-element.30.refs_1_.live_ref, bf16[1,4,1024,1024]{3,2,1,0:T(8,128)(2,1)} %refs_2_.15, bf16[1,4,512,512]{3,2,1,0:T(8,128)(2,1)} %refs_3_.15, ...), custom_call_target="tpu_custom_call" | custom-call | flops 200000000 | bytes 1000000 | tf_op jit(solution)/shard_map/term_slot3/pallas_call | solution.py:99
  45.2 2.8 %collective-permute-done.6.refs_0_.a_ref = f32[512,512]{1,0:T(8,128)S(1)} collective-permute-done((f32[512,512]{1,0:T(8,128)S(1)}, f32[512,512]{1,0:T(8,128)S(1)}, u32[]{:S(2)}, u32[]{:S(2)}) %collective-permute-start.6) | collective-permute-done | bytes 1048608 | tf_op jit(solution)/shard_map/ppermute | solution.py:261
  48.1 0.7 collective-permute-start.10
  48.9 5.1 %collective-permute-start.9 = (f32[512,512]{1,0:T(8,128)S(1)}, f32[512,512]{1,0:T(8,128)S(1)}, u32[]{:S(2)}, u32[]{:S(2)}) collective-permute-start(f32[512,512]{1,0:T(8,128)S(1)} %collective-permute-done.6.refs_0_.a_ref), channel_id=1, source_target_pairs={{0,4},{4,8},{8,12},{16,20},{20,24},{24,28}} | collective-permute-start | bytes 3145736 | tf_op jit(solution)/shard_map/ppermute | solution.py:244
  54.4 3.0 %term_slot3.3 = (f32[512,512]{1,0:T(8,128)S(1)}, f32[8,128]{1,0:T(8,128)}) custom-call(s32[7]{0:T(128)S(1)} %stack.19.refs_0_.info_ref, bf16[1024,512]{1,0:T(8,128)(2,1)S(1)} %get-tuple-element.30.refs_1_.live_ref, bf16[1,4,1024,1024]{3,2,1,0:T(8,128)(2,1)} %refs_2_.15, bf16[1,4,512,512]{3,2,1,0:T(8,128)(2,1)} %refs_3_.15, ...), custom_call_target="tpu_custom_call" | custom-call | flops 200000000 | bytes 1000000 | tf_op jit(solution)/shard_map/term_slot3/pallas_call | solution.py:99
  57.4 1.5 %finish_rows.2 = (bf16[1,1024,512]{2,1,0:T(8,128)(2,1)}, f32[16,128]{1,0:T(8,128)S(1)}) custom-call(s32[7]{0:T(128)S(1)} %stack.19.refs_0_.info_ref, bf16[1024,512]{1,0:T(8,128)(2,1)S(1)} %get-tuple-element.30.refs_1_.live_ref, f32[512,512]{1,0:T(8,128)S(1)} %get-tuple-element.52.own_ref, f32[512,512]{1,0:T(8,128)S(1)} %collective-permute-done.1.refs_0_.a_ref, ...), custom_call_target="tpu_custom_call" | custom-call | flops 200000000 | bytes 1000000 | tf_op jit(solution)/shard_map/finish_rows/pallas_call | solution.py:198
  58.9 7.2 %collective-permute-done.9.b_ref = f32[512,512]{1,0:T(8,128)S(1)} collective-permute-done((f32[512,512]{1,0:T(8,128)S(1)}, f32[512,512]{1,0:T(8,128)S(1)}, u32[]{:S(2)}, u32[]{:S(2)}) %collective-permute-start.9) | collective-permute-done | bytes 1048608 | tf_op jit(solution)/shard_map/ppermute | solution.py:244
  66.2 1.5 %finish_rows.3 = (bf16[1,1024,512]{2,1,0:T(8,128)(2,1)}, f32[16,128]{1,0:T(8,128)S(1)}) custom-call(s32[7]{0:T(128)S(1)} %stack.19.refs_0_.info_ref, bf16[1024,512]{1,0:T(8,128)(2,1)S(1)} %get-tuple-element.30.refs_1_.live_ref, f32[512,512]{1,0:T(8,128)S(1)} %get-tuple-element.50.own_ref, ...), custom_call_target="tpu_custom_call", output_to_operand_aliasing={{0}: (7, {})} | custom-call | flops 200000000 | bytes 1000000 | tf_op jit(solution)/shard_map/finish_rows/pallas_call | solution.py:198
  67.7 12.1 %all_to_all.11 = f32[16,1,128]{2,1,0:T(1,128)S(1)} all-to-all(f32[16,1,128]{2,1,0:T(1,128)S(1)} %bitcast.10), channel_id=1, replica_groups=mesh['grp'=2,'sec'=16] {'sec'}, dimensions={0} | all-to-all | bytes 16384 | tf_op jit(solution)/shard_map/all_to_all | solution.py:219
  (23 shorter events, 2.6 us)
Async XLA Ops:
  2.0 1.2 %copy-start = (bf16[1,1024,512]{2,1,0:T(8,128)(2,1)S(1)}, bf16[1,1024,512]{2,1,0:T(8,128)(2,1)}, u32[]{:S(2)}) copy-start(bf16[1,1024,512]{2,1,0:T(8,128)(2,1)} %param.5) | copy-start | bytes 3145732
  6.3 6.8 %collective-permute-start = (f32[512,512]{1,0:T(8,128)S(1)}, f32[512,512]{1,0:T(8,128)S(1)}, u32[]{:S(2)}, u32[]{:S(2)}) collective-permute-start(f32[512,512]{1,0:T(8,128)S(1)} %get-tuple-element.31.a_ref), channel_id=1, source_target_pairs={{0,1},{4,5},{8,9},{12,13},{2,3},{6,7},{10,11},{14,15},{16,17},{20,... | collective-permute-start | bytes 3145736 | tf_op jit(solution)/shard_map/ppermute | solution.py:244
  11.7 6.5 %collective-permute-start.2 = (f32[512,512]{1,0:T(8,128)S(1)}, f32[512,512]{1,0:T(8,128)S(1)}, u32[]{:S(2)}, u32[]{:S(2)}) collective-permute-start(f32[512,512]{1,0:T(8,128)S(1)} %get-tuple-element.35.a_ref), channel_id=1, source_target_pairs={{0,1},{4,5},{8,9},{12,13},{2,3},{6,7},{10,11},{14,15},{16,17},{20,... | collective-permute-start | bytes 3145736 | tf_op jit(solution)/shard_map/ppermute | solution.py:244
  13.2 17.8 %collective-permute-start.1 = (f32[512,512]{1,0:T(8,128)S(1)}, f32[512,512]{1,0:T(8,128)S(1)}, u32[]{:S(2)}, u32[]{:S(2)}) collective-permute-start(f32[512,512]{1,0:T(8,128)S(1)} %get-tuple-element.34), channel_id=1, source_target_pairs={{1,2},{5,6},{9,10},{13,14},{3,0},{7,4},{11,8},{17,18},{21,22},{25,... | collective-permute-start | bytes 3145736 | tf_op jit(solution)/shard_map/ppermute | solution.py:261
  17.5 16.6 %collective-permute-start.8 = (f32[512,512]{1,0:T(8,128)S(1)}, f32[512,512]{1,0:T(8,128)S(1)}, u32[]{:S(2)}, u32[]{:S(2)}) collective-permute-start(f32[512,512]{1,0:T(8,128)S(1)} %get-tuple-element.45.a_ref), channel_id=1, source_target_pairs={{3,6},{7,10},{11,14},{4,1},{8,5},{12,9},{19,22},{23,26},{27,30},{2... | collective-permute-start | bytes 3145736 | tf_op jit(solution)/shard_map/ppermute | solution.py:244
  25.3 16.9 %collective-permute-start.7 = (f32[512,512]{1,0:T(8,128)}, f32[512,512]{1,0:T(8,128)S(1)}, u32[]{:S(2)}, u32[]{:S(2)}) collective-permute-start(f32[512,512]{1,0:T(8,128)} %get-tuple-element.44), channel_id=1, source_target_pairs={{0,1},{4,5},{8,9},{12,13},{1,0},{5,4},{9,8},{13,12},{2,3},{6,7},{1... | collective-permute-start | bytes 3145736 | tf_op jit(solution)/shard_map/ppermute | solution.py:244
  29.0 19.0 %collective-permute-start.6 = (f32[512,512]{1,0:T(8,128)S(1)}, f32[512,512]{1,0:T(8,128)S(1)}, u32[]{:S(2)}, u32[]{:S(2)}) collective-permute-start(f32[512,512]{1,0:T(8,128)S(1)} %get-tuple-element.43), channel_id=1, source_target_pairs={{1,2},{5,6},{9,10},{13,14},{3,0},{7,4},{11,8},{17,18},{21,22},{25,... | collective-permute-start | bytes 3145736 | tf_op jit(solution)/shard_map/ppermute | solution.py:261
  30.3 17.7 %collective-permute-start.5 = (f32[512,512]{1,0:T(8,128)S(1)}, f32[512,512]{1,0:T(8,128)S(1)}, u32[]{:S(2)}, u32[]{:S(2)}) collective-permute-start(f32[512,512]{1,0:T(8,128)S(1)} %get-tuple-element.42.a_ref), channel_id=1, source_target_pairs={{3,6},{7,10},{11,14},{4,1},{8,5},{12,9},{19,22},{23,26},{27,30},{2... | collective-permute-start | bytes 3145736 | tf_op jit(solution)/shard_map/ppermute | solution.py:244
  34.2 23.2 %collective-permute-start.11 = (f32[512,512]{1,0:T(8,128)S(1)}, f32[512,512]{1,0:T(8,128)S(1)}, u32[]{:S(2)}, u32[]{:S(2)}) collective-permute-start(f32[512,512]{1,0:T(8,128)S(1)} %get-tuple-element.53), channel_id=1, source_target_pairs={{1,3},{5,7},{9,11},{13,15},{2,1},{6,5},{10,9},{14,13},{17,19},{21,... | collective-permute-start | bytes 3145736 | tf_op jit(solution)/shard_map/ppermute | solution.py:244
  34.9 19.5 %collective-permute-start.4 = (f32[512,512]{1,0:T(8,128)S(1)}, f32[512,512]{1,0:T(8,128)S(1)}, u32[]{:S(2)}, u32[]{:S(2)}) collective-permute-start(f32[512,512]{1,0:T(8,128)S(1)} %collective-permute-done.1.refs_0_.a_ref), channel_id=1, source_target_pairs={{0,4},{4,8},{8,12},{16,20},{20,24},{24,28}} | collective-permute-start | bytes 3145736 | tf_op jit(solution)/shard_map/ppermute | solution.py:244
  42.2 12.2 %collective-permute-start.3 = (f32[512,512]{1,0:T(8,128)S(1)}, f32[512,512]{1,0:T(8,128)S(1)}, u32[]{:S(2)}, u32[]{:S(2)}) collective-permute-start(f32[512,512]{1,0:T(8,128)S(1)} %get-tuple-element.41), channel_id=1, source_target_pairs={{0,1},{4,5},{8,9},{12,13},{1,0},{5,4},{9,8},{13,12},{2,3},{6,7},{1... | collective-permute-start | bytes 3145736 | tf_op jit(solution)/shard_map/ppermute | solution.py:244
  48.1 10.8 %collective-permute-start.10 = (f32[512,512]{1,0:T(8,128)S(1)}, f32[512,512]{1,0:T(8,128)S(1)}, u32[]{:S(2)}, u32[]{:S(2)}) collective-permute-start(f32[512,512]{1,0:T(8,128)S(1)} %get-tuple-element.51), channel_id=1, source_target_pairs={{1,3},{5,7},{9,11},{13,15},{2,1},{6,5},{10,9},{14,13},{17,19},{21,... | collective-permute-start | bytes 3145736 | tf_op jit(solution)/shard_map/ppermute | solution.py:244
  48.9 17.3 %collective-permute-start.9 = (f32[512,512]{1,0:T(8,128)S(1)}, f32[512,512]{1,0:T(8,128)S(1)}, u32[]{:S(2)}, u32[]{:S(2)}) collective-permute-start(f32[512,512]{1,0:T(8,128)S(1)} %collective-permute-done.6.refs_0_.a_ref), channel_id=1, source_target_pairs={{0,4},{4,8},{8,12},{16,20},{20,24},{24,28}} | collective-permute-start | bytes 3145736 | tf_op jit(solution)/shard_map/ppermute | solution.py:244

commit v4 on v3

--- a/solution.py
+++ b/solution.py
@@ -21,24 +21,57 @@
     return pltpu.CompilerParams(vmem_limit_bytes=mib * MIB)
 
 
-def term_kernel(slot, first, blocks, masks, adds, tokens, *refs):
+def mask_kernel(first, info_ref, psi_hbm, live_ref, wide_ref, _, psi_buf, sems):
+    pieces = sems.shape[0]
+    rows, cols = psi_buf.shape
+    step = rows // pieces
+
+    def copy(i):
+        span = pl.ds(i * step, step)
+        return pltpu.make_async_copy(psi_hbm.at[span, :], psi_buf.at[span, :], sems.at[i])
+
+    for i in range(pieces):
+        copy(i).start()
+    col = lax.broadcasted_iota(jnp.int32, (step, cols), 1) < info_ref[5]
+    row = lax.broadcasted_iota(jnp.int32, (step, cols), 0)
+    for i in range(pieces):
+        copy(i).wait()
+        start = i * step
+        inside = jnp.logical_and(row < info_ref[4] - start, col)
+        values = jnp.where(inside, psi_buf[start : start + step, :].astype(jnp.float32), 0.0)
+        live_ref[start : start + step, :] = values.astype(live_ref.dtype)
+        if start >= first:
+            wide_ref[start - first : start - first + step, :] = values
+
+
+def masked(info, psi, first):
+    rows, cols = psi.shape
+    return pl.pallas_call(
+        functools.partial(mask_kernel, first),
+        out_shape=(
+            jax.ShapeDtypeStruct(psi.shape, psi.dtype),
+            jax.ShapeDtypeStruct((rows - first, cols), jnp.float32),
+            TOKEN,
+        ),
+        in_specs=[SMEM, HBM],
+        out_specs=(WHOLE, WHOLE, ANY),
+        scratch_shapes=[pltpu.VMEM(psi.shape, psi.dtype), pltpu.SemaphoreType.DMA((8,))],
+        compiler_params=params(52),
+        cost_estimate=SMALL,
+        name="mask_psi",
+    )(info, psi)
+
+
+def term_kernel(slot, first, blocks, adds, tokens, *refs):
     refs = list(refs)
     info_ref, live_ref, left_hbm, right_hbm = refs[:4]
     refs = refs[4:]
     add_ref = refs.pop(0) if adds else None
     refs = refs[tokens:]
-    out_ref, _ = refs[:2]
-    refs = refs[2:]
-    live_out = refs.pop(0) if masks else None
-    left_buf, right_buf = refs[:2]
-    sems = refs[-1]
-    psi_buf = refs[2] if masks else None
+    out_ref, _, left_buf, right_buf, sems = refs
     block = left_buf.shape[1]
     term = info_ref[slot]
     copies = []
-    if masks:
-        psi_copy = pltpu.make_async_copy(live_ref, psi_buf, sems.at[blocks + 1])
-        psi_copy.start()
     for i in range(blocks):
         copy = pltpu.make_async_copy(
             left_hbm.at[0, term, pl.ds(first + i * block, block), :], left_buf.at[i], sems.at[i]
@@ -50,17 +83,6 @@
                 right_hbm.at[0, term], right_buf, sems.at[blocks]
             )
             right_copy.start()
-    if masks:
-        psi_copy.wait()
-        rows, cols = psi_buf.shape
-        step = 128
-        col = lax.broadcasted_iota(jnp.int32, (step, cols), 1) < info_ref[5]
-        row = lax.broadcasted_iota(jnp.int32, (step, cols), 0)
-        for r in range(0, rows, step):
-            inside = jnp.logical_and(row < info_ref[4] - r, col)
-            values = psi_buf[r : r + step, :].astype(jnp.float32)
-            live_out[r : r + step, :] = jnp.where(inside, values, 0.0).astype(jnp.bfloat16)
-        live_ref = live_out
     for i in range(blocks):
         copies[i].wait()
         left = jnp.dot(left_buf[i], live_ref[...], preferred_element_type=jnp.float32)
@@ -76,11 +98,11 @@
 
 
 def term_rows(
-    info, slot, live, left_env, right_env, first, count, block, masks=False, added=None, tokens=()
+    info, slot, live, left_env, right_env, first, count, added=None, tokens=()
 ):
     width, cols = live.shape[-2:]
-    blocks = count // block
-    in_specs = [SMEM, HBM if masks else WHOLE, HBM, HBM]
+    blocks, block = 1, count
+    in_specs = [SMEM, WHOLE, HBM, HBM]
     operands = [info, live, left_env, right_env]
     if added is not None:
         in_specs.append(WHOLE)
@@ -92,17 +114,14 @@
         pltpu.VMEM((blocks, block, width), jnp.bfloat16),
         pltpu.VMEM((cols, cols), jnp.bfloat16),
     ]
-    if masks:
-        out_shape.append(jax.ShapeDtypeStruct((width, cols), jnp.bfloat16))
-        scratch.append(pltpu.VMEM((width, cols), jnp.bfloat16))
-    scratch.append(pltpu.SemaphoreType.DMA((blocks + 2,)))
+    scratch.append(pltpu.SemaphoreType.DMA((blocks + 1,)))
     out = pl.pallas_call(
         functools.partial(
-            term_kernel, slot, first, blocks, masks, added is not None, len(tokens)
+            term_kernel, slot, first, blocks, added is not None, len(tokens)
         ),
         out_shape=out_shape,
         in_specs=in_specs,
-        out_specs=[WHOLE, ANY] + [WHOLE] * (len(out_shape) - 2),
+        out_specs=[WHOLE, ANY],
         scratch_shapes=scratch,
         compiler_params=params(50),
         cost_estimate=SMALL,
@@ -113,7 +132,6 @@
 
 def add_kernel(a_ref, b_ref, *refs):
     out_ref = refs[-2]
-    rows = a_ref.shape[0]
     step = 64
 
     def body(i, _):
@@ -121,7 +139,7 @@
         out_ref[span, :] = a_ref[span, :] + b_ref[span, :]
         return _
 
-    lax.fori_loop(0, rows // step, body, 0)
+    lax.fori_loop(0, a_ref.shape[0] // step, body, 0)
 
 
 def add(a, b, *tokens):
@@ -136,6 +154,73 @@
     )(a, b, *tokens)
 
 
+def folded(values):
+    rows, cols = values.shape
+    return jnp.sum(jnp.reshape(values, (rows // 8, 8, cols)), axis=0)
+
+
+def add_energy_kernel(a_ref, b_ref, psi_ref, _, out_ref, energy_ref, token_ref):
+    step = 64
+
+    def body(i, energy):
+        span = pl.ds(pl.multiple_of(i * step, step), step)
+        value = a_ref[span, :] + b_ref[span, :]
+        out_ref[span, :] = value
+        return energy + folded(value * psi_ref[span, :])
+
+    zero = jnp.zeros((8, a_ref.shape[1]), jnp.float32)
+    energy_ref[...] = lax.fori_loop(0, a_ref.shape[0] // step, body, zero)
+
+
+def add_energy(a, b, psi, token):
+    return pl.pallas_call(
+        add_energy_kernel,
+        out_shape=(
+            jax.ShapeDtypeStruct(a.shape, a.dtype),
+            jax.ShapeDtypeStruct((8, a.shape[1]), jnp.float32),
+            TOKEN,
+        ),
+        in_specs=[WHOLE, WHOLE, WHOLE, ANY],
+        out_specs=(WHOLE, WHOLE, ANY),
+        compiler_params=params(),
+        cost_estimate=SMALL,
+        name="add_blocks_energy",
+    )(a, b, psi, token)
+
+
+def rest_kernel(first, info_ref, live_ref, own_ref, a_ref, b_ref, before_ref, out_ref):
+    count, cols = own_ref.shape
+    step = 64
+
+    def work(arrival):
+        def body(i, energy):
+            start = pl.multiple_of(i * step, step)
+            span = pl.ds(start, step)
+            value = own_ref[span, :]
+            if arrival is not None:
+                value = value + arrival[span, :]
+            here = pl.ds(pl.multiple_of(first + start, step), step)
+            return energy + folded(value * live_ref[here, :].astype(jnp.float32))
+
+        energy = lax.fori_loop(0, count // step, body, before_ref[...])
+        out_ref[...] = jnp.full(out_ref.shape, jnp.sum(energy), jnp.float32)
+
+    for n, arrival in enumerate((a_ref, b_ref, None)):
+        pl.when(info_ref[6] == n)(functools.partial(work, arrival))
+
+
+def rest(info, live, own, arrivals, before, first, sectors):
+    return pl.pallas_call(
+        functools.partial(rest_kernel, first),
+        out_shape=jax.ShapeDtypeStruct((sectors, 128), jnp.float32),
+        in_specs=[SMEM] + [WHOLE] * 5,
+        out_specs=WHOLE,
+        compiler_params=params(),
+        cost_estimate=SMALL,
+        name="rest_of_energy",
+    )(info, live, own, *arrivals, before)
+
+
 def touch(*values):
     return pl.pallas_call(
         lambda *refs: None,
@@ -151,7 +236,7 @@
 def finish_kernel(first, info_ref, live_ref, own_ref, a_ref, b_ref, c_ref, before_ref, *refs):
     sigma_hbm, energy_ref, sigma_buf, sems = refs[-4:]
     count, cols = own_ref.shape
-    step = 64
+    step = 32
     piece = count // sems.shape[0]
     col = lax.broadcasted_iota(jnp.int32, (step, cols), 1) < info_ref[5]
     row = lax.broadcasted_iota(jnp.int32, (step, cols), 0)
@@ -163,7 +248,7 @@
         )
 
     def work(arrival):
-        energy = jnp.zeros((8, cols), jnp.float32)
+        energy = before_ref[...]
         for i in range(count // piece):
 
             def body(n, energy):
@@ -172,13 +257,14 @@
                 inside = jnp.logical_and(row < info_ref[4] - first - start, col)
                 total = jnp.where(inside, own_ref[span, :] + arrival[span, :], 0.0)
                 sigma_buf[span, :] = total.astype(sigma_buf.dtype)
+                if first > 0:
+                    return energy
                 here = pl.ds(pl.multiple_of(first + start, step), step)
-                product = live_ref[here, :].astype(jnp.float32) * total
-                return energy + jnp.sum(jnp.reshape(product, (step // 8, 8, cols)), axis=0)
+                return energy + folded(live_ref[here, :].astype(jnp.float32) * total)
 
             energy = lax.fori_loop(0, piece // step, body, energy)
             copy(i).start()
-        energy_ref[...] = before_ref[...] + jnp.sum(energy)
+        energy_ref[...] = energy
 
     for n, arrival in enumerate((a_ref, b_ref, c_ref)):
         pl.when(info_ref[6] == n)(functools.partial(work, arrival))
@@ -186,7 +272,7 @@
         copy(i).wait()
 
 
-def finish(info, live, own, arrivals, before, sigma, first):
+def finish(info, live, own, arrivals, before, sigma, first, *tokens):
     count, cols = own.shape
     in_specs = [SMEM] + [WHOLE] * 6
     operands = [info, live, own, *arrivals, before]
@@ -195,6 +281,8 @@
         in_specs.append(ANY)
         aliases = {len(operands): 0}
         operands.append(sigma)
+    in_specs += [ANY] * len(tokens)
+    operands += tokens
     return pl.pallas_call(
         functools.partial(finish_kernel, first),
         out_shape=(
@@ -244,14 +332,15 @@
         return lax.ppermute(value, "sec", pairs)
 
     rows = psi.shape[1]
-    part = rows // 2
+    part = rows * 5 // 8
     which = jnp.where(place == 0, 1, jnp.where(place == 2, 0, 2))
     orders = [jnp.where(even, 2, 1), jnp.where(even, 3, 2), jnp.where(even, 1, 3), 0]
     info = jnp.stack([*orders, row_sizes[0], col_sizes[0], which]).astype(jnp.int32)
 
     def rows_of(slot, p, *tokens, added=None):
+        count = rows - part if p else part
         return term_rows(
-            info, slot, live, left_env, right_env, p * part, part, 512, added=added, tokens=tokens
+            info, slot, live, left_env, right_env, p * part, count, added=added, tokens=tokens
         )
 
     pairs_up = [(s, s + 1) for s in range(1, sectors, 4) if s + 1 < sectors]
@@ -275,15 +364,15 @@
     def relay(value):
         return send(value, (0, 4))
 
-    first0, token, live = term_rows(
-        info, 0, psi[0], left_env, right_env, 0, part, 512, masks=True
-    )
+    live, wide, token = masked(info, psi[0], part)
+    seen = send(wide, (3, -2), (1, 1))
+    first0, token = rows_of(0, 0, token)
     paired0 = up_chip(first0)
     first1, token = rows_of(0, 1, token)
     paired1 = up_chip(first1)
     both0, token = add(first0, paired0, token)
     raised0 = raise_one(both0)
-    second0, token = rows_of(1, 0, token)
+    second0, token = rows_of(1, 0, token, seen)
     moved0 = along(second0)
     both1, token = add(first1, paired1, token)
     raised1 = raise_one(both1)
@@ -297,18 +386,22 @@
     swapped1 = swap(third1)
     summed0, token = add(second0, moved0, token)
     crossed0 = across(summed0)
-    own0, token = rows_of(3, 0, token, added=swapped0)
     token = touch(raised1, token)
     relayed1 = relay(raised1)
-    summed1, token = add(second1, moved1, token)
+    own0, token = rows_of(3, 0, token, added=swapped0)
+    summed1, energy, token = add_energy(second1, moved1, seen, token)
     crossed1 = across(summed1)
     token = touch(relayed0, token)
     own1, token = rows_of(3, 1, token, added=swapped1)
 
-    energy = jnp.zeros((sectors, 128), jnp.float32)
     sigma, energy = finish(info, live, own0, (raised0, relayed0, crossed0), energy, None, 0)
-    sigma, energy = finish(info, live, own1, (raised1, relayed1, crossed1), energy, sigma, part)
-    return sigma, sum_over_sectors(energy)
+    energy = rest(info, live, own1, (raised1, relayed1), energy, part, sectors)
+    energy = sum_over_sectors(energy)
+    none = jnp.zeros((8, 128), jnp.float32)
+    sigma, _ = finish(
+        info, live, own1, (raised1, relayed1, crossed1), none, sigma, part, energy
+    )
+    return sigma, energy
 
 
 def solution(mesh):

time: 81 us -> 88.4 us (1.091)
  Pallas kernels: 28.9 us -> 37.1 us
  starting transfers between devices: 25.4 us -> 31.3 us
  waiting for transfers between devices: 10.5 us -> 4.93 us
  local copies, waits for them, and re-layouts: 1.31 us -> 0.11 us
    ppermute x10 -> x11, starting transfers between devices: 22.8 us -> 28.7 us  [send(): return lax.ppermute(value, 'sec', pairs)]
    pallas_call x8 -> x11, Pallas kernels: 24.7 us -> 29.6 us  [the longest x8 25.5 us: term_rows(): pl.pallas_call(functools.partial(term_kernel, slot, first, blocks, added...]
    ppermute x10 -> x11, waiting for transfers between devices: 7.7 us -> 4.65 us  [send(): return lax.ppermute(value, 'sec', pairs)]
    ppermute x2, waiting for transfers between devices: 2.78 us -> 0.28 us  [raise_one(): return lax.ppermute(value, 'sec', pairs_up)]
    pallas_call x4 -> x3, Pallas kernels: 0.54 us -> 2.47 us  [add(): pl.pallas_call(add_kernel, out_shape=(jax.ShapeDtypeStruct(a.shape, a.dty...]
    pallas_call x2, Pallas kernels: 3.09 us -> 4.33 us  [finish(): pl.pallas_call(functools.partial(finish_kernel, first), out_shape=(jax.Sh...]
    unnamed x2 -> x6, local copies, waits for them, and re-layouts: 1.23 us -> 0.02 us
  transfers between devices with their start and end apart: 12 -> 13, of which waited for: 3 -> 3; matrix products, arithmetic and copies ran while one was open for 0% -> 0% of each run, Pallas kernels for 30% -> 33%
where the time goes in v4:
time: 88.4 us; the launch traced here: 87.8 us
  Pallas kernels  37.1 us (42%)
  starting transfers between devices  31.3 us (35%)
  blocking collectives  12.1 us (14%)
  waiting for transfers between devices  4.93 us (6%)
  between operations  2.28 us (3%)
    ppermute x11, starting transfers between devices, send(): return lax.ppermute(value, 'sec', pairs)  28.7 us
    pallas_call x8, Pallas kernels, term_rows(): pl.pallas_call(functools.partial(term_kernel, slot, first, blocks, added...  25.5 us
    all_to_all x1, blocking collectives, sum_over_sectors(): arrived = lax.all_to_all(value, 'sec', 0, 0, tiled=True)  12.1 us
    ppermute x11, waiting for transfers between devices, send(): return lax.ppermute(value, 'sec', pairs)  4.65 us
    pallas_call x2, Pallas kernels, finish(): pl.pallas_call(functools.partial(finish_kernel, first), out_shape=(jax.Sh...  4.33 us
    ppermute x2, starting transfers between devices, raise_one(): return lax.ppermute(value, 'sec', pairs_up)  2.57 us
    pallas_call x3, Pallas kernels, add(): pl.pallas_call(add_kernel, out_shape=(jax.ShapeDtypeStruct(a.shape, a.dty...  2.47 us
    pallas_call x1, Pallas kernels, masked(): pl.pallas_call(functools.partial(mask_kernel, first), out_shape=(jax.Shap...  1.93 us
  transfers between devices with their start and end apart: 13, of which 3 were waited for; matrix products, arithmetic and copies ran while one was open for 0% of the time, Pallas kernels for 33%

profile of v4, /device:TPU:0, one launch (start us, length us, event | category | flops | bytes accessed | tf_op | source)
XLA Modules:
  0.0 87.8 jit_solution(6979897545856286961)
XLA Ops:
  2.0 1.9 %mask_psi.1 = (bf16[1024,512]{1,0:T(8,128)(2,1)S(1)}, f32[384,512]{1,0:T(8,128)S(1)}, f32[8,128]{1,0:T(8,128)S(1)}) custom-call(s32[7]{0:T(128)S(1)} %stack.19.info_ref.refs_0_, bf16[1024,512]{1,0:T(8,128)(2,1)} %bitcast.11), custom_call_target="tpu_custom_call" | custom-call | flops 200000000 | bytes 1000000 | tf_op jit(solution)/shard_map/mask_psi/pallas_call | solution.py:49
  4.0 3.3 %term_slot0.2 = (f32[640,512]{1,0:T(8,128)S(1)}, f32[8,128]{1,0:T(8,128)S(1)}) custom-call(s32[7]{0:T(128)S(1)} %stack.19.info_ref.refs_0_, bf16[1024,512]{1,0:T(8,128)(2,1)S(1)} %get-tuple-element.32.refs_1_.live_ref, bf16[1,4,1024,1024]{3,2,1,0:T(8,128)(2,1)} %refs_2_.15, bf16[1,4,512,512]{3,2,1,0:T(8,128)(2,1)} %refs_3_.15, ...), custom_call_target="tpu_custom_call" | custom-call | flops 200000000 | bytes 1000000 | tf_op jit(solution)/shard_map/term_slot0/pallas_call | solution.py:118
  7.3 2.4 %collective-permute-start = (f32[640,512]{1,0:T(8,128)S(1)}, f32[640,512]{1,0:T(8,128)S(1)}, u32[]{:S(2)}, u32[]{:S(2)}) collective-permute-start(f32[640,512]{1,0:T(8,128)S(1)} %get-tuple-element.34.a_ref), channel_id=1, source_target_pairs={{0,1},{4,5},{8,9},{12,13},{2,3},{6,7},{10,11},{14,15},{16,17},{20,... | collective-permute-start | bytes 3932168 | tf_op jit(solution)/shard_map/ppermute | solution.py:332
  10.5 2.6 %term_slot0.3 = (f32[384,512]{1,0:T(8,128)S(1)}, f32[8,128]{1,0:T(8,128)S(1)}) custom-call(s32[7]{0:T(128)S(1)} %stack.19.info_ref.refs_0_, bf16[1024,512]{1,0:T(8,128)(2,1)S(1)} %get-tuple-element.32.refs_1_.live_ref, bf16[1,4,1024,1024]{3,2,1,0:T(8,128)(2,1)} %refs_2_.15, bf16[1,4,512,512]{3,2,1,0:T(8,128)(2,1)S(1)} %copy-done, ...), custom_call_target="tpu_custom_call" | custom-call | flops 200000000 | bytes 1000000 | tf_op jit(solution)/shard_map/term_slot0/pallas_call | solution.py:118
  13.1 5.6 %collective-permute-start.2 = (f32[384,512]{1,0:T(8,128)S(1)}, f32[384,512]{1,0:T(8,128)S(1)}, u32[]{:S(2)}, u32[]{:S(2)}) collective-permute-start(f32[384,512]{1,0:T(8,128)S(1)} %get-tuple-element.38.a_ref), channel_id=1, source_target_pairs={{0,1},{4,5},{8,9},{12,13},{2,3},{6,7},{10,11},{14,15},{16,17},{20,... | collective-permute-start | bytes 2359304 | tf_op jit(solution)/shard_map/ppermute | solution.py:332
  19.0 1.3 %collective-permute-start.1 = (f32[640,512]{1,0:T(8,128)S(1)}, f32[640,512]{1,0:T(8,128)S(1)}, u32[]{:S(2)}, u32[]{:S(2)}) collective-permute-start(f32[640,512]{1,0:T(8,128)S(1)} %get-tuple-element.37), channel_id=1, source_target_pairs={{1,2},{5,6},{9,10},{13,14},{3,0},{7,4},{11,8},{17,18},{21,22},{25,... | collective-permute-start | bytes 3932168 | tf_op jit(solution)/shard_map/ppermute | solution.py:350
  20.3 3.3 %term_slot1.2 = (f32[640,512]{1,0:T(8,128)S(1)}, f32[8,128]{1,0:T(8,128)S(1)}) custom-call(s32[7]{0:T(128)S(1)} %stack.19.info_ref.refs_0_, bf16[1024,512]{1,0:T(8,128)(2,1)S(1)} %get-tuple-element.32.refs_1_.live_ref, bf16[1,4,1024,1024]{3,2,1,0:T(8,128)(2,1)} %refs_2_.15, bf16[1,4,512,512]{3,2,1,0:T(8,128)(2,1)} %refs_3_.15, ...), custom_call_target="tpu_custom_call" | custom-call | flops 200000000 | bytes 1000000 | tf_op jit(solution)/shard_map/term_slot1/pallas_call | solution.py:118
  24.4 1.0 %add_blocks.4 = (f32[384,512]{1,0:T(8,128)}, f32[8,128]{1,0:T(8,128)S(1)}) custom-call(f32[384,512]{1,0:T(8,128)S(1)} %get-tuple-element.38.a_ref, f32[384,512]{1,0:T(8,128)S(1)} %collective-permute-done.2.b_ref, f32[8,128]{1,0:T(8,128)S(1)} %get-tuple-element.41.refs_0_), custom_call_target="tpu_custom_call" | custom-call | flops 200000000 | bytes 1000000 | tf_op jit(solution)/shard_map/add_blocks/pallas_call | solution.py:146
  25.4 3.5 %term_slot1.3 = (f32[384,512]{1,0:T(8,128)}, f32[8,128]{1,0:T(8,128)S(1)}) custom-call(s32[7]{0:T(128)S(1)} %stack.19.info_ref.refs_0_, bf16[1024,512]{1,0:T(8,128)(2,1)S(1)} %get-tuple-element.32.refs_1_.live_ref, bf16[1,4,1024,1024]{3,2,1,0:T(8,128)(2,1)} %refs_2_.15, bf16[1,4,512,512]{3,2,1,0:T(8,128)(2,1)S(1)} %copy-done.1, ...), custom_call_target="tpu_custom_call" | custom-call | flops 200000000 | bytes 1000000 | tf_op jit(solution)/shard_map/term_slot1/pallas_call | solution.py:118
  28.9 3.3 %term_slot2.2 = (f32[640,512]{1,0:T(8,128)S(1)}, f32[8,128]{1,0:T(8,128)S(1)}) custom-call(s32[7]{0:T(128)S(1)} %stack.19.info_ref.refs_0_, bf16[1024,512]{1,0:T(8,128)(2,1)S(1)} %get-tuple-element.32.refs_1_.live_ref, bf16[1,4,1024,1024]{3,2,1,0:T(8,128)(2,1)} %refs_2_.15, bf16[1,4,512,512]{3,2,1,0:T(8,128)(2,1)} %refs_3_.15, ...), custom_call_target="tpu_custom_call" | custom-call | flops 200000000 | bytes 1000000 | tf_op jit(solution)/shard_map/term_slot2/pallas_call | solution.py:118
  32.2 3.4 %collective-permute-start.7 = (f32[640,512]{1,0:T(8,128)S(1)}, f32[640,512]{1,0:T(8,128)S(1)}, u32[]{:S(2)}, u32[]{:S(2)}) collective-permute-start(f32[640,512]{1,0:T(8,128)S(1)} %get-tuple-element.47), channel_id=1, source_target_pairs={{0,1},{4,5},{8,9},{12,13},{1,0},{5,4},{9,8},{13,12},{2,3},{6,7},{1... | collective-permute-start | bytes 3932168 | tf_op jit(solution)/shard_map/ppermute | solution.py:332
  35.6 1.3 %collective-permute-start.8 = (f32[384,512]{1,0:T(8,128)}, f32[384,512]{1,0:T(8,128)S(1)}, u32[]{:S(2)}, u32[]{:S(2)}) collective-permute-start(f32[384,512]{1,0:T(8,128)} %get-tuple-element.48), channel_id=1, source_target_pairs={{1,2},{5,6},{9,10},{13,14},{3,0},{7,4},{11,8},{17,18},{21,22},{25,... | collective-permute-start | bytes 2359304 | tf_op jit(solution)/shard_map/ppermute | solution.py:350
  37.9 10.1 %collective-permute-start.5 = (f32[640,512]{1,0:T(8,128)S(1)}, f32[640,512]{1,0:T(8,128)S(1)}, u32[]{:S(2)}, u32[]{:S(2)}) collective-permute-start(f32[640,512]{1,0:T(8,128)S(1)} %collective-permute-done.1.refs_0_.a_ref), channel_id=1, source_target_pairs={{0,4},{4,8},{8,12},{16,20},{20,24},{24,28}} | collective-permute-start | bytes 3932168 | tf_op jit(solution)/shard_map/ppermute | solution.py:332
  48.0 3.5 %term_slot2.3 = (f32[384,512]{1,0:T(8,128)}, f32[8,128]{1,0:T(8,128)S(1)}) custom-call(s32[7]{0:T(128)S(1)} %stack.19.info_ref.refs_0_, bf16[1024,512]{1,0:T(8,128)(2,1)S(1)} %get-tuple-element.32.refs_1_.live_ref, bf16[1,4,1024,1024]{3,2,1,0:T(8,128)(2,1)} %refs_2_.15, bf16[1,4,512,512]{3,2,1,0:T(8,128)(2,1)S(1)} %copy-done.2, f32[8,128]{1,0:T(8,128)S(1)} %touch.3.refs_4_), custom_call_target="tpu_custom_call" | custom-call | flops 200000000 | bytes 1000000 | tf_op jit(solution)/shard_map/term_slot2/pallas_call | solution.py:118
  51.6 1.3 %add_blocks.5 = (f32[640,512]{1,0:T(8,128)}, f32[8,128]{1,0:T(8,128)S(1)}) custom-call(f32[640,512]{1,0:T(8,128)S(1)} %get-tuple-element.49.a_ref, f32[640,512]{1,0:T(8,128)S(1)} %collective-permute-done.9.b_ref, f32[8,128]{1,0:T(8,128)S(1)} %get-tuple-element.50.refs_0_), custom_call_target="tpu_custom_call" | custom-call | flops 200000000 | bytes 1000000 | tf_op jit(solution)/shard_map/add_blocks/pallas_call | solution.py:146
  53.7 3.5 %collective-permute-start.10 = (f32[384,512]{1,0:T(8,128)S(1)}, f32[384,512]{1,0:T(8,128)S(1)}, u32[]{:S(2)}, u32[]{:S(2)}) collective-permute-start(f32[384,512]{1,0:T(8,128)S(1)} %collective-permute-done.8.refs_0_.a_ref), channel_id=1, source_target_pairs={{0,4},{4,8},{8,12},{16,20},{20,24},{24,28}} | collective-permute-start | bytes 2359304 | tf_op jit(solution)/shard_map/ppermute | solution.py:332
  57.2 3.2 %term_slot3.2 = (f32[640,512]{1,0:T(8,128)S(1)}, f32[8,128]{1,0:T(8,128)S(1)}) custom-call(s32[7]{0:T(128)S(1)} %stack.19.info_ref.refs_0_, bf16[1024,512]{1,0:T(8,128)(2,1)S(1)} %get-tuple-element.32.refs_1_.live_ref, bf16[1,4,1024,1024]{3,2,1,0:T(8,128)(2,1)} %refs_2_.15, bf16[1,4,512,512]{3,2,1,0:T(8,128)(2,1)} %refs_3_.15, ...), custom_call_target="tpu_custom_call" | custom-call | flops 200000000 | bytes 1000000 | tf_op jit(solution)/shard_map/term_slot3/pallas_call | solution.py:118
  60.4 1.3 %add_blocks_energy.1 = (f32[384,512]{1,0:T(8,128)S(1)}, f32[8,512]{1,0:T(8,128)S(1)}, f32[8,128]{1,0:T(8,128)S(1)}) custom-call(f32[384,512]{1,0:T(8,128)} %get-tuple-element.46.a_ref, f32[384,512]{1,0:T(8,128)S(1)} %collective-permute-done.6.b_ref, f32[384,512]{1,0:T(8,128)S(1)} %collective-permute-done.3.refs_5_.psi_ref, f32[8,128]{1,0:T(8,128)S(1)} %get-tuple-element.52._), custom_call_target="tpu_custom_call" | custom-call | flops 200000000 | bytes 1000000 | tf_op jit(solution)/shard_map/add_blocks_energy/pallas_call | solution.py:176
  63.1 2.6 %term_slot3.3 = (f32[384,512]{1,0:T(8,128)S(1)}, f32[8,128]{1,0:T(8,128)}) custom-call(s32[7]{0:T(128)S(1)} %stack.19.info_ref.refs_0_, bf16[1024,512]{1,0:T(8,128)(2,1)S(1)} %get-tuple-element.32.refs_1_.live_ref, bf16[1,4,1024,1024]{3,2,1,0:T(8,128)(2,1)} %refs_2_.15, bf16[1,4,512,512]{3,2,1,0:T(8,128)(2,1)} %refs_3_.15, ...), custom_call_target="tpu_custom_call" | custom-call | flops 200000000 | bytes 1000000 | tf_op jit(solution)/shard_map/term_slot3/pallas_call | solution.py:118
  65.7 1.7 %finish_rows.2 = (bf16[1,1024,512]{2,1,0:T(8,128)(2,1)}, f32[8,512]{1,0:T(8,128)S(1)}) custom-call(s32[7]{0:T(128)S(1)} %stack.19.info_ref.refs_0_, bf16[1024,512]{1,0:T(8,128)(2,1)S(1)} %get-tuple-element.32.refs_1_.live_ref, f32[640,512]{1,0:T(8,128)S(1)} %get-tuple-element.56.own_ref, f32[640,512]{1,0:T(8,128)S(1)} %collective-permute-done.1.refs_0_.a_ref, ...), custom_call_target="tpu_custom_call" | custom-call | flops 200000000 | bytes 1000000 | tf_op jit(solution)/shard_map/finish_rows/pallas_call | solution.py:286
  67.4 4.1 %collective-permute-done.10.b_ref = f32[384,512]{1,0:T(8,128)S(1)} collective-permute-done((f32[384,512]{1,0:T(8,128)S(1)}, f32[384,512]{1,0:T(8,128)S(1)}, u32[]{:S(2)}, u32[]{:S(2)}) %collective-permute-start.10) | collective-permute-done | bytes 786464 | tf_op jit(solution)/shard_map/ppermute | solution.py:332
  71.5 0.9 rest_of_energy.1
  72.3 12.1 %all_to_all.11 = f32[16,1,128]{2,1,0:T(1,128)S(1)} all-to-all(f32[16,1,128]{2,1,0:T(1,128)S(1)} %bitcast.9), channel_id=1, replica_groups=mesh['grp'=2,'sec'=16] {'sec'}, dimensions={0} | all-to-all | bytes 16384 | tf_op jit(solution)/shard_map/all_to_all | solution.py:307
  85.1 2.7 %finish_rows.3 = (bf16[1,1024,512]{2,1,0:T(8,128)(2,1)}, f32[8,128]{1,0:T(8,128)}) custom-call(s32[7]{0:T(128)S(1)} %stack.19.info_ref.refs_0_, bf16[1024,512]{1,0:T(8,128)(2,1)S(1)} %get-tuple-element.32.refs_1_.live_ref, f32[384,512]{1,0:T(8,128)S(1)} %get-tuple-element.54.own_ref, ...), custom_call_target="tpu_custom_call", output_to_operand_aliasing={{0}: (7, {})} | custom-call | flops 200000000 | bytes 1000000 | tf_op jit(solution)/shard_map/finish_rows/pallas_call | solution.py:286
  (31 shorter events, 5.5 us)
Async XLA Ops:
  4.0 6.5 %copy-start = (bf16[1,4,512,512]{3,2,1,0:T(8,128)(2,1)S(1)}, bf16[1,4,512,512]{3,2,1,0:T(8,128)(2,1)}, u32[]{:S(2)}) copy-start(bf16[1,4,512,512]{3,2,1,0:T(8,128)(2,1)} %refs_3_.15) | copy-start | bytes 6291460
  7.3 11.5 %collective-permute-start = (f32[640,512]{1,0:T(8,128)S(1)}, f32[640,512]{1,0:T(8,128)S(1)}, u32[]{:S(2)}, u32[]{:S(2)}) collective-permute-start(f32[640,512]{1,0:T(8,128)S(1)} %get-tuple-element.34.a_ref), channel_id=1, source_target_pairs={{0,1},{4,5},{8,9},{12,13},{2,3},{6,7},{10,11},{14,15},{16,17},{20,... | collective-permute-start | bytes 3932168 | tf_op jit(solution)/shard_map/ppermute | solution.py:332
  9.7 10.5 %collective-permute-start.3 = (f32[384,512]{1,0:T(8,128)S(1)}, f32[384,512]{1,0:T(8,128)S(1)}, u32[]{:S(2)}, u32[]{:S(2)}) collective-permute-start(f32[384,512]{1,0:T(8,128)S(1)} %get-tuple-element.40), channel_id=1, source_target_pairs={{3,1},{7,5},{11,9},{15,13},{1,2},{5,6},{9,10},{13,14},{19,17},{23,... | collective-permute-start | bytes 2359304 | tf_op jit(solution)/shard_map/ppermute | solution.py:332
  13.1 11.2 %collective-permute-start.2 = (f32[384,512]{1,0:T(8,128)S(1)}, f32[384,512]{1,0:T(8,128)S(1)}, u32[]{:S(2)}, u32[]{:S(2)}) collective-permute-start(f32[384,512]{1,0:T(8,128)S(1)} %get-tuple-element.38.a_ref), channel_id=1, source_target_pairs={{0,1},{4,5},{8,9},{12,13},{2,3},{6,7},{10,11},{14,15},{16,17},{20,... | collective-permute-start | bytes 2359304 | tf_op jit(solution)/shard_map/ppermute | solution.py:332
  19.0 18.9 %collective-permute-start.1 = (f32[640,512]{1,0:T(8,128)S(1)}, f32[640,512]{1,0:T(8,128)S(1)}, u32[]{:S(2)}, u32[]{:S(2)}) collective-permute-start(f32[640,512]{1,0:T(8,128)S(1)} %get-tuple-element.37), channel_id=1, source_target_pairs={{1,2},{5,6},{9,10},{13,14},{3,0},{7,4},{11,8},{17,18},{21,22},{25,... | collective-permute-start | bytes 3932168 | tf_op jit(solution)/shard_map/ppermute | solution.py:350
  20.3 5.1 %copy-start.1 = (bf16[1,4,512,512]{3,2,1,0:T(8,128)(2,1)S(1)}, bf16[1,4,512,512]{3,2,1,0:T(8,128)(2,1)}, u32[]{:S(2)}) copy-start(bf16[1,4,512,512]{3,2,1,0:T(8,128)(2,1)} %refs_3_.15) | copy-start | bytes 6291460
  23.6 28.0 %collective-permute-start.9 = (f32[640,512]{1,0:T(8,128)S(1)}, f32[640,512]{1,0:T(8,128)S(1)}, u32[]{:S(2)}, u32[]{:S(2)}) collective-permute-start(f32[640,512]{1,0:T(8,128)S(1)} %get-tuple-element.49.a_ref), channel_id=1, source_target_pairs={{3,6},{7,10},{11,14},{4,1},{8,5},{12,9},{19,22},{23,26},{27,30},{2... | collective-permute-start | bytes 3932168 | tf_op jit(solution)/shard_map/ppermute | solution.py:332
  28.9 19.1 %copy-start.2 = (bf16[1,4,512,512]{3,2,1,0:T(8,128)(2,1)S(1)}, bf16[1,4,512,512]{3,2,1,0:T(8,128)(2,1)}, u32[]{:S(2)}) copy-start(bf16[1,4,512,512]{3,2,1,0:T(8,128)(2,1)} %refs_3_.15) | copy-start | bytes 6291460
  32.2 21.5 %collective-permute-start.7 = (f32[640,512]{1,0:T(8,128)S(1)}, f32[640,512]{1,0:T(8,128)S(1)}, u32[]{:S(2)}, u32[]{:S(2)}) collective-permute-start(f32[640,512]{1,0:T(8,128)S(1)} %get-tuple-element.47), channel_id=1, source_target_pairs={{0,1},{4,5},{8,9},{12,13},{1,0},{5,4},{9,8},{13,12},{2,3},{6,7},{1... | collective-permute-start | bytes 3932168 | tf_op jit(solution)/shard_map/ppermute | solution.py:332
  35.6 18.0 %collective-permute-start.8 = (f32[384,512]{1,0:T(8,128)}, f32[384,512]{1,0:T(8,128)S(1)}, u32[]{:S(2)}, u32[]{:S(2)}) collective-permute-start(f32[384,512]{1,0:T(8,128)} %get-tuple-element.48), channel_id=1, source_target_pairs={{1,2},{5,6},{9,10},{13,14},{3,0},{7,4},{11,8},{17,18},{21,22},{25,... | collective-permute-start | bytes 2359304 | tf_op jit(solution)/shard_map/ppermute | solution.py:350
  36.9 23.5 %collective-permute-start.6 = (f32[384,512]{1,0:T(8,128)}, f32[384,512]{1,0:T(8,128)S(1)}, u32[]{:S(2)}, u32[]{:S(2)}) collective-permute-start(f32[384,512]{1,0:T(8,128)} %get-tuple-element.46.a_ref), channel_id=1, source_target_pairs={{3,6},{7,10},{11,14},{4,1},{8,5},{12,9},{19,22},{23,26},{27,30},{2... | collective-permute-start | bytes 2359304 | tf_op jit(solution)/shard_map/ppermute | solution.py:332
  37.9 25.2 %collective-permute-start.5 = (f32[640,512]{1,0:T(8,128)S(1)}, f32[640,512]{1,0:T(8,128)S(1)}, u32[]{:S(2)}, u32[]{:S(2)}) collective-permute-start(f32[640,512]{1,0:T(8,128)S(1)} %collective-permute-done.1.refs_0_.a_ref), channel_id=1, source_target_pairs={{0,4},{4,8},{8,12},{16,20},{20,24},{24,28}} | collective-permute-start | bytes 3932168 | tf_op jit(solution)/shard_map/ppermute | solution.py:332
  52.9 12.8 %collective-permute-start.12 = (f32[640,512]{1,0:T(8,128)}, f32[640,512]{1,0:T(8,128)S(1)}, u32[]{:S(2)}, u32[]{:S(2)}) collective-permute-start(f32[640,512]{1,0:T(8,128)} %get-tuple-element.57), channel_id=1, source_target_pairs={{1,3},{5,7},{9,11},{13,15},{2,1},{6,5},{10,9},{14,13},{17,19},{21,... | collective-permute-start | bytes 3932168 | tf_op jit(solution)/shard_map/ppermute | solution.py:332
  53.6 9.4 %collective-permute-start.4 = (f32[384,512]{1,0:T(8,128)}, f32[384,512]{1,0:T(8,128)S(1)}, u32[]{:S(2)}, u32[]{:S(2)}) collective-permute-start(f32[384,512]{1,0:T(8,128)} %get-tuple-element.45), channel_id=1, source_target_pairs={{0,1},{4,5},{8,9},{12,13},{1,0},{5,4},{9,8},{13,12},{2,3},{6,7},{1... | collective-permute-start | bytes 2359304 | tf_op jit(solution)/shard_map/ppermute | solution.py:332
  53.7 17.8 %collective-permute-start.10 = (f32[384,512]{1,0:T(8,128)S(1)}, f32[384,512]{1,0:T(8,128)S(1)}, u32[]{:S(2)}, u32[]{:S(2)}) collective-permute-start(f32[384,512]{1,0:T(8,128)S(1)} %collective-permute-done.8.refs_0_.a_ref), channel_id=1, source_target_pairs={{0,4},{4,8},{8,12},{16,20},{20,24},{24,28}} | collective-permute-start | bytes 2359304 | tf_op jit(solution)/shard_map/ppermute | solution.py:332
  61.8 23.3 %collective-permute-start.11 = (f32[384,512]{1,0:T(8,128)S(1)}, f32[384,512]{1,0:T(8,128)S(1)}, u32[]{:S(2)}, u32[]{:S(2)}) collective-permute-start(f32[384,512]{1,0:T(8,128)S(1)} %get-tuple-element.55), channel_id=1, source_target_pairs={{1,3},{5,7},{9,11},{13,15},{2,1},{6,5},{10,9},{14,13},{17,19},{21,... | collective-permute-start | bytes 2359304 | tf_op jit(solution)/shard_map/ppermute | solution.py:332

commit v5 on v3

--- a/solution.py
+++ b/solution.py
@@ -8,6 +8,8 @@
 from jax.sharding import PartitionSpec as P
 
 MIB = 1024 * 1024
+FIRST_MIB = 44
+BRING_MIB = 42
 
 ANY = pl.BlockSpec(memory_space=pl.ANY)
 HBM = pl.BlockSpec(memory_space=pltpu.HBM)
@@ -21,94 +23,138 @@
     return pltpu.CompilerParams(vmem_limit_bytes=mib * MIB)
 
 
-def term_kernel(slot, first, blocks, masks, adds, tokens, *refs):
+def fetch(info_ref, slot, left_hbm, right_hbm, left_ref, right_ref, sems):
+    term = info_ref[slot]
+    half = left_ref.shape[0] // 2
+    copies = []
+    for i in range(2):
+        span = pl.ds(i * half, half)
+        copies.append(
+            pltpu.make_async_copy(left_hbm.at[0, term, span, :], left_ref.at[span, :], sems.at[i])
+        )
+    copies.insert(1, pltpu.make_async_copy(right_hbm.at[0, term], right_ref, sems.at[2]))
+    return copies
+
+
+def multiply(left, live, right):
+    first = jnp.dot(left, live, preferred_element_type=jnp.float32).astype(jnp.bfloat16)
+    return jnp.dot(first, right, preferred_element_type=jnp.float32)
+
+
+def first_kernel(info_ref, psi_hbm, left_hbm, right_hbm, *refs):
+    out_ref, _, live_ref, left0, right0, left1, right1, psi_buf, sems, psi_sems = refs
+    pieces = psi_sems.shape[0]
+    rows, cols = psi_buf.shape
+    step = rows // pieces
+
+    def copy(i):
+        span = pl.ds(i * step, step)
+        return pltpu.make_async_copy(psi_hbm.at[span, :], psi_buf.at[span, :], psi_sems.at[i])
+
+    for i in range(pieces):
+        copy(i).start()
+    needed = fetch(info_ref, 0, left_hbm, right_hbm, left0, right0, sems.at[0])
+    ahead = fetch(info_ref, 1, left_hbm, right_hbm, left1, right1, sems.at[1])
+    needed[0].start()
+    needed[1].start()
+    col = lax.broadcasted_iota(jnp.int32, (step, cols), 1) < info_ref[5]
+    row = lax.broadcasted_iota(jnp.int32, (step, cols), 0)
+    for i in range(pieces):
+        copy(i).wait()
+        inside = jnp.logical_and(row < info_ref[4] - i * step, col)
+        values = psi_buf[i * step : (i + 1) * step, :].astype(jnp.float32)
+        live_ref[i * step : (i + 1) * step, :] = jnp.where(inside, values, 0.0).astype(
+            live_ref.dtype
+        )
+    for later in (needed[2], *ahead):
+        later.start()
+    needed[0].wait()
+    needed[1].wait()
+    out_ref[...] = multiply(left0[: out_ref.shape[0], :], live_ref[...], right0[...])
+    for later in (needed[2], *ahead):
+        later.wait()
+
+
+def operand_shapes(width, cols):
+    return [
+        jax.ShapeDtypeStruct((width, width), jnp.bfloat16),
+        jax.ShapeDtypeStruct((cols, cols), jnp.bfloat16),
+    ]
+
+
+def first_rows(info, psi, left_env, right_env, count):
+    width, cols = psi.shape
+    out_shape = [jax.ShapeDtypeStruct((count, cols), jnp.float32), TOKEN]
+    out_shape += [jax.ShapeDtypeStruct(psi.shape, psi.dtype), *operand_shapes(width, cols) * 2]
+    return pl.pallas_call(
+        first_kernel,
+        out_shape=out_shape,
+        in_specs=[SMEM, HBM, HBM, HBM],
+        out_specs=[WHOLE, ANY] + [WHOLE] * 5,
+        scratch_shapes=[
+            pltpu.VMEM(psi.shape, psi.dtype),
+            pltpu.SemaphoreType.DMA((2, 3)),
+            pltpu.SemaphoreType.DMA((4,)),
+        ],
+        compiler_params=params(FIRST_MIB),
+        cost_estimate=SMALL,
+        name="first_rows",
+    )(info, psi, left_env, right_env)
+
+
+def term_kernel(first, adds, slot, tokens, info_ref, live_ref, left_ref, right_ref, *refs):
     refs = list(refs)
-    info_ref, live_ref, left_hbm, right_hbm = refs[:4]
-    refs = refs[4:]
     add_ref = refs.pop(0) if adds else None
-    refs = refs[tokens:]
-    out_ref, _ = refs[:2]
-    refs = refs[2:]
-    live_out = refs.pop(0) if masks else None
-    left_buf, right_buf = refs[:2]
-    sems = refs[-1]
-    psi_buf = refs[2] if masks else None
-    block = left_buf.shape[1]
-    term = info_ref[slot]
     copies = []
-    if masks:
-        psi_copy = pltpu.make_async_copy(live_ref, psi_buf, sems.at[blocks + 1])
-        psi_copy.start()
-    for i in range(blocks):
-        copy = pltpu.make_async_copy(
-            left_hbm.at[0, term, pl.ds(first + i * block, block), :], left_buf.at[i], sems.at[i]
-        )
-        copy.start()
-        copies.append(copy)
-        if i == 0:
-            right_copy = pltpu.make_async_copy(
-                right_hbm.at[0, term], right_buf, sems.at[blocks]
-            )
-            right_copy.start()
-    if masks:
-        psi_copy.wait()
-        rows, cols = psi_buf.shape
-        step = 128
-        col = lax.broadcasted_iota(jnp.int32, (step, cols), 1) < info_ref[5]
-        row = lax.broadcasted_iota(jnp.int32, (step, cols), 0)
-        for r in range(0, rows, step):
-            inside = jnp.logical_and(row < info_ref[4] - r, col)
-            values = psi_buf[r : r + step, :].astype(jnp.float32)
-            live_out[r : r + step, :] = jnp.where(inside, values, 0.0).astype(jnp.bfloat16)
-        live_ref = live_out
-    for i in range(blocks):
-        copies[i].wait()
-        left = jnp.dot(left_buf[i], live_ref[...], preferred_element_type=jnp.float32)
-        if i == 0:
-            right_copy.wait()
-        value = jnp.dot(
-            left.astype(jnp.bfloat16), right_buf[...], preferred_element_type=jnp.float32
-        )
+    if slot is not None:
+        left_hbm, right_hbm = refs[:2]
+        sems = refs[-1]
+        out_ref, _, left_next, right_next = refs[2 + tokens : -1]
+        copies = fetch(info_ref, slot, left_hbm, right_hbm, left_next, right_next, sems)
+        for copy in copies:
+            copy.start()
+    else:
+        out_ref, _ = refs[tokens:]
+    count = out_ref.shape[0]
+    block = min(count, 512)
+    for i in range(count // block):
         span = pl.ds(i * block, block)
+        value = multiply(left_ref[pl.ds(first + i * block, block), :], live_ref[...], right_ref[...])
         if adds:
             value = value + add_ref[span, :]
         out_ref[span, :] = value
-
-
-def term_rows(
-    info, slot, live, left_env, right_env, first, count, block, masks=False, added=None, tokens=()
-):
-    width, cols = live.shape[-2:]
-    blocks = count // block
-    in_specs = [SMEM, HBM if masks else WHOLE, HBM, HBM]
-    operands = [info, live, left_env, right_env]
+    for copy in copies:
+        copy.wait()
+
+
+def term_rows(info, live, operands, first, count, *tokens, added=None, bring=None):
+    width, cols = live.shape
+    in_specs = [SMEM, WHOLE, WHOLE, WHOLE]
+    args = [info, live, *operands]
+    out_shape = [jax.ShapeDtypeStruct((count, cols), jnp.float32), TOKEN]
+    out_specs = [WHOLE, ANY]
+    scratch = []
+    slot = None
     if added is not None:
         in_specs.append(WHOLE)
-        operands.append(added)
-    in_specs += [ANY] * len(tokens)
-    operands += tokens
-    out_shape = [jax.ShapeDtypeStruct((count, cols), jnp.float32), TOKEN]
-    scratch = [
-        pltpu.VMEM((blocks, block, width), jnp.bfloat16),
-        pltpu.VMEM((cols, cols), jnp.bfloat16),
-    ]
-    if masks:
-        out_shape.append(jax.ShapeDtypeStruct((width, cols), jnp.bfloat16))
-        scratch.append(pltpu.VMEM((width, cols), jnp.bfloat16))
-    scratch.append(pltpu.SemaphoreType.DMA((blocks + 2,)))
-    out = pl.pallas_call(
-        functools.partial(
-            term_kernel, slot, first, blocks, masks, added is not None, len(tokens)
-        ),
+        args.append(added)
+    if bring is not None:
+        slot = bring[0]
+        in_specs += [HBM, HBM]
+        args += bring[1:]
+        out_shape += operand_shapes(width, cols)
+        out_specs += [WHOLE, WHOLE]
+        scratch.append(pltpu.SemaphoreType.DMA((3,)))
+    return pl.pallas_call(
+        functools.partial(term_kernel, first, added is not None, slot, len(tokens)),
         out_shape=out_shape,
-        in_specs=in_specs,
-        out_specs=[WHOLE, ANY] + [WHOLE] * (len(out_shape) - 2),
+        in_specs=in_specs + [ANY] * len(tokens),
+        out_specs=out_specs,
         scratch_shapes=scratch,
-        compiler_params=params(50),
-        cost_estimate=SMALL,
-        name=f"term_slot{slot}",
-    )(*operands)
-    return out
+        compiler_params=params(12 if slot is None else BRING_MIB),
+        cost_estimate=SMALL,
+        name="term_rows",
+    )(*args, *tokens)
 
 
 def add_kernel(a_ref, b_ref, *refs):
@@ -249,11 +295,6 @@
     orders = [jnp.where(even, 2, 1), jnp.where(even, 3, 2), jnp.where(even, 1, 3), 0]
     info = jnp.stack([*orders, row_sizes[0], col_sizes[0], which]).astype(jnp.int32)
 
-    def rows_of(slot, p, *tokens, added=None):
-        return term_rows(
-            info, slot, live, left_env, right_env, p * part, part, 512, added=added, tokens=tokens
-        )
-
     pairs_up = [(s, s + 1) for s in range(1, sectors, 4) if s + 1 < sectors]
     pairs_up += [(s, s - 3) for s in range(3, sectors, 4) if s + 1 < sectors]
 
@@ -275,35 +316,38 @@
     def relay(value):
         return send(value, (0, 4))
 
-    first0, token, live = term_rows(
-        info, 0, psi[0], left_env, right_env, 0, part, 512, masks=True
+    first0, token, live, *ops = first_rows(info, psi[0], left_env, right_env, part)
+    ops0, ops1 = ops[:2], ops[2:]
+    paired0 = up_chip(first0)
+    first1, token, *ops2 = term_rows(
+        info, live, ops0, part, part, token, bring=(2, left_env, right_env)
     )
-    paired0 = up_chip(first0)
-    first1, token = rows_of(0, 1, token)
     paired1 = up_chip(first1)
     both0, token = add(first0, paired0, token)
     raised0 = raise_one(both0)
-    second0, token = rows_of(1, 0, token)
+    second0, token, *ops3 = term_rows(
+        info, live, ops1, 0, part, token, bring=(3, left_env, right_env)
+    )
     moved0 = along(second0)
     both1, token = add(first1, paired1, token)
     raised1 = raise_one(both1)
-    second1, token = rows_of(1, 1, token)
+    second1, token = term_rows(info, live, ops1, part, part, token)
     moved1 = along(second1)
-    third0, token = rows_of(2, 0, token)
+    third0, token = term_rows(info, live, ops2, 0, part, token)
     swapped0 = swap(third0)
     token = touch(raised0, token)
     relayed0 = relay(raised0)
-    third1, token = rows_of(2, 1, token)
+    third1, token = term_rows(info, live, ops2, part, part, token)
     swapped1 = swap(third1)
     summed0, token = add(second0, moved0, token)
     crossed0 = across(summed0)
-    own0, token = rows_of(3, 0, token, added=swapped0)
+    own0, token = term_rows(info, live, ops3, 0, part, token, added=swapped0)
     token = touch(raised1, token)
     relayed1 = relay(raised1)
     summed1, token = add(second1, moved1, token)
     crossed1 = across(summed1)
     token = touch(relayed0, token)
-    own1, token = rows_of(3, 1, token, added=swapped1)
+    own1, token = term_rows(info, live, ops3, part, part, token, added=swapped1)
 
     energy = jnp.zeros((sectors, 128), jnp.float32)
     sigma, energy = finish(info, live, own0, (raised0, relayed0, crossed0), energy, None, 0)

time: 81 us -> 81.6 us (level)
  waiting for transfers between devices: 10.5 us -> 26.1 us
  Pallas kernels: 28.9 us -> 19.5 us
  starting transfers between devices: 25.4 us -> 21 us
  blocking collectives: 12.1 us -> 11.1 us
    pallas_call x8, Pallas kernels: 24.7 us -> 15.2 us  [the longest x7 11.9 us: term_rows(): pl.pallas_call(functools.partial(term_kernel, first, added is not None, s...]
    ppermute x2, waiting for transfers between devices: 2.78 us -> 11.6 us  [raise_one(): return lax.ppermute(value, 'sec', pairs_up)]
    ppermute x10, waiting for transfers between devices: 7.7 us -> 14.5 us  [send(): return lax.ppermute(value, 'sec', pairs)]
    ppermute x10, starting transfers between devices: 22.8 us -> 18.4 us  [send(): return lax.ppermute(value, 'sec', pairs)]
    all_to_all x1, blocking collectives: 12.1 us -> 11.1 us  [sum_over_sectors(): arrived = lax.all_to_all(value, 'sec', 0, 0, tiled=True)]
  transfers between devices with their start and end apart: 12 -> 12, of which waited for: 3 -> 4; matrix products, arithmetic and copies ran while one was open for 0% -> 0% of each run, Pallas kernels for 30% -> 17%
where the time goes in v5:
time: 81.6 us; the launch traced here: 81.2 us
  waiting for transfers between devices  26.1 us (32%)
  starting transfers between devices  21 us (26%)
  Pallas kernels  19.5 us (24%)
  blocking collectives  11.1 us (14%)
  between operations  2.2 us (3%)
  local copies, waits for them, and re-layouts  1.32 us (2%)
    ppermute x10, starting transfers between devices, send(): return lax.ppermute(value, 'sec', pairs)  18.4 us
    ppermute x10, waiting for transfers between devices, send(): return lax.ppermute(value, 'sec', pairs)  14.5 us
    pallas_call x7, Pallas kernels, term_rows(): pl.pallas_call(functools.partial(term_kernel, first, added is not None, s...  11.9 us
    ppermute x2, waiting for transfers between devices, raise_one(): return lax.ppermute(value, 'sec', pairs_up)  11.6 us
    all_to_all x1, blocking collectives, sum_over_sectors(): arrived = lax.all_to_all(value, 'sec', 0, 0, tiled=True)  11.1 us
    pallas_call x1, Pallas kernels, first_rows(): pl.pallas_call(first_kernel, out_shape=out_shape, in_specs=[SMEM, HBM, HB...  3.27 us
    pallas_call x2, Pallas kernels, finish(): pl.pallas_call(functools.partial(finish_kernel, first), out_shape=(jax.Sh...  3.07 us
    ppermute x2, starting transfers between devices, raise_one(): return lax.ppermute(value, 'sec', pairs_up)  2.58 us
  transfers between devices with their start and end apart: 12, of which 4 were waited for; matrix products, arithmetic and copies ran while one was open for 0% of the time, Pallas kernels for 17%

profile of v5, /device:TPU:0, one launch (start us, length us, event | category | flops | bytes accessed | tf_op | source)
XLA Modules:
  0.0 81.2 jit_solution(1999415131249301798)
XLA Ops:
  2.0 1.2 %copy-done.1 = bf16[1,1024,512]{2,1,0:T(8,128)(2,1)S(1)} copy-done((bf16[1,1024,512]{2,1,0:T(8,128)(2,1)S(1)}, bf16[1,1024,512]{2,1,0:T(8,128)(2,1)}, u32[]{:S(2)}) %copy-start.1) | copy-done | bytes 1048600
  3.3 3.3 %first_rows.1 = (f32[512,512]{1,0:T(8,128)S(1)}, f32[8,128]{1,0:T(8,128)S(1)}, bf16[1024,512]{1,0:T(8,128)(2,1)S(1)}, bf16[1024,1024]{1,0:T(8,128)(2,1)S(1)}, bf...) custom-call(s32[7]{0:T(128)S(1)} %stack.19.info_ref, ...), custom_call_target="tpu_custom_call" | custom-call | flops 200000000 | bytes 1000000 | tf_op jit(solution)/shard_map/first_rows/pallas_call | solution.py:89
  6.5 2.4 %collective-permute-start = (f32[512,512]{1,0:T(8,128)S(1)}, f32[512,512]{1,0:T(8,128)S(1)}, u32[]{:S(2)}, u32[]{:S(2)}) collective-permute-start(f32[512,512]{1,0:T(8,128)S(1)} %get-tuple-element.41.a_ref), channel_id=1, source_target_pairs={{0,1},{4,5},{8,9},{12,13},{2,3},{6,7},{10,11},{14,15},{16,17},{20,... | collective-permute-start | bytes 3145736 | tf_op jit(solution)/shard_map/ppermute | solution.py:290
  9.0 2.2 %term_rows.7 = (f32[512,512]{1,0:T(8,128)S(1)}, f32[8,128]{1,0:T(8,128)S(1)}, bf16[1024,1024]{1,0:T(8,128)(2,1)S(1)}, bf16[512,512]{1,0:T(8,128)(2,1)S(1)}) custom-call(s32[7]{0:T(128)S(1)} %stack.19.info_ref, bf16[1024,512]{1,0:T(8,128)(2,1)S(1)} %get-tuple-element.38.live_ref, bf16[1024,1024]{1,0:T(8,128)(2,1)S(1)} %get-tuple-element.42.left_ref, ...), custom_call_target="tpu_custom_call" | custom-call | flops 200000000 | bytes 1000000 | tf_op jit(solution)/shard_map/term_rows/pallas_call | solution.py:148
  11.1 1.4 %collective-permute-start.2 = (f32[512,512]{1,0:T(8,128)S(1)}, f32[512,512]{1,0:T(8,128)S(1)}, u32[]{:S(2)}, u32[]{:S(2)}) collective-permute-start(f32[512,512]{1,0:T(8,128)S(1)} %get-tuple-element.52.a_ref), channel_id=1, source_target_pairs={{0,1},{4,5},{8,9},{12,13},{2,3},{6,7},{10,11},{14,15},{16,17},{20,... | collective-permute-start | bytes 3145736 | tf_op jit(solution)/shard_map/ppermute | solution.py:290
  12.7 1.3 %collective-permute-start.1 = (f32[512,512]{1,0:T(8,128)S(1)}, f32[512,512]{1,0:T(8,128)S(1)}, u32[]{:S(2)}, u32[]{:S(2)}) collective-permute-start(f32[512,512]{1,0:T(8,128)S(1)} %get-tuple-element.51), channel_id=1, source_target_pairs={{1,2},{5,6},{9,10},{13,14},{3,0},{7,4},{11,8},{17,18},{21,22},{25,... | collective-permute-start | bytes 3145736 | tf_op jit(solution)/shard_map/ppermute | solution.py:302
  14.0 2.2 %term_rows.8 = (f32[512,512]{1,0:T(8,128)S(1)}, f32[8,128]{1,0:T(8,128)S(1)}, bf16[1024,1024]{1,0:T(8,128)(2,1)S(1)}, bf16[512,512]{1,0:T(8,128)(2,1)S(1)}) custom-call(s32[7]{0:T(128)S(1)} %stack.19.info_ref, bf16[1024,512]{1,0:T(8,128)(2,1)S(1)} %get-tuple-element.38.live_ref, bf16[1024,1024]{1,0:T(8,128)(2,1)S(1)} %get-tuple-element.39.left_ref, ...), custom_call_target="tpu_custom_call" | custom-call | flops 200000000 | bytes 1000000 | tf_op jit(solution)/shard_map/term_rows/pallas_call | solution.py:148
  16.1 0.7 collective-permute-start.8
  17.1 1.5 %term_rows.9 = (f32[512,512]{1,0:T(8,128)S(1)}, f32[8,128]{1,0:T(8,128)S(1)}) custom-call(s32[7]{0:T(128)S(1)} %stack.19.info_ref, bf16[1024,512]{1,0:T(8,128)(2,1)S(1)} %get-tuple-element.38.live_ref, bf16[1024,1024]{1,0:T(8,128)(2,1)S(1)} %get-tuple-element.39.left_ref, bf16[512,512]{1,0:T(8,128)(2,1)S(1)} %get-tuple-element.40.right_ref, ...), custom_call_target="tpu_custom_call" | custom-call | flops 200000000 | bytes 1000000 | tf_op jit(solution)/shard_map/term_rows/pallas_call | solution.py:148
  18.6 1.3 %collective-permute-start.6 = (f32[512,512]{1,0:T(8,128)S(1)}, f32[512,512]{1,0:T(8,128)S(1)}, u32[]{:S(2)}, u32[]{:S(2)}) collective-permute-start(f32[512,512]{1,0:T(8,128)S(1)} %get-tuple-element.59), channel_id=1, source_target_pairs={{1,2},{5,6},{9,10},{13,14},{3,0},{7,4},{11,8},{17,18},{21,22},{25,... | collective-permute-start | bytes 3145736 | tf_op jit(solution)/shard_map/ppermute | solution.py:302
  19.9 1.5 %term_rows.10 = (f32[512,512]{1,0:T(8,128)S(1)}, f32[8,128]{1,0:T(8,128)S(1)}) custom-call(s32[7]{0:T(128)S(1)} %stack.19.info_ref, bf16[1024,512]{1,0:T(8,128)(2,1)S(1)} %get-tuple-element.38.live_ref, bf16[1024,1024]{1,0:T(8,128)(2,1)S(1)} %get-tuple-element.49.left_ref, bf16[512,512]{1,0:T(8,128)(2,1)S(1)} %get-tuple-element.50.right_ref, ...), custom_call_target="tpu_custom_call" | custom-call | flops 200000000 | bytes 1000000 | tf_op jit(solution)/shard_map/term_rows/pallas_call | solution.py:148
  21.4 3.8 %collective-permute-start.7 = (f32[512,512]{1,0:T(8,128)S(1)}, f32[512,512]{1,0:T(8,128)S(1)}, u32[]{:S(2)}, u32[]{:S(2)}) collective-permute-start(f32[512,512]{1,0:T(8,128)S(1)} %get-tuple-element.60), channel_id=1, source_target_pairs={{0,1},{4,5},{8,9},{12,13},{1,0},{5,4},{9,8},{13,12},{2,3},{6,7},{1... | collective-permute-start | bytes 3145736 | tf_op jit(solution)/shard_map/ppermute | solution.py:290
  26.0 2.8 %collective-permute-done.1.refs_0_.a_ref = f32[512,512]{1,0:T(8,128)S(1)} collective-permute-done((f32[512,512]{1,0:T(8,128)S(1)}, f32[512,512]{1,0:T(8,128)S(1)}, u32[]{:S(2)}, u32[]{:S(2)}) %collective-permute-start.1) | collective-permute-done | bytes 1048608 | tf_op jit(solution)/shard_map/ppermute | solution.py:302
  28.8 1.5 %term_rows.11 = (f32[512,512]{1,0:T(8,128)S(1)}, f32[8,128]{1,0:T(8,128)S(1)}) custom-call(s32[7]{0:T(128)S(1)} %stack.19.info_ref, bf16[1024,512]{1,0:T(8,128)(2,1)S(1)} %get-tuple-element.38.live_ref, bf16[1024,1024]{1,0:T(8,128)(2,1)S(1)} %get-tuple-element.49.left_ref, bf16[512,512]{1,0:T(8,128)(2,1)S(1)} %get-tuple-element.50.right_ref, ...), custom_call_target="tpu_custom_call" | custom-call | flops 200000000 | bytes 1000000 | tf_op jit(solution)/shard_map/term_rows/pallas_call | solution.py:148
  31.3 8.7 %collective-permute-done.6.refs_0_.a_ref = f32[512,512]{1,0:T(8,128)S(1)} collective-permute-done((f32[512,512]{1,0:T(8,128)S(1)}, f32[512,512]{1,0:T(8,128)S(1)}, u32[]{:S(2)}, u32[]{:S(2)}) %collective-permute-start.6) | collective-permute-done | bytes 1048608 | tf_op jit(solution)/shard_map/ppermute | solution.py:302
  40.0 4.4 %collective-permute-start.4 = (f32[512,512]{1,0:T(8,128)S(1)}, f32[512,512]{1,0:T(8,128)S(1)}, u32[]{:S(2)}, u32[]{:S(2)}) collective-permute-start(f32[512,512]{1,0:T(8,128)S(1)} %collective-permute-done.1.refs_0_.a_ref), channel_id=1, source_target_pairs={{0,4},{4,8},{8,12},{16,20},{20,24},{24,28}} | collective-permute-start | bytes 3145736 | tf_op jit(solution)/shard_map/ppermute | solution.py:290
  44.4 3.5 %collective-permute-start.9 = (f32[512,512]{1,0:T(8,128)S(1)}, f32[512,512]{1,0:T(8,128)S(1)}, u32[]{:S(2)}, u32[]{:S(2)}) collective-permute-start(f32[512,512]{1,0:T(8,128)S(1)} %collective-permute-done.6.refs_0_.a_ref), channel_id=1, source_target_pairs={{0,4},{4,8},{8,12},{16,20},{20,24},{24,28}} | collective-permute-start | bytes 3145736 | tf_op jit(solution)/shard_map/ppermute | solution.py:290
  47.9 1.5 %term_rows.12 = (f32[512,512]{1,0:T(8,128)S(1)}, f32[8,128]{1,0:T(8,128)S(1)}) custom-call(s32[7]{0:T(128)S(1)} %stack.19.info_ref, bf16[1024,512]{1,0:T(8,128)(2,1)S(1)} %get-tuple-element.38.live_ref, bf16[1024,1024]{1,0:T(8,128)(2,1)S(1)} %get-tuple-element.47.left_ref, bf16[512,512]{1,0:T(8,128)(2,1)S(1)} %get-tuple-element.48.right_ref, ...), custom_call_target="tpu_custom_call" | custom-call | flops 200000000 | bytes 1000000 | tf_op jit(solution)/shard_map/term_rows/pallas_call | solution.py:148
  50.3 6.3 %collective-permute-done.4.refs_0_.b_ref = f32[512,512]{1,0:T(8,128)S(1)} collective-permute-done((f32[512,512]{1,0:T(8,128)S(1)}, f32[512,512]{1,0:T(8,128)S(1)}, u32[]{:S(2)}, u32[]{:S(2)}) %collective-permute-start.4) | collective-permute-done | bytes 1048608 | tf_op jit(solution)/shard_map/ppermute | solution.py:290
  56.6 1.5 %term_rows.13 = (f32[512,512]{1,0:T(8,128)S(1)}, f32[8,128]{1,0:T(8,128)}) custom-call(s32[7]{0:T(128)S(1)} %stack.19.info_ref, bf16[1024,512]{1,0:T(8,128)(2,1)S(1)} %get-tuple-element.38.live_ref, bf16[1024,1024]{1,0:T(8,128)(2,1)S(1)} %get-tuple-element.47.left_ref, bf16[512,512]{1,0:T(8,128)(2,1)S(1)} %get-tuple-element.48.right_ref, ...), custom_call_target="tpu_custom_call" | custom-call | flops 200000000 | bytes 1000000 | tf_op jit(solution)/shard_map/term_rows/pallas_call | solution.py:148
  58.2 1.5 %finish_rows.2 = (bf16[1,1024,512]{2,1,0:T(8,128)(2,1)}, f32[16,128]{1,0:T(8,128)S(1)}) custom-call(s32[7]{0:T(128)S(1)} %stack.19.info_ref, bf16[1024,512]{1,0:T(8,128)(2,1)S(1)} %get-tuple-element.38.live_ref, f32[512,512]{1,0:T(8,128)S(1)} %get-tuple-element.68.own_ref, f32[512,512]{1,0:T(8,128)S(1)} %collective-permute-done.1.refs_0_.a_ref, ...), custom_call_target="tpu_custom_call" | custom-call | flops 200000000 | bytes 1000000 | tf_op jit(solution)/shard_map/finish_rows/pallas_call | solution.py:244
  59.7 8.1 %collective-permute-done.9.b_ref = f32[512,512]{1,0:T(8,128)S(1)} collective-permute-done((f32[512,512]{1,0:T(8,128)S(1)}, f32[512,512]{1,0:T(8,128)S(1)}, u32[]{:S(2)}, u32[]{:S(2)}) %collective-permute-start.9) | collective-permute-done | bytes 1048608 | tf_op jit(solution)/shard_map/ppermute | solution.py:290
  67.9 1.5 %finish_rows.3 = (bf16[1,1024,512]{2,1,0:T(8,128)(2,1)}, f32[16,128]{1,0:T(8,128)S(1)}) custom-call(s32[7]{0:T(128)S(1)} %stack.19.info_ref, bf16[1024,512]{1,0:T(8,128)(2,1)S(1)} %get-tuple-element.38.live_ref, f32[512,512]{1,0:T(8,128)S(1)} %get-tuple-element.66.own_ref, ...), custom_call_target="tpu_custom_call", output_to_operand_aliasing={{0}: (7, {})} | custom-call | flops 200000000 | bytes 1000000 | tf_op jit(solution)/shard_map/finish_rows/pallas_call | solution.py:244
  69.4 11.1 %all_to_all.11 = f32[16,1,128]{2,1,0:T(1,128)S(1)} all-to-all(f32[16,1,128]{2,1,0:T(1,128)S(1)} %bitcast.10), channel_id=1, replica_groups=mesh['grp'=2,'sec'=16] {'sec'}, dimensions={0} | all-to-all | bytes 16384 | tf_op jit(solution)/shard_map/all_to_all | solution.py:265
  (25 shorter events, 3.6 us)
Async XLA Ops:
  2.0 1.2 %copy-start.1 = (bf16[1,1024,512]{2,1,0:T(8,128)(2,1)S(1)}, bf16[1,1024,512]{2,1,0:T(8,128)(2,1)}, u32[]{:S(2)}) copy-start(bf16[1,1024,512]{2,1,0:T(8,128)(2,1)} %param.5) | copy-start | bytes 3145732
  3.3 5.7 %copy-start = (bf16[1,4,512,512]{3,2,1,0:T(8,128)(2,1)S(1)}, bf16[1,4,512,512]{3,2,1,0:T(8,128)(2,1)}, u32[]{:S(2)}) copy-start(bf16[1,4,512,512]{3,2,1,0:T(8,128)(2,1)} %refs_1_.3) | copy-start | bytes 6291460
  6.5 6.0 %collective-permute-start = (f32[512,512]{1,0:T(8,128)S(1)}, f32[512,512]{1,0:T(8,128)S(1)}, u32[]{:S(2)}, u32[]{:S(2)}) collective-permute-start(f32[512,512]{1,0:T(8,128)S(1)} %get-tuple-element.41.a_ref), channel_id=1, source_target_pairs={{0,1},{4,5},{8,9},{12,13},{2,3},{6,7},{10,11},{14,15},{16,17},{20,... | collective-permute-start | bytes 3145736 | tf_op jit(solution)/shard_map/ppermute | solution.py:290
  11.1 5.7 %collective-permute-start.2 = (f32[512,512]{1,0:T(8,128)S(1)}, f32[512,512]{1,0:T(8,128)S(1)}, u32[]{:S(2)}, u32[]{:S(2)}) collective-permute-start(f32[512,512]{1,0:T(8,128)S(1)} %get-tuple-element.52.a_ref), channel_id=1, source_target_pairs={{0,1},{4,5},{8,9},{12,13},{2,3},{6,7},{10,11},{14,15},{16,17},{20,... | collective-permute-start | bytes 3145736 | tf_op jit(solution)/shard_map/ppermute | solution.py:290
  12.7 16.1 %collective-permute-start.1 = (f32[512,512]{1,0:T(8,128)S(1)}, f32[512,512]{1,0:T(8,128)S(1)}, u32[]{:S(2)}, u32[]{:S(2)}) collective-permute-start(f32[512,512]{1,0:T(8,128)S(1)} %get-tuple-element.51), channel_id=1, source_target_pairs={{1,2},{5,6},{9,10},{13,14},{3,0},{7,4},{11,8},{17,18},{21,22},{25,... | collective-permute-start | bytes 3145736 | tf_op jit(solution)/shard_map/ppermute | solution.py:302
  16.1 14.3 %collective-permute-start.8 = (f32[512,512]{1,0:T(8,128)S(1)}, f32[512,512]{1,0:T(8,128)S(1)}, u32[]{:S(2)}, u32[]{:S(2)}) collective-permute-start(f32[512,512]{1,0:T(8,128)S(1)} %get-tuple-element.61.a_ref), channel_id=1, source_target_pairs={{3,6},{7,10},{11,14},{4,1},{8,5},{12,9},{19,22},{23,26},{27,30},{2... | collective-permute-start | bytes 3145736 | tf_op jit(solution)/shard_map/ppermute | solution.py:290
  18.6 21.5 %collective-permute-start.6 = (f32[512,512]{1,0:T(8,128)S(1)}, f32[512,512]{1,0:T(8,128)S(1)}, u32[]{:S(2)}, u32[]{:S(2)}) collective-permute-start(f32[512,512]{1,0:T(8,128)S(1)} %get-tuple-element.59), channel_id=1, source_target_pairs={{1,2},{5,6},{9,10},{13,14},{3,0},{7,4},{11,8},{17,18},{21,22},{25,... | collective-permute-start | bytes 3145736 | tf_op jit(solution)/shard_map/ppermute | solution.py:302
  21.4 23.0 %collective-permute-start.7 = (f32[512,512]{1,0:T(8,128)S(1)}, f32[512,512]{1,0:T(8,128)S(1)}, u32[]{:S(2)}, u32[]{:S(2)}) collective-permute-start(f32[512,512]{1,0:T(8,128)S(1)} %get-tuple-element.60), channel_id=1, source_target_pairs={{0,1},{4,5},{8,9},{12,13},{1,0},{5,4},{9,8},{13,12},{2,3},{6,7},{1... | collective-permute-start | bytes 3145736 | tf_op jit(solution)/shard_map/ppermute | solution.py:290
  25.2 24.2 %collective-permute-start.5 = (f32[512,512]{1,0:T(8,128)S(1)}, f32[512,512]{1,0:T(8,128)S(1)}, u32[]{:S(2)}, u32[]{:S(2)}) collective-permute-start(f32[512,512]{1,0:T(8,128)S(1)} %get-tuple-element.58.a_ref), channel_id=1, source_target_pairs={{3,6},{7,10},{11,14},{4,1},{8,5},{12,9},{19,22},{23,26},{27,30},{2... | collective-permute-start | bytes 3145736 | tf_op jit(solution)/shard_map/ppermute | solution.py:290
  30.3 26.3 %collective-permute-start.3 = (f32[512,512]{1,0:T(8,128)S(1)}, f32[512,512]{1,0:T(8,128)S(1)}, u32[]{:S(2)}, u32[]{:S(2)}) collective-permute-start(f32[512,512]{1,0:T(8,128)S(1)} %get-tuple-element.57), channel_id=1, source_target_pairs={{0,1},{4,5},{8,9},{12,13},{1,0},{5,4},{9,8},{13,12},{2,3},{6,7},{1... | collective-permute-start | bytes 3145736 | tf_op jit(solution)/shard_map/ppermute | solution.py:290
  30.6 27.6 %collective-permute-start.11 = (f32[512,512]{1,0:T(8,128)S(1)}, f32[512,512]{1,0:T(8,128)S(1)}, u32[]{:S(2)}, u32[]{:S(2)}) collective-permute-start(f32[512,512]{1,0:T(8,128)S(1)} %get-tuple-element.69), channel_id=1, source_target_pairs={{1,3},{5,7},{9,11},{13,15},{2,1},{6,5},{10,9},{14,13},{17,19},{21,... | collective-permute-start | bytes 3145736 | tf_op jit(solution)/shard_map/ppermute | solution.py:290
  40.0 16.6 %collective-permute-start.4 = (f32[512,512]{1,0:T(8,128)S(1)}, f32[512,512]{1,0:T(8,128)S(1)}, u32[]{:S(2)}, u32[]{:S(2)}) collective-permute-start(f32[512,512]{1,0:T(8,128)S(1)} %collective-permute-done.1.refs_0_.a_ref), channel_id=1, source_target_pairs={{0,4},{4,8},{8,12},{16,20},{20,24},{24,28}} | collective-permute-start | bytes 3145736 | tf_op jit(solution)/shard_map/ppermute | solution.py:290
  44.4 23.5 %collective-permute-start.9 = (f32[512,512]{1,0:T(8,128)S(1)}, f32[512,512]{1,0:T(8,128)S(1)}, u32[]{:S(2)}, u32[]{:S(2)}) collective-permute-start(f32[512,512]{1,0:T(8,128)S(1)} %collective-permute-done.6.refs_0_.a_ref), channel_id=1, source_target_pairs={{0,4},{4,8},{8,12},{16,20},{20,24},{24,28}} | collective-permute-start | bytes 3145736 | tf_op jit(solution)/shard_map/ppermute | solution.py:290
  49.6 18.3 %collective-permute-start.10 = (f32[512,512]{1,0:T(8,128)S(1)}, f32[512,512]{1,0:T(8,128)S(1)}, u32[]{:S(2)}, u32[]{:S(2)}) collective-permute-start(f32[512,512]{1,0:T(8,128)S(1)} %get-tuple-element.67), channel_id=1, source_target_pairs={{1,3},{5,7},{9,11},{13,15},{2,1},{6,5},{10,9},{14,13},{17,19},{21,... | collective-permute-start | bytes 3145736 | tf_op jit(solution)/shard_map/ppermute | solution.py:290

commit v6 on v5

--- a/solution.py
+++ b/solution.py
@@ -194,6 +194,19 @@
     )(*values)
 
 
+def hold(value, token):
+    return pl.pallas_call(
+        lambda *refs: None,
+        out_shape=(jax.ShapeDtypeStruct(value.shape, value.dtype), TOKEN),
+        in_specs=[ANY, ANY],
+        out_specs=(ANY, ANY),
+        input_output_aliases={0: 0},
+        compiler_params=params(),
+        cost_estimate=SMALL,
+        name="hold",
+    )(value, token)
+
+
 def finish_kernel(first, info_ref, live_ref, own_ref, a_ref, b_ref, c_ref, before_ref, *refs):
     sigma_hbm, energy_ref, sigma_buf, sems = refs[-4:]
     count, cols = own_ref.shape
@@ -335,22 +348,22 @@
     moved1 = along(second1)
     third0, token = term_rows(info, live, ops2, 0, part, token)
     swapped0 = swap(third0)
-    token = touch(raised0, token)
+    raised0, token = hold(raised0, token)
     relayed0 = relay(raised0)
     third1, token = term_rows(info, live, ops2, part, part, token)
     swapped1 = swap(third1)
     summed0, token = add(second0, moved0, token)
     crossed0 = across(summed0)
     own0, token = term_rows(info, live, ops3, 0, part, token, added=swapped0)
-    token = touch(raised1, token)
+    raised1, token = hold(raised1, token)
     relayed1 = relay(raised1)
+    token = touch(relayed0, token)
     summed1, token = add(second1, moved1, token)
     crossed1 = across(summed1)
-    token = touch(relayed0, token)
-    own1, token = term_rows(info, live, ops3, part, part, token, added=swapped1)
 
     energy = jnp.zeros((sectors, 128), jnp.float32)
     sigma, energy = finish(info, live, own0, (raised0, relayed0, crossed0), energy, None, 0)
+    own1, token = term_rows(info, live, ops3, part, part, token, energy, added=swapped1)
     sigma, energy = finish(info, live, own1, (raised1, relayed1, crossed1), energy, sigma, part)
     return sigma, sum_over_sectors(energy)
 

time: 81.6 us -> 77.5 us (0.950)
  waiting for transfers between devices: 26.1 us -> 13.8 us
  blocking collectives: 11.1 us -> 18.3 us
  starting transfers between devices: 21 us -> 22 us
    all_to_all x1, blocking collectives: 11.1 us -> 18.3 us  [sum_over_sectors(): arrived = lax.all_to_all(value, 'sec', 0, 0, tiled=True)]
    ppermute x10, waiting for transfers between devices: 14.5 us -> 8.28 us  [send(): return lax.ppermute(value, 'sec', pairs)]
    ppermute x2, waiting for transfers between devices: 11.6 us -> 5.56 us  [raise_one(): return lax.ppermute(value, 'sec', pairs_up)]
    ppermute x10, starting transfers between devices: 18.4 us -> 19.4 us  [send(): return lax.ppermute(value, 'sec', pairs)]
  transfers between devices with their start and end apart: 12 -> 12, of which waited for: 4 -> 4; matrix products, arithmetic and copies ran while one was open for 0% -> 0% of each run, Pallas kernels for 17% -> 18%
where the time goes in v6:
time: 77.5 us; the launch traced here: 77.1 us
  starting transfers between devices  22 us (28%)
  Pallas kernels  19.5 us (25%)
  blocking collectives  18.3 us (24%)
  waiting for transfers between devices  13.8 us (18%)
  between operations  2.19 us (3%)
  local copies, waits for them, and re-layouts  1.32 us (2%)
    ppermute x10, starting transfers between devices, send(): return lax.ppermute(value, 'sec', pairs)  19.4 us
    all_to_all x1, blocking collectives, sum_over_sectors(): arrived = lax.all_to_all(value, 'sec', 0, 0, tiled=True)  18.3 us
    pallas_call x7, Pallas kernels, term_rows(): pl.pallas_call(functools.partial(term_kernel, first, added is not None, s...  11.9 us
    ppermute x10, waiting for transfers between devices, send(): return lax.ppermute(value, 'sec', pairs)  8.28 us
    ppermute x2, waiting for transfers between devices, raise_one(): return lax.ppermute(value, 'sec', pairs_up)  5.56 us
    pallas_call x1, Pallas kernels, first_rows(): pl.pallas_call(first_kernel, out_shape=out_shape, in_specs=[SMEM, HBM, HB...  3.27 us
    pallas_call x2, Pallas kernels, finish(): pl.pallas_call(functools.partial(finish_kernel, first), out_shape=(jax.Sh...  3.06 us
    ppermute x2, starting transfers between devices, raise_one(): return lax.ppermute(value, 'sec', pairs_up)  2.57 us
  transfers between devices with their start and end apart: 12, of which 4 were waited for; matrix products, arithmetic and copies ran while one was open for 0% of the time, Pallas kernels for 18%

profile of v6, /device:TPU:0, one launch (start us, length us, event | category | flops | bytes accessed | tf_op | source)
XLA Modules:
  0.0 77.1 jit_solution(9027799906421860914)
XLA Ops:
  2.0 1.2 %copy-done.1 = bf16[1,1024,512]{2,1,0:T(8,128)(2,1)S(1)} copy-done((bf16[1,1024,512]{2,1,0:T(8,128)(2,1)S(1)}, bf16[1,1024,512]{2,1,0:T(8,128)(2,1)}, u32[]{:S(2)}) %copy-start.1) | copy-done | bytes 1048600
  3.3 3.3 %first_rows.1 = (f32[512,512]{1,0:T(8,128)S(1)}, f32[8,128]{1,0:T(8,128)S(1)}, bf16[1024,512]{1,0:T(8,128)(2,1)S(1)}, bf16[1024,1024]{1,0:T(8,128)(2,1)S(1)}, bf...) custom-call(s32[7]{0:T(128)S(1)} %stack.19.info_ref, ...), custom_call_target="tpu_custom_call" | custom-call | flops 200000000 | bytes 1000000 | tf_op jit(solution)/shard_map/first_rows/pallas_call | solution.py:89
  6.5 2.4 %collective-permute-start = (f32[512,512]{1,0:T(8,128)S(1)}, f32[512,512]{1,0:T(8,128)S(1)}, u32[]{:S(2)}, u32[]{:S(2)}) collective-permute-start(f32[512,512]{1,0:T(8,128)S(1)} %get-tuple-element.45.a_ref), channel_id=1, source_target_pairs={{0,1},{4,5},{8,9},{12,13},{2,3},{6,7},{10,11},{14,15},{16,17},{20,... | collective-permute-start | bytes 3145736 | tf_op jit(solution)/shard_map/ppermute | solution.py:303
  9.0 2.2 %term_rows.7 = (f32[512,512]{1,0:T(8,128)S(1)}, f32[8,128]{1,0:T(8,128)S(1)}, bf16[1024,1024]{1,0:T(8,128)(2,1)S(1)}, bf16[512,512]{1,0:T(8,128)(2,1)S(1)}) custom-call(s32[7]{0:T(128)S(1)} %stack.19.info_ref, bf16[1024,512]{1,0:T(8,128)(2,1)S(1)} %get-tuple-element.42.live_ref, bf16[1024,1024]{1,0:T(8,128)(2,1)S(1)} %get-tuple-element.46.left_ref, ...), custom_call_target="tpu_custom_call" | custom-call | flops 200000000 | bytes 1000000 | tf_op jit(solution)/shard_map/term_rows/pallas_call | solution.py:148
  11.1 1.4 %collective-permute-start.2 = (f32[512,512]{1,0:T(8,128)S(1)}, f32[512,512]{1,0:T(8,128)S(1)}, u32[]{:S(2)}, u32[]{:S(2)}) collective-permute-start(f32[512,512]{1,0:T(8,128)S(1)} %get-tuple-element.56.a_ref), channel_id=1, source_target_pairs={{0,1},{4,5},{8,9},{12,13},{2,3},{6,7},{10,11},{14,15},{16,17},{20,... | collective-permute-start | bytes 3145736 | tf_op jit(solution)/shard_map/ppermute | solution.py:303
  12.7 1.3 %collective-permute-start.1 = (f32[512,512]{1,0:T(8,128)S(1)}, f32[512,512]{1,0:T(8,128)S(1)}, u32[]{:S(2)}, u32[]{:S(2)}) collective-permute-start(f32[512,512]{1,0:T(8,128)S(1)} %get-tuple-element.55), channel_id=1, source_target_pairs={{1,2},{5,6},{9,10},{13,14},{3,0},{7,4},{11,8},{17,18},{21,22},{25,... | collective-permute-start | bytes 3145736 | tf_op jit(solution)/shard_map/ppermute | solution.py:315
  14.0 2.2 %term_rows.8 = (f32[512,512]{1,0:T(8,128)S(1)}, f32[8,128]{1,0:T(8,128)S(1)}, bf16[1024,1024]{1,0:T(8,128)(2,1)S(1)}, bf16[512,512]{1,0:T(8,128)(2,1)S(1)}) custom-call(s32[7]{0:T(128)S(1)} %stack.19.info_ref, bf16[1024,512]{1,0:T(8,128)(2,1)S(1)} %get-tuple-element.42.live_ref, bf16[1024,1024]{1,0:T(8,128)(2,1)S(1)} %get-tuple-element.43.left_ref, ...), custom_call_target="tpu_custom_call" | custom-call | flops 200000000 | bytes 1000000 | tf_op jit(solution)/shard_map/term_rows/pallas_call | solution.py:148
  16.1 0.7 collective-permute-start.8
  17.1 1.5 %term_rows.9 = (f32[512,512]{1,0:T(8,128)S(1)}, f32[8,128]{1,0:T(8,128)S(1)}) custom-call(s32[7]{0:T(128)S(1)} %stack.19.info_ref, bf16[1024,512]{1,0:T(8,128)(2,1)S(1)} %get-tuple-element.42.live_ref, bf16[1024,1024]{1,0:T(8,128)(2,1)S(1)} %get-tuple-element.43.left_ref, bf16[512,512]{1,0:T(8,128)(2,1)S(1)} %get-tuple-element.44.right_ref, ...), custom_call_target="tpu_custom_call" | custom-call | flops 200000000 | bytes 1000000 | tf_op jit(solution)/shard_map/term_rows/pallas_call | solution.py:148
  18.6 1.5 %term_rows.10 = (f32[512,512]{1,0:T(8,128)S(1)}, f32[8,128]{1,0:T(8,128)S(1)}) custom-call(s32[7]{0:T(128)S(1)} %stack.19.info_ref, bf16[1024,512]{1,0:T(8,128)(2,1)S(1)} %get-tuple-element.42.live_ref, bf16[1024,1024]{1,0:T(8,128)(2,1)S(1)} %get-tuple-element.53.left_ref, bf16[512,512]{1,0:T(8,128)(2,1)S(1)} %get-tuple-element.54.right_ref, ...), custom_call_target="tpu_custom_call" | custom-call | flops 200000000 | bytes 1000000 | tf_op jit(solution)/shard_map/term_rows/pallas_call | solution.py:148
  20.1 3.8 %collective-permute-start.7 = (f32[512,512]{1,0:T(8,128)S(1)}, f32[512,512]{1,0:T(8,128)S(1)}, u32[]{:S(2)}, u32[]{:S(2)}) collective-permute-start(f32[512,512]{1,0:T(8,128)S(1)} %get-tuple-element.66), channel_id=1, source_target_pairs={{0,1},{4,5},{8,9},{12,13},{1,0},{5,4},{9,8},{13,12},{2,3},{6,7},{1... | collective-permute-start | bytes 3145736 | tf_op jit(solution)/shard_map/ppermute | solution.py:303
  23.9 1.3 %collective-permute-start.6 = (f32[512,512]{1,0:T(8,128)S(1)}, f32[512,512]{1,0:T(8,128)S(1)}, u32[]{:S(2)}, u32[]{:S(2)}) collective-permute-start(f32[512,512]{1,0:T(8,128)S(1)} %get-tuple-element.65), channel_id=1, source_target_pairs={{1,2},{5,6},{9,10},{13,14},{3,0},{7,4},{11,8},{17,18},{21,22},{25,... | collective-permute-start | bytes 3145736 | tf_op jit(solution)/shard_map/ppermute | solution.py:315
  25.2 3.6 %collective-permute-done.1.refs_0_ = f32[512,512]{1,0:T(8,128)S(1)} collective-permute-done((f32[512,512]{1,0:T(8,128)S(1)}, f32[512,512]{1,0:T(8,128)S(1)}, u32[]{:S(2)}, u32[]{:S(2)}) %collective-permute-start.1) | collective-permute-done | bytes 1048608 | tf_op jit(solution)/shard_map/ppermute | solution.py:315
  28.8 4.4 %collective-permute-start.5 = (f32[512,512]{1,0:T(8,128)S(1)}, f32[512,512]{1,0:T(8,128)S(1)}, u32[]{:S(2)}, u32[]{:S(2)}) collective-permute-start(f32[512,512]{1,0:T(8,128)S(1)} %get-tuple-element.64.a_ref), channel_id=1, source_target_pairs={{0,4},{4,8},{8,12},{16,20},{20,24},{24,28}} | collective-permute-start | bytes 3145736 | tf_op jit(solution)/shard_map/ppermute | solution.py:303
  33.9 1.5 %term_rows.11 = (f32[512,512]{1,0:T(8,128)S(1)}, f32[8,128]{1,0:T(8,128)S(1)}) custom-call(s32[7]{0:T(128)S(1)} %stack.19.info_ref, bf16[1024,512]{1,0:T(8,128)(2,1)S(1)} %get-tuple-element.42.live_ref, bf16[1024,1024]{1,0:T(8,128)(2,1)S(1)} %get-tuple-element.53.left_ref, bf16[512,512]{1,0:T(8,128)(2,1)S(1)} %get-tuple-element.54.right_ref, ...), custom_call_target="tpu_custom_call" | custom-call | flops 200000000 | bytes 1000000 | tf_op jit(solution)/shard_map/term_rows/pallas_call | solution.py:148
  36.6 1.5 %term_rows.12 = (f32[512,512]{1,0:T(8,128)S(1)}, f32[8,128]{1,0:T(8,128)S(1)}) custom-call(s32[7]{0:T(128)S(1)} %stack.19.info_ref, bf16[1024,512]{1,0:T(8,128)(2,1)S(1)} %get-tuple-element.42.live_ref, bf16[1024,1024]{1,0:T(8,128)(2,1)S(1)} %get-tuple-element.51.left_ref, bf16[512,512]{1,0:T(8,128)(2,1)S(1)} %get-tuple-element.52.right_ref, ...), custom_call_target="tpu_custom_call" | custom-call | flops 200000000 | bytes 1000000 | tf_op jit(solution)/shard_map/term_rows/pallas_call | solution.py:148
  38.1 1.9 %collective-permute-done.6.refs_0_ = f32[512,512]{1,0:T(8,128)S(1)} collective-permute-done((f32[512,512]{1,0:T(8,128)S(1)}, f32[512,512]{1,0:T(8,128)S(1)}, u32[]{:S(2)}, u32[]{:S(2)}) %collective-permute-start.6) | collective-permute-done | bytes 1048608 | tf_op jit(solution)/shard_map/ppermute | solution.py:315
  40.0 4.4 %collective-permute-start.10 = (f32[512,512]{1,0:T(8,128)S(1)}, f32[512,512]{1,0:T(8,128)S(1)}, u32[]{:S(2)}, u32[]{:S(2)}) collective-permute-start(f32[512,512]{1,0:T(8,128)S(1)} %get-tuple-element.77.a_ref), channel_id=1, source_target_pairs={{0,4},{4,8},{8,12},{16,20},{20,24},{24,28}} | collective-permute-start | bytes 3145736 | tf_op jit(solution)/shard_map/ppermute | solution.py:303
  44.4 1.0 %collective-permute-done.5.refs_0_.b_ref = f32[512,512]{1,0:T(8,128)S(1)} collective-permute-done((f32[512,512]{1,0:T(8,128)S(1)}, f32[512,512]{1,0:T(8,128)S(1)}, u32[]{:S(2)}, u32[]{:S(2)}) %collective-permute-start.5) | collective-permute-done | bytes 1048608 | tf_op jit(solution)/shard_map/ppermute | solution.py:303
  46.3 1.5 %finish_rows.2 = (bf16[1,1024,512]{2,1,0:T(8,128)(2,1)}, f32[16,128]{1,0:T(8,128)S(1)}) custom-call(s32[7]{0:T(128)S(1)} %stack.19.info_ref, bf16[1024,512]{1,0:T(8,128)(2,1)S(1)} %get-tuple-element.42.live_ref, f32[512,512]{1,0:T(8,128)S(1)} %get-tuple-element.73.own_ref, f32[512,512]{1,0:T(8,128)S(1)} %get-tuple-element.64.a_ref, ...), custom_call_target="tpu_custom_call" | custom-call | flops 200000000 | bytes 1000000 | tf_op jit(solution)/shard_map/finish_rows/pallas_call | solution.py:257
  47.8 1.5 %term_rows.13 = (f32[512,512]{1,0:T(8,128)S(1)}, f32[8,128]{1,0:T(8,128)}) custom-call(s32[7]{0:T(128)S(1)} %stack.19.info_ref, bf16[1024,512]{1,0:T(8,128)(2,1)S(1)} %get-tuple-element.42.live_ref, bf16[1024,1024]{1,0:T(8,128)(2,1)S(1)} %get-tuple-element.51.left_ref, bf16[512,512]{1,0:T(8,128)(2,1)S(1)} %get-tuple-element.52.right_ref, ...), custom_call_target="tpu_custom_call" | custom-call | flops 200000000 | bytes 1000000 | tf_op jit(solution)/shard_map/term_rows/pallas_call | solution.py:148
  49.4 7.3 %collective-permute-done.10.b_ref = f32[512,512]{1,0:T(8,128)S(1)} collective-permute-done((f32[512,512]{1,0:T(8,128)S(1)}, f32[512,512]{1,0:T(8,128)S(1)}, u32[]{:S(2)}, u32[]{:S(2)}) %collective-permute-start.10) | collective-permute-done | bytes 1048608 | tf_op jit(solution)/shard_map/ppermute | solution.py:303
  56.6 1.5 %finish_rows.3 = (bf16[1,1024,512]{2,1,0:T(8,128)(2,1)}, f32[16,128]{1,0:T(8,128)S(1)}) custom-call(s32[7]{0:T(128)S(1)} %stack.19.info_ref, bf16[1024,512]{1,0:T(8,128)(2,1)S(1)} %get-tuple-element.42.live_ref, f32[512,512]{1,0:T(8,128)S(1)} %get-tuple-element.76.own_ref, f32[512,512]{1,0:T(8,128)S(1)} %get-tuple-element.77.a_ref, ...), custom_call_target="tpu_custom_call", output_to_operand_aliasing={{0}: (7, {})} | custom-call | flops 200000000 | bytes 1000000 | tf_op jit(solution)/shard_map/finish_rows/pallas_call | solution.py:257
  58.2 18.3 %all_to_all.11 = f32[16,1,128]{2,1,0:T(1,128)S(1)} all-to-all(f32[16,1,128]{2,1,0:T(1,128)S(1)} %bitcast.10), channel_id=1, replica_groups=mesh['grp'=2,'sec'=16] {'sec'}, dimensions={0} | all-to-all | bytes 16384 | tf_op jit(solution)/shard_map/all_to_all | solution.py:278
  (25 shorter events, 3.8 us)
Async XLA Ops:
  2.0 1.2 %copy-start.1 = (bf16[1,1024,512]{2,1,0:T(8,128)(2,1)S(1)}, bf16[1,1024,512]{2,1,0:T(8,128)(2,1)}, u32[]{:S(2)}) copy-start(bf16[1,1024,512]{2,1,0:T(8,128)(2,1)} %param.5) | copy-start | bytes 3145732
  3.3 5.7 %copy-start = (bf16[1,4,512,512]{3,2,1,0:T(8,128)(2,1)S(1)}, bf16[1,4,512,512]{3,2,1,0:T(8,128)(2,1)}, u32[]{:S(2)}) copy-start(bf16[1,4,512,512]{3,2,1,0:T(8,128)(2,1)} %refs_1_.3) | copy-start | bytes 6291460
  6.5 6.0 %collective-permute-start = (f32[512,512]{1,0:T(8,128)S(1)}, f32[512,512]{1,0:T(8,128)S(1)}, u32[]{:S(2)}, u32[]{:S(2)}) collective-permute-start(f32[512,512]{1,0:T(8,128)S(1)} %get-tuple-element.45.a_ref), channel_id=1, source_target_pairs={{0,1},{4,5},{8,9},{12,13},{2,3},{6,7},{10,11},{14,15},{16,17},{20,... | collective-permute-start | bytes 3145736 | tf_op jit(solution)/shard_map/ppermute | solution.py:303
  11.1 5.7 %collective-permute-start.2 = (f32[512,512]{1,0:T(8,128)S(1)}, f32[512,512]{1,0:T(8,128)S(1)}, u32[]{:S(2)}, u32[]{:S(2)}) collective-permute-start(f32[512,512]{1,0:T(8,128)S(1)} %get-tuple-element.56.a_ref), channel_id=1, source_target_pairs={{0,1},{4,5},{8,9},{12,13},{2,3},{6,7},{10,11},{14,15},{16,17},{20,... | collective-permute-start | bytes 3145736 | tf_op jit(solution)/shard_map/ppermute | solution.py:303
  12.7 16.1 %collective-permute-start.1 = (f32[512,512]{1,0:T(8,128)S(1)}, f32[512,512]{1,0:T(8,128)S(1)}, u32[]{:S(2)}, u32[]{:S(2)}) collective-permute-start(f32[512,512]{1,0:T(8,128)S(1)} %get-tuple-element.55), channel_id=1, source_target_pairs={{1,2},{5,6},{9,10},{13,14},{3,0},{7,4},{11,8},{17,18},{21,22},{25,... | collective-permute-start | bytes 3145736 | tf_op jit(solution)/shard_map/ppermute | solution.py:315
  16.1 19.3 %collective-permute-start.8 = (f32[512,512]{1,0:T(8,128)S(1)}, f32[512,512]{1,0:T(8,128)S(1)}, u32[]{:S(2)}, u32[]{:S(2)}) collective-permute-start(f32[512,512]{1,0:T(8,128)S(1)} %get-tuple-element.67.a_ref), channel_id=1, source_target_pairs={{3,6},{7,10},{11,14},{4,1},{8,5},{12,9},{19,22},{23,26},{27,30},{2... | collective-permute-start | bytes 3145736 | tf_op jit(solution)/shard_map/ppermute | solution.py:303
  20.1 15.7 %collective-permute-start.7 = (f32[512,512]{1,0:T(8,128)S(1)}, f32[512,512]{1,0:T(8,128)S(1)}, u32[]{:S(2)}, u32[]{:S(2)}) collective-permute-start(f32[512,512]{1,0:T(8,128)S(1)} %get-tuple-element.66), channel_id=1, source_target_pairs={{0,1},{4,5},{8,9},{12,13},{1,0},{5,4},{9,8},{13,12},{2,3},{6,7},{1... | collective-permute-start | bytes 3145736 | tf_op jit(solution)/shard_map/ppermute | solution.py:303
  23.9 16.2 %collective-permute-start.6 = (f32[512,512]{1,0:T(8,128)S(1)}, f32[512,512]{1,0:T(8,128)S(1)}, u32[]{:S(2)}, u32[]{:S(2)}) collective-permute-start(f32[512,512]{1,0:T(8,128)S(1)} %get-tuple-element.65), channel_id=1, source_target_pairs={{1,2},{5,6},{9,10},{13,14},{3,0},{7,4},{11,8},{17,18},{21,22},{25,... | collective-permute-start | bytes 3145736 | tf_op jit(solution)/shard_map/ppermute | solution.py:315
  28.8 16.6 %collective-permute-start.5 = (f32[512,512]{1,0:T(8,128)S(1)}, f32[512,512]{1,0:T(8,128)S(1)}, u32[]{:S(2)}, u32[]{:S(2)}) collective-permute-start(f32[512,512]{1,0:T(8,128)S(1)} %get-tuple-element.64.a_ref), channel_id=1, source_target_pairs={{0,4},{4,8},{8,12},{16,20},{20,24},{24,28}} | collective-permute-start | bytes 3145736 | tf_op jit(solution)/shard_map/ppermute | solution.py:303
  33.2 12.2 %collective-permute-start.4 = (f32[512,512]{1,0:T(8,128)S(1)}, f32[512,512]{1,0:T(8,128)S(1)}, u32[]{:S(2)}, u32[]{:S(2)}) collective-permute-start(f32[512,512]{1,0:T(8,128)S(1)} %get-tuple-element.63.a_ref), channel_id=1, source_target_pairs={{3,6},{7,10},{11,14},{4,1},{8,5},{12,9},{19,22},{23,26},{27,30},{2... | collective-permute-start | bytes 3145736 | tf_op jit(solution)/shard_map/ppermute | solution.py:303
  35.4 12.4 %collective-permute-start.3 = (f32[512,512]{1,0:T(8,128)S(1)}, f32[512,512]{1,0:T(8,128)S(1)}, u32[]{:S(2)}, u32[]{:S(2)}) collective-permute-start(f32[512,512]{1,0:T(8,128)S(1)} %get-tuple-element.62), channel_id=1, source_target_pairs={{0,1},{4,5},{8,9},{12,13},{1,0},{5,4},{9,8},{13,12},{2,3},{6,7},{1... | collective-permute-start | bytes 3145736 | tf_op jit(solution)/shard_map/ppermute | solution.py:303
  35.8 10.4 %collective-permute-start.9 = (f32[512,512]{1,0:T(8,128)S(1)}, f32[512,512]{1,0:T(8,128)S(1)}, u32[]{:S(2)}, u32[]{:S(2)}) collective-permute-start(f32[512,512]{1,0:T(8,128)S(1)} %get-tuple-element.74), channel_id=1, source_target_pairs={{1,3},{5,7},{9,11},{13,15},{2,1},{6,5},{10,9},{14,13},{17,19},{21,... | collective-permute-start | bytes 3145736 | tf_op jit(solution)/shard_map/ppermute | solution.py:303
  40.0 16.6 %collective-permute-start.10 = (f32[512,512]{1,0:T(8,128)S(1)}, f32[512,512]{1,0:T(8,128)S(1)}, u32[]{:S(2)}, u32[]{:S(2)}) collective-permute-start(f32[512,512]{1,0:T(8,128)S(1)} %get-tuple-element.77.a_ref), channel_id=1, source_target_pairs={{0,4},{4,8},{8,12},{16,20},{20,24},{24,28}} | collective-permute-start | bytes 3145736 | tf_op jit(solution)/shard_map/ppermute | solution.py:303
  45.5 11.1 %collective-permute-start.11 = (f32[512,512]{1,0:T(8,128)S(1)}, f32[512,512]{1,0:T(8,128)S(1)}, u32[]{:S(2)}, u32[]{:S(2)}) collective-permute-start(f32[512,512]{1,0:T(8,128)S(1)} %get-tuple-element.78), channel_id=1, source_target_pairs={{1,3},{5,7},{9,11},{13,15},{2,1},{6,5},{10,9},{14,13},{17,19},{21,... | collective-permute-start | bytes 3145736 | tf_op jit(solution)/shard_map/ppermute | solution.py:303

commit v7 on v6

--- a/solution.py
+++ b/solution.py
@@ -207,8 +207,16 @@
     )(value, token)
 
 
-def finish_kernel(first, info_ref, live_ref, own_ref, a_ref, b_ref, c_ref, before_ref, *refs):
-    sigma_hbm, energy_ref, sigma_buf, sems = refs[-4:]
+def folded(values):
+    rows, cols = values.shape
+    return jnp.sum(jnp.reshape(values, (rows // 8, 8, cols)), axis=0)
+
+
+def finish_kernel(first, info_ref, live_ref, own_ref, a_ref, b_ref, c_ref, *refs):
+    refs = list(refs)
+    sigma_buf, sems = refs[-2:]
+    energy_ref = refs.pop(-3) if first == 0 else None
+    sigma_hbm = refs[-3]
     count, cols = own_ref.shape
     step = 64
     piece = count // sems.shape[0]
@@ -224,20 +232,16 @@
     def work(arrival):
         energy = jnp.zeros((8, cols), jnp.float32)
         for i in range(count // piece):
-
-            def body(n, energy):
-                start = pl.multiple_of(i * piece + n * step, step)
+            for start in range(i * piece, (i + 1) * piece, step):
                 span = pl.ds(start, step)
-                inside = jnp.logical_and(row < info_ref[4] - first - start, col)
+                inside = jnp.logical_and(row < info_ref[4] - (first + start), col)
                 total = jnp.where(inside, own_ref[span, :] + arrival[span, :], 0.0)
                 sigma_buf[span, :] = total.astype(sigma_buf.dtype)
-                here = pl.ds(pl.multiple_of(first + start, step), step)
-                product = live_ref[here, :].astype(jnp.float32) * total
-                return energy + jnp.sum(jnp.reshape(product, (step // 8, 8, cols)), axis=0)
-
-            energy = lax.fori_loop(0, piece // step, body, energy)
+                if energy_ref is not None:
+                    energy += folded(live_ref[span, :].astype(jnp.float32) * total)
             copy(i).start()
-        energy_ref[...] = before_ref[...] + jnp.sum(energy)
+        if energy_ref is not None:
+            energy_ref[...] = energy
 
     for n, arrival in enumerate((a_ref, b_ref, c_ref)):
         pl.when(info_ref[6] == n)(functools.partial(work, arrival))
@@ -245,23 +249,25 @@
         copy(i).wait()
 
 
-def finish(info, live, own, arrivals, before, sigma, first):
+def finish(info, live, own, arrivals, sigma, first):
     count, cols = own.shape
-    in_specs = [SMEM] + [WHOLE] * 6
-    operands = [info, live, own, *arrivals, before]
+    in_specs = [SMEM] + [WHOLE] * 5
+    operands = [info, live, own, *arrivals]
+    out_shape = [jax.ShapeDtypeStruct((1, *live.shape), jnp.bfloat16)]
+    out_specs = [ANY]
     aliases = {}
     if sigma is not None:
         in_specs.append(ANY)
         aliases = {len(operands): 0}
         operands.append(sigma)
+    if first == 0:
+        out_shape.append(jax.ShapeDtypeStruct((8, cols), jnp.float32))
+        out_specs.append(WHOLE)
     return pl.pallas_call(
         functools.partial(finish_kernel, first),
-        out_shape=(
-            jax.ShapeDtypeStruct((1, *live.shape), jnp.bfloat16),
-            jax.ShapeDtypeStruct(before.shape, jnp.float32),
-        ),
+        out_shape=out_shape,
         in_specs=in_specs,
-        out_specs=(ANY, WHOLE),
+        out_specs=out_specs,
         scratch_shapes=[pltpu.VMEM((count, cols), jnp.bfloat16), pltpu.SemaphoreType.DMA((4,))],
         input_output_aliases=aliases,
         compiler_params=params(),
@@ -270,12 +276,41 @@
     )(*operands)
 
 
+def energy_kernel(first, info_ref, live_ref, own_ref, a_ref, b_ref, c_ref, before_ref, out_ref):
+    count, cols = own_ref.shape
+    step = 64
+
+    def work(arrival):
+        energy = before_ref[...]
+        for start in range(0, count, step):
+            span = pl.ds(start, step)
+            total = own_ref[span, :] + arrival[span, :]
+            live = live_ref[pl.ds(first + start, step), :].astype(jnp.float32)
+            energy += folded(live * total)
+        out_ref[...] = jnp.full(out_ref.shape, jnp.sum(energy), jnp.float32)
+
+    for n, arrival in enumerate((a_ref, b_ref, c_ref)):
+        pl.when(info_ref[6] == n)(functools.partial(work, arrival))
+
+
+def energy_of(info, live, own, arrivals, before, first):
+    return pl.pallas_call(
+        functools.partial(energy_kernel, first),
+        out_shape=jax.ShapeDtypeStruct((1, 128), jnp.float32),
+        in_specs=[SMEM] + [WHOLE] * 6,
+        out_specs=WHOLE,
+        compiler_params=params(),
+        cost_estimate=SMALL,
+        name="energy_rows",
+    )(info, live, own, *arrivals, before)
+
+
 def sum_kernel(in_ref, out_ref):
     out_ref[0] = jnp.sum(in_ref[:, :1])
 
 
 def sum_over_sectors(value):
-    arrived = lax.all_to_all(value, "sec", 0, 0, tiled=True)
+    arrived = lax.all_gather(value, "sec", axis=0, tiled=True)
     return pl.pallas_call(
         sum_kernel,
         out_shape=jax.ShapeDtypeStruct((1,), jnp.float32),
@@ -361,11 +396,12 @@
     summed1, token = add(second1, moved1, token)
     crossed1 = across(summed1)
 
-    energy = jnp.zeros((sectors, 128), jnp.float32)
-    sigma, energy = finish(info, live, own0, (raised0, relayed0, crossed0), energy, None, 0)
+    sigma, energy = finish(info, live, own0, (raised0, relayed0, crossed0), None, 0)
     own1, token = term_rows(info, live, ops3, part, part, token, energy, added=swapped1)
-    sigma, energy = finish(info, live, own1, (raised1, relayed1, crossed1), energy, sigma, part)
-    return sigma, sum_over_sectors(energy)
+    arrivals = (raised1, relayed1, crossed1)
+    energy = sum_over_sectors(energy_of(info, live, own1, arrivals, energy, part))
+    (sigma,) = finish(info, live, own1, arrivals, sigma, part)
+    return sigma, energy
 
 
 def solution(mesh):

time: 77.5 us -> 85.2 us (1.099)
  blocking collectives: 18.3 us -> 25.2 us
    all_gather x0 -> x1, blocking collectives: none -> 25.2 us  [sum_over_sectors(): arrived = lax.all_gather(value, 'sec', axis=0, tiled=True)]
    all_to_all x1 -> x0, blocking collectives: 18.3 us -> none  [sum_over_sectors(): arrived = lax.all_to_all(value, 'sec', 0, 0, tiled=True)]
    pallas_call x2 -> x3, Pallas kernels: 3.06 us -> 3.77 us  [the longest x2 2.91 us: finish(): pl.pallas_call(functools.partial(finish_kernel, first), out_shape=out_sha...]
  transfers between devices with their start and end apart: 12 -> 12, of which waited for: 4 -> 4; matrix products, arithmetic and copies ran while one was open for 0% -> 0% of each run, Pallas kernels for 18% -> 16%
where the time goes in v7:
time: 85.2 us; the launch traced here: 84.8 us
  blocking collectives  25.2 us (30%)
  starting transfers between devices  22 us (26%)
  Pallas kernels  20.1 us (24%)
  waiting for transfers between devices  13.9 us (16%)
  between operations  2.19 us (3%)
  local copies, waits for them, and re-layouts  1.32 us (2%)
    all_gather x1, blocking collectives, sum_over_sectors(): arrived = lax.all_gather(value, 'sec', axis=0, tiled=True)  25.2 us
    ppermute x10, starting transfers between devices, send(): return lax.ppermute(value, 'sec', pairs)  19.4 us
    pallas_call x7, Pallas kernels, term_rows(): pl.pallas_call(functools.partial(term_kernel, first, added is not None, s...  11.9 us
    ppermute x10, waiting for transfers between devices, send(): return lax.ppermute(value, 'sec', pairs)  8.3 us
    ppermute x2, waiting for transfers between devices, raise_one(): return lax.ppermute(value, 'sec', pairs_up)  5.58 us
    pallas_call x1, Pallas kernels, first_rows(): pl.pallas_call(first_kernel, out_shape=out_shape, in_specs=[SMEM, HBM, HB...  3.27 us
    pallas_call x2, Pallas kernels, finish(): pl.pallas_call(functools.partial(finish_kernel, first), out_shape=out_sha...  2.91 us
    ppermute x2, starting transfers between devices, raise_one(): return lax.ppermute(value, 'sec', pairs_up)  2.57 us
  transfers between devices with their start and end apart: 12, of which 4 were waited for; matrix products, arithmetic and copies ran while one was open for 0% of the time, Pallas kernels for 16%

profile of v7, /device:TPU:0, one launch (start us, length us, event | category | flops | bytes accessed | tf_op | source)
XLA Modules:
  0.0 84.8 jit_solution(7011094355332739598)
XLA Ops:
  2.0 1.2 %copy-done.1 = bf16[1,1024,512]{2,1,0:T(8,128)(2,1)S(1)} copy-done((bf16[1,1024,512]{2,1,0:T(8,128)(2,1)S(1)}, bf16[1,1024,512]{2,1,0:T(8,128)(2,1)}, u32[]{:S(2)}) %copy-start.1) | copy-done | bytes 1048600
  3.3 3.3 %first_rows.1 = (f32[512,512]{1,0:T(8,128)S(1)}, f32[8,128]{1,0:T(8,128)S(1)}, bf16[1024,512]{1,0:T(8,128)(2,1)S(1)}, bf16[1024,1024]{1,0:T(8,128)(2,1)S(1)}, bf...) custom-call(s32[7]{0:T(128)S(1)} %stack.19.info_ref, ...), custom_call_target="tpu_custom_call" | custom-call | flops 200000000 | bytes 1000000 | tf_op jit(solution)/shard_map/first_rows/pallas_call | solution.py:89
  6.5 2.4 %collective-permute-start = (f32[512,512]{1,0:T(8,128)S(1)}, f32[512,512]{1,0:T(8,128)S(1)}, u32[]{:S(2)}, u32[]{:S(2)}) collective-permute-start(f32[512,512]{1,0:T(8,128)S(1)} %get-tuple-element.43.a_ref), channel_id=1, source_target_pairs={{0,1},{4,5},{8,9},{12,13},{2,3},{6,7},{10,11},{14,15},{16,17},{20,... | collective-permute-start | bytes 3145736 | tf_op jit(solution)/shard_map/ppermute | solution.py:338
  9.0 2.2 %term_rows.7 = (f32[512,512]{1,0:T(8,128)S(1)}, f32[8,128]{1,0:T(8,128)S(1)}, bf16[1024,1024]{1,0:T(8,128)(2,1)S(1)}, bf16[512,512]{1,0:T(8,128)(2,1)S(1)}) custom-call(s32[7]{0:T(128)S(1)} %stack.19.info_ref, bf16[1024,512]{1,0:T(8,128)(2,1)S(1)} %get-tuple-element.40.live_ref, bf16[1024,1024]{1,0:T(8,128)(2,1)S(1)} %get-tuple-element.44.left_ref, ...), custom_call_target="tpu_custom_call" | custom-call | flops 200000000 | bytes 1000000 | tf_op jit(solution)/shard_map/term_rows/pallas_call | solution.py:148
  11.1 1.4 %collective-permute-start.2 = (f32[512,512]{1,0:T(8,128)S(1)}, f32[512,512]{1,0:T(8,128)S(1)}, u32[]{:S(2)}, u32[]{:S(2)}) collective-permute-start(f32[512,512]{1,0:T(8,128)S(1)} %get-tuple-element.54.a_ref), channel_id=1, source_target_pairs={{0,1},{4,5},{8,9},{12,13},{2,3},{6,7},{10,11},{14,15},{16,17},{20,... | collective-permute-start | bytes 3145736 | tf_op jit(solution)/shard_map/ppermute | solution.py:338
  12.7 1.3 %collective-permute-start.1 = (f32[512,512]{1,0:T(8,128)S(1)}, f32[512,512]{1,0:T(8,128)S(1)}, u32[]{:S(2)}, u32[]{:S(2)}) collective-permute-start(f32[512,512]{1,0:T(8,128)S(1)} %get-tuple-element.53), channel_id=1, source_target_pairs={{1,2},{5,6},{9,10},{13,14},{3,0},{7,4},{11,8},{17,18},{21,22},{25,... | collective-permute-start | bytes 3145736 | tf_op jit(solution)/shard_map/ppermute | solution.py:350
  14.0 2.2 %term_rows.8 = (f32[512,512]{1,0:T(8,128)S(1)}, f32[8,128]{1,0:T(8,128)S(1)}, bf16[1024,1024]{1,0:T(8,128)(2,1)S(1)}, bf16[512,512]{1,0:T(8,128)(2,1)S(1)}) custom-call(s32[7]{0:T(128)S(1)} %stack.19.info_ref, bf16[1024,512]{1,0:T(8,128)(2,1)S(1)} %get-tuple-element.40.live_ref, bf16[1024,1024]{1,0:T(8,128)(2,1)S(1)} %get-tuple-element.41.left_ref, ...), custom_call_target="tpu_custom_call" | custom-call | flops 200000000 | bytes 1000000 | tf_op jit(solution)/shard_map/term_rows/pallas_call | solution.py:148
  17.0 1.5 %term_rows.9 = (f32[512,512]{1,0:T(8,128)S(1)}, f32[8,128]{1,0:T(8,128)S(1)}) custom-call(s32[7]{0:T(128)S(1)} %stack.19.info_ref, bf16[1024,512]{1,0:T(8,128)(2,1)S(1)} %get-tuple-element.40.live_ref, bf16[1024,1024]{1,0:T(8,128)(2,1)S(1)} %get-tuple-element.41.left_ref, bf16[512,512]{1,0:T(8,128)(2,1)S(1)} %get-tuple-element.42.right_ref, ...), custom_call_target="tpu_custom_call" | custom-call | flops 200000000 | bytes 1000000 | tf_op jit(solution)/shard_map/term_rows/pallas_call | solution.py:148
  18.5 1.5 %term_rows.10 = (f32[512,512]{1,0:T(8,128)S(1)}, f32[8,128]{1,0:T(8,128)S(1)}) custom-call(s32[7]{0:T(128)S(1)} %stack.19.info_ref, bf16[1024,512]{1,0:T(8,128)(2,1)S(1)} %get-tuple-element.40.live_ref, bf16[1024,1024]{1,0:T(8,128)(2,1)S(1)} %get-tuple-element.51.left_ref, bf16[512,512]{1,0:T(8,128)(2,1)S(1)} %get-tuple-element.52.right_ref, ...), custom_call_target="tpu_custom_call" | custom-call | flops 200000000 | bytes 1000000 | tf_op jit(solution)/shard_map/term_rows/pallas_call | solution.py:148
  20.1 3.8 %collective-permute-start.7 = (f32[512,512]{1,0:T(8,128)S(1)}, f32[512,512]{1,0:T(8,128)S(1)}, u32[]{:S(2)}, u32[]{:S(2)}) collective-permute-start(f32[512,512]{1,0:T(8,128)S(1)} %get-tuple-element.64), channel_id=1, source_target_pairs={{0,1},{4,5},{8,9},{12,13},{1,0},{5,4},{9,8},{13,12},{2,3},{6,7},{1... | collective-permute-start | bytes 3145736 | tf_op jit(solution)/shard_map/ppermute | solution.py:338
  23.8 1.3 %collective-permute-start.6 = (f32[512,512]{1,0:T(8,128)S(1)}, f32[512,512]{1,0:T(8,128)S(1)}, u32[]{:S(2)}, u32[]{:S(2)}) collective-permute-start(f32[512,512]{1,0:T(8,128)S(1)} %get-tuple-element.63), channel_id=1, source_target_pairs={{1,2},{5,6},{9,10},{13,14},{3,0},{7,4},{11,8},{17,18},{21,22},{25,... | collective-permute-start | bytes 3145736 | tf_op jit(solution)/shard_map/ppermute | solution.py:350
  25.1 3.7 %collective-permute-done.1.refs_0_ = f32[512,512]{1,0:T(8,128)S(1)} collective-permute-done((f32[512,512]{1,0:T(8,128)S(1)}, f32[512,512]{1,0:T(8,128)S(1)}, u32[]{:S(2)}, u32[]{:S(2)}) %collective-permute-start.1) | collective-permute-done | bytes 1048608 | tf_op jit(solution)/shard_map/ppermute | solution.py:350
  28.8 4.4 %collective-permute-start.5 = (f32[512,512]{1,0:T(8,128)S(1)}, f32[512,512]{1,0:T(8,128)S(1)}, u32[]{:S(2)}, u32[]{:S(2)}) collective-permute-start(f32[512,512]{1,0:T(8,128)S(1)} %get-tuple-element.62.a_ref), channel_id=1, source_target_pairs={{0,4},{4,8},{8,12},{16,20},{20,24},{24,28}} | collective-permute-start | bytes 3145736 | tf_op jit(solution)/shard_map/ppermute | solution.py:338
  33.9 1.5 %term_rows.11 = (f32[512,512]{1,0:T(8,128)S(1)}, f32[8,128]{1,0:T(8,128)S(1)}) custom-call(s32[7]{0:T(128)S(1)} %stack.19.info_ref, bf16[1024,512]{1,0:T(8,128)(2,1)S(1)} %get-tuple-element.40.live_ref, bf16[1024,1024]{1,0:T(8,128)(2,1)S(1)} %get-tuple-element.51.left_ref, bf16[512,512]{1,0:T(8,128)(2,1)S(1)} %get-tuple-element.52.right_ref, ...), custom_call_target="tpu_custom_call" | custom-call | flops 200000000 | bytes 1000000 | tf_op jit(solution)/shard_map/term_rows/pallas_call | solution.py:148
  36.6 1.5 %term_rows.12 = (f32[512,512]{1,0:T(8,128)S(1)}, f32[8,128]{1,0:T(8,128)S(1)}) custom-call(s32[7]{0:T(128)S(1)} %stack.19.info_ref, bf16[1024,512]{1,0:T(8,128)(2,1)S(1)} %get-tuple-element.40.live_ref, bf16[1024,1024]{1,0:T(8,128)(2,1)S(1)} %get-tuple-element.49.left_ref, bf16[512,512]{1,0:T(8,128)(2,1)S(1)} %get-tuple-element.50.right_ref, ...), custom_call_target="tpu_custom_call" | custom-call | flops 200000000 | bytes 1000000 | tf_op jit(solution)/shard_map/term_rows/pallas_call | solution.py:148
  38.1 1.9 %collective-permute-done.6.refs_0_ = f32[512,512]{1,0:T(8,128)S(1)} collective-permute-done((f32[512,512]{1,0:T(8,128)S(1)}, f32[512,512]{1,0:T(8,128)S(1)}, u32[]{:S(2)}, u32[]{:S(2)}) %collective-permute-start.6) | collective-permute-done | bytes 1048608 | tf_op jit(solution)/shard_map/ppermute | solution.py:350
  40.0 4.4 %collective-permute-start.10 = (f32[512,512]{1,0:T(8,128)S(1)}, f32[512,512]{1,0:T(8,128)S(1)}, u32[]{:S(2)}, u32[]{:S(2)}) collective-permute-start(f32[512,512]{1,0:T(8,128)S(1)} %get-tuple-element.75.a_ref), channel_id=1, source_target_pairs={{0,4},{4,8},{8,12},{16,20},{20,24},{24,28}} | collective-permute-start | bytes 3145736 | tf_op jit(solution)/shard_map/ppermute | solution.py:338
  44.4 1.0 %collective-permute-done.5.refs_0_.b_ref = f32[512,512]{1,0:T(8,128)S(1)} collective-permute-done((f32[512,512]{1,0:T(8,128)S(1)}, f32[512,512]{1,0:T(8,128)S(1)}, u32[]{:S(2)}, u32[]{:S(2)}) %collective-permute-start.5) | collective-permute-done | bytes 1048608 | tf_op jit(solution)/shard_map/ppermute | solution.py:338
  46.3 1.5 %finish_rows.2 = (bf16[1,1024,512]{2,1,0:T(8,128)(2,1)}, f32[8,512]{1,0:T(8,128)S(1)}) custom-call(s32[7]{0:T(128)S(1)} %stack.19.info_ref, bf16[1024,512]{1,0:T(8,128)(2,1)S(1)} %get-tuple-element.40.live_ref, f32[512,512]{1,0:T(8,128)S(1)} %get-tuple-element.71.own_ref, f32[512,512]{1,0:T(8,128)S(1)} %get-tuple-element.62.a_ref, ...), custom_call_target="tpu_custom_call" | custom-call | flops 200000000 | bytes 1000000 | tf_op jit(solution)/shard_map/finish_rows/pallas_call | solution.py:266
  47.8 1.5 %term_rows.13 = (f32[512,512]{1,0:T(8,128)S(1)}, f32[8,128]{1,0:T(8,128)}) custom-call(s32[7]{0:T(128)S(1)} %stack.19.info_ref, bf16[1024,512]{1,0:T(8,128)(2,1)S(1)} %get-tuple-element.40.live_ref, bf16[1024,1024]{1,0:T(8,128)(2,1)S(1)} %get-tuple-element.49.left_ref, bf16[512,512]{1,0:T(8,128)(2,1)S(1)} %get-tuple-element.50.right_ref, ...), custom_call_target="tpu_custom_call" | custom-call | flops 200000000 | bytes 1000000 | tf_op jit(solution)/shard_map/term_rows/pallas_call | solution.py:148
  49.3 7.3 %collective-permute-done.10.b_ref = f32[512,512]{1,0:T(8,128)S(1)} collective-permute-done((f32[512,512]{1,0:T(8,128)S(1)}, f32[512,512]{1,0:T(8,128)S(1)}, u32[]{:S(2)}, u32[]{:S(2)}) %collective-permute-start.10) | collective-permute-done | bytes 1048608 | tf_op jit(solution)/shard_map/ppermute | solution.py:338
  56.6 0.9 %energy_rows.1 = f32[1,128]{1,0:T(1,128)S(1)} custom-call(s32[7]{0:T(128)S(1)} %stack.19.info_ref, bf16[1024,512]{1,0:T(8,128)(2,1)S(1)} %get-tuple-element.40.live_ref, f32[512,512]{1,0:T(8,128)S(1)} %get-tuple-element.74.own_ref, f32[512,512]{1,0:T(8,128)S(1)} %get-tuple-element.75.a_ref, f32[512,512]{1,0:T(8,128)S(1)} %collective-permute-done.10.b_ref, ...), custom_call_target="tpu_custom_call" | custom-call | flops 200000000 | bytes 1000000 | tf_op jit(solution)/shard_map/energy_rows/pallas_call | solution.py:297
  57.5 25.2 %all-gather = f32[16,1,128]{2,1,0:T(1,128)S(1)} all-gather(f32[1,1,128]{2,1,0:T(1,128)S(1)} %bitcast.9), channel_id=1, replica_groups=mesh['grp'=2,'sec'=16] {'sec'}, dimensions={0}, use_global_device_ids=true | all-gather | bytes 8704 | tf_op jit(solution)/shard_map/all_gather | solution.py:313
  83.4 1.4 %finish_rows.3 = bf16[1,1024,512]{2,1,0:T(8,128)(2,1)} custom-call(s32[7]{0:T(128)S(1)} %stack.19.info_ref, bf16[1024,512]{1,0:T(8,128)(2,1)S(1)} %get-tuple-element.40.live_ref, f32[512,512]{1,0:T(8,128)S(1)} %get-tuple-element.74.own_ref, f32[512,512]{1,0:T(8,128)S(1)} %get-tuple-element.75.a_ref, ...), custom_call_target="tpu_custom_call", output_to_operand_aliasing={{}: (6, {})} | custom-call | flops 200000000 | bytes 1000000 | tf_op jit(solution)/shard_map/finish_rows/pallas_call | solution.py:266
  (25 shorter events, 4.5 us)
Async XLA Ops:
  2.0 1.2 %copy-start.1 = (bf16[1,1024,512]{2,1,0:T(8,128)(2,1)S(1)}, bf16[1,1024,512]{2,1,0:T(8,128)(2,1)}, u32[]{:S(2)}) copy-start(bf16[1,1024,512]{2,1,0:T(8,128)(2,1)} %param.5) | copy-start | bytes 3145732
  3.3 5.7 %copy-start = (bf16[1,4,512,512]{3,2,1,0:T(8,128)(2,1)S(1)}, bf16[1,4,512,512]{3,2,1,0:T(8,128)(2,1)}, u32[]{:S(2)}) copy-start(bf16[1,4,512,512]{3,2,1,0:T(8,128)(2,1)} %refs_1_.3) | copy-start | bytes 6291460
  6.5 6.0 %collective-permute-start = (f32[512,512]{1,0:T(8,128)S(1)}, f32[512,512]{1,0:T(8,128)S(1)}, u32[]{:S(2)}, u32[]{:S(2)}) collective-permute-start(f32[512,512]{1,0:T(8,128)S(1)} %get-tuple-element.43.a_ref), channel_id=1, source_target_pairs={{0,1},{4,5},{8,9},{12,13},{2,3},{6,7},{10,11},{14,15},{16,17},{20,... | collective-permute-start | bytes 3145736 | tf_op jit(solution)/shard_map/ppermute | solution.py:338
  11.1 5.7 %collective-permute-start.2 = (f32[512,512]{1,0:T(8,128)S(1)}, f32[512,512]{1,0:T(8,128)S(1)}, u32[]{:S(2)}, u32[]{:S(2)}) collective-permute-start(f32[512,512]{1,0:T(8,128)S(1)} %get-tuple-element.54.a_ref), channel_id=1, source_target_pairs={{0,1},{4,5},{8,9},{12,13},{2,3},{6,7},{10,11},{14,15},{16,17},{20,... | collective-permute-start | bytes 3145736 | tf_op jit(solution)/shard_map/ppermute | solution.py:338
  12.7 16.1 %collective-permute-start.1 = (f32[512,512]{1,0:T(8,128)S(1)}, f32[512,512]{1,0:T(8,128)S(1)}, u32[]{:S(2)}, u32[]{:S(2)}) collective-permute-start(f32[512,512]{1,0:T(8,128)S(1)} %get-tuple-element.53), channel_id=1, source_target_pairs={{1,2},{5,6},{9,10},{13,14},{3,0},{7,4},{11,8},{17,18},{21,22},{25,... | collective-permute-start | bytes 3145736 | tf_op jit(solution)/shard_map/ppermute | solution.py:350
  16.1 19.3 %collective-permute-start.8 = (f32[512,512]{1,0:T(8,128)S(1)}, f32[512,512]{1,0:T(8,128)S(1)}, u32[]{:S(2)}, u32[]{:S(2)}) collective-permute-start(f32[512,512]{1,0:T(8,128)S(1)} %get-tuple-element.65.a_ref), channel_id=1, source_target_pairs={{3,6},{7,10},{11,14},{4,1},{8,5},{12,9},{19,22},{23,26},{27,30},{2... | collective-permute-start | bytes 3145736 | tf_op jit(solution)/shard_map/ppermute | solution.py:338
  20.1 15.8 %collective-permute-start.7 = (f32[512,512]{1,0:T(8,128)S(1)}, f32[512,512]{1,0:T(8,128)S(1)}, u32[]{:S(2)}, u32[]{:S(2)}) collective-permute-start(f32[512,512]{1,0:T(8,128)S(1)} %get-tuple-element.64), channel_id=1, source_target_pairs={{0,1},{4,5},{8,9},{12,13},{1,0},{5,4},{9,8},{13,12},{2,3},{6,7},{1... | collective-permute-start | bytes 3145736 | tf_op jit(solution)/shard_map/ppermute | solution.py:338
  23.8 16.2 %collective-permute-start.6 = (f32[512,512]{1,0:T(8,128)S(1)}, f32[512,512]{1,0:T(8,128)S(1)}, u32[]{:S(2)}, u32[]{:S(2)}) collective-permute-start(f32[512,512]{1,0:T(8,128)S(1)} %get-tuple-element.63), channel_id=1, source_target_pairs={{1,2},{5,6},{9,10},{13,14},{3,0},{7,4},{11,8},{17,18},{21,22},{25,... | collective-permute-start | bytes 3145736 | tf_op jit(solution)/shard_map/ppermute | solution.py:350
  28.8 16.6 %collective-permute-start.5 = (f32[512,512]{1,0:T(8,128)S(1)}, f32[512,512]{1,0:T(8,128)S(1)}, u32[]{:S(2)}, u32[]{:S(2)}) collective-permute-start(f32[512,512]{1,0:T(8,128)S(1)} %get-tuple-element.62.a_ref), channel_id=1, source_target_pairs={{0,4},{4,8},{8,12},{16,20},{20,24},{24,28}} | collective-permute-start | bytes 3145736 | tf_op jit(solution)/shard_map/ppermute | solution.py:338
  33.2 12.2 %collective-permute-start.4 = (f32[512,512]{1,0:T(8,128)S(1)}, f32[512,512]{1,0:T(8,128)S(1)}, u32[]{:S(2)}, u32[]{:S(2)}) collective-permute-start(f32[512,512]{1,0:T(8,128)S(1)} %get-tuple-element.61.a_ref), channel_id=1, source_target_pairs={{3,6},{7,10},{11,14},{4,1},{8,5},{12,9},{19,22},{23,26},{27,30},{2... | collective-permute-start | bytes 3145736 | tf_op jit(solution)/shard_map/ppermute | solution.py:338
  35.4 12.4 %collective-permute-start.3 = (f32[512,512]{1,0:T(8,128)S(1)}, f32[512,512]{1,0:T(8,128)S(1)}, u32[]{:S(2)}, u32[]{:S(2)}) collective-permute-start(f32[512,512]{1,0:T(8,128)S(1)} %get-tuple-element.60), channel_id=1, source_target_pairs={{0,1},{4,5},{8,9},{12,13},{1,0},{5,4},{9,8},{13,12},{2,3},{6,7},{1... | collective-permute-start | bytes 3145736 | tf_op jit(solution)/shard_map/ppermute | solution.py:338
  35.8 10.5 %collective-permute-start.9 = (f32[512,512]{1,0:T(8,128)S(1)}, f32[512,512]{1,0:T(8,128)S(1)}, u32[]{:S(2)}, u32[]{:S(2)}) collective-permute-start(f32[512,512]{1,0:T(8,128)S(1)} %get-tuple-element.72), channel_id=1, source_target_pairs={{1,3},{5,7},{9,11},{13,15},{2,1},{6,5},{10,9},{14,13},{17,19},{21,... | collective-permute-start | bytes 3145736 | tf_op jit(solution)/shard_map/ppermute | solution.py:338
  40.0 16.6 %collective-permute-start.10 = (f32[512,512]{1,0:T(8,128)S(1)}, f32[512,512]{1,0:T(8,128)S(1)}, u32[]{:S(2)}, u32[]{:S(2)}) collective-permute-start(f32[512,512]{1,0:T(8,128)S(1)} %get-tuple-element.75.a_ref), channel_id=1, source_target_pairs={{0,4},{4,8},{8,12},{16,20},{20,24},{24,28}} | collective-permute-start | bytes 3145736 | tf_op jit(solution)/shard_map/ppermute | solution.py:338
  45.6 11.1 %collective-permute-start.11 = (f32[512,512]{1,0:T(8,128)S(1)}, f32[512,512]{1,0:T(8,128)S(1)}, u32[]{:S(2)}, u32[]{:S(2)}) collective-permute-start(f32[512,512]{1,0:T(8,128)S(1)} %get-tuple-element.76), channel_id=1, source_target_pairs={{1,3},{5,7},{9,11},{13,15},{2,1},{6,5},{10,9},{14,13},{17,19},{21,... | collective-permute-start | bytes 3145736 | tf_op jit(solution)/shard_map/ppermute | solution.py:338

commit v8 on v6

--- a/solution.py
+++ b/solution.py
@@ -8,7 +8,7 @@
 from jax.sharding import PartitionSpec as P
 
 MIB = 1024 * 1024
-FIRST_MIB = 44
+FIRST_MIB = 48
 BRING_MIB = 42
 
 ANY = pl.BlockSpec(memory_space=pl.ANY)
@@ -41,38 +41,37 @@
     return jnp.dot(first, right, preferred_element_type=jnp.float32)
 
 
-def first_kernel(info_ref, psi_hbm, left_hbm, right_hbm, *refs):
-    out_ref, _, live_ref, left0, right0, left1, right1, psi_buf, sems, psi_sems = refs
-    pieces = psi_sems.shape[0]
-    rows, cols = psi_buf.shape
-    step = rows // pieces
-
-    def copy(i):
-        span = pl.ds(i * step, step)
-        return pltpu.make_async_copy(psi_hbm.at[span, :], psi_buf.at[span, :], psi_sems.at[i])
-
-    for i in range(pieces):
-        copy(i).start()
-    needed = fetch(info_ref, 0, left_hbm, right_hbm, left0, right0, sems.at[0])
-    ahead = fetch(info_ref, 1, left_hbm, right_hbm, left1, right1, sems.at[1])
-    needed[0].start()
-    needed[1].start()
-    col = lax.broadcasted_iota(jnp.int32, (step, cols), 1) < info_ref[5]
-    row = lax.broadcasted_iota(jnp.int32, (step, cols), 0)
-    for i in range(pieces):
-        copy(i).wait()
-        inside = jnp.logical_and(row < info_ref[4] - i * step, col)
-        values = psi_buf[i * step : (i + 1) * step, :].astype(jnp.float32)
-        live_ref[i * step : (i + 1) * step, :] = jnp.where(inside, values, 0.0).astype(
-            live_ref.dtype
-        )
-    for later in (needed[2], *ahead):
-        later.start()
-    needed[0].wait()
-    needed[1].wait()
-    out_ref[...] = multiply(left0[: out_ref.shape[0], :], live_ref[...], right0[...])
-    for later in (needed[2], *ahead):
-        later.wait()
+def opening_kernel(slot, following, masks, tokens, info_ref, live_ref, left_hbm, right_hbm, *refs):
+    refs = list(refs[tokens:])
+    out_ref, _ = refs[:2]
+    sems = refs[-1]
+    operands = refs[2:-1]
+    psi_ref = live_ref
+    if masks:
+        live_ref = operands.pop(0)
+    own = fetch(info_ref, slot, left_hbm, right_hbm, *operands[:2], sems.at[0])
+    late = [own.pop()]
+    if following is not None:
+        late += fetch(info_ref, following, left_hbm, right_hbm, *operands[2:], sems.at[1])
+    for copy in own:
+        copy.start()
+    if masks:
+        rows, cols = psi_ref.shape
+        step = 128
+        col = lax.broadcasted_iota(jnp.int32, (step, cols), 1) < info_ref[5]
+        row = lax.broadcasted_iota(jnp.int32, (step, cols), 0)
+        for start in range(0, rows, step):
+            span = pl.ds(start, step)
+            inside = jnp.logical_and(row < info_ref[4] - start, col)
+            values = jnp.where(inside, psi_ref[span, :].astype(jnp.float32), 0.0)
+            live_ref[span, :] = values.astype(live_ref.dtype)
+    for copy in own:
+        copy.wait()
+    for copy in late:
+        copy.start()
+    out_ref[...] = multiply(operands[0][: out_ref.shape[0], :], live_ref[...], operands[1][...])
+    for copy in late:
+        copy.wait()
 
 
 def operand_shapes(width, cols):
@@ -82,24 +81,22 @@
     ]
 
 
-def first_rows(info, psi, left_env, right_env, count):
-    width, cols = psi.shape
+def opening_rows(info, live, envs, slot, count, *tokens, following=None, masks=False):
+    width, cols = live.shape
     out_shape = [jax.ShapeDtypeStruct((count, cols), jnp.float32), TOKEN]
-    out_shape += [jax.ShapeDtypeStruct(psi.shape, psi.dtype), *operand_shapes(width, cols) * 2]
-    return pl.pallas_call(
-        first_kernel,
+    if masks:
+        out_shape.append(jax.ShapeDtypeStruct(live.shape, live.dtype))
+    out_shape += operand_shapes(width, cols) * (1 if following is None else 2)
+    return pl.pallas_call(
+        functools.partial(opening_kernel, slot, following, masks, len(tokens)),
         out_shape=out_shape,
-        in_specs=[SMEM, HBM, HBM, HBM],
-        out_specs=[WHOLE, ANY] + [WHOLE] * 5,
-        scratch_shapes=[
-            pltpu.VMEM(psi.shape, psi.dtype),
-            pltpu.SemaphoreType.DMA((2, 3)),
-            pltpu.SemaphoreType.DMA((4,)),
-        ],
-        compiler_params=params(FIRST_MIB),
-        cost_estimate=SMALL,
-        name="first_rows",
-    )(info, psi, left_env, right_env)
+        in_specs=[SMEM, WHOLE, HBM, HBM] + [ANY] * len(tokens),
+        out_specs=[WHOLE, ANY] + [WHOLE] * (len(out_shape) - 2),
+        scratch_shapes=[pltpu.SemaphoreType.DMA((2, 3))],
+        compiler_params=params(FIRST_MIB if masks else BRING_MIB),
+        cost_estimate=SMALL,
+        name="opening_rows",
+    )(info, live, *envs, *tokens)
 
 
 def term_kernel(first, adds, slot, tokens, info_ref, live_ref, left_ref, right_ref, *refs):
@@ -329,22 +326,19 @@
     def relay(value):
         return send(value, (0, 4))
 
-    first0, token, live, *ops = first_rows(info, psi[0], left_env, right_env, part)
-    ops0, ops1 = ops[:2], ops[2:]
+    envs = (left_env, right_env)
+    first0, token, live, *ops0 = opening_rows(info, psi[0], envs, 0, part, masks=True)
     paired0 = up_chip(first0)
-    first1, token, *ops2 = term_rows(
-        info, live, ops0, part, part, token, bring=(2, left_env, right_env)
-    )
+    first1, token = term_rows(info, live, ops0, part, part, token)
     paired1 = up_chip(first1)
     both0, token = add(first0, paired0, token)
     raised0 = raise_one(both0)
-    second0, token, *ops3 = term_rows(
-        info, live, ops1, 0, part, token, bring=(3, left_env, right_env)
-    )
+    second0, token, *ops = opening_rows(info, live, envs, 1, part, token, following=2)
+    ops1, ops2 = ops[:2], ops[2:]
     moved0 = along(second0)
     both1, token = add(first1, paired1, token)
     raised1 = raise_one(both1)
-    second1, token = term_rows(info, live, ops1, part, part, token)
+    second1, token, *ops3 = term_rows(info, live, ops1, part, part, token, bring=(3, *envs))
     moved1 = along(second1)
     third0, token = term_rows(info, live, ops2, 0, part, token)
     swapped0 = swap(third0)

time: 77.5 us -> 77.3 us (level)
  starting transfers between devices: 22 us -> 25.2 us
  waiting for transfers between devices: 13.8 us -> 10.9 us
  blocking collectives: 18.3 us -> 16.1 us
  Pallas kernels: 19.5 us -> 21 us
    pallas_call x1 -> x2, Pallas kernels: 3.27 us -> 6.9 us  [opening_rows(): pl.pallas_call(functools.partial(opening_kernel, slot, following, masks,...]
    ppermute x10, starting transfers between devices: 19.4 us -> 22.6 us  [send(): return lax.ppermute(value, 'sec', pairs)]
    ppermute x2, waiting for transfers between devices: 5.56 us -> 2.67 us  [raise_one(): return lax.ppermute(value, 'sec', pairs_up)]
    pallas_call x7 -> x6, Pallas kernels: 11.9 us -> 9.76 us  [term_rows(): pl.pallas_call(functools.partial(term_kernel, first, added is not None, s...]
    all_to_all x1, blocking collectives: 18.3 us -> 16.1 us  [sum_over_sectors(): arrived = lax.all_to_all(value, 'sec', 0, 0, tiled=True)]
  transfers between devices with their start and end apart: 12 -> 12, of which waited for: 4 -> 3; matrix products, arithmetic and copies ran while one was open for 0% -> 0% of each run, Pallas kernels for 18% -> 20%
where the time goes in v8:
time: 77.3 us; the launch traced here: 76.8 us
  starting transfers between devices  25.2 us (33%)
  Pallas kernels  21 us (27%)
  blocking collectives  16.1 us (21%)
  waiting for transfers between devices  10.9 us (14%)
  between operations  2.22 us (3%)
  local copies, waits for them, and re-layouts  1.32 us (2%)
    ppermute x10, starting transfers between devices, send(): return lax.ppermute(value, 'sec', pairs)  22.6 us
    all_to_all x1, blocking collectives, sum_over_sectors(): arrived = lax.all_to_all(value, 'sec', 0, 0, tiled=True)  16.1 us
    pallas_call x6, Pallas kernels, term_rows(): pl.pallas_call(functools.partial(term_kernel, first, added is not None, s...  9.76 us
    ppermute x10, waiting for transfers between devices, send(): return lax.ppermute(value, 'sec', pairs)  8.22 us
    pallas_call x2, Pallas kernels, opening_rows(): pl.pallas_call(functools.partial(opening_kernel, slot, following, masks,...  6.9 us
    pallas_call x2, Pallas kernels, finish(): pl.pallas_call(functools.partial(finish_kernel, first), out_shape=(jax.Sh...  3.14 us
    ppermute x2, waiting for transfers between devices, raise_one(): return lax.ppermute(value, 'sec', pairs_up)  2.67 us
    ppermute x2, starting transfers between devices, raise_one(): return lax.ppermute(value, 'sec', pairs_up)  2.57 us
  transfers between devices with their start and end apart: 12, of which 3 were waited for; matrix products, arithmetic and copies ran while one was open for 0% of the time, Pallas kernels for 20%

profile of v8, /device:TPU:0, one launch (start us, length us, event | category | flops | bytes accessed | tf_op | source)
XLA Modules:
  0.0 76.8 jit_solution(9802131195305621621)
XLA Ops:
  2.0 1.2 %copy-done.1 = bf16[1,1024,512]{2,1,0:T(8,128)(2,1)S(1)} copy-done((bf16[1,1024,512]{2,1,0:T(8,128)(2,1)S(1)}, bf16[1,1024,512]{2,1,0:T(8,128)(2,1)}, u32[]{:S(2)}) %copy-start.1) | copy-done | bytes 1048600
  3.3 3.2 %opening_rows.2 = (f32[512,512]{1,0:T(8,128)S(1)}, f32[8,128]{1,0:T(8,128)S(1)}, bf16[1024,512]{1,0:T(8,128)(2,1)S(1)}, bf16[1024,1024]{1,0:T(8,128)(2,1)S(1)}, bf16[512,512]{1,0:T(8,128)(2,1)S(1)}) custom-call(s32[7]{0:T(128)S(1)} %stack.19.info_ref, bf16[1024,512]{1,0:T(8,128)(2,1)S(1)} %bitcast.9, bf16[1,4,1024,1024]{3,2,1,0:T(8,128)(2,1)} %refs_0_.1, ...), custom_call_target="tpu_custom_call" | custom-call | flops 200000000 | bytes 1000000 | tf_op jit(solution)/shard_map/opening_rows/pallas_call | solution.py:90
  6.4 2.4 %collective-permute-start = (f32[512,512]{1,0:T(8,128)S(1)}, f32[512,512]{1,0:T(8,128)S(1)}, u32[]{:S(2)}, u32[]{:S(2)}) collective-permute-start(f32[512,512]{1,0:T(8,128)S(1)} %get-tuple-element.43.a_ref), channel_id=1, source_target_pairs={{0,1},{4,5},{8,9},{12,13},{2,3},{6,7},{10,11},{14,15},{16,17},{20,... | collective-permute-start | bytes 3145736 | tf_op jit(solution)/shard_map/ppermute | solution.py:300
  8.9 1.5 %term_rows.6 = (f32[512,512]{1,0:T(8,128)S(1)}, f32[8,128]{1,0:T(8,128)S(1)}) custom-call(s32[7]{0:T(128)S(1)} %stack.19.info_ref, bf16[1024,512]{1,0:T(8,128)(2,1)S(1)} %get-tuple-element.42.live_ref, bf16[1024,1024]{1,0:T(8,128)(2,1)S(1)} %get-tuple-element.44.left_ref, bf16[512,512]{1,0:T(8,128)(2,1)S(1)} %get-tuple-element.45.right_ref, ...), custom_call_target="tpu_custom_call" | custom-call | flops 200000000 | bytes 1000000 | tf_op jit(solution)/shard_map/term_rows/pallas_call | solution.py:145
  10.4 1.4 %collective-permute-start.1 = (f32[512,512]{1,0:T(8,128)S(1)}, f32[512,512]{1,0:T(8,128)S(1)}, u32[]{:S(2)}, u32[]{:S(2)}) collective-permute-start(f32[512,512]{1,0:T(8,128)S(1)} %get-tuple-element.51.a_ref), channel_id=1, source_target_pairs={{0,1},{4,5},{8,9},{12,13},{2,3},{6,7},{10,11},{14,15},{16,17},{20,... | collective-permute-start | bytes 3145736 | tf_op jit(solution)/shard_map/ppermute | solution.py:300
  11.9 1.3 %collective-permute-start.2 = (f32[512,512]{1,0:T(8,128)S(1)}, f32[512,512]{1,0:T(8,128)S(1)}, u32[]{:S(2)}, u32[]{:S(2)}) collective-permute-start(f32[512,512]{1,0:T(8,128)S(1)} %get-tuple-element.58), channel_id=1, source_target_pairs={{1,2},{5,6},{9,10},{13,14},{3,0},{7,4},{11,8},{17,18},{21,22},{25,... | collective-permute-start | bytes 3145736 | tf_op jit(solution)/shard_map/ppermute | solution.py:312
  13.3 3.7 %opening_rows.3 = (f32[512,512]{1,0:T(8,128)S(1)}, f32[8,128]{1,0:T(8,128)S(1)}, bf16[1024,1024]{1,0:T(8,128)(2,1)S(1)}, bf16[512,512]{1,0:T(8,128)(2,1)S(1)}, b...) custom-call(s32[7]{0:T(128)S(1)} %stack.19.info_ref, bf16[1024,512]{1,0:T(8,128)(2,1)S(1)} %get-tuple-element.42.live_ref, ...), custom_call_target="tpu_custom_call" | custom-call | flops 200000000 | bytes 1000000 | tf_op jit(solution)/shard_map/opening_rows/pallas_call | solution.py:90
  17.0 0.7 collective-permute-start.8
  17.9 2.2 %term_rows.7 = (f32[512,512]{1,0:T(8,128)S(1)}, f32[8,128]{1,0:T(8,128)S(1)}, bf16[1024,1024]{1,0:T(8,128)(2,1)S(1)}, bf16[512,512]{1,0:T(8,128)(2,1)S(1)}) custom-call(s32[7]{0:T(128)S(1)} %stack.19.info_ref, bf16[1024,512]{1,0:T(8,128)(2,1)S(1)} %get-tuple-element.42.live_ref, bf16[1024,1024]{1,0:T(8,128)(2,1)S(1)} %get-tuple-element.49.left_ref, ...), custom_call_target="tpu_custom_call" | custom-call | flops 200000000 | bytes 1000000 | tf_op jit(solution)/shard_map/term_rows/pallas_call | solution.py:145
  20.1 1.5 %term_rows.8 = (f32[512,512]{1,0:T(8,128)S(1)}, f32[8,128]{1,0:T(8,128)S(1)}) custom-call(s32[7]{0:T(128)S(1)} %stack.19.info_ref, bf16[1024,512]{1,0:T(8,128)(2,1)S(1)} %get-tuple-element.42.live_ref, bf16[1024,1024]{1,0:T(8,128)(2,1)S(1)} %get-tuple-element.56.left_ref, bf16[512,512]{1,0:T(8,128)(2,1)S(1)} %get-tuple-element.57.right_ref, ...), custom_call_target="tpu_custom_call" | custom-call | flops 200000000 | bytes 1000000 | tf_op jit(solution)/shard_map/term_rows/pallas_call | solution.py:145
  21.6 3.8 %collective-permute-start.7 = (f32[512,512]{1,0:T(8,128)S(1)}, f32[512,512]{1,0:T(8,128)S(1)}, u32[]{:S(2)}, u32[]{:S(2)}) collective-permute-start(f32[512,512]{1,0:T(8,128)S(1)} %get-tuple-element.66), channel_id=1, source_target_pairs={{0,1},{4,5},{8,9},{12,13},{1,0},{5,4},{9,8},{13,12},{2,3},{6,7},{1... | collective-permute-start | bytes 3145736 | tf_op jit(solution)/shard_map/ppermute | solution.py:300
  25.4 1.3 %collective-permute-start.6 = (f32[512,512]{1,0:T(8,128)S(1)}, f32[512,512]{1,0:T(8,128)S(1)}, u32[]{:S(2)}, u32[]{:S(2)}) collective-permute-start(f32[512,512]{1,0:T(8,128)S(1)} %get-tuple-element.65), channel_id=1, source_target_pairs={{1,2},{5,6},{9,10},{13,14},{3,0},{7,4},{11,8},{17,18},{21,22},{25,... | collective-permute-start | bytes 3145736 | tf_op jit(solution)/shard_map/ppermute | solution.py:312
  26.6 1.4 %collective-permute-done.2.refs_0_ = f32[512,512]{1,0:T(8,128)S(1)} collective-permute-done((f32[512,512]{1,0:T(8,128)S(1)}, f32[512,512]{1,0:T(8,128)S(1)}, u32[]{:S(2)}, u32[]{:S(2)}) %collective-permute-start.2) | collective-permute-done | bytes 1048608 | tf_op jit(solution)/shard_map/ppermute | solution.py:312
  28.1 4.4 %collective-permute-start.5 = (f32[512,512]{1,0:T(8,128)S(1)}, f32[512,512]{1,0:T(8,128)S(1)}, u32[]{:S(2)}, u32[]{:S(2)}) collective-permute-start(f32[512,512]{1,0:T(8,128)S(1)} %get-tuple-element.64.a_ref), channel_id=1, source_target_pairs={{0,4},{4,8},{8,12},{16,20},{20,24},{24,28}} | collective-permute-start | bytes 3145736 | tf_op jit(solution)/shard_map/ppermute | solution.py:300
  33.2 1.5 %term_rows.9 = (f32[512,512]{1,0:T(8,128)S(1)}, f32[8,128]{1,0:T(8,128)S(1)}) custom-call(s32[7]{0:T(128)S(1)} %stack.19.info_ref, bf16[1024,512]{1,0:T(8,128)(2,1)S(1)} %get-tuple-element.42.live_ref, bf16[1024,1024]{1,0:T(8,128)(2,1)S(1)} %get-tuple-element.56.left_ref, bf16[512,512]{1,0:T(8,128)(2,1)S(1)} %get-tuple-element.57.right_ref, ...), custom_call_target="tpu_custom_call" | custom-call | flops 200000000 | bytes 1000000 | tf_op jit(solution)/shard_map/term_rows/pallas_call | solution.py:145
  35.6 3.1 %collective-permute-start.3 = (f32[512,512]{1,0:T(8,128)S(1)}, f32[512,512]{1,0:T(8,128)S(1)}, u32[]{:S(2)}, u32[]{:S(2)}) collective-permute-start(f32[512,512]{1,0:T(8,128)S(1)} %get-tuple-element.62), channel_id=1, source_target_pairs={{0,1},{4,5},{8,9},{12,13},{1,0},{5,4},{9,8},{13,12},{2,3},{6,7},{1... | collective-permute-start | bytes 3145736 | tf_op jit(solution)/shard_map/ppermute | solution.py:300
  38.7 1.5 %term_rows.10 = (f32[512,512]{1,0:T(8,128)S(1)}, f32[8,128]{1,0:T(8,128)S(1)}) custom-call(s32[7]{0:T(128)S(1)} %stack.19.info_ref, bf16[1024,512]{1,0:T(8,128)(2,1)S(1)} %get-tuple-element.42.live_ref, bf16[1024,1024]{1,0:T(8,128)(2,1)S(1)} %get-tuple-element.54.left_ref, bf16[512,512]{1,0:T(8,128)(2,1)S(1)} %get-tuple-element.55.right_ref, ...), custom_call_target="tpu_custom_call" | custom-call | flops 200000000 | bytes 1000000 | tf_op jit(solution)/shard_map/term_rows/pallas_call | solution.py:145
  40.2 1.2 %collective-permute-done.6.refs_0_ = f32[512,512]{1,0:T(8,128)S(1)} collective-permute-done((f32[512,512]{1,0:T(8,128)S(1)}, f32[512,512]{1,0:T(8,128)S(1)}, u32[]{:S(2)}, u32[]{:S(2)}) %collective-permute-start.6) | collective-permute-done | bytes 1048608 | tf_op jit(solution)/shard_map/ppermute | solution.py:312
  41.5 4.7 %collective-permute-start.10 = (f32[512,512]{1,0:T(8,128)S(1)}, f32[512,512]{1,0:T(8,128)S(1)}, u32[]{:S(2)}, u32[]{:S(2)}) collective-permute-start(f32[512,512]{1,0:T(8,128)S(1)} %get-tuple-element.77.a_ref), channel_id=1, source_target_pairs={{0,4},{4,8},{8,12},{16,20},{20,24},{24,28}} | collective-permute-start | bytes 3145736 | tf_op jit(solution)/shard_map/ppermute | solution.py:300
  47.1 1.6 %finish_rows.2 = (bf16[1,1024,512]{2,1,0:T(8,128)(2,1)}, f32[16,128]{1,0:T(8,128)S(1)}) custom-call(s32[7]{0:T(128)S(1)} %stack.19.info_ref, bf16[1024,512]{1,0:T(8,128)(2,1)S(1)} %get-tuple-element.42.live_ref, f32[512,512]{1,0:T(8,128)S(1)} %get-tuple-element.73.own_ref, f32[512,512]{1,0:T(8,128)S(1)} %get-tuple-element.64.a_ref, ...), custom_call_target="tpu_custom_call" | custom-call | flops 200000000 | bytes 1000000 | tf_op jit(solution)/shard_map/finish_rows/pallas_call | solution.py:254
  48.7 1.5 %term_rows.11 = (f32[512,512]{1,0:T(8,128)S(1)}, f32[8,128]{1,0:T(8,128)}) custom-call(s32[7]{0:T(128)S(1)} %stack.19.info_ref, bf16[1024,512]{1,0:T(8,128)(2,1)S(1)} %get-tuple-element.42.live_ref, bf16[1024,1024]{1,0:T(8,128)(2,1)S(1)} %get-tuple-element.54.left_ref, bf16[512,512]{1,0:T(8,128)(2,1)S(1)} %get-tuple-element.55.right_ref, ...), custom_call_target="tpu_custom_call" | custom-call | flops 200000000 | bytes 1000000 | tf_op jit(solution)/shard_map/term_rows/pallas_call | solution.py:145
  50.2 8.2 %collective-permute-done.10.b_ref = f32[512,512]{1,0:T(8,128)S(1)} collective-permute-done((f32[512,512]{1,0:T(8,128)S(1)}, f32[512,512]{1,0:T(8,128)S(1)}, u32[]{:S(2)}, u32[]{:S(2)}) %collective-permute-start.10) | collective-permute-done | bytes 1048608 | tf_op jit(solution)/shard_map/ppermute | solution.py:300
  58.4 1.6 %finish_rows.3 = (bf16[1,1024,512]{2,1,0:T(8,128)(2,1)}, f32[16,128]{1,0:T(8,128)S(1)}) custom-call(s32[7]{0:T(128)S(1)} %stack.19.info_ref, bf16[1024,512]{1,0:T(8,128)(2,1)S(1)} %get-tuple-element.42.live_ref, f32[512,512]{1,0:T(8,128)S(1)} %get-tuple-element.76.own_ref, f32[512,512]{1,0:T(8,128)S(1)} %get-tuple-element.77.a_ref, ...), custom_call_target="tpu_custom_call", output_to_operand_aliasing={{0}: (7, {})} | custom-call | flops 200000000 | bytes 1000000 | tf_op jit(solution)/shard_map/finish_rows/pallas_call | solution.py:254
  60.0 16.1 %all_to_all.11 = f32[16,1,128]{2,1,0:T(1,128)S(1)} all-to-all(f32[16,1,128]{2,1,0:T(1,128)S(1)} %bitcast.10), channel_id=1, replica_groups=mesh['grp'=2,'sec'=16] {'sec'}, dimensions={0} | all-to-all | bytes 16384 | tf_op jit(solution)/shard_map/all_to_all | solution.py:275
  (25 shorter events, 3.5 us)
Async XLA Ops:
  2.0 1.2 %copy-start.1 = (bf16[1,1024,512]{2,1,0:T(8,128)(2,1)S(1)}, bf16[1,1024,512]{2,1,0:T(8,128)(2,1)}, u32[]{:S(2)}) copy-start(bf16[1,1024,512]{2,1,0:T(8,128)(2,1)} %param.5) | copy-start | bytes 3145732
  6.4 5.3 %collective-permute-start = (f32[512,512]{1,0:T(8,128)S(1)}, f32[512,512]{1,0:T(8,128)S(1)}, u32[]{:S(2)}, u32[]{:S(2)}) collective-permute-start(f32[512,512]{1,0:T(8,128)S(1)} %get-tuple-element.43.a_ref), channel_id=1, source_target_pairs={{0,1},{4,5},{8,9},{12,13},{2,3},{6,7},{10,11},{14,15},{16,17},{20,... | collective-permute-start | bytes 3145736 | tf_op jit(solution)/shard_map/ppermute | solution.py:300
  8.9 4.4 %copy-start = (bf16[1,4,512,512]{3,2,1,0:T(8,128)(2,1)S(1)}, bf16[1,4,512,512]{3,2,1,0:T(8,128)(2,1)}, u32[]{:S(2)}) copy-start(bf16[1,4,512,512]{3,2,1,0:T(8,128)(2,1)} %refs_1_.1) | copy-start | bytes 6291460
  10.4 7.3 %collective-permute-start.1 = (f32[512,512]{1,0:T(8,128)S(1)}, f32[512,512]{1,0:T(8,128)S(1)}, u32[]{:S(2)}, u32[]{:S(2)}) collective-permute-start(f32[512,512]{1,0:T(8,128)S(1)} %get-tuple-element.51.a_ref), channel_id=1, source_target_pairs={{0,1},{4,5},{8,9},{12,13},{2,3},{6,7},{10,11},{14,15},{16,17},{20,... | collective-permute-start | bytes 3145736 | tf_op jit(solution)/shard_map/ppermute | solution.py:300
  11.9 16.1 %collective-permute-start.2 = (f32[512,512]{1,0:T(8,128)S(1)}, f32[512,512]{1,0:T(8,128)S(1)}, u32[]{:S(2)}, u32[]{:S(2)}) collective-permute-start(f32[512,512]{1,0:T(8,128)S(1)} %get-tuple-element.58), channel_id=1, source_target_pairs={{1,2},{5,6},{9,10},{13,14},{3,0},{7,4},{11,8},{17,18},{21,22},{25,... | collective-permute-start | bytes 3145736 | tf_op jit(solution)/shard_map/ppermute | solution.py:312
  17.0 17.7 %collective-permute-start.8 = (f32[512,512]{1,0:T(8,128)S(1)}, f32[512,512]{1,0:T(8,128)S(1)}, u32[]{:S(2)}, u32[]{:S(2)}) collective-permute-start(f32[512,512]{1,0:T(8,128)S(1)} %get-tuple-element.67.a_ref), channel_id=1, source_target_pairs={{3,6},{7,10},{11,14},{4,1},{8,5},{12,9},{19,22},{23,26},{27,30},{2... | collective-permute-start | bytes 3145736 | tf_op jit(solution)/shard_map/ppermute | solution.py:300
  21.6 14.0 %collective-permute-start.7 = (f32[512,512]{1,0:T(8,128)S(1)}, f32[512,512]{1,0:T(8,128)S(1)}, u32[]{:S(2)}, u32[]{:S(2)}) collective-permute-start(f32[512,512]{1,0:T(8,128)S(1)} %get-tuple-element.66), channel_id=1, source_target_pairs={{0,1},{4,5},{8,9},{12,13},{1,0},{5,4},{9,8},{13,12},{2,3},{6,7},{1... | collective-permute-start | bytes 3145736 | tf_op jit(solution)/shard_map/ppermute | solution.py:300
  25.4 16.1 %collective-permute-start.6 = (f32[512,512]{1,0:T(8,128)S(1)}, f32[512,512]{1,0:T(8,128)S(1)}, u32[]{:S(2)}, u32[]{:S(2)}) collective-permute-start(f32[512,512]{1,0:T(8,128)S(1)} %get-tuple-element.65), channel_id=1, source_target_pairs={{1,2},{5,6},{9,10},{13,14},{3,0},{7,4},{11,8},{17,18},{21,22},{25,... | collective-permute-start | bytes 3145736 | tf_op jit(solution)/shard_map/ppermute | solution.py:312
  28.1 18.1 %collective-permute-start.5 = (f32[512,512]{1,0:T(8,128)S(1)}, f32[512,512]{1,0:T(8,128)S(1)}, u32[]{:S(2)}, u32[]{:S(2)}) collective-permute-start(f32[512,512]{1,0:T(8,128)S(1)} %get-tuple-element.64.a_ref), channel_id=1, source_target_pairs={{0,4},{4,8},{8,12},{16,20},{20,24},{24,28}} | collective-permute-start | bytes 3145736 | tf_op jit(solution)/shard_map/ppermute | solution.py:300
  32.4 13.7 %collective-permute-start.4 = (f32[512,512]{1,0:T(8,128)S(1)}, f32[512,512]{1,0:T(8,128)S(1)}, u32[]{:S(2)}, u32[]{:S(2)}) collective-permute-start(f32[512,512]{1,0:T(8,128)S(1)} %get-tuple-element.63.a_ref), channel_id=1, source_target_pairs={{3,6},{7,10},{11,14},{4,1},{8,5},{12,9},{19,22},{23,26},{27,30},{2... | collective-permute-start | bytes 3145736 | tf_op jit(solution)/shard_map/ppermute | solution.py:300
  34.9 12.2 %collective-permute-start.9 = (f32[512,512]{1,0:T(8,128)S(1)}, f32[512,512]{1,0:T(8,128)S(1)}, u32[]{:S(2)}, u32[]{:S(2)}) collective-permute-start(f32[512,512]{1,0:T(8,128)S(1)} %get-tuple-element.74), channel_id=1, source_target_pairs={{1,3},{5,7},{9,11},{13,15},{2,1},{6,5},{10,9},{14,13},{17,19},{21,... | collective-permute-start | bytes 3145736 | tf_op jit(solution)/shard_map/ppermute | solution.py:300
  35.6 13.1 %collective-permute-start.3 = (f32[512,512]{1,0:T(8,128)S(1)}, f32[512,512]{1,0:T(8,128)S(1)}, u32[]{:S(2)}, u32[]{:S(2)}) collective-permute-start(f32[512,512]{1,0:T(8,128)S(1)} %get-tuple-element.62), channel_id=1, source_target_pairs={{0,1},{4,5},{8,9},{12,13},{1,0},{5,4},{9,8},{13,12},{2,3},{6,7},{1... | collective-permute-start | bytes 3145736 | tf_op jit(solution)/shard_map/ppermute | solution.py:300
  41.5 16.9 %collective-permute-start.10 = (f32[512,512]{1,0:T(8,128)S(1)}, f32[512,512]{1,0:T(8,128)S(1)}, u32[]{:S(2)}, u32[]{:S(2)}) collective-permute-start(f32[512,512]{1,0:T(8,128)S(1)} %get-tuple-element.77.a_ref), channel_id=1, source_target_pairs={{0,4},{4,8},{8,12},{16,20},{20,24},{24,28}} | collective-permute-start | bytes 3145736 | tf_op jit(solution)/shard_map/ppermute | solution.py:300
  46.3 12.1 %collective-permute-start.11 = (f32[512,512]{1,0:T(8,128)S(1)}, f32[512,512]{1,0:T(8,128)S(1)}, u32[]{:S(2)}, u32[]{:S(2)}) collective-permute-start(f32[512,512]{1,0:T(8,128)S(1)} %get-tuple-element.78), channel_id=1, source_target_pairs={{1,3},{5,7},{9,11},{13,15},{2,1},{6,5},{10,9},{14,13},{17,19},{21,... | collective-permute-start | bytes 3145736 | tf_op jit(solution)/shard_map/ppermute | solution.py:300

commit v9 on v8

--- a/solution.py
+++ b/solution.py
@@ -8,6 +8,7 @@
 from jax.sharding import PartitionSpec as P
 
 MIB = 1024 * 1024
+LEFT_PIECES, RIGHT_PIECES = 8, 2
 FIRST_MIB = 48
 BRING_MIB = 42
 
@@ -25,15 +26,24 @@
 
 def fetch(info_ref, slot, left_hbm, right_hbm, left_ref, right_ref, sems):
     term = info_ref[slot]
-    half = left_ref.shape[0] // 2
-    copies = []
-    for i in range(2):
-        span = pl.ds(i * half, half)
-        copies.append(
+    rows, cols = left_ref.shape[0], right_ref.shape[0]
+    step = rows // LEFT_PIECES
+    left, right = [], []
+    for i in range(LEFT_PIECES):
+        span = pl.ds(i * step, step)
+        left.append(
             pltpu.make_async_copy(left_hbm.at[0, term, span, :], left_ref.at[span, :], sems.at[i])
         )
-    copies.insert(1, pltpu.make_async_copy(right_hbm.at[0, term], right_ref, sems.at[2]))
-    return copies
+    step = cols // RIGHT_PIECES
+    for i in range(RIGHT_PIECES):
+        span = pl.ds(i * step, step)
+        right.append(
+            pltpu.make_async_copy(
+                right_hbm.at[0, term, span, :], right_ref.at[span, :], sems.at[LEFT_PIECES + i]
+            )
+        )
+    half = LEFT_PIECES // 2
+    return left[:half] + right, left[half:]
 
 
 def multiply(left, live, right):
@@ -41,7 +51,7 @@
     return jnp.dot(first, right, preferred_element_type=jnp.float32)
 
 
-def opening_kernel(slot, following, masks, tokens, info_ref, live_ref, left_hbm, right_hbm, *refs):
+def opening_kernel(slot, masks, tokens, info_ref, live_ref, left_hbm, right_hbm, *refs):
     refs = list(refs[tokens:])
     out_ref, _ = refs[:2]
     sems = refs[-1]
@@ -49,11 +59,8 @@
     psi_ref = live_ref
     if masks:
         live_ref = operands.pop(0)
-    own = fetch(info_ref, slot, left_hbm, right_hbm, *operands[:2], sems.at[0])
-    late = [own.pop()]
-    if following is not None:
-        late += fetch(info_ref, following, left_hbm, right_hbm, *operands[2:], sems.at[1])
-    for copy in own:
+    own, late = fetch(info_ref, slot, left_hbm, right_hbm, *operands, sems)
+    for copy in own + late:
         copy.start()
     if masks:
         rows, cols = psi_ref.shape
@@ -67,8 +74,6 @@
             live_ref[span, :] = values.astype(live_ref.dtype)
     for copy in own:
         copy.wait()
-    for copy in late:
-        copy.start()
     out_ref[...] = multiply(operands[0][: out_ref.shape[0], :], live_ref[...], operands[1][...])
     for copy in late:
         copy.wait()
@@ -81,18 +86,18 @@
     ]
 
 
-def opening_rows(info, live, envs, slot, count, *tokens, following=None, masks=False):
+def opening_rows(info, live, envs, slot, count, *tokens, masks=False):
     width, cols = live.shape
     out_shape = [jax.ShapeDtypeStruct((count, cols), jnp.float32), TOKEN]
     if masks:
         out_shape.append(jax.ShapeDtypeStruct(live.shape, live.dtype))
-    out_shape += operand_shapes(width, cols) * (1 if following is None else 2)
-    return pl.pallas_call(
-        functools.partial(opening_kernel, slot, following, masks, len(tokens)),
+    out_shape += operand_shapes(width, cols)
+    return pl.pallas_call(
+        functools.partial(opening_kernel, slot, masks, len(tokens)),
         out_shape=out_shape,
         in_specs=[SMEM, WHOLE, HBM, HBM] + [ANY] * len(tokens),
         out_specs=[WHOLE, ANY] + [WHOLE] * (len(out_shape) - 2),
-        scratch_shapes=[pltpu.SemaphoreType.DMA((2, 3))],
+        scratch_shapes=[pltpu.SemaphoreType.DMA((LEFT_PIECES + RIGHT_PIECES,))],
         compiler_params=params(FIRST_MIB if masks else BRING_MIB),
         cost_estimate=SMALL,
         name="opening_rows",
@@ -107,7 +112,7 @@
         left_hbm, right_hbm = refs[:2]
         sems = refs[-1]
         out_ref, _, left_next, right_next = refs[2 + tokens : -1]
-        copies = fetch(info_ref, slot, left_hbm, right_hbm, left_next, right_next, sems)
+        copies = sum(fetch(info_ref, slot, left_hbm, right_hbm, left_next, right_next, sems), [])
         for copy in copies:
             copy.start()
     else:
@@ -141,7 +146,7 @@
         args += bring[1:]
         out_shape += operand_shapes(width, cols)
         out_specs += [WHOLE, WHOLE]
-        scratch.append(pltpu.SemaphoreType.DMA((3,)))
+        scratch.append(pltpu.SemaphoreType.DMA((LEFT_PIECES + RIGHT_PIECES,)))
     return pl.pallas_call(
         functools.partial(term_kernel, first, added is not None, slot, len(tokens)),
         out_shape=out_shape,
@@ -333,14 +338,13 @@
     paired1 = up_chip(first1)
     both0, token = add(first0, paired0, token)
     raised0 = raise_one(both0)
-    second0, token, *ops = opening_rows(info, live, envs, 1, part, token, following=2)
-    ops1, ops2 = ops[:2], ops[2:]
+    second0, token, *ops1 = opening_rows(info, live, envs, 1, part, token)
     moved0 = along(second0)
     both1, token = add(first1, paired1, token)
     raised1 = raise_one(both1)
-    second1, token, *ops3 = term_rows(info, live, ops1, part, part, token, bring=(3, *envs))
+    second1, token, *ops2 = term_rows(info, live, ops1, part, part, token, bring=(2, *envs))
     moved1 = along(second1)
-    third0, token = term_rows(info, live, ops2, 0, part, token)
+    third0, token, *ops3 = term_rows(info, live, ops2, 0, part, token, bring=(3, *envs))
     swapped0 = swap(third0)
     raised0, token = hold(raised0, token)
     relayed0 = relay(raised0)
@@ -348,9 +352,9 @@
     swapped1 = swap(third1)
     summed0, token = add(second0, moved0, token)
     crossed0 = across(summed0)
-    own0, token = term_rows(info, live, ops3, 0, part, token, added=swapped0)
     raised1, token = hold(raised1, token)
     relayed1 = relay(raised1)
+    own0, token = term_rows(info, live, ops3, 0, part, token, added=swapped0)
     token = touch(relayed0, token)
     summed1, token = add(second1, moved1, token)
     crossed1 = across(summed1)

time: 77.3 us -> 76.6 us (level)
  starting transfers between devices: 25.2 us -> 21.8 us
  blocking collectives: 16.1 us -> 18.2 us
  waiting for transfers between devices: 10.9 us -> 12 us
    ppermute x10, starting transfers between devices: 22.6 us -> 19.3 us  [send(): return lax.ppermute(value, 'sec', pairs)]
    ppermute x2, waiting for transfers between devices: 2.67 us -> 5.29 us  [raise_one(): return lax.ppermute(value, 'sec', pairs_up)]
    all_to_all x1, blocking collectives: 16.1 us -> 18.2 us  [sum_over_sectors(): arrived = lax.all_to_all(value, 'sec', 0, 0, tiled=True)]
    ppermute x10, waiting for transfers between devices: 8.22 us -> 6.72 us  [send(): return lax.ppermute(value, 'sec', pairs)]
    pallas_call x2, Pallas kernels: 6.9 us -> 5.77 us  [opening_rows(): pl.pallas_call(functools.partial(opening_kernel, slot, masks, len(tokens)...]
where the time goes in v9:
time: 76.6 us; the launch traced here: 76.1 us
  starting transfers between devices  21.8 us (28%)
  Pallas kernels  20.5 us (27%)
  blocking collectives  18.2 us (24%)
  waiting for transfers between devices  12 us (16%)
  between operations  2.21 us (3%)
  local copies, waits for them, and re-layouts  1.32 us (2%)
    ppermute x10, starting transfers between devices, send(): return lax.ppermute(value, 'sec', pairs)  19.3 us
    all_to_all x1, blocking collectives, sum_over_sectors(): arrived = lax.all_to_all(value, 'sec', 0, 0, tiled=True)  18.2 us
    pallas_call x6, Pallas kernels, term_rows(): pl.pallas_call(functools.partial(term_kernel, first, added is not None, s...  10.4 us
    ppermute x10, waiting for transfers between devices, send(): return lax.ppermute(value, 'sec', pairs)  6.72 us
    pallas_call x2, Pallas kernels, opening_rows(): pl.pallas_call(functools.partial(opening_kernel, slot, masks, len(tokens)...  5.77 us
    ppermute x2, waiting for transfers between devices, raise_one(): return lax.ppermute(value, 'sec', pairs_up)  5.29 us
    pallas_call x2, Pallas kernels, finish(): pl.pallas_call(functools.partial(finish_kernel, first), out_shape=(jax.Sh...  3.07 us
    ppermute x2, starting transfers between devices, raise_one(): return lax.ppermute(value, 'sec', pairs_up)  2.58 us
  transfers between devices with their start and end apart: 12, of which 3 were waited for; matrix products, arithmetic and copies ran while one was open for 0% of the time, Pallas kernels for 20%

profile of v9, /device:TPU:0, one launch (start us, length us, event | category | flops | bytes accessed | tf_op | source)
XLA Modules:
  0.0 76.1 jit_solution(13649211719557549609)
XLA Ops:
  2.0 1.2 %copy-done.1 = bf16[1,1024,512]{2,1,0:T(8,128)(2,1)S(1)} copy-done((bf16[1,1024,512]{2,1,0:T(8,128)(2,1)S(1)}, bf16[1,1024,512]{2,1,0:T(8,128)(2,1)}, u32[]{:S(2)}) %copy-start.1) | copy-done | bytes 1048600
  3.3 3.0 %opening_rows.2 = (f32[512,512]{1,0:T(8,128)S(1)}, f32[8,128]{1,0:T(8,128)S(1)}, bf16[1024,512]{1,0:T(8,128)(2,1)S(1)}, bf16[1024,1024]{1,0:T(8,128)(2,1)S(1)}, bf16[512,512]{1,0:T(8,128)(2,1)S(1)}) custom-call(s32[7]{0:T(128)S(1)} %stack.19.info_ref, bf16[1024,512]{1,0:T(8,128)(2,1)S(1)} %bitcast.9, bf16[1,4,1024,1024]{3,2,1,0:T(8,128)(2,1)} %refs_0_.3, ...), custom_call_target="tpu_custom_call" | custom-call | flops 200000000 | bytes 1000000 | tf_op jit(solution)/shard_map/opening_rows/pallas_call | solution.py:95
  6.2 2.4 %collective-permute-start = (f32[512,512]{1,0:T(8,128)S(1)}, f32[512,512]{1,0:T(8,128)S(1)}, u32[]{:S(2)}, u32[]{:S(2)}) collective-permute-start(f32[512,512]{1,0:T(8,128)S(1)} %get-tuple-element.43.a_ref), channel_id=1, source_target_pairs={{0,1},{4,5},{8,9},{12,13},{2,3},{6,7},{10,11},{14,15},{16,17},{20,... | collective-permute-start | bytes 3145736 | tf_op jit(solution)/shard_map/ppermute | solution.py:305
  8.7 1.5 %term_rows.6 = (f32[512,512]{1,0:T(8,128)S(1)}, f32[8,128]{1,0:T(8,128)S(1)}) custom-call(s32[7]{0:T(128)S(1)} %stack.19.info_ref, bf16[1024,512]{1,0:T(8,128)(2,1)S(1)} %get-tuple-element.42.live_ref, bf16[1024,1024]{1,0:T(8,128)(2,1)S(1)} %get-tuple-element.44.left_ref, bf16[512,512]{1,0:T(8,128)(2,1)S(1)} %get-tuple-element.45.right_ref, ...), custom_call_target="tpu_custom_call" | custom-call | flops 200000000 | bytes 1000000 | tf_op jit(solution)/shard_map/term_rows/pallas_call | solution.py:150
  10.2 1.4 %collective-permute-start.1 = (f32[512,512]{1,0:T(8,128)S(1)}, f32[512,512]{1,0:T(8,128)S(1)}, u32[]{:S(2)}, u32[]{:S(2)}) collective-permute-start(f32[512,512]{1,0:T(8,128)S(1)} %get-tuple-element.51.a_ref), channel_id=1, source_target_pairs={{0,1},{4,5},{8,9},{12,13},{2,3},{6,7},{10,11},{14,15},{16,17},{20,... | collective-permute-start | bytes 3145736 | tf_op jit(solution)/shard_map/ppermute | solution.py:305
  11.7 1.3 %collective-permute-start.2 = (f32[512,512]{1,0:T(8,128)S(1)}, f32[512,512]{1,0:T(8,128)S(1)}, u32[]{:S(2)}, u32[]{:S(2)}) collective-permute-start(f32[512,512]{1,0:T(8,128)S(1)} %get-tuple-element.59), channel_id=1, source_target_pairs={{1,2},{5,6},{9,10},{13,14},{3,0},{7,4},{11,8},{17,18},{21,22},{25,... | collective-permute-start | bytes 3145736 | tf_op jit(solution)/shard_map/ppermute | solution.py:317
  13.0 2.8 %opening_rows.3 = (f32[512,512]{1,0:T(8,128)S(1)}, f32[8,128]{1,0:T(8,128)S(1)}, bf16[1024,1024]{1,0:T(8,128)(2,1)S(1)}, bf16[512,512]{1,0:T(8,128)(2,1)S(1)}) custom-call(s32[7]{0:T(128)S(1)} %stack.19.info_ref, bf16[1024,512]{1,0:T(8,128)(2,1)S(1)} %get-tuple-element.42.live_ref, bf16[1,4,1024,1024]{3,2,1,0:T(8,128)(2,1)} %refs_0_.3, ...), custom_call_target="tpu_custom_call" | custom-call | flops 200000000 | bytes 1000000 | tf_op jit(solution)/shard_map/opening_rows/pallas_call | solution.py:95
  15.9 0.7 collective-permute-start.8
  16.8 1.3 %collective-permute-start.7 = (f32[512,512]{1,0:T(8,128)S(1)}, f32[512,512]{1,0:T(8,128)S(1)}, u32[]{:S(2)}, u32[]{:S(2)}) collective-permute-start(f32[512,512]{1,0:T(8,128)S(1)} %get-tuple-element.66), channel_id=1, source_target_pairs={{1,2},{5,6},{9,10},{13,14},{3,0},{7,4},{11,8},{17,18},{21,22},{25,... | collective-permute-start | bytes 3145736 | tf_op jit(solution)/shard_map/ppermute | solution.py:317
  18.1 2.2 %term_rows.7 = (f32[512,512]{1,0:T(8,128)S(1)}, f32[8,128]{1,0:T(8,128)S(1)}, bf16[1024,1024]{1,0:T(8,128)(2,1)S(1)}, bf16[512,512]{1,0:T(8,128)(2,1)S(1)}) custom-call(s32[7]{0:T(128)S(1)} %stack.19.info_ref, bf16[1024,512]{1,0:T(8,128)(2,1)S(1)} %get-tuple-element.42.live_ref, bf16[1024,1024]{1,0:T(8,128)(2,1)S(1)} %get-tuple-element.49.left_ref, ...), custom_call_target="tpu_custom_call" | custom-call | flops 200000000 | bytes 1000000 | tf_op jit(solution)/shard_map/term_rows/pallas_call | solution.py:150
  20.2 2.2 %term_rows.8 = (f32[512,512]{1,0:T(8,128)S(1)}, f32[8,128]{1,0:T(8,128)S(1)}, bf16[1024,1024]{1,0:T(8,128)(2,1)S(1)}, bf16[512,512]{1,0:T(8,128)(2,1)S(1)}) custom-call(s32[7]{0:T(128)S(1)} %stack.19.info_ref, bf16[1024,512]{1,0:T(8,128)(2,1)S(1)} %get-tuple-element.42.live_ref, bf16[1024,1024]{1,0:T(8,128)(2,1)S(1)} %get-tuple-element.54.left_ref, ...), custom_call_target="tpu_custom_call" | custom-call | flops 200000000 | bytes 1000000 | tf_op jit(solution)/shard_map/term_rows/pallas_call | solution.py:150
  22.4 3.8 %collective-permute-start.6 = (f32[512,512]{1,0:T(8,128)S(1)}, f32[512,512]{1,0:T(8,128)S(1)}, u32[]{:S(2)}, u32[]{:S(2)}) collective-permute-start(f32[512,512]{1,0:T(8,128)S(1)} %get-tuple-element.65), channel_id=1, source_target_pairs={{0,1},{4,5},{8,9},{12,13},{1,0},{5,4},{9,8},{13,12},{2,3},{6,7},{1... | collective-permute-start | bytes 3145736 | tf_op jit(solution)/shard_map/ppermute | solution.py:305
  26.3 1.6 %collective-permute-done.2.refs_0_ = f32[512,512]{1,0:T(8,128)S(1)} collective-permute-done((f32[512,512]{1,0:T(8,128)S(1)}, f32[512,512]{1,0:T(8,128)S(1)}, u32[]{:S(2)}, u32[]{:S(2)}) %collective-permute-start.2) | collective-permute-done | bytes 1048608 | tf_op jit(solution)/shard_map/ppermute | solution.py:317
  27.8 4.4 %collective-permute-start.5 = (f32[512,512]{1,0:T(8,128)S(1)}, f32[512,512]{1,0:T(8,128)S(1)}, u32[]{:S(2)}, u32[]{:S(2)}) collective-permute-start(f32[512,512]{1,0:T(8,128)S(1)} %get-tuple-element.64.a_ref), channel_id=1, source_target_pairs={{0,4},{4,8},{8,12},{16,20},{20,24},{24,28}} | collective-permute-start | bytes 3145736 | tf_op jit(solution)/shard_map/ppermute | solution.py:305
  32.2 0.7 collective-permute-start.4
  33.0 1.5 %term_rows.9 = (f32[512,512]{1,0:T(8,128)S(1)}, f32[8,128]{1,0:T(8,128)S(1)}) custom-call(s32[7]{0:T(128)S(1)} %stack.19.info_ref, bf16[1024,512]{1,0:T(8,128)(2,1)S(1)} %get-tuple-element.42.live_ref, bf16[1024,1024]{1,0:T(8,128)(2,1)S(1)} %get-tuple-element.54.left_ref, bf16[512,512]{1,0:T(8,128)(2,1)S(1)} %get-tuple-element.55.right_ref, ...), custom_call_target="tpu_custom_call" | custom-call | flops 200000000 | bytes 1000000 | tf_op jit(solution)/shard_map/term_rows/pallas_call | solution.py:150
  35.4 3.7 %collective-permute-done.7.refs_0_ = f32[512,512]{1,0:T(8,128)S(1)} collective-permute-done((f32[512,512]{1,0:T(8,128)S(1)}, f32[512,512]{1,0:T(8,128)S(1)}, u32[]{:S(2)}, u32[]{:S(2)}) %collective-permute-start.7) | collective-permute-done | bytes 1048608 | tf_op jit(solution)/shard_map/ppermute | solution.py:317
  39.1 4.4 %collective-permute-start.10 = (f32[512,512]{1,0:T(8,128)S(1)}, f32[512,512]{1,0:T(8,128)S(1)}, u32[]{:S(2)}, u32[]{:S(2)}) collective-permute-start(f32[512,512]{1,0:T(8,128)S(1)} %get-tuple-element.77.a_ref), channel_id=1, source_target_pairs={{0,4},{4,8},{8,12},{16,20},{20,24},{24,28}} | collective-permute-start | bytes 3145736 | tf_op jit(solution)/shard_map/ppermute | solution.py:305
  43.5 1.5 %term_rows.10 = (f32[512,512]{1,0:T(8,128)S(1)}, f32[8,128]{1,0:T(8,128)S(1)}) custom-call(s32[7]{0:T(128)S(1)} %stack.19.info_ref, bf16[1024,512]{1,0:T(8,128)(2,1)S(1)} %get-tuple-element.42.live_ref, bf16[1024,1024]{1,0:T(8,128)(2,1)S(1)} %get-tuple-element.57.left_ref, bf16[512,512]{1,0:T(8,128)(2,1)S(1)} %get-tuple-element.58.right_ref, ...), custom_call_target="tpu_custom_call" | custom-call | flops 200000000 | bytes 1000000 | tf_op jit(solution)/shard_map/term_rows/pallas_call | solution.py:150
  45.9 1.5 %finish_rows.2 = (bf16[1,1024,512]{2,1,0:T(8,128)(2,1)}, f32[16,128]{1,0:T(8,128)S(1)}) custom-call(s32[7]{0:T(128)S(1)} %stack.19.info_ref, bf16[1024,512]{1,0:T(8,128)(2,1)S(1)} %get-tuple-element.42.live_ref, f32[512,512]{1,0:T(8,128)S(1)} %get-tuple-element.73.own_ref, f32[512,512]{1,0:T(8,128)S(1)} %get-tuple-element.64.a_ref, ...), custom_call_target="tpu_custom_call" | custom-call | flops 200000000 | bytes 1000000 | tf_op jit(solution)/shard_map/finish_rows/pallas_call | solution.py:259
  47.5 1.5 %term_rows.11 = (f32[512,512]{1,0:T(8,128)S(1)}, f32[8,128]{1,0:T(8,128)}) custom-call(s32[7]{0:T(128)S(1)} %stack.19.info_ref, bf16[1024,512]{1,0:T(8,128)(2,1)S(1)} %get-tuple-element.42.live_ref, bf16[1024,1024]{1,0:T(8,128)(2,1)S(1)} %get-tuple-element.57.left_ref, bf16[512,512]{1,0:T(8,128)(2,1)S(1)} %get-tuple-element.58.right_ref, ...), custom_call_target="tpu_custom_call" | custom-call | flops 200000000 | bytes 1000000 | tf_op jit(solution)/shard_map/term_rows/pallas_call | solution.py:150
  49.0 6.7 %collective-permute-done.10.b_ref = f32[512,512]{1,0:T(8,128)S(1)} collective-permute-done((f32[512,512]{1,0:T(8,128)S(1)}, f32[512,512]{1,0:T(8,128)S(1)}, u32[]{:S(2)}, u32[]{:S(2)}) %collective-permute-start.10) | collective-permute-done | bytes 1048608 | tf_op jit(solution)/shard_map/ppermute | solution.py:305
  55.7 1.5 %finish_rows.3 = (bf16[1,1024,512]{2,1,0:T(8,128)(2,1)}, f32[16,128]{1,0:T(8,128)S(1)}) custom-call(s32[7]{0:T(128)S(1)} %stack.19.info_ref, bf16[1024,512]{1,0:T(8,128)(2,1)S(1)} %get-tuple-element.42.live_ref, f32[512,512]{1,0:T(8,128)S(1)} %get-tuple-element.76.own_ref, f32[512,512]{1,0:T(8,128)S(1)} %get-tuple-element.77.a_ref, ...), custom_call_target="tpu_custom_call", output_to_operand_aliasing={{0}: (7, {})} | custom-call | flops 200000000 | bytes 1000000 | tf_op jit(solution)/shard_map/finish_rows/pallas_call | solution.py:259
  57.3 18.2 %all_to_all.11 = f32[16,1,128]{2,1,0:T(1,128)S(1)} all-to-all(f32[16,1,128]{2,1,0:T(1,128)S(1)} %bitcast.10), channel_id=1, replica_groups=mesh['grp'=2,'sec'=16] {'sec'}, dimensions={0} | all-to-all | bytes 16384 | tf_op jit(solution)/shard_map/all_to_all | solution.py:280
  (25 shorter events, 2.8 us)
Async XLA Ops:
  2.0 1.2 %copy-start.1 = (bf16[1,1024,512]{2,1,0:T(8,128)(2,1)S(1)}, bf16[1,1024,512]{2,1,0:T(8,128)(2,1)}, u32[]{:S(2)}) copy-start(bf16[1,1024,512]{2,1,0:T(8,128)(2,1)} %param.5) | copy-start | bytes 3145732
  6.2 5.3 %collective-permute-start = (f32[512,512]{1,0:T(8,128)S(1)}, f32[512,512]{1,0:T(8,128)S(1)}, u32[]{:S(2)}, u32[]{:S(2)}) collective-permute-start(f32[512,512]{1,0:T(8,128)S(1)} %get-tuple-element.43.a_ref), channel_id=1, source_target_pairs={{0,1},{4,5},{8,9},{12,13},{2,3},{6,7},{10,11},{14,15},{16,17},{20,... | collective-permute-start | bytes 3145736 | tf_op jit(solution)/shard_map/ppermute | solution.py:305
  8.7 4.4 %copy-start = (bf16[1,4,512,512]{3,2,1,0:T(8,128)(2,1)S(1)}, bf16[1,4,512,512]{3,2,1,0:T(8,128)(2,1)}, u32[]{:S(2)}) copy-start(bf16[1,4,512,512]{3,2,1,0:T(8,128)(2,1)} %refs_1_.3) | copy-start | bytes 6291460
  10.2 6.4 %collective-permute-start.1 = (f32[512,512]{1,0:T(8,128)S(1)}, f32[512,512]{1,0:T(8,128)S(1)}, u32[]{:S(2)}, u32[]{:S(2)}) collective-permute-start(f32[512,512]{1,0:T(8,128)S(1)} %get-tuple-element.51.a_ref), channel_id=1, source_target_pairs={{0,1},{4,5},{8,9},{12,13},{2,3},{6,7},{10,11},{14,15},{16,17},{20,... | collective-permute-start | bytes 3145736 | tf_op jit(solution)/shard_map/ppermute | solution.py:305
  11.7 16.1 %collective-permute-start.2 = (f32[512,512]{1,0:T(8,128)S(1)}, f32[512,512]{1,0:T(8,128)S(1)}, u32[]{:S(2)}, u32[]{:S(2)}) collective-permute-start(f32[512,512]{1,0:T(8,128)S(1)} %get-tuple-element.59), channel_id=1, source_target_pairs={{1,2},{5,6},{9,10},{13,14},{3,0},{7,4},{11,8},{17,18},{21,22},{25,... | collective-permute-start | bytes 3145736 | tf_op jit(solution)/shard_map/ppermute | solution.py:317
  15.9 18.6 %collective-permute-start.8 = (f32[512,512]{1,0:T(8,128)S(1)}, f32[512,512]{1,0:T(8,128)S(1)}, u32[]{:S(2)}, u32[]{:S(2)}) collective-permute-start(f32[512,512]{1,0:T(8,128)S(1)} %get-tuple-element.67.a_ref), channel_id=1, source_target_pairs={{3,6},{7,10},{11,14},{4,1},{8,5},{12,9},{19,22},{23,26},{27,30},{2... | collective-permute-start | bytes 3145736 | tf_op jit(solution)/shard_map/ppermute | solution.py:305
  16.8 22.3 %collective-permute-start.7 = (f32[512,512]{1,0:T(8,128)S(1)}, f32[512,512]{1,0:T(8,128)S(1)}, u32[]{:S(2)}, u32[]{:S(2)}) collective-permute-start(f32[512,512]{1,0:T(8,128)S(1)} %get-tuple-element.66), channel_id=1, source_target_pairs={{1,2},{5,6},{9,10},{13,14},{3,0},{7,4},{11,8},{17,18},{21,22},{25,... | collective-permute-start | bytes 3145736 | tf_op jit(solution)/shard_map/ppermute | solution.py:317
  22.4 16.7 %collective-permute-start.6 = (f32[512,512]{1,0:T(8,128)S(1)}, f32[512,512]{1,0:T(8,128)S(1)}, u32[]{:S(2)}, u32[]{:S(2)}) collective-permute-start(f32[512,512]{1,0:T(8,128)S(1)} %get-tuple-element.65), channel_id=1, source_target_pairs={{0,1},{4,5},{8,9},{12,13},{1,0},{5,4},{9,8},{13,12},{2,3},{6,7},{1... | collective-permute-start | bytes 3145736 | tf_op jit(solution)/shard_map/ppermute | solution.py:305
  27.8 17.1 %collective-permute-start.5 = (f32[512,512]{1,0:T(8,128)S(1)}, f32[512,512]{1,0:T(8,128)S(1)}, u32[]{:S(2)}, u32[]{:S(2)}) collective-permute-start(f32[512,512]{1,0:T(8,128)S(1)} %get-tuple-element.64.a_ref), channel_id=1, source_target_pairs={{0,4},{4,8},{8,12},{16,20},{20,24},{24,28}} | collective-permute-start | bytes 3145736 | tf_op jit(solution)/shard_map/ppermute | solution.py:305
  32.2 12.8 %collective-permute-start.4 = (f32[512,512]{1,0:T(8,128)S(1)}, f32[512,512]{1,0:T(8,128)S(1)}, u32[]{:S(2)}, u32[]{:S(2)}) collective-permute-start(f32[512,512]{1,0:T(8,128)S(1)} %get-tuple-element.63.a_ref), channel_id=1, source_target_pairs={{3,6},{7,10},{11,14},{4,1},{8,5},{12,9},{19,22},{23,26},{27,30},{2... | collective-permute-start | bytes 3145736 | tf_op jit(solution)/shard_map/ppermute | solution.py:305
  34.6 11.3 %collective-permute-start.9 = (f32[512,512]{1,0:T(8,128)S(1)}, f32[512,512]{1,0:T(8,128)S(1)}, u32[]{:S(2)}, u32[]{:S(2)}) collective-permute-start(f32[512,512]{1,0:T(8,128)S(1)} %get-tuple-element.74), channel_id=1, source_target_pairs={{1,3},{5,7},{9,11},{13,15},{2,1},{6,5},{10,9},{14,13},{17,19},{21,... | collective-permute-start | bytes 3145736 | tf_op jit(solution)/shard_map/ppermute | solution.py:305
  39.1 8.4 %collective-permute-start.3 = (f32[512,512]{1,0:T(8,128)S(1)}, f32[512,512]{1,0:T(8,128)S(1)}, u32[]{:S(2)}, u32[]{:S(2)}) collective-permute-start(f32[512,512]{1,0:T(8,128)S(1)} %get-tuple-element.62), channel_id=1, source_target_pairs={{0,1},{4,5},{8,9},{12,13},{1,0},{5,4},{9,8},{13,12},{2,3},{6,7},{1... | collective-permute-start | bytes 3145736 | tf_op jit(solution)/shard_map/ppermute | solution.py:305
  39.1 16.6 %collective-permute-start.10 = (f32[512,512]{1,0:T(8,128)S(1)}, f32[512,512]{1,0:T(8,128)S(1)}, u32[]{:S(2)}, u32[]{:S(2)}) collective-permute-start(f32[512,512]{1,0:T(8,128)S(1)} %get-tuple-element.77.a_ref), channel_id=1, source_target_pairs={{0,4},{4,8},{8,12},{16,20},{20,24},{24,28}} | collective-permute-start | bytes 3145736 | tf_op jit(solution)/shard_map/ppermute | solution.py:305
  45.2 10.5 %collective-permute-start.11 = (f32[512,512]{1,0:T(8,128)S(1)}, f32[512,512]{1,0:T(8,128)S(1)}, u32[]{:S(2)}, u32[]{:S(2)}) collective-permute-start(f32[512,512]{1,0:T(8,128)S(1)} %get-tuple-element.78), channel_id=1, source_target_pairs={{1,3},{5,7},{9,11},{13,15},{2,1},{6,5},{10,9},{14,13},{17,19},{21,... | collective-permute-start | bytes 3145736 | tf_op jit(solution)/shard_map/ppermute | solution.py:305

commit v10 on v9

--- a/solution.py
+++ b/solution.py
@@ -8,7 +8,8 @@
 from jax.sharding import PartitionSpec as P
 
 MIB = 1024 * 1024
-LEFT_PIECES, RIGHT_PIECES = 8, 2
+LEFT_PIECES, RIGHT_PIECES = 4, 2
+PRE_MIB = 48
 FIRST_MIB = 48
 BRING_MIB = 42
 
@@ -24,44 +25,77 @@
     return pltpu.CompilerParams(vmem_limit_bytes=mib * MIB)
 
 
-def fetch(info_ref, slot, left_hbm, right_hbm, left_ref, right_ref, sems):
+def fetch(info_ref, bring, left_hbm, right_hbm, left_ref, right_ref, sems):
+    slot, half, _ = bring
     term = info_ref[slot]
-    rows, cols = left_ref.shape[0], right_ref.shape[0]
+    rows = left_ref.shape[0]
     step = rows // LEFT_PIECES
-    left, right = [], []
+    copies = []
     for i in range(LEFT_PIECES):
-        span = pl.ds(i * step, step)
-        left.append(
-            pltpu.make_async_copy(left_hbm.at[0, term, span, :], left_ref.at[span, :], sems.at[i])
-        )
-    step = cols // RIGHT_PIECES
-    for i in range(RIGHT_PIECES):
-        span = pl.ds(i * step, step)
-        right.append(
-            pltpu.make_async_copy(
-                right_hbm.at[0, term, span, :], right_ref.at[span, :], sems.at[LEFT_PIECES + i]
+        there = left_hbm.at[0, term, pl.ds(half * rows + i * step, step), :]
+        here = left_ref.at[pl.ds(i * step, step), :]
+        copies.append(pltpu.make_async_copy(there, here, sems.at[i]))
+    if right_ref is not None:
+        step = right_ref.shape[0] // RIGHT_PIECES
+        for i in range(RIGHT_PIECES):
+            span = pl.ds(i * step, step)
+            there = right_hbm.at[0, term, span, :]
+            copies.append(
+                pltpu.make_async_copy(there, right_ref.at[span, :], sems.at[LEFT_PIECES + i])
             )
-        )
-    half = LEFT_PIECES // 2
-    return left[:half] + right, left[half:]
-
-
-def multiply(left, live, right):
-    first = jnp.dot(left, live, preferred_element_type=jnp.float32).astype(jnp.bfloat16)
-    return jnp.dot(first, right, preferred_element_type=jnp.float32)
-
-
-def opening_kernel(slot, masks, tokens, info_ref, live_ref, left_hbm, right_hbm, *refs):
-    refs = list(refs[tokens:])
+    return copies
+
+
+def bring_kernel(bring, info_ref, left_hbm, left_ref, _, sems):
+    copies = fetch(info_ref, bring, left_hbm, None, left_ref, None, sems)
+    for copy in copies:
+        copy.start()
+    for copy in copies:
+        copy.wait()
+
+
+def operand_shapes(width, cols, bring):
+    left = jax.ShapeDtypeStruct((width // 2, width), jnp.bfloat16)
+    right = jax.ShapeDtypeStruct((cols, cols), jnp.bfloat16)
+    return [left, right] if bring[2] else [left]
+
+
+def bring_left(info, left_env, bring):
+    return pl.pallas_call(
+        functools.partial(bring_kernel, bring),
+        out_shape=[*operand_shapes(left_env.shape[-1], 0, bring), TOKEN],
+        in_specs=[SMEM, HBM],
+        out_specs=[WHOLE, ANY],
+        scratch_shapes=[pltpu.SemaphoreType.DMA((LEFT_PIECES,))],
+        compiler_params=params(PRE_MIB),
+        cost_estimate=SMALL,
+        name="bring_left",
+    )(info, left_env)
+
+
+def term_kernel(masks, adds, bring, tokens, info_ref, live_ref, left_ref, *refs):
+    refs = list(refs)
+    right_ref = None if masks else refs.pop(0)
+    add_ref = refs.pop(0) if adds else None
+    copies, right_copies = [], []
+    if bring is not None:
+        left_hbm, right_hbm = refs[:2]
+        refs = refs[2:]
+        sems = refs.pop()
+    refs = refs[tokens:]
     out_ref, _ = refs[:2]
-    sems = refs[-1]
-    operands = refs[2:-1]
+    refs = refs[2:]
     psi_ref = live_ref
     if masks:
-        live_ref = operands.pop(0)
-    own, late = fetch(info_ref, slot, left_hbm, right_hbm, *operands, sems)
-    for copy in own + late:
-        copy.start()
+        live_ref = refs.pop(0)
+    if bring is not None:
+        right_next = refs[1] if bring[2] else None
+        copies = fetch(info_ref, bring, left_hbm, right_hbm, refs[0], right_next, sems)
+        if masks:
+            right_ref = right_next
+            copies, right_copies = copies[:LEFT_PIECES], copies[LEFT_PIECES:]
+        for copy in right_copies + copies:
+            copy.start()
     if masks:
         rows, cols = psi_ref.shape
         step = 128
@@ -72,88 +106,43 @@
             inside = jnp.logical_and(row < info_ref[4] - start, col)
             values = jnp.where(inside, psi_ref[span, :].astype(jnp.float32), 0.0)
             live_ref[span, :] = values.astype(live_ref.dtype)
-    for copy in own:
+    value = jnp.dot(left_ref[...], live_ref[...], preferred_element_type=jnp.float32)
+    for copy in right_copies:
         copy.wait()
-    out_ref[...] = multiply(operands[0][: out_ref.shape[0], :], live_ref[...], operands[1][...])
-    for copy in late:
-        copy.wait()
-
-
-def operand_shapes(width, cols):
-    return [
-        jax.ShapeDtypeStruct((width, width), jnp.bfloat16),
-        jax.ShapeDtypeStruct((cols, cols), jnp.bfloat16),
-    ]
-
-
-def opening_rows(info, live, envs, slot, count, *tokens, masks=False):
-    width, cols = live.shape
-    out_shape = [jax.ShapeDtypeStruct((count, cols), jnp.float32), TOKEN]
-    if masks:
-        out_shape.append(jax.ShapeDtypeStruct(live.shape, live.dtype))
-    out_shape += operand_shapes(width, cols)
-    return pl.pallas_call(
-        functools.partial(opening_kernel, slot, masks, len(tokens)),
-        out_shape=out_shape,
-        in_specs=[SMEM, WHOLE, HBM, HBM] + [ANY] * len(tokens),
-        out_specs=[WHOLE, ANY] + [WHOLE] * (len(out_shape) - 2),
-        scratch_shapes=[pltpu.SemaphoreType.DMA((LEFT_PIECES + RIGHT_PIECES,))],
-        compiler_params=params(FIRST_MIB if masks else BRING_MIB),
-        cost_estimate=SMALL,
-        name="opening_rows",
-    )(info, live, *envs, *tokens)
-
-
-def term_kernel(first, adds, slot, tokens, info_ref, live_ref, left_ref, right_ref, *refs):
-    refs = list(refs)
-    add_ref = refs.pop(0) if adds else None
-    copies = []
-    if slot is not None:
-        left_hbm, right_hbm = refs[:2]
-        sems = refs[-1]
-        out_ref, _, left_next, right_next = refs[2 + tokens : -1]
-        copies = sum(fetch(info_ref, slot, left_hbm, right_hbm, left_next, right_next, sems), [])
-        for copy in copies:
-            copy.start()
-    else:
-        out_ref, _ = refs[tokens:]
-    count = out_ref.shape[0]
-    block = min(count, 512)
-    for i in range(count // block):
-        span = pl.ds(i * block, block)
-        value = multiply(left_ref[pl.ds(first + i * block, block), :], live_ref[...], right_ref[...])
-        if adds:
-            value = value + add_ref[span, :]
-        out_ref[span, :] = value
+    value = jnp.dot(
+        value.astype(jnp.bfloat16), right_ref[...], preferred_element_type=jnp.float32
+    )
+    out_ref[...] = value + add_ref[...] if adds else value
     for copy in copies:
         copy.wait()
 
 
-def term_rows(info, live, operands, first, count, *tokens, added=None, bring=None):
+def term_rows(info, live, envs, left, right, *tokens, added=None, bring=None, masks=False):
     width, cols = live.shape
-    in_specs = [SMEM, WHOLE, WHOLE, WHOLE]
-    args = [info, live, *operands]
-    out_shape = [jax.ShapeDtypeStruct((count, cols), jnp.float32), TOKEN]
-    out_specs = [WHOLE, ANY]
+    in_specs = [SMEM, WHOLE, WHOLE]
+    args = [info, live, left]
+    if not masks:
+        in_specs.append(WHOLE)
+        args.append(right)
+    out_shape = [jax.ShapeDtypeStruct((left.shape[0], cols), jnp.float32), TOKEN]
     scratch = []
-    slot = None
     if added is not None:
         in_specs.append(WHOLE)
         args.append(added)
+    if masks:
+        out_shape.append(jax.ShapeDtypeStruct(live.shape, live.dtype))
     if bring is not None:
-        slot = bring[0]
         in_specs += [HBM, HBM]
-        args += bring[1:]
-        out_shape += operand_shapes(width, cols)
-        out_specs += [WHOLE, WHOLE]
+        args += envs
+        out_shape += operand_shapes(width, cols, bring)
         scratch.append(pltpu.SemaphoreType.DMA((LEFT_PIECES + RIGHT_PIECES,)))
     return pl.pallas_call(
-        functools.partial(term_kernel, first, added is not None, slot, len(tokens)),
+        functools.partial(term_kernel, masks, added is not None, bring, len(tokens)),
         out_shape=out_shape,
         in_specs=in_specs + [ANY] * len(tokens),
-        out_specs=out_specs,
+        out_specs=[WHOLE, ANY] + [WHOLE] * (len(out_shape) - 2),
         scratch_shapes=scratch,
-        compiler_params=params(12 if slot is None else BRING_MIB),
+        compiler_params=params(12 if bring is None else FIRST_MIB if masks else BRING_MIB),
         cost_estimate=SMALL,
         name="term_rows",
     )(*args, *tokens)
@@ -332,36 +321,43 @@
         return send(value, (0, 4))
 
     envs = (left_env, right_env)
-    first0, token, live, *ops0 = opening_rows(info, psi[0], envs, 0, part, masks=True)
+
+    def term(left, right, *tokens, **more):
+        return term_rows(info, live, envs, left, right, *tokens, **more)
+
+    left, token = bring_left(info, left_env, (0, 0, False))
+    first0, token, live, left, right = term_rows(
+        info, psi[0], envs, left, None, token, bring=(0, 1, True), masks=True
+    )
     paired0 = up_chip(first0)
-    first1, token = term_rows(info, live, ops0, part, part, token)
+    first1, token, left, right = term(left, right, token, bring=(1, 0, True))
     paired1 = up_chip(first1)
     both0, token = add(first0, paired0, token)
     raised0 = raise_one(both0)
-    second0, token, *ops1 = opening_rows(info, live, envs, 1, part, token)
+    second0, token, left = term(left, right, token, bring=(1, 1, False))
     moved0 = along(second0)
     both1, token = add(first1, paired1, token)
     raised1 = raise_one(both1)
-    second1, token, *ops2 = term_rows(info, live, ops1, part, part, token, bring=(2, *envs))
+    second1, token, left, right = term(left, right, token, bring=(2, 0, True))
     moved1 = along(second1)
-    third0, token, *ops3 = term_rows(info, live, ops2, 0, part, token, bring=(3, *envs))
+    third0, token, left = term(left, right, token, bring=(2, 1, False))
     swapped0 = swap(third0)
     raised0, token = hold(raised0, token)
     relayed0 = relay(raised0)
-    third1, token = term_rows(info, live, ops2, part, part, token)
+    third1, token, left, right = term(left, right, token, bring=(3, 0, True))
     swapped1 = swap(third1)
     summed0, token = add(second0, moved0, token)
     crossed0 = across(summed0)
     raised1, token = hold(raised1, token)
     relayed1 = relay(raised1)
-    own0, token = term_rows(info, live, ops3, 0, part, token, added=swapped0)
+    own0, token, left = term(left, right, token, added=swapped0, bring=(3, 1, False))
     token = touch(relayed0, token)
     summed1, token = add(second1, moved1, token)
     crossed1 = across(summed1)
 
     energy = jnp.zeros((sectors, 128), jnp.float32)
     sigma, energy = finish(info, live, own0, (raised0, relayed0, crossed0), energy, None, 0)
-    own1, token = term_rows(info, live, ops3, part, part, token, energy, added=swapped1)
+    own1, token = term(left, right, token, energy, added=swapped1)
     sigma, energy = finish(info, live, own1, (raised1, relayed1, crossed1), energy, sigma, part)
     return sigma, sum_over_sectors(energy)
 

time: 76.6 us -> 77.2 us (level)
  Pallas kernels: 20.5 us -> 22.3 us
  local copies, waits for them, and re-layouts: 1.32 us -> 0.1 us
    pallas_call x8 -> x9, Pallas kernels: 16.2 us -> 17.9 us  [the longest x8 16.2 us: term_rows(): pl.pallas_call(functools.partial(term_kernel, masks, added is not None, b...]
    unnamed x4, local copies, waits for them, and re-layouts: 1.23 us -> 0.01 us
where the time goes in v10:
time: 77.2 us; the launch traced here: 76.7 us
  Pallas kernels  22.3 us (29%)
  starting transfers between devices  21.9 us (28%)
  blocking collectives  18.2 us (24%)
  waiting for transfers between devices  11.9 us (15%)
  between operations  2.32 us (3%)
    ppermute x10, starting transfers between devices, send(): return lax.ppermute(value, 'sec', pairs)  19.3 us
    all_to_all x1, blocking collectives, sum_over_sectors(): arrived = lax.all_to_all(value, 'sec', 0, 0, tiled=True)  18.2 us
    pallas_call x8, Pallas kernels, term_rows(): pl.pallas_call(functools.partial(term_kernel, masks, added is not None, b...  16.2 us
    ppermute x10, waiting for transfers between devices, send(): return lax.ppermute(value, 'sec', pairs)  6.41 us
    ppermute x2, waiting for transfers between devices, raise_one(): return lax.ppermute(value, 'sec', pairs_up)  5.52 us
    pallas_call x2, Pallas kernels, finish(): pl.pallas_call(functools.partial(finish_kernel, first), out_shape=(jax.Sh...  3.1 us
    ppermute x2, starting transfers between devices, raise_one(): return lax.ppermute(value, 'sec', pairs_up)  2.58 us
    pallas_call x1, Pallas kernels, bring_left(): pl.pallas_call(functools.partial(bring_kernel, bring), out_shape=[*operan...  1.77 us
  transfers between devices with their start and end apart: 12, of which 3 were waited for; matrix products, arithmetic and copies ran while one was open for 0% of the time, Pallas kernels for 20%

profile of v10, /device:TPU:0, one launch (start us, length us, event | category | flops | bytes accessed | tf_op | source)
XLA Modules:
  0.0 76.7 jit_solution(2507642188138472769)
XLA Ops:
  2.1 1.8 %bring_left.1 = (bf16[512,1024]{1,0:T(8,128)(2,1)S(1)}, f32[8,128]{1,0:T(8,128)S(1)}) custom-call(s32[7]{0:T(128)S(1)} %stack.19.info_ref, bf16[1,4,1024,1024]{3,2,1,0:T(8,128)(2,1)} %refs_2_.11), custom_call_target="tpu_custom_call" | custom-call | flops 200000000 | bytes 1000000 | tf_op jit(solution)/shard_map/bring_left/pallas_call | solution.py:64
  3.9 2.6 %term_rows.8 = (f32[512,512]{1,0:T(8,128)S(1)}, f32[8,128]{1,0:T(8,128)S(1)}, bf16[1024,512]{1,0:T(8,128)(2,1)S(1)}, bf16[512,1024]{1,0:T(8,128)(2,1)S(1)}, bf16[512,512]{1,0:T(8,128)(2,1)S(1)}) custom-call(s32[7]{0:T(128)S(1)} %stack.19.info_ref, bf16[1024,512]{1,0:T(8,128)(2,1)S(1)} %bitcast.9, bf16[512,1024]{1,0:T(8,128)(2,1)S(1)} %get-tuple-element.47.left_ref, ...), custom_call_target="tpu_custom_call" | custom-call | flops 200000000 | bytes 1000000 | tf_op jit(solution)/shard_map/term_rows/pallas_call | solution.py:139
  6.6 2.4 %collective-permute-start = (f32[512,512]{1,0:T(8,128)S(1)}, f32[512,512]{1,0:T(8,128)S(1)}, u32[]{:S(2)}, u32[]{:S(2)}) collective-permute-start(f32[512,512]{1,0:T(8,128)S(1)} %get-tuple-element.55.a_ref), channel_id=1, source_target_pairs={{0,1},{4,5},{8,9},{12,13},{2,3},{6,7},{10,11},{14,15},{16,17},{20,... | collective-permute-start | bytes 3145736 | tf_op jit(solution)/shard_map/ppermute | solution.py:294
  9.0 1.8 %term_rows.9 = (f32[512,512]{1,0:T(8,128)S(1)}, f32[8,128]{1,0:T(8,128)S(1)}, bf16[512,1024]{1,0:T(8,128)(2,1)S(1)}, bf16[512,512]{1,0:T(8,128)(2,1)S(1)}) custom-call(s32[7]{0:T(128)S(1)} %stack.19.info_ref, bf16[1024,512]{1,0:T(8,128)(2,1)S(1)} %get-tuple-element.49.live_ref, bf16[512,1024]{1,0:T(8,128)(2,1)S(1)} %get-tuple-element.50.left_ref, ...), custom_call_target="tpu_custom_call" | custom-call | flops 200000000 | bytes 1000000 | tf_op jit(solution)/shard_map/term_rows/pallas_call | solution.py:139
  10.8 1.4 %collective-permute-start.1 = (f32[512,512]{1,0:T(8,128)S(1)}, f32[512,512]{1,0:T(8,128)S(1)}, u32[]{:S(2)}, u32[]{:S(2)}) collective-permute-start(f32[512,512]{1,0:T(8,128)S(1)} %get-tuple-element.59.a_ref), channel_id=1, source_target_pairs={{0,1},{4,5},{8,9},{12,13},{2,3},{6,7},{10,11},{14,15},{16,17},{20,... | collective-permute-start | bytes 3145736 | tf_op jit(solution)/shard_map/ppermute | solution.py:294
  12.3 1.3 %collective-permute-start.2 = (f32[512,512]{1,0:T(8,128)S(1)}, f32[512,512]{1,0:T(8,128)S(1)}, u32[]{:S(2)}, u32[]{:S(2)}) collective-permute-start(f32[512,512]{1,0:T(8,128)S(1)} %get-tuple-element.66), channel_id=1, source_target_pairs={{1,2},{5,6},{9,10},{13,14},{3,0},{7,4},{11,8},{17,18},{21,22},{25,... | collective-permute-start | bytes 3145736 | tf_op jit(solution)/shard_map/ppermute | solution.py:306
  13.6 2.4 %term_rows.10 = (f32[512,512]{1,0:T(8,128)S(1)}, f32[8,128]{1,0:T(8,128)S(1)}, bf16[512,1024]{1,0:T(8,128)(2,1)S(1)}) custom-call(s32[7]{0:T(128)S(1)} %stack.19.info_ref, bf16[1024,512]{1,0:T(8,128)(2,1)S(1)} %get-tuple-element.49.live_ref, bf16[512,1024]{1,0:T(8,128)(2,1)S(1)} %get-tuple-element.53.left_ref, ...), custom_call_target="tpu_custom_call" | custom-call | flops 200000000 | bytes 1000000 | tf_op jit(solution)/shard_map/term_rows/pallas_call | solution.py:139
  16.1 0.7 collective-permute-start.5
  17.0 1.3 %collective-permute-start.4 = (f32[512,512]{1,0:T(8,128)S(1)}, f32[512,512]{1,0:T(8,128)S(1)}, u32[]{:S(2)}, u32[]{:S(2)}) collective-permute-start(f32[512,512]{1,0:T(8,128)S(1)} %get-tuple-element.72), channel_id=1, source_target_pairs={{1,2},{5,6},{9,10},{13,14},{3,0},{7,4},{11,8},{17,18},{21,22},{25,... | collective-permute-start | bytes 3145736 | tf_op jit(solution)/shard_map/ppermute | solution.py:306
  18.3 1.8 %term_rows.11 = (f32[512,512]{1,0:T(8,128)S(1)}, f32[8,128]{1,0:T(8,128)S(1)}, bf16[512,1024]{1,0:T(8,128)(2,1)S(1)}, bf16[512,512]{1,0:T(8,128)(2,1)S(1)}) custom-call(s32[7]{0:T(128)S(1)} %stack.19.info_ref, bf16[1024,512]{1,0:T(8,128)(2,1)S(1)} %get-tuple-element.49.live_ref, bf16[512,1024]{1,0:T(8,128)(2,1)S(1)} %get-tuple-element.58.left_ref, ...), custom_call_target="tpu_custom_call" | custom-call | flops 200000000 | bytes 1000000 | tf_op jit(solution)/shard_map/term_rows/pallas_call | solution.py:139
  20.1 2.4 %term_rows.12 = (f32[512,512]{1,0:T(8,128)S(1)}, f32[8,128]{1,0:T(8,128)S(1)}, bf16[512,1024]{1,0:T(8,128)(2,1)S(1)}) custom-call(s32[7]{0:T(128)S(1)} %stack.19.info_ref, bf16[1024,512]{1,0:T(8,128)(2,1)S(1)} %get-tuple-element.49.live_ref, bf16[512,1024]{1,0:T(8,128)(2,1)S(1)} %get-tuple-element.62.left_ref, ...), custom_call_target="tpu_custom_call" | custom-call | flops 200000000 | bytes 1000000 | tf_op jit(solution)/shard_map/term_rows/pallas_call | solution.py:139
  22.5 3.8 %collective-permute-start.3 = (f32[512,512]{1,0:T(8,128)S(1)}, f32[512,512]{1,0:T(8,128)S(1)}, u32[]{:S(2)}, u32[]{:S(2)}) collective-permute-start(f32[512,512]{1,0:T(8,128)S(1)} %get-tuple-element.71), channel_id=1, source_target_pairs={{0,1},{4,5},{8,9},{12,13},{1,0},{5,4},{9,8},{13,12},{2,3},{6,7},{1... | collective-permute-start | bytes 3145736 | tf_op jit(solution)/shard_map/ppermute | solution.py:294
  26.3 2.1 %collective-permute-done.2.refs_0_ = f32[512,512]{1,0:T(8,128)S(1)} collective-permute-done((f32[512,512]{1,0:T(8,128)S(1)}, f32[512,512]{1,0:T(8,128)S(1)}, u32[]{:S(2)}, u32[]{:S(2)}) %collective-permute-start.2) | collective-permute-done | bytes 1048608 | tf_op jit(solution)/shard_map/ppermute | solution.py:306
  28.4 4.4 %collective-permute-start.8 = (f32[512,512]{1,0:T(8,128)S(1)}, f32[512,512]{1,0:T(8,128)S(1)}, u32[]{:S(2)}, u32[]{:S(2)}) collective-permute-start(f32[512,512]{1,0:T(8,128)S(1)} %get-tuple-element.80.a_ref), channel_id=1, source_target_pairs={{0,4},{4,8},{8,12},{16,20},{20,24},{24,28}} | collective-permute-start | bytes 3145736 | tf_op jit(solution)/shard_map/ppermute | solution.py:294
  32.8 0.7 collective-permute-start.7
  33.5 1.8 %term_rows.13 = (f32[512,512]{1,0:T(8,128)S(1)}, f32[8,128]{1,0:T(8,128)S(1)}, bf16[512,1024]{1,0:T(8,128)(2,1)S(1)}, bf16[512,512]{1,0:T(8,128)(2,1)S(1)}) custom-call(s32[7]{0:T(128)S(1)} %stack.19.info_ref, bf16[1024,512]{1,0:T(8,128)(2,1)S(1)} %get-tuple-element.49.live_ref, bf16[512,1024]{1,0:T(8,128)(2,1)S(1)} %get-tuple-element.65.left_ref, ...), custom_call_target="tpu_custom_call" | custom-call | flops 200000000 | bytes 1000000 | tf_op jit(solution)/shard_map/term_rows/pallas_call | solution.py:139
  36.2 3.4 %collective-permute-done.4.refs_0_ = f32[512,512]{1,0:T(8,128)S(1)} collective-permute-done((f32[512,512]{1,0:T(8,128)S(1)}, f32[512,512]{1,0:T(8,128)S(1)}, u32[]{:S(2)}, u32[]{:S(2)}) %collective-permute-start.4) | collective-permute-done | bytes 1048608 | tf_op jit(solution)/shard_map/ppermute | solution.py:306
  39.7 4.4 %collective-permute-start.10 = (f32[512,512]{1,0:T(8,128)S(1)}, f32[512,512]{1,0:T(8,128)S(1)}, u32[]{:S(2)}, u32[]{:S(2)}) collective-permute-start(f32[512,512]{1,0:T(8,128)S(1)} %get-tuple-element.87.a_ref), channel_id=1, source_target_pairs={{0,4},{4,8},{8,12},{16,20},{20,24},{24,28}} | collective-permute-start | bytes 3145736 | tf_op jit(solution)/shard_map/ppermute | solution.py:294
  44.1 1.8 %term_rows.14 = (f32[512,512]{1,0:T(8,128)S(1)}, f32[8,128]{1,0:T(8,128)S(1)}, bf16[512,1024]{1,0:T(8,128)(2,1)S(1)}) custom-call(s32[7]{0:T(128)S(1)} %stack.19.info_ref, bf16[1024,512]{1,0:T(8,128)(2,1)S(1)} %get-tuple-element.49.live_ref, bf16[512,1024]{1,0:T(8,128)(2,1)S(1)} %get-tuple-element.69.left_ref, ...), custom_call_target="tpu_custom_call" | custom-call | flops 200000000 | bytes 1000000 | tf_op jit(solution)/shard_map/term_rows/pallas_call | solution.py:139
  46.8 1.5 %finish_rows.2 = (bf16[1,1024,512]{2,1,0:T(8,128)(2,1)}, f32[16,128]{1,0:T(8,128)S(1)}) custom-call(s32[7]{0:T(128)S(1)} %stack.19.info_ref, bf16[1024,512]{1,0:T(8,128)(2,1)S(1)} %get-tuple-element.49.live_ref, f32[512,512]{1,0:T(8,128)S(1)} %get-tuple-element.83.own_ref, f32[512,512]{1,0:T(8,128)S(1)} %get-tuple-element.80.a_ref, ...), custom_call_target="tpu_custom_call" | custom-call | flops 200000000 | bytes 1000000 | tf_op jit(solution)/shard_map/finish_rows/pallas_call | solution.py:248
  48.4 1.5 %term_rows.15 = (f32[512,512]{1,0:T(8,128)S(1)}, f32[8,128]{1,0:T(8,128)}) custom-call(s32[7]{0:T(128)S(1)} %stack.19.info_ref, bf16[1024,512]{1,0:T(8,128)(2,1)S(1)} %get-tuple-element.49.live_ref, bf16[512,1024]{1,0:T(8,128)(2,1)S(1)} %get-tuple-element.77.left_ref, bf16[512,512]{1,0:T(8,128)(2,1)S(1)} %get-tuple-element.70.refs_0_, ...), custom_call_target="tpu_custom_call" | custom-call | flops 200000000 | bytes 1000000 | tf_op jit(solution)/shard_map/term_rows/pallas_call | solution.py:139
  49.9 6.4 %collective-permute-done.10.b_ref = f32[512,512]{1,0:T(8,128)S(1)} collective-permute-done((f32[512,512]{1,0:T(8,128)S(1)}, f32[512,512]{1,0:T(8,128)S(1)}, u32[]{:S(2)}, u32[]{:S(2)}) %collective-permute-start.10) | collective-permute-done | bytes 1048608 | tf_op jit(solution)/shard_map/ppermute | solution.py:294
  56.3 1.6 %finish_rows.3 = (bf16[1,1024,512]{2,1,0:T(8,128)(2,1)}, f32[16,128]{1,0:T(8,128)S(1)}) custom-call(s32[7]{0:T(128)S(1)} %stack.19.info_ref, bf16[1024,512]{1,0:T(8,128)(2,1)S(1)} %get-tuple-element.49.live_ref, f32[512,512]{1,0:T(8,128)S(1)} %get-tuple-element.86.own_ref, f32[512,512]{1,0:T(8,128)S(1)} %get-tuple-element.87.a_ref, ...), custom_call_target="tpu_custom_call", output_to_operand_aliasing={{0}: (7, {})} | custom-call | flops 200000000 | bytes 1000000 | tf_op jit(solution)/shard_map/finish_rows/pallas_call | solution.py:248
  57.9 18.2 %all_to_all.11 = f32[16,1,128]{2,1,0:T(1,128)S(1)} all-to-all(f32[16,1,128]{2,1,0:T(1,128)S(1)} %bitcast.10), channel_id=1, replica_groups=mesh['grp'=2,'sec'=16] {'sec'}, dimensions={0} | all-to-all | bytes 16384 | tf_op jit(solution)/shard_map/all_to_all | solution.py:269
  (26 shorter events, 2.8 us)
Async XLA Ops:
  0.6 3.3 %copy-start.1 = (bf16[1,1024,512]{2,1,0:T(8,128)(2,1)S(1)}, bf16[1,1024,512]{2,1,0:T(8,128)(2,1)}, u32[]{:S(2)}) copy-start(bf16[1,1024,512]{2,1,0:T(8,128)(2,1)} %param.5) | copy-start | bytes 3145732
  3.9 5.1 %copy-start = (bf16[1,4,512,512]{3,2,1,0:T(8,128)(2,1)S(1)}, bf16[1,4,512,512]{3,2,1,0:T(8,128)(2,1)}, u32[]{:S(2)}) copy-start(bf16[1,4,512,512]{3,2,1,0:T(8,128)(2,1)} %refs_3_.1) | copy-start | bytes 6291460
  6.6 5.6 %collective-permute-start = (f32[512,512]{1,0:T(8,128)S(1)}, f32[512,512]{1,0:T(8,128)S(1)}, u32[]{:S(2)}, u32[]{:S(2)}) collective-permute-start(f32[512,512]{1,0:T(8,128)S(1)} %get-tuple-element.55.a_ref), channel_id=1, source_target_pairs={{0,1},{4,5},{8,9},{12,13},{2,3},{6,7},{10,11},{14,15},{16,17},{20,... | collective-permute-start | bytes 3145736 | tf_op jit(solution)/shard_map/ppermute | solution.py:294
  10.8 6.0 %collective-permute-start.1 = (f32[512,512]{1,0:T(8,128)S(1)}, f32[512,512]{1,0:T(8,128)S(1)}, u32[]{:S(2)}, u32[]{:S(2)}) collective-permute-start(f32[512,512]{1,0:T(8,128)S(1)} %get-tuple-element.59.a_ref), channel_id=1, source_target_pairs={{0,1},{4,5},{8,9},{12,13},{2,3},{6,7},{10,11},{14,15},{16,17},{20,... | collective-permute-start | bytes 3145736 | tf_op jit(solution)/shard_map/ppermute | solution.py:294
  12.3 16.1 %collective-permute-start.2 = (f32[512,512]{1,0:T(8,128)S(1)}, f32[512,512]{1,0:T(8,128)S(1)}, u32[]{:S(2)}, u32[]{:S(2)}) collective-permute-start(f32[512,512]{1,0:T(8,128)S(1)} %get-tuple-element.66), channel_id=1, source_target_pairs={{1,2},{5,6},{9,10},{13,14},{3,0},{7,4},{11,8},{17,18},{21,22},{25,... | collective-permute-start | bytes 3145736 | tf_op jit(solution)/shard_map/ppermute | solution.py:306
  16.1 19.3 %collective-permute-start.5 = (f32[512,512]{1,0:T(8,128)S(1)}, f32[512,512]{1,0:T(8,128)S(1)}, u32[]{:S(2)}, u32[]{:S(2)}) collective-permute-start(f32[512,512]{1,0:T(8,128)S(1)} %get-tuple-element.73.a_ref), channel_id=1, source_target_pairs={{3,6},{7,10},{11,14},{4,1},{8,5},{12,9},{19,22},{23,26},{27,30},{2... | collective-permute-start | bytes 3145736 | tf_op jit(solution)/shard_map/ppermute | solution.py:294
  17.0 22.7 %collective-permute-start.4 = (f32[512,512]{1,0:T(8,128)S(1)}, f32[512,512]{1,0:T(8,128)S(1)}, u32[]{:S(2)}, u32[]{:S(2)}) collective-permute-start(f32[512,512]{1,0:T(8,128)S(1)} %get-tuple-element.72), channel_id=1, source_target_pairs={{1,2},{5,6},{9,10},{13,14},{3,0},{7,4},{11,8},{17,18},{21,22},{25,... | collective-permute-start | bytes 3145736 | tf_op jit(solution)/shard_map/ppermute | solution.py:306
  22.5 17.2 %collective-permute-start.3 = (f32[512,512]{1,0:T(8,128)S(1)}, f32[512,512]{1,0:T(8,128)S(1)}, u32[]{:S(2)}, u32[]{:S(2)}) collective-permute-start(f32[512,512]{1,0:T(8,128)S(1)} %get-tuple-element.71), channel_id=1, source_target_pairs={{0,1},{4,5},{8,9},{12,13},{1,0},{5,4},{9,8},{13,12},{2,3},{6,7},{1... | collective-permute-start | bytes 3145736 | tf_op jit(solution)/shard_map/ppermute | solution.py:294
  28.4 17.4 %collective-permute-start.8 = (f32[512,512]{1,0:T(8,128)S(1)}, f32[512,512]{1,0:T(8,128)S(1)}, u32[]{:S(2)}, u32[]{:S(2)}) collective-permute-start(f32[512,512]{1,0:T(8,128)S(1)} %get-tuple-element.80.a_ref), channel_id=1, source_target_pairs={{0,4},{4,8},{8,12},{16,20},{20,24},{24,28}} | collective-permute-start | bytes 3145736 | tf_op jit(solution)/shard_map/ppermute | solution.py:294
  32.8 13.1 %collective-permute-start.7 = (f32[512,512]{1,0:T(8,128)S(1)}, f32[512,512]{1,0:T(8,128)S(1)}, u32[]{:S(2)}, u32[]{:S(2)}) collective-permute-start(f32[512,512]{1,0:T(8,128)S(1)} %get-tuple-element.79.a_ref), channel_id=1, source_target_pairs={{3,6},{7,10},{11,14},{4,1},{8,5},{12,9},{19,22},{23,26},{27,30},{2... | collective-permute-start | bytes 3145736 | tf_op jit(solution)/shard_map/ppermute | solution.py:294
  35.5 11.3 %collective-permute-start.9 = (f32[512,512]{1,0:T(8,128)S(1)}, f32[512,512]{1,0:T(8,128)S(1)}, u32[]{:S(2)}, u32[]{:S(2)}) collective-permute-start(f32[512,512]{1,0:T(8,128)S(1)} %get-tuple-element.84), channel_id=1, source_target_pairs={{1,3},{5,7},{9,11},{13,15},{2,1},{6,5},{10,9},{14,13},{17,19},{21,... | collective-permute-start | bytes 3145736 | tf_op jit(solution)/shard_map/ppermute | solution.py:294
  39.7 8.7 %collective-permute-start.6 = (f32[512,512]{1,0:T(8,128)S(1)}, f32[512,512]{1,0:T(8,128)S(1)}, u32[]{:S(2)}, u32[]{:S(2)}) collective-permute-start(f32[512,512]{1,0:T(8,128)S(1)} %get-tuple-element.78), channel_id=1, source_target_pairs={{0,1},{4,5},{8,9},{12,13},{1,0},{5,4},{9,8},{13,12},{2,3},{6,7},{1... | collective-permute-start | bytes 3145736 | tf_op jit(solution)/shard_map/ppermute | solution.py:294
  39.7 16.6 %collective-permute-start.10 = (f32[512,512]{1,0:T(8,128)S(1)}, f32[512,512]{1,0:T(8,128)S(1)}, u32[]{:S(2)}, u32[]{:S(2)}) collective-permute-start(f32[512,512]{1,0:T(8,128)S(1)} %get-tuple-element.87.a_ref), channel_id=1, source_target_pairs={{0,4},{4,8},{8,12},{16,20},{20,24},{24,28}} | collective-permute-start | bytes 3145736 | tf_op jit(solution)/shard_map/ppermute | solution.py:294
  46.1 10.2 %collective-permute-start.11 = (f32[512,512]{1,0:T(8,128)S(1)}, f32[512,512]{1,0:T(8,128)S(1)}, u32[]{:S(2)}, u32[]{:S(2)}) collective-permute-start(f32[512,512]{1,0:T(8,128)S(1)} %get-tuple-element.88), channel_id=1, source_target_pairs={{1,3},{5,7},{9,11},{13,15},{2,1},{6,5},{10,9},{14,13},{17,19},{21,... | collective-permute-start | bytes 3145736 | tf_op jit(solution)/shard_map/ppermute | solution.py:294

commit v11 on v9

--- a/solution.py
+++ b/solution.py
@@ -8,8 +8,9 @@
 from jax.sharding import PartitionSpec as P
 
 MIB = 1024 * 1024
+PIECE = 128
 LEFT_PIECES, RIGHT_PIECES = 8, 2
-FIRST_MIB = 48
+FIRST_MIB = 46
 BRING_MIB = 42
 
 ANY = pl.BlockSpec(memory_space=pl.ANY)
@@ -51,14 +52,16 @@
     return jnp.dot(first, right, preferred_element_type=jnp.float32)
 
 
-def opening_kernel(slot, masks, tokens, info_ref, live_ref, left_hbm, right_hbm, *refs):
+def opening_kernel(slot, cut, tokens, info_ref, live_ref, left_hbm, right_hbm, *refs):
+    masks = cut is not None
     refs = list(refs[tokens:])
     out_ref, _ = refs[:2]
     sems = refs[-1]
     operands = refs[2:-1]
     psi_ref = live_ref
     if masks:
-        live_ref = operands.pop(0)
+        live_ref, wide_ref = operands[:2]
+        operands = operands[2:]
     own, late = fetch(info_ref, slot, left_hbm, right_hbm, *operands, sems)
     for copy in own + late:
         copy.start()
@@ -72,6 +75,8 @@
             inside = jnp.logical_and(row < info_ref[4] - start, col)
             values = jnp.where(inside, psi_ref[span, :].astype(jnp.float32), 0.0)
             live_ref[span, :] = values.astype(live_ref.dtype)
+            if start >= cut:
+                wide_ref[pl.ds(start - cut, step), :] = values
     for copy in own:
         copy.wait()
     out_ref[...] = multiply(operands[0][: out_ref.shape[0], :], live_ref[...], operands[1][...])
@@ -86,27 +91,28 @@
     ]
 
 
-def opening_rows(info, live, envs, slot, count, *tokens, masks=False):
+def opening_rows(info, live, envs, slot, count, *tokens, cut=None):
     width, cols = live.shape
     out_shape = [jax.ShapeDtypeStruct((count, cols), jnp.float32), TOKEN]
-    if masks:
+    if cut is not None:
         out_shape.append(jax.ShapeDtypeStruct(live.shape, live.dtype))
+        out_shape.append(jax.ShapeDtypeStruct((width - cut, cols), jnp.float32))
     out_shape += operand_shapes(width, cols)
     return pl.pallas_call(
-        functools.partial(opening_kernel, slot, masks, len(tokens)),
+        functools.partial(opening_kernel, slot, cut, len(tokens)),
         out_shape=out_shape,
         in_specs=[SMEM, WHOLE, HBM, HBM] + [ANY] * len(tokens),
         out_specs=[WHOLE, ANY] + [WHOLE] * (len(out_shape) - 2),
         scratch_shapes=[pltpu.SemaphoreType.DMA((LEFT_PIECES + RIGHT_PIECES,))],
-        compiler_params=params(FIRST_MIB if masks else BRING_MIB),
+        compiler_params=params(BRING_MIB if cut is None else FIRST_MIB),
         cost_estimate=SMALL,
         name="opening_rows",
     )(info, live, *envs, *tokens)
 
 
-def term_kernel(first, adds, slot, tokens, info_ref, live_ref, left_ref, right_ref, *refs):
+def term_kernel(first, parts, slot, tokens, info_ref, live_ref, left_ref, right_ref, *refs):
     refs = list(refs)
-    add_ref = refs.pop(0) if adds else None
+    add_refs = [refs.pop(0) for _ in range(parts)]
     copies = []
     if slot is not None:
         left_hbm, right_hbm = refs[:2]
@@ -118,12 +124,12 @@
     else:
         out_ref, _ = refs[tokens:]
     count = out_ref.shape[0]
-    block = min(count, 512)
+    block = count // max(parts, 1)
     for i in range(count // block):
         span = pl.ds(i * block, block)
         value = multiply(left_ref[pl.ds(first + i * block, block), :], live_ref[...], right_ref[...])
-        if adds:
-            value = value + add_ref[span, :]
+        if parts:
+            value = value + add_refs[i][...]
         out_ref[span, :] = value
     for copy in copies:
         copy.wait()
@@ -138,8 +144,8 @@
     scratch = []
     slot = None
     if added is not None:
-        in_specs.append(WHOLE)
-        args.append(added)
+        in_specs += [WHOLE] * len(added)
+        args += added
     if bring is not None:
         slot = bring[0]
         in_specs += [HBM, HBM]
@@ -148,7 +154,7 @@
         out_specs += [WHOLE, WHOLE]
         scratch.append(pltpu.SemaphoreType.DMA((LEFT_PIECES + RIGHT_PIECES,)))
     return pl.pallas_call(
-        functools.partial(term_kernel, first, added is not None, slot, len(tokens)),
+        functools.partial(term_kernel, first, len(added or ()), slot, len(tokens)),
         out_shape=out_shape,
         in_specs=in_specs + [ANY] * len(tokens),
         out_specs=out_specs,
@@ -182,6 +188,40 @@
         cost_estimate=SMALL,
         name="add_blocks",
     )(a, b, *tokens)
+
+
+def folded(values):
+    rows, cols = values.shape
+    return jnp.sum(jnp.reshape(values, (rows // 8, 8, cols)), axis=0)
+
+
+def add_energy_kernel(a_ref, b_ref, psi_ref, _, out_ref, energy_ref, token_ref):
+    step = 64
+
+    def body(i, energy):
+        span = pl.ds(pl.multiple_of(i * step, step), step)
+        value = a_ref[span, :] + b_ref[span, :]
+        out_ref[span, :] = value
+        return energy + folded(value * psi_ref[span, :])
+
+    zero = jnp.zeros((8, a_ref.shape[1]), jnp.float32)
+    energy_ref[...] = lax.fori_loop(0, a_ref.shape[0] // step, body, zero)
+
+
+def add_energy(a, b, psi, token):
+    return pl.pallas_call(
+        add_energy_kernel,
+        out_shape=(
+            jax.ShapeDtypeStruct(a.shape, a.dtype),
+            jax.ShapeDtypeStruct((8, a.shape[1]), jnp.float32),
+            TOKEN,
+        ),
+        in_specs=[WHOLE, WHOLE, WHOLE, ANY],
+        out_specs=(WHOLE, WHOLE, ANY),
+        compiler_params=params(),
+        cost_estimate=SMALL,
+        name="add_blocks_energy",
+    )(a, b, psi, token)
 
 
 def touch(*values):
@@ -209,84 +249,115 @@
     )(value, token)
 
 
-def finish_kernel(first, info_ref, live_ref, own_ref, a_ref, b_ref, c_ref, before_ref, *refs):
-    sigma_hbm, energy_ref, sigma_buf, sems = refs[-4:]
-    count, cols = own_ref.shape
+def own_rows(owns, start):
+    half = owns[0].shape[0]
+    return owns[start // half][pl.ds(start % half, 64), :]
+
+
+def finish_rows(first, info_ref, owns, arrival, sigma_hbm, buf, sems, live_ref=None):
+    count, cols = arrival.shape
     step = 64
-    piece = count // sems.shape[0]
     col = lax.broadcasted_iota(jnp.int32, (step, cols), 1) < info_ref[5]
     row = lax.broadcasted_iota(jnp.int32, (step, cols), 0)
-
-    def copy(i):
-        span = pl.ds(i * piece, piece)
-        return pltpu.make_async_copy(
-            sigma_buf.at[span, :], sigma_hbm.at[0, pl.ds(first + i * piece, piece), :], sems.at[i]
+    energy = jnp.zeros((8, cols), jnp.float32)
+    copies = finish_copies(first, count, sigma_hbm, buf, sems)
+    for start in range(0, count, step):
+        span, here = pl.ds(start, step), pl.ds(first + start, step)
+        inside = jnp.logical_and(row < info_ref[4] - (first + start), col)
+        total = jnp.where(inside, own_rows(owns, first + start) + arrival[span, :], 0.0)
+        buf[span, :] = total.astype(buf.dtype)
+        if live_ref is not None:
+            energy += folded(live_ref[here, :].astype(jnp.float32) * total)
+        if (start + step) % PIECE == 0:
+            copies[start // PIECE].start()
+    return energy
+
+
+def finish_copies(first, count, sigma_hbm, buf, sems):
+    copies = []
+    for i in range(count // PIECE):
+        here = buf.at[pl.ds(i * PIECE, PIECE), :]
+        there = sigma_hbm.at[0, pl.ds(first + i * PIECE, PIECE), :]
+        copies.append(pltpu.make_async_copy(here, there, sems.at[i]))
+    return copies
+
+
+def middle_kernel(cut, info_ref, own0_ref, own1_ref, live_ref, *refs):
+    owns, raised, relayed, crossed = (own0_ref, own1_ref), refs[:2], refs[2:4], refs[4]
+    sent_ref, sigma_hbm, energy_ref, buf, sems = refs[5:]
+    rows = live_ref.shape[0]
+
+    def put(energy):
+        energy = jnp.sum(energy + sent_ref[...])
+        energy_ref[...] = jnp.full(energy_ref.shape, energy, jnp.float32)
+
+    for n, halves in enumerate((raised, relayed)):
+
+        @pl.when(info_ref[6] == n)
+        def _(halves=halves):
+            half = rows // 2
+            energy = jnp.zeros(sent_ref.shape, jnp.float32)
+            for i, arrival in enumerate(halves):
+                here = buf.at[pl.ds(i * half, half), :]
+                energy += finish_rows(
+                    i * half, info_ref, owns, arrival, sigma_hbm, here, sems.at[i], live_ref
+                )
+            put(energy)
+            for i in range(2):
+                here = buf.at[pl.ds(i * half, half), :]
+                for copy in finish_copies(i * half, half, sigma_hbm, here, sems.at[i]):
+                    copy.wait()
+
+    @pl.when(info_ref[6] == 2)
+    def _():
+        energy = finish_rows(
+            0, info_ref, owns, crossed, sigma_hbm, buf, sems.at[0], live_ref
         )
-
-    def work(arrival):
-        energy = jnp.zeros((8, cols), jnp.float32)
-        for i in range(count // piece):
-
-            def body(n, energy):
-                start = pl.multiple_of(i * piece + n * step, step)
-                span = pl.ds(start, step)
-                inside = jnp.logical_and(row < info_ref[4] - first - start, col)
-                total = jnp.where(inside, own_ref[span, :] + arrival[span, :], 0.0)
-                sigma_buf[span, :] = total.astype(sigma_buf.dtype)
-                here = pl.ds(pl.multiple_of(first + start, step), step)
-                product = live_ref[here, :].astype(jnp.float32) * total
-                return energy + jnp.sum(jnp.reshape(product, (step // 8, 8, cols)), axis=0)
-
-            energy = lax.fori_loop(0, piece // step, body, energy)
-            copy(i).start()
-        energy_ref[...] = before_ref[...] + jnp.sum(energy)
-
-    for n, arrival in enumerate((a_ref, b_ref, c_ref)):
-        pl.when(info_ref[6] == n)(functools.partial(work, arrival))
-    for i in range(count // piece):
-        copy(i).wait()
-
-
-def finish(info, live, own, arrivals, before, sigma, first):
-    count, cols = own.shape
-    in_specs = [SMEM] + [WHOLE] * 6
-    operands = [info, live, own, *arrivals, before]
+        for start in range(cut, rows, 64):
+            span = pl.ds(start, 64)
+            energy += folded(live_ref[span, :].astype(jnp.float32) * own_rows(owns, start))
+        put(energy)
+        for copy in finish_copies(0, cut, sigma_hbm, buf, sems.at[0]):
+            copy.wait()
+
+
+def last_kernel(cut, info_ref, own0_ref, own1_ref, c_ref, energies_ref, _, sigma_hbm, energy_ref, buf, sems):
+    odd = info_ref[6] == 2
+
+    @pl.when(odd)
+    def _():
+        finish_rows(cut, info_ref, (own0_ref, own1_ref), c_ref, sigma_hbm, buf, sems.at[0])
+
+    energy_ref[0] = jnp.sum(energies_ref[:, :1])
+
+    @pl.when(odd)
+    def _():
+        for copy in finish_copies(cut, c_ref.shape[0], sigma_hbm, buf, sems.at[0]):
+            copy.wait()
+
+
+def finish(kernel, name, args, sigma, energy, count):
+    rows, cols = 2 * args[2].shape[0], args[2].shape[1]
+    in_specs = [SMEM] + [WHOLE] * (len(args) - 1)
     aliases = {}
     if sigma is not None:
         in_specs.append(ANY)
-        aliases = {len(operands): 0}
-        operands.append(sigma)
-    return pl.pallas_call(
-        functools.partial(finish_kernel, first),
-        out_shape=(
-            jax.ShapeDtypeStruct((1, *live.shape), jnp.bfloat16),
-            jax.ShapeDtypeStruct(before.shape, jnp.float32),
-        ),
+        aliases = {len(args): 0}
+        args = [*args, sigma]
+    return pl.pallas_call(
+        kernel,
+        out_shape=(jax.ShapeDtypeStruct((1, rows, cols), jnp.bfloat16), energy),
         in_specs=in_specs,
-        out_specs=(ANY, WHOLE),
-        scratch_shapes=[pltpu.VMEM((count, cols), jnp.bfloat16), pltpu.SemaphoreType.DMA((4,))],
+        out_specs=(ANY, SMEM if energy.shape == (1,) else WHOLE),
+        scratch_shapes=[
+            pltpu.VMEM((count, cols), jnp.bfloat16),
+            pltpu.SemaphoreType.DMA((2, rows // PIECE)),
+        ],
         input_output_aliases=aliases,
         compiler_params=params(),
         cost_estimate=SMALL,
-        name="finish_rows",
-    )(*operands)
-
-
-def sum_kernel(in_ref, out_ref):
-    out_ref[0] = jnp.sum(in_ref[:, :1])
-
-
-def sum_over_sectors(value):
-    arrived = lax.all_to_all(value, "sec", 0, 0, tiled=True)
-    return pl.pallas_call(
-        sum_kernel,
-        out_shape=jax.ShapeDtypeStruct((1,), jnp.float32),
-        in_specs=[WHOLE],
-        out_specs=SMEM,
-        compiler_params=params(),
-        cost_estimate=SMALL,
-        name="sum_energy",
-    )(arrived)
+        name=name,
+    )(*args)
 
 
 def on_device(psi, left_env, right_env, row_sizes, col_sizes):
@@ -306,6 +377,7 @@
 
     rows = psi.shape[1]
     part = rows // 2
+    cut = rows * 5 // 8
     which = jnp.where(place == 0, 1, jnp.where(place == 2, 0, 2))
     orders = [jnp.where(even, 2, 1), jnp.where(even, 3, 2), jnp.where(even, 1, 3), 0]
     info = jnp.stack([*orders, row_sizes[0], col_sizes[0], which]).astype(jnp.int32)
@@ -332,17 +404,20 @@
         return send(value, (0, 4))
 
     envs = (left_env, right_env)
-    first0, token, live, *ops0 = opening_rows(info, psi[0], envs, 0, part, masks=True)
+    first0, token, live, wide, *ops0 = opening_rows(info, psi[0], envs, 0, part, cut=cut)
     paired0 = up_chip(first0)
+    seen = send(wide, (3, -2), (1, 1))
     first1, token = term_rows(info, live, ops0, part, part, token)
     paired1 = up_chip(first1)
     both0, token = add(first0, paired0, token)
     raised0 = raise_one(both0)
-    second0, token, *ops1 = opening_rows(info, live, envs, 1, part, token)
+    second0, token, *ops1 = opening_rows(info, live, envs, 1, cut, token, seen)
     moved0 = along(second0)
     both1, token = add(first1, paired1, token)
     raised1 = raise_one(both1)
-    second1, token, *ops2 = term_rows(info, live, ops1, part, part, token, bring=(2, *envs))
+    second1, token, *ops2 = term_rows(
+        info, live, ops1, cut, rows - cut, token, bring=(2, *envs)
+    )
     moved1 = along(second1)
     third0, token, *ops3 = term_rows(info, live, ops2, 0, part, token, bring=(3, *envs))
     swapped0 = swap(third0)
@@ -354,16 +429,31 @@
     crossed0 = across(summed0)
     raised1, token = hold(raised1, token)
     relayed1 = relay(raised1)
-    own0, token = term_rows(info, live, ops3, 0, part, token, added=swapped0)
+    own0, token = term_rows(info, live, ops3, 0, part, token, added=(swapped0,))
     token = touch(relayed0, token)
-    summed1, token = add(second1, moved1, token)
+    summed1, sent, token = add_energy(second1, moved1, seen, token)
     crossed1 = across(summed1)
-
-    energy = jnp.zeros((sectors, 128), jnp.float32)
-    sigma, energy = finish(info, live, own0, (raised0, relayed0, crossed0), energy, None, 0)
-    own1, token = term_rows(info, live, ops3, part, part, token, energy, added=swapped1)
-    sigma, energy = finish(info, live, own1, (raised1, relayed1, crossed1), energy, sigma, part)
-    return sigma, sum_over_sectors(energy)
+    own1, token = term_rows(info, live, ops3, part, part, token, added=(swapped1,))
+
+    whole = jax.ShapeDtypeStruct((sectors, 128), jnp.float32)
+    single = jax.ShapeDtypeStruct((1,), jnp.float32)
+    sigma, energy = finish(
+        functools.partial(middle_kernel, cut),
+        "finish_middle",
+        [info, own0, own1, live, raised0, raised1, relayed0, relayed1, crossed0, sent],
+        None,
+        whole,
+        rows,
+    )
+    energies = lax.all_to_all(energy, "sec", 0, 0, tiled=True)
+    return finish(
+        functools.partial(last_kernel, cut),
+        "finish_last",
+        [info, own0, own1, crossed1, energies],
+        sigma,
+        single,
+        rows - cut,
+    )
 
 
 def solution(mesh):

time: 76.6 us -> 78.4 us (1.023)
  starting transfers between devices: 21.8 us -> 31.8 us
  blocking collectives: 18.2 us -> 11.3 us
  waiting for transfers between devices: 12 us -> 10.7 us
    ppermute x10 -> x11, starting transfers between devices: 19.3 us -> 29.2 us  [send(): return lax.ppermute(value, 'sec', pairs)]
    all_to_all x1, blocking collectives: 18.2 us -> 11.3 us  [on_device(): energies = lax.all_to_all(energy, 'sec', 0, 0, tiled=True)]
    ppermute x2, waiting for transfers between devices: 5.29 us -> 2.49 us  [raise_one(): return lax.ppermute(value, 'sec', pairs_up)]
    ppermute x10 -> x11, waiting for transfers between devices: 6.72 us -> 8.23 us  [send(): return lax.ppermute(value, 'sec', pairs)]
  transfers between devices with their start and end apart: 12 -> 13, of which waited for: 3 -> 2; matrix products, arithmetic and copies ran while one was open for 0% -> 0% of each run, Pallas kernels for 20% -> 21%
where the time goes in v11:
time: 78.4 us; the launch traced here: 78 us
  starting transfers between devices  31.8 us (41%)
  Pallas kernels  20.6 us (26%)
  blocking collectives  11.3 us (14%)
  waiting for transfers between devices  10.7 us (14%)
  between operations  2.21 us (3%)
  local copies, waits for them, and re-layouts  1.32 us (2%)
    ppermute x11, starting transfers between devices, send(): return lax.ppermute(value, 'sec', pairs)  29.2 us
    all_to_all x1, blocking collectives, on_device(): energies = lax.all_to_all(energy, 'sec', 0, 0, tiled=True)  11.3 us
    pallas_call x6, Pallas kernels, term_rows(): pl.pallas_call(functools.partial(term_kernel, first, len(added or ()), sl...  10.4 us
    ppermute x11, waiting for transfers between devices, send(): return lax.ppermute(value, 'sec', pairs)  8.23 us
    pallas_call x2, Pallas kernels, opening_rows(): pl.pallas_call(functools.partial(opening_kernel, slot, cut, len(tokens)),...  5.98 us
    pallas_call x2, Pallas kernels, finish(): pl.pallas_call(kernel, out_shape=(jax.ShapeDtypeStruct((1, rows, cols), j...  3.49 us
    ppermute x2, starting transfers between devices, raise_one(): return lax.ppermute(value, 'sec', pairs_up)  2.58 us
    ppermute x2, waiting for transfers between devices, raise_one(): return lax.ppermute(value, 'sec', pairs_up)  2.49 us
  transfers between devices with their start and end apart: 13, of which 2 were waited for; matrix products, arithmetic and copies ran while one was open for 0% of the time, Pallas kernels for 21%

profile of v11, /device:TPU:0, one launch (start us, length us, event | category | flops | bytes accessed | tf_op | source)
XLA Modules:
  0.0 78.0 jit_solution(7766908026012454371)
XLA Ops:
  2.0 1.2 %copy-done.1 = bf16[1,1024,512]{2,1,0:T(8,128)(2,1)S(1)} copy-done((bf16[1,1024,512]{2,1,0:T(8,128)(2,1)S(1)}, bf16[1,1024,512]{2,1,0:T(8,128)(2,1)}, u32[]{:S(2)}) %copy-start.1) | copy-done | bytes 1048600
  3.3 3.0 %opening_rows.2 = (f32[512,512]{1,0:T(8,128)S(1)}, f32[8,128]{1,0:T(8,128)S(1)}, bf16[1024,512]{1,0:T(8,128)(2,1)S(1)}, f32[384,512]{1,0:T(8,128)S(1)}, bf16[102...) custom-call(s32[7]{0:T(128)S(1)} %stack.19.info_ref, bf16[1024,512]{1,0:T(8,128)(2,1)S(1)} %bitcast.9, ...), custom_call_target="tpu_custom_call" | custom-call | flops 200000000 | bytes 1000000 | tf_op jit(solution)/shard_map/opening_rows/pallas_call | solution.py:101
  6.2 2.4 %collective-permute-start = (f32[512,512]{1,0:T(8,128)S(1)}, f32[512,512]{1,0:T(8,128)S(1)}, u32[]{:S(2)}, u32[]{:S(2)}) collective-permute-start(f32[512,512]{1,0:T(8,128)S(1)} %get-tuple-element.43.a_ref), channel_id=1, source_target_pairs={{0,1},{4,5},{8,9},{12,13},{2,3},{6,7},{10,11},{14,15},{16,17},{20,... | collective-permute-start | bytes 3145736 | tf_op jit(solution)/shard_map/ppermute | solution.py:376
  9.4 1.5 %term_rows.6 = (f32[512,512]{1,0:T(8,128)S(1)}, f32[8,128]{1,0:T(8,128)S(1)}) custom-call(s32[7]{0:T(128)S(1)} %stack.19.info_ref, bf16[1024,512]{1,0:T(8,128)(2,1)S(1)} %get-tuple-element.42.live_ref, bf16[1024,1024]{1,0:T(8,128)(2,1)S(1)} %get-tuple-element.44.left_ref, bf16[512,512]{1,0:T(8,128)(2,1)S(1)} %get-tuple-element.45.right_ref, ...), custom_call_target="tpu_custom_call" | custom-call | flops 200000000 | bytes 1000000 | tf_op jit(solution)/shard_map/term_rows/pallas_call | solution.py:156
  10.9 5.6 %collective-permute-start.2 = (f32[512,512]{1,0:T(8,128)S(1)}, f32[512,512]{1,0:T(8,128)S(1)}, u32[]{:S(2)}, u32[]{:S(2)}) collective-permute-start(f32[512,512]{1,0:T(8,128)S(1)} %get-tuple-element.52.a_ref), channel_id=1, source_target_pairs={{0,1},{4,5},{8,9},{12,13},{2,3},{6,7},{10,11},{14,15},{16,17},{20,... | collective-permute-start | bytes 3145736 | tf_op jit(solution)/shard_map/ppermute | solution.py:376
  16.7 1.3 %collective-permute-start.6 = (f32[512,512]{1,0:T(8,128)S(1)}, f32[512,512]{1,0:T(8,128)S(1)}, u32[]{:S(2)}, u32[]{:S(2)}) collective-permute-start(f32[512,512]{1,0:T(8,128)S(1)} %get-tuple-element.63), channel_id=1, source_target_pairs={{1,2},{5,6},{9,10},{13,14},{3,0},{7,4},{11,8},{17,18},{21,22},{25,... | collective-permute-start | bytes 3145736 | tf_op jit(solution)/shard_map/ppermute | solution.py:389
  18.1 3.0 %opening_rows.3 = (f32[640,512]{1,0:T(8,128)S(1)}, f32[8,128]{1,0:T(8,128)S(1)}, bf16[1024,1024]{1,0:T(8,128)(2,1)S(1)}, bf16[512,512]{1,0:T(8,128)(2,1)S(1)}) custom-call(s32[7]{0:T(128)S(1)} %stack.19.info_ref, bf16[1024,512]{1,0:T(8,128)(2,1)S(1)} %get-tuple-element.42.live_ref, bf16[1,4,1024,1024]{3,2,1,0:T(8,128)(2,1)} %refs_0_.3, ...), custom_call_target="tpu_custom_call" | custom-call | flops 200000000 | bytes 1000000 | tf_op jit(solution)/shard_map/opening_rows/pallas_call | solution.py:101
  21.1 0.7 collective-permute-start.5
  22.0 1.3 %collective-permute-start.4 = (f32[512,512]{1,0:T(8,128)S(1)}, f32[512,512]{1,0:T(8,128)S(1)}, u32[]{:S(2)}, u32[]{:S(2)}) collective-permute-start(f32[512,512]{1,0:T(8,128)S(1)} %get-tuple-element.61), channel_id=1, source_target_pairs={{1,2},{5,6},{9,10},{13,14},{3,0},{7,4},{11,8},{17,18},{21,22},{25,... | collective-permute-start | bytes 3145736 | tf_op jit(solution)/shard_map/ppermute | solution.py:389
  23.3 2.2 %term_rows.7 = (f32[384,512]{1,0:T(8,128)S(1)}, f32[8,128]{1,0:T(8,128)S(1)}, bf16[1024,1024]{1,0:T(8,128)(2,1)S(1)}, bf16[512,512]{1,0:T(8,128)(2,1)S(1)}) custom-call(s32[7]{0:T(128)S(1)} %stack.19.info_ref, bf16[1024,512]{1,0:T(8,128)(2,1)S(1)} %get-tuple-element.42.live_ref, bf16[1024,1024]{1,0:T(8,128)(2,1)S(1)} %get-tuple-element.50.left_ref, ...), custom_call_target="tpu_custom_call" | custom-call | flops 200000000 | bytes 1000000 | tf_op jit(solution)/shard_map/term_rows/pallas_call | solution.py:156
  25.5 2.2 %term_rows.8 = (f32[512,512]{1,0:T(8,128)S(1)}, f32[8,128]{1,0:T(8,128)S(1)}, bf16[1024,1024]{1,0:T(8,128)(2,1)S(1)}, bf16[512,512]{1,0:T(8,128)(2,1)S(1)}) custom-call(s32[7]{0:T(128)S(1)} %stack.19.info_ref, bf16[1024,512]{1,0:T(8,128)(2,1)S(1)} %get-tuple-element.42.live_ref, bf16[1024,1024]{1,0:T(8,128)(2,1)S(1)} %get-tuple-element.55.left_ref, ...), custom_call_target="tpu_custom_call" | custom-call | flops 200000000 | bytes 1000000 | tf_op jit(solution)/shard_map/term_rows/pallas_call | solution.py:156
  27.7 7.1 %collective-permute-start.3 = (f32[512,512]{1,0:T(8,128)S(1)}, f32[512,512]{1,0:T(8,128)S(1)}, u32[]{:S(2)}, u32[]{:S(2)}) collective-permute-start(f32[512,512]{1,0:T(8,128)S(1)} %get-tuple-element.60), channel_id=1, source_target_pairs={{0,1},{4,5},{8,9},{12,13},{1,0},{5,4},{9,8},{13,12},{2,3},{6,7},{1... | collective-permute-start | bytes 3145736 | tf_op jit(solution)/shard_map/ppermute | solution.py:376
  34.8 4.1 %collective-permute-start.9 = (f32[512,512]{1,0:T(8,128)S(1)}, f32[512,512]{1,0:T(8,128)S(1)}, u32[]{:S(2)}, u32[]{:S(2)}) collective-permute-start(f32[512,512]{1,0:T(8,128)S(1)} %get-tuple-element.72.refs_0_), channel_id=1, source_target_pairs={{0,4},{4,8},{8,12},{16,20},{20,24},{24,28}} | collective-permute-start | bytes 3145736 | tf_op jit(solution)/shard_map/ppermute | solution.py:376
  39.6 1.5 %term_rows.9 = (f32[512,512]{1,0:T(8,128)S(1)}, f32[8,128]{1,0:T(8,128)S(1)}) custom-call(s32[7]{0:T(128)S(1)} %stack.19.info_ref, bf16[1024,512]{1,0:T(8,128)(2,1)S(1)} %get-tuple-element.42.live_ref, bf16[1024,1024]{1,0:T(8,128)(2,1)S(1)} %get-tuple-element.55.left_ref, bf16[512,512]{1,0:T(8,128)(2,1)S(1)} %get-tuple-element.56.right_ref, ...), custom_call_target="tpu_custom_call" | custom-call | flops 200000000 | bytes 1000000 | tf_op jit(solution)/shard_map/term_rows/pallas_call | solution.py:156
  41.3 0.7 collective-permute-start.12
  42.1 2.5 %collective-permute-done.4.refs_0_ = f32[512,512]{1,0:T(8,128)S(1)} collective-permute-done((f32[512,512]{1,0:T(8,128)S(1)}, f32[512,512]{1,0:T(8,128)S(1)}, u32[]{:S(2)}, u32[]{:S(2)}) %collective-permute-start.4) | collective-permute-done | bytes 1048608 | tf_op jit(solution)/shard_map/ppermute | solution.py:389
  44.6 2.8 %collective-permute-start.7 = (f32[512,512]{1,0:T(8,128)S(1)}, f32[512,512]{1,0:T(8,128)S(1)}, u32[]{:S(2)}, u32[]{:S(2)}) collective-permute-start(f32[512,512]{1,0:T(8,128)S(1)} %get-tuple-element.70), channel_id=1, source_target_pairs={{0,1},{4,5},{8,9},{12,13},{1,0},{5,4},{9,8},{13,12},{2,3},{6,7},{1... | collective-permute-start | bytes 3145736 | tf_op jit(solution)/shard_map/ppermute | solution.py:376
  47.4 3.5 %collective-permute-start.11 = (f32[512,512]{1,0:T(8,128)S(1)}, f32[512,512]{1,0:T(8,128)S(1)}, u32[]{:S(2)}, u32[]{:S(2)}) collective-permute-start(f32[512,512]{1,0:T(8,128)S(1)} %get-tuple-element.77.refs_1_), channel_id=1, source_target_pairs={{0,4},{4,8},{8,12},{16,20},{20,24},{24,28}} | collective-permute-start | bytes 3145736 | tf_op jit(solution)/shard_map/ppermute | solution.py:376
  50.9 1.5 %term_rows.10 = (f32[512,512]{1,0:T(8,128)S(1)}, f32[8,128]{1,0:T(8,128)S(1)}) custom-call(s32[7]{0:T(128)S(1)} %stack.19.info_ref, bf16[1024,512]{1,0:T(8,128)(2,1)S(1)} %get-tuple-element.42.live_ref, bf16[1024,1024]{1,0:T(8,128)(2,1)S(1)} %get-tuple-element.58.left_ref, bf16[512,512]{1,0:T(8,128)(2,1)S(1)} %get-tuple-element.59.right_ref, ...), custom_call_target="tpu_custom_call" | custom-call | flops 200000000 | bytes 1000000 | tf_op jit(solution)/shard_map/term_rows/pallas_call | solution.py:156
  53.4 1.5 %term_rows.11 = (f32[512,512]{1,0:T(8,128)S(1)}, f32[8,128]{1,0:T(8,128)}) custom-call(s32[7]{0:T(128)S(1)} %stack.19.info_ref, bf16[1024,512]{1,0:T(8,128)(2,1)S(1)} %get-tuple-element.42.live_ref, bf16[1024,1024]{1,0:T(8,128)(2,1)S(1)} %get-tuple-element.58.left_ref, bf16[512,512]{1,0:T(8,128)(2,1)S(1)} %get-tuple-element.59.right_ref, ...), custom_call_target="tpu_custom_call" | custom-call | flops 200000000 | bytes 1000000 | tf_op jit(solution)/shard_map/term_rows/pallas_call | solution.py:156
  54.9 8.2 %collective-permute-done.11.refs_3_ = f32[512,512]{1,0:T(8,128)S(1)} collective-permute-done((f32[512,512]{1,0:T(8,128)S(1)}, f32[512,512]{1,0:T(8,128)S(1)}, u32[]{:S(2)}, u32[]{:S(2)}) %collective-permute-start.11) | collective-permute-done | bytes 1048608 | tf_op jit(solution)/shard_map/ppermute | solution.py:376
  63.2 2.2 %finish_middle.1 = (bf16[1,1024,512]{2,1,0:T(8,128)(2,1)}, f32[16,128]{1,0:T(8,128)S(1)}) custom-call(s32[7]{0:T(128)S(1)} %stack.19.info_ref, f32[512,512]{1,0:T(8,128)S(1)} %get-tuple-element.69.own0_ref, f32[512,512]{1,0:T(8,128)S(1)} %get-tuple-element.75.own1_ref, bf16[1024,512]{1,0:T(8,128)(2,1)S(1)} %get-tuple-element.42.live_ref, ...), custom_call_target="tpu_custom_call" | custom-call | flops 200000000 | bytes 1000000 | tf_op jit(solution)/shard_map/finish_middle/pallas_call | solution.py:347
  65.3 11.3 %all_to_all.11 = f32[16,1,128]{2,1,0:T(1,128)S(1)} all-to-all(f32[16,1,128]{2,1,0:T(1,128)S(1)} %bitcast.11), channel_id=1, replica_groups=mesh['grp'=2,'sec'=16] {'sec'}, dimensions={0} | all-to-all | bytes 16384 | tf_op jit(solution)/shard_map/all_to_all | solution.py:448
  76.6 1.3 %finish_last.1 = (bf16[1,1024,512]{2,1,0:T(8,128)(2,1)}, f32[1]{0:T(128)}) custom-call(s32[7]{0:T(128)S(1)} %stack.19.info_ref, f32[512,512]{1,0:T(8,128)S(1)} %get-tuple-element.69.own0_ref, f32[512,512]{1,0:T(8,128)S(1)} %get-tuple-element.75.own1_ref, f32[384,512]{1,0:T(8,128)S(1)} %collective-permute-done.10.c_ref, ...), custom_call_target="tpu_custom_call", output_to_operand_aliasing={{0}: (5, {})} | custom-call | flops 200000000 | bytes 1000000 | tf_op jit(solution)/shard_map/finish_last/pallas_call | solution.py:347
  (25 shorter events, 2.9 us)
Async XLA Ops:
  2.0 1.2 %copy-start.1 = (bf16[1,1024,512]{2,1,0:T(8,128)(2,1)S(1)}, bf16[1,1024,512]{2,1,0:T(8,128)(2,1)}, u32[]{:S(2)}) copy-start(bf16[1,1024,512]{2,1,0:T(8,128)(2,1)} %param.5) | copy-start | bytes 3145732
  6.2 10.3 %collective-permute-start = (f32[512,512]{1,0:T(8,128)S(1)}, f32[512,512]{1,0:T(8,128)S(1)}, u32[]{:S(2)}, u32[]{:S(2)}) collective-permute-start(f32[512,512]{1,0:T(8,128)S(1)} %get-tuple-element.43.a_ref), channel_id=1, source_target_pairs={{0,1},{4,5},{8,9},{12,13},{2,3},{6,7},{10,11},{14,15},{16,17},{20,... | collective-permute-start | bytes 3145736 | tf_op jit(solution)/shard_map/ppermute | solution.py:376
  8.7 9.4 %collective-permute-start.1 = (f32[384,512]{1,0:T(8,128)S(1)}, f32[384,512]{1,0:T(8,128)S(1)}, u32[]{:S(2)}, u32[]{:S(2)}) collective-permute-start(f32[384,512]{1,0:T(8,128)S(1)} %get-tuple-element.49), channel_id=1, source_target_pairs={{3,1},{7,5},{11,9},{15,13},{1,2},{5,6},{9,10},{13,14},{19,17},{23,... | collective-permute-start | bytes 2359304 | tf_op jit(solution)/shard_map/ppermute | solution.py:376
  9.4 8.7 %copy-start = (bf16[1,4,512,512]{3,2,1,0:T(8,128)(2,1)S(1)}, bf16[1,4,512,512]{3,2,1,0:T(8,128)(2,1)}, u32[]{:S(2)}) copy-start(bf16[1,4,512,512]{3,2,1,0:T(8,128)(2,1)} %refs_1_.3) | copy-start | bytes 6291460
  10.9 10.9 %collective-permute-start.2 = (f32[512,512]{1,0:T(8,128)S(1)}, f32[512,512]{1,0:T(8,128)S(1)}, u32[]{:S(2)}, u32[]{:S(2)}) collective-permute-start(f32[512,512]{1,0:T(8,128)S(1)} %get-tuple-element.52.a_ref), channel_id=1, source_target_pairs={{0,1},{4,5},{8,9},{12,13},{2,3},{6,7},{10,11},{14,15},{16,17},{20,... | collective-permute-start | bytes 3145736 | tf_op jit(solution)/shard_map/ppermute | solution.py:376
  16.7 18.1 %collective-permute-start.6 = (f32[512,512]{1,0:T(8,128)S(1)}, f32[512,512]{1,0:T(8,128)S(1)}, u32[]{:S(2)}, u32[]{:S(2)}) collective-permute-start(f32[512,512]{1,0:T(8,128)S(1)} %get-tuple-element.63), channel_id=1, source_target_pairs={{1,2},{5,6},{9,10},{13,14},{3,0},{7,4},{11,8},{17,18},{21,22},{25,... | collective-permute-start | bytes 3145736 | tf_op jit(solution)/shard_map/ppermute | solution.py:389
  21.1 20.1 %collective-permute-start.5 = (f32[640,512]{1,0:T(8,128)S(1)}, f32[640,512]{1,0:T(8,128)S(1)}, u32[]{:S(2)}, u32[]{:S(2)}) collective-permute-start(f32[640,512]{1,0:T(8,128)S(1)} %get-tuple-element.62.a_ref), channel_id=1, source_target_pairs={{3,6},{7,10},{11,14},{4,1},{8,5},{12,9},{19,22},{23,26},{27,30},{2... | collective-permute-start | bytes 3932168 | tf_op jit(solution)/shard_map/ppermute | solution.py:376
  22.0 22.6 %collective-permute-start.4 = (f32[512,512]{1,0:T(8,128)S(1)}, f32[512,512]{1,0:T(8,128)S(1)}, u32[]{:S(2)}, u32[]{:S(2)}) collective-permute-start(f32[512,512]{1,0:T(8,128)S(1)} %get-tuple-element.61), channel_id=1, source_target_pairs={{1,2},{5,6},{9,10},{13,14},{3,0},{7,4},{11,8},{17,18},{21,22},{25,... | collective-permute-start | bytes 3145736 | tf_op jit(solution)/shard_map/ppermute | solution.py:389
  27.7 19.7 %collective-permute-start.3 = (f32[512,512]{1,0:T(8,128)S(1)}, f32[512,512]{1,0:T(8,128)S(1)}, u32[]{:S(2)}, u32[]{:S(2)}) collective-permute-start(f32[512,512]{1,0:T(8,128)S(1)} %get-tuple-element.60), channel_id=1, source_target_pairs={{0,1},{4,5},{8,9},{12,13},{1,0},{5,4},{9,8},{13,12},{2,3},{6,7},{1... | collective-permute-start | bytes 3145736 | tf_op jit(solution)/shard_map/ppermute | solution.py:376
  34.8 17.7 %collective-permute-start.9 = (f32[512,512]{1,0:T(8,128)S(1)}, f32[512,512]{1,0:T(8,128)S(1)}, u32[]{:S(2)}, u32[]{:S(2)}) collective-permute-start(f32[512,512]{1,0:T(8,128)S(1)} %get-tuple-element.72.refs_0_), channel_id=1, source_target_pairs={{0,4},{4,8},{8,12},{16,20},{20,24},{24,28}} | collective-permute-start | bytes 3145736 | tf_op jit(solution)/shard_map/ppermute | solution.py:376
  38.9 13.6 %collective-permute-start.8 = (f32[384,512]{1,0:T(8,128)S(1)}, f32[384,512]{1,0:T(8,128)S(1)}, u32[]{:S(2)}, u32[]{:S(2)}) collective-permute-start(f32[384,512]{1,0:T(8,128)S(1)} %get-tuple-element.71.a_ref), channel_id=1, source_target_pairs={{3,6},{7,10},{11,14},{4,1},{8,5},{12,9},{19,22},{23,26},{27,30},{2... | collective-permute-start | bytes 2359304 | tf_op jit(solution)/shard_map/ppermute | solution.py:376
  41.3 21.8 %collective-permute-start.12 = (f32[640,512]{1,0:T(8,128)S(1)}, f32[640,512]{1,0:T(8,128)S(1)}, u32[]{:S(2)}, u32[]{:S(2)}) collective-permute-start(f32[640,512]{1,0:T(8,128)S(1)} %get-tuple-element.78), channel_id=1, source_target_pairs={{1,3},{5,7},{9,11},{13,15},{2,1},{6,5},{10,9},{14,13},{17,19},{21,... | collective-permute-start | bytes 3932168 | tf_op jit(solution)/shard_map/ppermute | solution.py:376
  44.6 8.9 %collective-permute-start.7 = (f32[512,512]{1,0:T(8,128)S(1)}, f32[512,512]{1,0:T(8,128)S(1)}, u32[]{:S(2)}, u32[]{:S(2)}) collective-permute-start(f32[512,512]{1,0:T(8,128)S(1)} %get-tuple-element.70), channel_id=1, source_target_pairs={{0,1},{4,5},{8,9},{12,13},{1,0},{5,4},{9,8},{13,12},{2,3},{6,7},{1... | collective-permute-start | bytes 3145736 | tf_op jit(solution)/shard_map/ppermute | solution.py:376
  47.4 15.8 %collective-permute-start.11 = (f32[512,512]{1,0:T(8,128)S(1)}, f32[512,512]{1,0:T(8,128)S(1)}, u32[]{:S(2)}, u32[]{:S(2)}) collective-permute-start(f32[512,512]{1,0:T(8,128)S(1)} %get-tuple-element.77.refs_1_), channel_id=1, source_target_pairs={{0,4},{4,8},{8,12},{16,20},{20,24},{24,28}} | collective-permute-start | bytes 3145736 | tf_op jit(solution)/shard_map/ppermute | solution.py:376
  52.7 23.9 %collective-permute-start.10 = (f32[384,512]{1,0:T(8,128)S(1)}, f32[384,512]{1,0:T(8,128)S(1)}, u32[]{:S(2)}, u32[]{:S(2)}) collective-permute-start(f32[384,512]{1,0:T(8,128)S(1)} %get-tuple-element.76), channel_id=1, source_target_pairs={{1,3},{5,7},{9,11},{13,15},{2,1},{6,5},{10,9},{14,13},{17,19},{21,... | collective-permute-start | bytes 2359304 | tf_op jit(solution)/shard_map/ppermute | solution.py:376

commit v12 on v9

--- a/solution.py
+++ b/solution.py
@@ -9,7 +9,7 @@
 
 MIB = 1024 * 1024
 LEFT_PIECES, RIGHT_PIECES = 8, 2
-FIRST_MIB = 48
+FIRST_MIB = 44
 BRING_MIB = 42
 
 ANY = pl.BlockSpec(memory_space=pl.ANY)
@@ -24,7 +24,7 @@
     return pltpu.CompilerParams(vmem_limit_bytes=mib * MIB)
 
 
-def fetch(info_ref, slot, left_hbm, right_hbm, left_ref, right_ref, sems):
+def fetch(info_ref, slot, count, left_hbm, right_hbm, left_ref, right_ref, sems):
     term = info_ref[slot]
     rows, cols = left_ref.shape[0], right_ref.shape[0]
     step = rows // LEFT_PIECES
@@ -42,8 +42,8 @@
                 right_hbm.at[0, term, span, :], right_ref.at[span, :], sems.at[LEFT_PIECES + i]
             )
         )
-    half = LEFT_PIECES // 2
-    return left[:half] + right, left[half:]
+    first = -(-count * LEFT_PIECES // rows)
+    return left[:first] + right, left[first:]
 
 
 def multiply(left, live, right):
@@ -59,9 +59,12 @@
     psi_ref = live_ref
     if masks:
         live_ref = operands.pop(0)
-    own, late = fetch(info_ref, slot, left_hbm, right_hbm, *operands, sems)
-    for copy in own + late:
+    own, late = fetch(info_ref, slot, out_ref.shape[0], left_hbm, right_hbm, *operands[:2], sems.at[0])
+    for copy in own:
         copy.start()
+    if len(operands) > 2:
+        later = fetch(info_ref, slot + 1, 0, left_hbm, right_hbm, *operands[2:], sems.at[1])
+        late = late + later[0] + later[1]
     if masks:
         rows, cols = psi_ref.shape
         step = 128
@@ -74,6 +77,8 @@
             live_ref[span, :] = values.astype(live_ref.dtype)
     for copy in own:
         copy.wait()
+    for copy in late:
+        copy.start()
     out_ref[...] = multiply(operands[0][: out_ref.shape[0], :], live_ref[...], operands[1][...])
     for copy in late:
         copy.wait()
@@ -91,13 +96,13 @@
     out_shape = [jax.ShapeDtypeStruct((count, cols), jnp.float32), TOKEN]
     if masks:
         out_shape.append(jax.ShapeDtypeStruct(live.shape, live.dtype))
-    out_shape += operand_shapes(width, cols)
+    out_shape += operand_shapes(width, cols) * 2
     return pl.pallas_call(
         functools.partial(opening_kernel, slot, masks, len(tokens)),
         out_shape=out_shape,
         in_specs=[SMEM, WHOLE, HBM, HBM] + [ANY] * len(tokens),
         out_specs=[WHOLE, ANY] + [WHOLE] * (len(out_shape) - 2),
-        scratch_shapes=[pltpu.SemaphoreType.DMA((LEFT_PIECES + RIGHT_PIECES,))],
+        scratch_shapes=[pltpu.SemaphoreType.DMA((2, LEFT_PIECES + RIGHT_PIECES))],
         compiler_params=params(FIRST_MIB if masks else BRING_MIB),
         cost_estimate=SMALL,
         name="opening_rows",
@@ -106,24 +111,25 @@
 
 def term_kernel(first, adds, slot, tokens, info_ref, live_ref, left_ref, right_ref, *refs):
     refs = list(refs)
-    add_ref = refs.pop(0) if adds else None
+    add_refs = [refs.pop(0), refs.pop(0)] if adds else None
     copies = []
     if slot is not None:
         left_hbm, right_hbm = refs[:2]
         sems = refs[-1]
         out_ref, _, left_next, right_next = refs[2 + tokens : -1]
-        copies = sum(fetch(info_ref, slot, left_hbm, right_hbm, left_next, right_next, sems), [])
+        copies = sum(fetch(info_ref, slot, 0, left_hbm, right_hbm, left_next, right_next, sems), [])
         for copy in copies:
             copy.start()
     else:
         out_ref, _ = refs[tokens:]
     count = out_ref.shape[0]
-    block = min(count, 512)
+    block = count
     for i in range(count // block):
         span = pl.ds(i * block, block)
         value = multiply(left_ref[pl.ds(first + i * block, block), :], live_ref[...], right_ref[...])
         if adds:
-            value = value + add_ref[span, :]
+            odd = info_ref[7] == 1
+            value = value + jnp.where(odd, add_refs[1][span, :], add_refs[0][span, :])
         out_ref[span, :] = value
     for copy in copies:
         copy.wait()
@@ -138,8 +144,8 @@
     scratch = []
     slot = None
     if added is not None:
-        in_specs.append(WHOLE)
-        args.append(added)
+        in_specs += [WHOLE, WHOLE]
+        args += added
     if bring is not None:
         slot = bring[0]
         in_specs += [HBM, HBM]
@@ -159,29 +165,39 @@
     )(*args, *tokens)
 
 
-def add_kernel(a_ref, b_ref, *refs):
+def add_kernel(odd_only, info_ref, a_ref, b_ref, *refs):
     out_ref = refs[-2]
-    rows = a_ref.shape[0]
     step = 64
 
-    def body(i, _):
+    def sums(i, _):
         span = pl.ds(pl.multiple_of(i * step, step), step)
         out_ref[span, :] = a_ref[span, :] + b_ref[span, :]
         return _
 
-    lax.fori_loop(0, rows // step, body, 0)
-
-
-def add(a, b, *tokens):
-    return pl.pallas_call(
-        add_kernel,
+    def copies(i, _):
+        span = pl.ds(pl.multiple_of(i * step, step), step)
+        out_ref[span, :] = a_ref[span, :]
+        return _
+
+    count = a_ref.shape[0] // step
+    if odd_only:
+        odd = info_ref[7] == 1
+        pl.when(odd)(lambda: lax.fori_loop(0, count, sums, None))
+        pl.when(jnp.logical_not(odd))(lambda: lax.fori_loop(0, count, copies, None))
+    else:
+        lax.fori_loop(0, count, sums, None)
+
+
+def add(info, a, b, token, odd_only=False):
+    return pl.pallas_call(
+        functools.partial(add_kernel, odd_only),
         out_shape=(jax.ShapeDtypeStruct(a.shape, a.dtype), TOKEN),
-        in_specs=[WHOLE, WHOLE] + [ANY] * len(tokens),
+        in_specs=[SMEM, WHOLE, WHOLE, ANY],
         out_specs=(WHOLE, ANY),
         compiler_params=params(),
         cost_estimate=SMALL,
         name="add_blocks",
-    )(a, b, *tokens)
+    )(info, a, b, token)
 
 
 def touch(*values):
@@ -213,7 +229,7 @@
     sigma_hbm, energy_ref, sigma_buf, sems = refs[-4:]
     count, cols = own_ref.shape
     step = 64
-    piece = count // sems.shape[0]
+    piece = 64
     col = lax.broadcasted_iota(jnp.int32, (step, cols), 1) < info_ref[5]
     row = lax.broadcasted_iota(jnp.int32, (step, cols), 0)
 
@@ -264,7 +280,7 @@
         ),
         in_specs=in_specs,
         out_specs=(ANY, WHOLE),
-        scratch_shapes=[pltpu.VMEM((count, cols), jnp.bfloat16), pltpu.SemaphoreType.DMA((4,))],
+        scratch_shapes=[pltpu.VMEM((count, cols), jnp.bfloat16), pltpu.SemaphoreType.DMA((count // 64,))],
         input_output_aliases=aliases,
         compiler_params=params(),
         cost_estimate=SMALL,
@@ -305,19 +321,20 @@
         return lax.ppermute(value, "sec", pairs)
 
     rows = psi.shape[1]
-    part = rows // 2
+    part = rows * 5 // 8
+    rest = rows - part
     which = jnp.where(place == 0, 1, jnp.where(place == 2, 0, 2))
-    orders = [jnp.where(even, 2, 1), jnp.where(even, 3, 2), jnp.where(even, 1, 3), 0]
-    info = jnp.stack([*orders, row_sizes[0], col_sizes[0], which]).astype(jnp.int32)
-
-    pairs_up = [(s, s + 1) for s in range(1, sectors, 4) if s + 1 < sectors]
-    pairs_up += [(s, s - 3) for s in range(3, sectors, 4) if s + 1 < sectors]
+    slots = [jnp.where(even, 2, 3), 1, jnp.where(even, 3, 2), 0]
+    info = jnp.stack([*slots, row_sizes[0], col_sizes[0], which, sector % 2]).astype(jnp.int32)
+    up = [(s, s + 1) for s in range(1, sectors, 4) if s + 1 < sectors]
+    up += [(s, s - 3) for s in range(3, sectors, 4) if s + 1 < sectors]
+    up += [(s, s + 1) for s in range(0, sectors, 2)]
+
+    def swap(value):
+        return send(value, (0, 1), (1, -1), (2, 1), (3, -1))
 
     def raise_one(value):
-        return lax.ppermute(value, "sec", pairs_up)
-
-    def up_chip(value):
-        return send(value, (0, 1), (2, 1))
+        return lax.ppermute(value, "sec", up)
 
     def along(value):
         return send(value, (3, 3), (0, -3))
@@ -325,43 +342,38 @@
     def across(value):
         return send(value, (1, 2), (2, -1))
 
-    def swap(value):
-        return send(value, (0, 1), (1, -1), (2, 1), (3, -1))
-
     def relay(value):
         return send(value, (0, 4))
 
     envs = (left_env, right_env)
-    first0, token, live, *ops0 = opening_rows(info, psi[0], envs, 0, part, masks=True)
-    paired0 = up_chip(first0)
-    first1, token = term_rows(info, live, ops0, part, part, token)
-    paired1 = up_chip(first1)
-    both0, token = add(first0, paired0, token)
+    first0, token, live, *ops = opening_rows(info, psi[0], envs, 0, part, masks=True)
+    ops0, ops1 = ops[:2], ops[2:]
+    swapped0 = swap(first0)
+    second0, token, *ops2 = term_rows(info, live, ops1, 0, part, token, bring=(2, *envs))
+    both0, token = add(info, second0, swapped0, token, odd_only=True)
     raised0 = raise_one(both0)
-    second0, token, *ops1 = opening_rows(info, live, envs, 1, part, token)
-    moved0 = along(second0)
-    both1, token = add(first1, paired1, token)
+    third0, token, *ops3 = term_rows(info, live, ops2, 0, part, token, bring=(3, *envs))
+    moved0 = along(third0)
+    third1, token = term_rows(info, live, ops2, part, rest, token)
+    moved1 = along(third1)
+    first1, token = term_rows(info, live, ops0, part, rest, token)
+    swapped1 = swap(first1)
+    second1, token = term_rows(info, live, ops1, part, rest, token)
+    both1, token = add(info, second1, swapped1, token, odd_only=True)
     raised1 = raise_one(both1)
-    second1, token, *ops2 = term_rows(info, live, ops1, part, part, token, bring=(2, *envs))
-    moved1 = along(second1)
-    third0, token, *ops3 = term_rows(info, live, ops2, 0, part, token, bring=(3, *envs))
-    swapped0 = swap(third0)
     raised0, token = hold(raised0, token)
     relayed0 = relay(raised0)
-    third1, token = term_rows(info, live, ops2, part, part, token)
-    swapped1 = swap(third1)
-    summed0, token = add(second0, moved0, token)
+    summed0, token = add(info, third0, moved0, token)
     crossed0 = across(summed0)
     raised1, token = hold(raised1, token)
     relayed1 = relay(raised1)
-    own0, token = term_rows(info, live, ops3, 0, part, token, added=swapped0)
-    token = touch(relayed0, token)
-    summed1, token = add(second1, moved1, token)
+    summed1, token = add(info, third1, moved1, token)
     crossed1 = across(summed1)
-
+    own0, token = term_rows(info, live, ops3, 0, part, token, added=(swapped0, raised0))
     energy = jnp.zeros((sectors, 128), jnp.float32)
     sigma, energy = finish(info, live, own0, (raised0, relayed0, crossed0), energy, None, 0)
-    own1, token = term_rows(info, live, ops3, part, part, token, energy, added=swapped1)
+    token = energy
+    own1, token = term_rows(info, live, ops3, part, rest, token, added=(swapped1, raised1))
     sigma, energy = finish(info, live, own1, (raised1, relayed1, crossed1), energy, sigma, part)
     return sigma, sum_over_sectors(energy)
 

time: 76.6 us -> 79 us (1.031)
  Pallas kernels: 20.5 us -> 24 us
  waiting for transfers between devices: 12 us -> 15.2 us
  starting transfers between devices: 21.8 us -> 19.3 us
  blocking collectives: 18.2 us -> 16.6 us
    ppermute x10 -> x8, starting transfers between devices: 19.3 us -> 14.9 us  [send(): return lax.ppermute(value, 'sec', pairs)]
    ppermute x10 -> x8, waiting for transfers between devices: 6.72 us -> 10.1 us  [send(): return lax.ppermute(value, 'sec', pairs)]
    pallas_call x6 -> x7, Pallas kernels: 10.4 us -> 13.1 us  [term_rows(): pl.pallas_call(functools.partial(term_kernel, first, added is not None, s...]
    pallas_call x5 -> x4, Pallas kernels: 0.59 us -> 2.64 us  [add(): pl.pallas_call(functools.partial(add_kernel, odd_only), out_shape=(jax.Sh...]
    ppermute x2, starting transfers between devices: 2.58 us -> 4.38 us  [raise_one(): return lax.ppermute(value, 'sec', up)]
    all_to_all x1, blocking collectives: 18.2 us -> 16.6 us  [sum_over_sectors(): arrived = lax.all_to_all(value, 'sec', 0, 0, tiled=True)]
    pallas_call x2 -> x1, Pallas kernels: 5.77 us -> 4.31 us  [opening_rows(): pl.pallas_call(functools.partial(opening_kernel, slot, masks, len(tokens)...]
  transfers between devices with their start and end apart: 12 -> 10, of which waited for: 3 -> 5; matrix products, arithmetic and copies ran while one was open for 0% -> 0% of each run, Pallas kernels for 20% -> 21%
where the time goes in v12:
time: 79 us; the launch traced here: 78.6 us
  Pallas kernels  24 us (30%)
  starting transfers between devices  19.3 us (24%)
  blocking collectives  16.6 us (21%)
  waiting for transfers between devices  15.2 us (19%)
  between operations  2.16 us (3%)
  local copies, waits for them, and re-layouts  1.32 us (2%)
    all_to_all x1, blocking collectives, sum_over_sectors(): arrived = lax.all_to_all(value, 'sec', 0, 0, tiled=True)  16.6 us
    ppermute x8, starting transfers between devices, send(): return lax.ppermute(value, 'sec', pairs)  14.9 us
    pallas_call x7, Pallas kernels, term_rows(): pl.pallas_call(functools.partial(term_kernel, first, added is not None, s...  13.1 us
    ppermute x8, waiting for transfers between devices, send(): return lax.ppermute(value, 'sec', pairs)  10.1 us
    ppermute x2, waiting for transfers between devices, raise_one(): return lax.ppermute(value, 'sec', up)  5.11 us
    ppermute x2, starting transfers between devices, raise_one(): return lax.ppermute(value, 'sec', up)  4.38 us
    pallas_call x1, Pallas kernels, opening_rows(): pl.pallas_call(functools.partial(opening_kernel, slot, masks, len(tokens)...  4.31 us
    pallas_call x2, Pallas kernels, finish(): pl.pallas_call(functools.partial(finish_kernel, first), out_shape=(jax.Sh...  3.31 us
  transfers between devices with their start and end apart: 10, of which 5 were waited for; matrix products, arithmetic and copies ran while one was open for 0% of the time, Pallas kernels for 21%

profile of v12, /device:TPU:0, one launch (start us, length us, event | category | flops | bytes accessed | tf_op | source)
XLA Modules:
  0.0 78.6 jit_solution(16107807958508281300)
XLA Ops:
  2.0 1.2 %copy-done.1 = bf16[1,1024,512]{2,1,0:T(8,128)(2,1)S(1)} copy-done((bf16[1,1024,512]{2,1,0:T(8,128)(2,1)S(1)}, bf16[1,1024,512]{2,1,0:T(8,128)(2,1)}, u32[]{:S(2)}) %copy-start.1) | copy-done | bytes 1048600
  3.3 4.3 %opening_rows.1 = (f32[640,512]{1,0:T(8,128)S(1)}, f32[8,128]{1,0:T(8,128)S(1)}, bf16[1024,512]{1,0:T(8,128)(2,1)S(1)}, bf16[1024,1024]{1,0:T(8,128)(2,1)S(1)}, ...) custom-call(s32[8]{0:T(128)S(1)} %stack.19.info_ref, ...), custom_call_target="tpu_custom_call" | custom-call | flops 200000000 | bytes 1000000 | tf_op jit(solution)/shard_map/opening_rows/pallas_call | solution.py:100
  8.1 2.9 %term_rows.7 = (f32[640,512]{1,0:T(8,128)S(1)}, f32[8,128]{1,0:T(8,128)S(1)}, bf16[1024,1024]{1,0:T(8,128)(2,1)S(1)}, bf16[512,512]{1,0:T(8,128)(2,1)S(1)}) custom-call(s32[8]{0:T(128)S(1)} %stack.19.info_ref, bf16[1024,512]{1,0:T(8,128)(2,1)S(1)} %get-tuple-element.41.live_ref, bf16[1024,1024]{1,0:T(8,128)(2,1)S(1)} %get-tuple-element.42.left_ref, ...), custom_call_target="tpu_custom_call" | custom-call | flops 200000000 | bytes 1000000 | tf_op jit(solution)/shard_map/term_rows/pallas_call | solution.py:156
  11.7 2.0 %collective-permute-start.4 = (f32[640,512]{1,0:T(8,128)S(1)}, f32[640,512]{1,0:T(8,128)S(1)}, u32[]{:S(2)}, u32[]{:S(2)}) collective-permute-start(f32[640,512]{1,0:T(8,128)S(1)} %get-tuple-element.63), channel_id=1, source_target_pairs={{1,2},{5,6},{9,10},{13,14},{3,0},{7,4},{11,8},{0,1},{2,3},{4,5},{6... | collective-permute-start | bytes 3932168 | tf_op jit(solution)/shard_map/ppermute | solution.py:337
  13.8 2.9 %term_rows.8 = (f32[640,512]{1,0:T(8,128)S(1)}, f32[8,128]{1,0:T(8,128)S(1)}, bf16[1024,1024]{1,0:T(8,128)(2,1)S(1)}, bf16[512,512]{1,0:T(8,128)(2,1)S(1)}) custom-call(s32[8]{0:T(128)S(1)} %stack.19.info_ref, bf16[1024,512]{1,0:T(8,128)(2,1)S(1)} %get-tuple-element.41.live_ref, bf16[1024,1024]{1,0:T(8,128)(2,1)S(1)} %get-tuple-element.45.left_ref, ...), custom_call_target="tpu_custom_call" | custom-call | flops 200000000 | bytes 1000000 | tf_op jit(solution)/shard_map/term_rows/pallas_call | solution.py:156
  16.7 0.7 collective-permute-start.3
  17.5 1.4 %term_rows.9 = (f32[384,512]{1,0:T(8,128)S(1)}, f32[8,128]{1,0:T(8,128)S(1)}) custom-call(s32[8]{0:T(128)S(1)} %stack.19.info_ref, bf16[1024,512]{1,0:T(8,128)(2,1)S(1)} %get-tuple-element.41.live_ref, bf16[1024,1024]{1,0:T(8,128)(2,1)S(1)} %get-tuple-element.45.left_ref, bf16[512,512]{1,0:T(8,128)(2,1)S(1)} %get-tuple-element.46.right_ref, ...), custom_call_target="tpu_custom_call" | custom-call | flops 200000000 | bytes 1000000 | tf_op jit(solution)/shard_map/term_rows/pallas_call | solution.py:156
  18.8 1.4 %term_rows.10 = (f32[384,512]{1,0:T(8,128)S(1)}, f32[8,128]{1,0:T(8,128)S(1)}) custom-call(s32[8]{0:T(128)S(1)} %stack.19.info_ref, bf16[1024,512]{1,0:T(8,128)(2,1)S(1)} %get-tuple-element.41.live_ref, bf16[1024,1024]{1,0:T(8,128)(2,1)S(1)} %get-tuple-element.53.left_ref, bf16[512,512]{1,0:T(8,128)(2,1)S(1)} %get-tuple-element.54.right_ref, ...), custom_call_target="tpu_custom_call" | custom-call | flops 200000000 | bytes 1000000 | tf_op jit(solution)/shard_map/term_rows/pallas_call | solution.py:156
  20.2 3.2 %collective-permute-start.1 = (f32[384,512]{1,0:T(8,128)S(1)}, f32[384,512]{1,0:T(8,128)S(1)}, u32[]{:S(2)}, u32[]{:S(2)}) collective-permute-start(f32[384,512]{1,0:T(8,128)S(1)} %get-tuple-element.57), channel_id=1, source_target_pairs={{0,1},{4,5},{8,9},{12,13},{1,0},{5,4},{9,8},{13,12},{2,3},{6,7},{1... | collective-permute-start | bytes 2359304 | tf_op jit(solution)/shard_map/ppermute | solution.py:321
  23.4 1.3 %term_rows.11 = (f32[384,512]{1,0:T(8,128)S(1)}, f32[8,128]{1,0:T(8,128)S(1)}) custom-call(s32[8]{0:T(128)S(1)} %stack.19.info_ref, bf16[1024,512]{1,0:T(8,128)(2,1)S(1)} %get-tuple-element.41.live_ref, bf16[1024,1024]{1,0:T(8,128)(2,1)S(1)} %get-tuple-element.42.left_ref, bf16[512,512]{1,0:T(8,128)(2,1)S(1)} %get-tuple-element.43.right_ref, ...), custom_call_target="tpu_custom_call" | custom-call | flops 200000000 | bytes 1000000 | tf_op jit(solution)/shard_map/term_rows/pallas_call | solution.py:156
  25.9 2.3 %collective-permute-start.2 = (f32[384,512]{1,0:T(8,128)S(1)}, f32[384,512]{1,0:T(8,128)S(1)}, u32[]{:S(2)}, u32[]{:S(2)}) collective-permute-start(f32[384,512]{1,0:T(8,128)S(1)} %get-tuple-element.61), channel_id=1, source_target_pairs={{1,2},{5,6},{9,10},{13,14},{3,0},{7,4},{11,8},{0,1},{2,3},{4,5},{6... | collective-permute-start | bytes 2359304 | tf_op jit(solution)/shard_map/ppermute | solution.py:337
  29.0 2.6 %collective-permute-done.4.refs_0_ = f32[640,512]{1,0:T(8,128)S(1)} collective-permute-done((f32[640,512]{1,0:T(8,128)S(1)}, f32[640,512]{1,0:T(8,128)S(1)}, u32[]{:S(2)}, u32[]{:S(2)}) %collective-permute-start.4) | collective-permute-done | bytes 1310752 | tf_op jit(solution)/shard_map/ppermute | solution.py:337
  31.6 4.7 %collective-permute-start.6 = (f32[640,512]{1,0:T(8,128)S(1)}, f32[640,512]{1,0:T(8,128)S(1)}, u32[]{:S(2)}, u32[]{:S(2)}) collective-permute-start(f32[640,512]{1,0:T(8,128)S(1)} %get-tuple-element.68.refs_1_.a_ref), channel_id=1, source_target_pairs={{0,4},{4,8},{8,12},{16,20},{20,24},{24,28}} | collective-permute-start | bytes 3932168 | tf_op jit(solution)/shard_map/ppermute | solution.py:321
  36.3 0.7 add_blocks.6
  37.0 0.7 collective-permute-start.7
  37.8 2.5 %collective-permute-done.2.refs_0_ = f32[384,512]{1,0:T(8,128)S(1)} collective-permute-done((f32[384,512]{1,0:T(8,128)S(1)}, f32[384,512]{1,0:T(8,128)S(1)}, u32[]{:S(2)}, u32[]{:S(2)}) %collective-permute-start.2) | collective-permute-done | bytes 786464 | tf_op jit(solution)/shard_map/ppermute | solution.py:337
  40.3 3.6 %collective-permute-start.8 = (f32[384,512]{1,0:T(8,128)S(1)}, f32[384,512]{1,0:T(8,128)S(1)}, u32[]{:S(2)}, u32[]{:S(2)}) collective-permute-start(f32[384,512]{1,0:T(8,128)S(1)} %get-tuple-element.67.refs_1_.a_ref), channel_id=1, source_target_pairs={{0,4},{4,8},{8,12},{16,20},{20,24},{24,28}} | collective-permute-start | bytes 2359304 | tf_op jit(solution)/shard_map/ppermute | solution.py:321
  45.3 1.8 %term_rows.12 = (f32[640,512]{1,0:T(8,128)S(1)}, f32[8,128]{1,0:T(8,128)}) custom-call(s32[8]{0:T(128)S(1)} %stack.19.info_ref, bf16[1024,512]{1,0:T(8,128)(2,1)S(1)} %get-tuple-element.41.live_ref, bf16[1024,1024]{1,0:T(8,128)(2,1)S(1)} %get-tuple-element.51.left_ref, bf16[512,512]{1,0:T(8,128)(2,1)S(1)} %get-tuple-element.52.right_ref, ...), custom_call_target="tpu_custom_call" | custom-call | flops 200000000 | bytes 1000000 | tf_op jit(solution)/shard_map/term_rows/pallas_call | solution.py:156
  47.0 4.3 %collective-permute-done.6.b_ref = f32[640,512]{1,0:T(8,128)S(1)} collective-permute-done((f32[640,512]{1,0:T(8,128)S(1)}, f32[640,512]{1,0:T(8,128)S(1)}, u32[]{:S(2)}, u32[]{:S(2)}) %collective-permute-start.6) | collective-permute-done | bytes 1310752 | tf_op jit(solution)/shard_map/ppermute | solution.py:321
  51.3 1.8 %finish_rows.2 = (bf16[1,1024,512]{2,1,0:T(8,128)(2,1)}, f32[16,128]{1,0:T(8,128)S(1)}) custom-call(s32[8]{0:T(128)S(1)} %stack.19.info_ref, bf16[1024,512]{1,0:T(8,128)(2,1)S(1)} %get-tuple-element.41.live_ref, f32[640,512]{1,0:T(8,128)S(1)} %get-tuple-element.72.own_ref, f32[640,512]{1,0:T(8,128)S(1)} %get-tuple-element.68.refs_1_.a_ref, ...), custom_call_target="tpu_custom_call" | custom-call | flops 200000000 | bytes 1000000 | tf_op jit(solution)/shard_map/finish_rows/pallas_call | solution.py:275
  53.1 1.4 %term_rows.13 = (f32[384,512]{1,0:T(8,128)S(1)}, f32[8,128]{1,0:T(8,128)}) custom-call(s32[8]{0:T(128)S(1)} %stack.19.info_ref, bf16[1024,512]{1,0:T(8,128)(2,1)S(1)} %get-tuple-element.41.live_ref, bf16[1024,1024]{1,0:T(8,128)(2,1)S(1)} %get-tuple-element.51.left_ref, bf16[512,512]{1,0:T(8,128)(2,1)S(1)} %get-tuple-element.52.right_ref, ...), custom_call_target="tpu_custom_call" | custom-call | flops 200000000 | bytes 1000000 | tf_op jit(solution)/shard_map/term_rows/pallas_call | solution.py:156
  54.5 5.3 %collective-permute-done.8.b_ref = f32[384,512]{1,0:T(8,128)S(1)} collective-permute-done((f32[384,512]{1,0:T(8,128)S(1)}, f32[384,512]{1,0:T(8,128)S(1)}, u32[]{:S(2)}, u32[]{:S(2)}) %collective-permute-start.8) | collective-permute-done | bytes 786464 | tf_op jit(solution)/shard_map/ppermute | solution.py:321
  59.8 1.5 %finish_rows.3 = (bf16[1,1024,512]{2,1,0:T(8,128)(2,1)}, f32[16,128]{1,0:T(8,128)S(1)}) custom-call(s32[8]{0:T(128)S(1)} %stack.19.info_ref, bf16[1024,512]{1,0:T(8,128)(2,1)S(1)} %get-tuple-element.41.live_ref, f32[384,512]{1,0:T(8,128)S(1)} %get-tuple-element.75.own_ref, ...), custom_call_target="tpu_custom_call", output_to_operand_aliasing={{0}: (7, {})} | custom-call | flops 200000000 | bytes 1000000 | tf_op jit(solution)/shard_map/finish_rows/pallas_call | solution.py:275
  61.3 16.6 %all_to_all.11 = f32[16,1,128]{2,1,0:T(1,128)S(1)} all-to-all(f32[16,1,128]{2,1,0:T(1,128)S(1)} %bitcast.10), channel_id=1, replica_groups=mesh['grp'=2,'sec'=16] {'sec'}, dimensions={0} | all-to-all | bytes 16384 | tf_op jit(solution)/shard_map/all_to_all | solution.py:296
  (20 shorter events, 5.2 us)
Async XLA Ops:
  2.0 1.2 %copy-start.1 = (bf16[1,1024,512]{2,1,0:T(8,128)(2,1)S(1)}, bf16[1,1024,512]{2,1,0:T(8,128)(2,1)}, u32[]{:S(2)}) copy-start(bf16[1,1024,512]{2,1,0:T(8,128)(2,1)} %param.5) | copy-start | bytes 3145732
  3.3 4.8 %copy-start = (bf16[1,4,512,512]{3,2,1,0:T(8,128)(2,1)S(1)}, bf16[1,4,512,512]{3,2,1,0:T(8,128)(2,1)}, u32[]{:S(2)}) copy-start(bf16[1,4,512,512]{3,2,1,0:T(8,128)(2,1)} %refs_1_.3) | copy-start | bytes 6291460
  7.6 3.5 %collective-permute-start = (f32[640,512]{1,0:T(8,128)S(1)}, f32[640,512]{1,0:T(8,128)S(1)}, u32[]{:S(2)}, u32[]{:S(2)}) collective-permute-start(f32[640,512]{1,0:T(8,128)S(1)} %get-tuple-element.48), channel_id=1, source_target_pairs={{0,1},{4,5},{8,9},{12,13},{1,0},{5,4},{9,8},{13,12},{2,3},{6,7},{1... | collective-permute-start | bytes 3932168 | tf_op jit(solution)/shard_map/ppermute | solution.py:321
  11.7 19.9 %collective-permute-start.4 = (f32[640,512]{1,0:T(8,128)S(1)}, f32[640,512]{1,0:T(8,128)S(1)}, u32[]{:S(2)}, u32[]{:S(2)}) collective-permute-start(f32[640,512]{1,0:T(8,128)S(1)} %get-tuple-element.63), channel_id=1, source_target_pairs={{1,2},{5,6},{9,10},{13,14},{3,0},{7,4},{11,8},{0,1},{2,3},{4,5},{6... | collective-permute-start | bytes 3932168 | tf_op jit(solution)/shard_map/ppermute | solution.py:337
  16.7 19.6 %collective-permute-start.3 = (f32[640,512]{1,0:T(8,128)S(1)}, f32[640,512]{1,0:T(8,128)S(1)}, u32[]{:S(2)}, u32[]{:S(2)}) collective-permute-start(f32[640,512]{1,0:T(8,128)S(1)} %get-tuple-element.62.a_ref), channel_id=1, source_target_pairs={{3,6},{7,10},{11,14},{4,1},{8,5},{12,9},{19,22},{23,26},{27,30},{2... | collective-permute-start | bytes 3932168 | tf_op jit(solution)/shard_map/ppermute | solution.py:321
  20.2 5.1 %collective-permute-start.1 = (f32[384,512]{1,0:T(8,128)S(1)}, f32[384,512]{1,0:T(8,128)S(1)}, u32[]{:S(2)}, u32[]{:S(2)}) collective-permute-start(f32[384,512]{1,0:T(8,128)S(1)} %get-tuple-element.57), channel_id=1, source_target_pairs={{0,1},{4,5},{8,9},{12,13},{1,0},{5,4},{9,8},{13,12},{2,3},{6,7},{1... | collective-permute-start | bytes 2359304 | tf_op jit(solution)/shard_map/ppermute | solution.py:321
  25.9 14.4 %collective-permute-start.2 = (f32[384,512]{1,0:T(8,128)S(1)}, f32[384,512]{1,0:T(8,128)S(1)}, u32[]{:S(2)}, u32[]{:S(2)}) collective-permute-start(f32[384,512]{1,0:T(8,128)S(1)} %get-tuple-element.61), channel_id=1, source_target_pairs={{1,2},{5,6},{9,10},{13,14},{3,0},{7,4},{11,8},{0,1},{2,3},{4,5},{6... | collective-permute-start | bytes 2359304 | tf_op jit(solution)/shard_map/ppermute | solution.py:337
  28.2 15.6 %collective-permute-start.5 = (f32[384,512]{1,0:T(8,128)S(1)}, f32[384,512]{1,0:T(8,128)S(1)}, u32[]{:S(2)}, u32[]{:S(2)}) collective-permute-start(f32[384,512]{1,0:T(8,128)S(1)} %get-tuple-element.69.a_ref), channel_id=1, source_target_pairs={{3,6},{7,10},{11,14},{4,1},{8,5},{12,9},{19,22},{23,26},{27,30},{2... | collective-permute-start | bytes 2359304 | tf_op jit(solution)/shard_map/ppermute | solution.py:321
  31.6 19.7 %collective-permute-start.6 = (f32[640,512]{1,0:T(8,128)S(1)}, f32[640,512]{1,0:T(8,128)S(1)}, u32[]{:S(2)}, u32[]{:S(2)}) collective-permute-start(f32[640,512]{1,0:T(8,128)S(1)} %get-tuple-element.68.refs_1_.a_ref), channel_id=1, source_target_pairs={{0,4},{4,8},{8,12},{16,20},{20,24},{24,28}} | collective-permute-start | bytes 3932168 | tf_op jit(solution)/shard_map/ppermute | solution.py:321
  37.0 14.3 %collective-permute-start.7 = (f32[640,512]{1,0:T(8,128)S(1)}, f32[640,512]{1,0:T(8,128)S(1)}, u32[]{:S(2)}, u32[]{:S(2)}) collective-permute-start(f32[640,512]{1,0:T(8,128)S(1)} %get-tuple-element.73), channel_id=1, source_target_pairs={{1,3},{5,7},{9,11},{13,15},{2,1},{6,5},{10,9},{14,13},{17,19},{21,... | collective-permute-start | bytes 3932168 | tf_op jit(solution)/shard_map/ppermute | solution.py:321
  40.3 19.5 %collective-permute-start.8 = (f32[384,512]{1,0:T(8,128)S(1)}, f32[384,512]{1,0:T(8,128)S(1)}, u32[]{:S(2)}, u32[]{:S(2)}) collective-permute-start(f32[384,512]{1,0:T(8,128)S(1)} %get-tuple-element.67.refs_1_.a_ref), channel_id=1, source_target_pairs={{0,4},{4,8},{8,12},{16,20},{20,24},{24,28}} | collective-permute-start | bytes 2359304 | tf_op jit(solution)/shard_map/ppermute | solution.py:321
  44.5 15.2 %collective-permute-start.9 = (f32[384,512]{1,0:T(8,128)S(1)}, f32[384,512]{1,0:T(8,128)S(1)}, u32[]{:S(2)}, u32[]{:S(2)}) collective-permute-start(f32[384,512]{1,0:T(8,128)S(1)} %get-tuple-element.76), channel_id=1, source_target_pairs={{1,3},{5,7},{9,11},{13,15},{2,1},{6,5},{10,9},{14,13},{17,19},{21,... | collective-permute-start | bytes 2359304 | tf_op jit(solution)/shard_map/ppermute | solution.py:321

commit v13 on v12

--- a/solution.py
+++ b/solution.py
@@ -8,9 +8,9 @@
 from jax.sharding import PartitionSpec as P
 
 MIB = 1024 * 1024
-LEFT_PIECES, RIGHT_PIECES = 8, 2
-FIRST_MIB = 44
-BRING_MIB = 42
+PIECE = 128
+FIRST_MIB = 48
+BRING_MIB = 44
 
 ANY = pl.BlockSpec(memory_space=pl.ANY)
 HBM = pl.BlockSpec(memory_space=pltpu.HBM)
@@ -24,26 +24,87 @@
     return pltpu.CompilerParams(vmem_limit_bytes=mib * MIB)
 
 
-def fetch(info_ref, slot, count, left_hbm, right_hbm, left_ref, right_ref, sems):
+def fetch(info_ref, bring, left_hbm, right_hbm, left_ref, right_ref, sems):
+    slot, first, count, _ = bring
     term = info_ref[slot]
-    rows, cols = left_ref.shape[0], right_ref.shape[0]
-    step = rows // LEFT_PIECES
-    left, right = [], []
-    for i in range(LEFT_PIECES):
-        span = pl.ds(i * step, step)
-        left.append(
-            pltpu.make_async_copy(left_hbm.at[0, term, span, :], left_ref.at[span, :], sems.at[i])
-        )
-    step = cols // RIGHT_PIECES
-    for i in range(RIGHT_PIECES):
-        span = pl.ds(i * step, step)
-        right.append(
-            pltpu.make_async_copy(
-                right_hbm.at[0, term, span, :], right_ref.at[span, :], sems.at[LEFT_PIECES + i]
+    copies = []
+    for i in range(count // PIECE):
+        there = left_hbm.at[0, term, pl.ds(first + i * PIECE, PIECE), :]
+        here = left_ref.at[pl.ds(i * PIECE, PIECE), :]
+        copies.append(pltpu.make_async_copy(there, here, sems.at[len(copies)]))
+    if right_ref is not None:
+        for i in range(right_ref.shape[0] // (2 * PIECE)):
+            span = pl.ds(i * 2 * PIECE, 2 * PIECE)
+            there = right_hbm.at[0, term, span, :]
+            copies.append(
+                pltpu.make_async_copy(there, right_ref.at[span, :], sems.at[len(copies)])
             )
-        )
-    first = -(-count * LEFT_PIECES // rows)
-    return left[:first] + right, left[first:]
+    return copies
+
+
+def operand_shapes(width, cols, brings):
+    shapes = []
+    for _, _, count, with_right in brings:
+        shapes.append(jax.ShapeDtypeStruct((count, width), jnp.bfloat16))
+        if with_right:
+            shapes.append(jax.ShapeDtypeStruct((cols, cols), jnp.bfloat16))
+    return shapes
+
+
+def fetch_all(info_ref, brings, left_hbm, right_hbm, refs, sems):
+    copies = []
+    for i, bring in enumerate(brings):
+        left_ref = refs.pop(0)
+        right_ref = refs.pop(0) if bring[3] else None
+        copies += fetch(info_ref, bring, left_hbm, right_hbm, left_ref, right_ref, sems.at[i])
+    return copies
+
+
+def first_kernel(count, brings, info_ref, psi_ref, left_hbm, right_hbm, *refs):
+    out_ref, _, live_ref, right_ref = refs[:4]
+    left_ref, sems, own_sems = refs[-3:]
+    own = fetch(info_ref, (0, 0, count, True), left_hbm, right_hbm, left_ref, right_ref, own_sems)
+    copies = fetch_all(info_ref, brings, left_hbm, right_hbm, list(refs[4:-3]), sems)
+    for copy in own:
+        copy.start()
+    rows, cols = psi_ref.shape
+    step = 128
+    col = lax.broadcasted_iota(jnp.int32, (step, cols), 1) < info_ref[5]
+    row = lax.broadcasted_iota(jnp.int32, (step, cols), 0)
+    for start in range(0, rows, step):
+        span = pl.ds(start, step)
+        inside = jnp.logical_and(row < info_ref[4] - start, col)
+        values = jnp.where(inside, psi_ref[span, :].astype(jnp.float32), 0.0)
+        live_ref[span, :] = values.astype(live_ref.dtype)
+    for copy in own:
+        copy.wait()
+    for copy in copies:
+        copy.start()
+    out_ref[...] = multiply(left_ref[...], live_ref[...], right_ref[...])
+    for copy in copies:
+        copy.wait()
+
+
+def first_rows(info, psi, envs, count, brings):
+    rows, cols = psi.shape
+    out_shape = [jax.ShapeDtypeStruct((count, cols), jnp.float32), TOKEN]
+    out_shape.append(jax.ShapeDtypeStruct(psi.shape, psi.dtype))
+    out_shape.append(jax.ShapeDtypeStruct((cols, cols), jnp.bfloat16))
+    out_shape += operand_shapes(rows, cols, brings)
+    return pl.pallas_call(
+        functools.partial(first_kernel, count, brings),
+        out_shape=out_shape,
+        in_specs=[SMEM, WHOLE, HBM, HBM],
+        out_specs=[WHOLE, ANY] + [WHOLE] * (len(out_shape) - 2),
+        scratch_shapes=[
+            pltpu.VMEM((count, rows), jnp.bfloat16),
+            pltpu.SemaphoreType.DMA((len(brings), 16)),
+            pltpu.SemaphoreType.DMA((16,)),
+        ],
+        compiler_params=params(FIRST_MIB),
+        cost_estimate=SMALL,
+        name="first_rows",
+    )(info, psi, *envs)
 
 
 def multiply(left, live, right):
@@ -51,115 +112,49 @@
     return jnp.dot(first, right, preferred_element_type=jnp.float32)
 
 
-def opening_kernel(slot, masks, tokens, info_ref, live_ref, left_hbm, right_hbm, *refs):
-    refs = list(refs[tokens:])
-    out_ref, _ = refs[:2]
-    sems = refs[-1]
-    operands = refs[2:-1]
-    psi_ref = live_ref
-    if masks:
-        live_ref = operands.pop(0)
-    own, late = fetch(info_ref, slot, out_ref.shape[0], left_hbm, right_hbm, *operands[:2], sems.at[0])
-    for copy in own:
-        copy.start()
-    if len(operands) > 2:
-        later = fetch(info_ref, slot + 1, 0, left_hbm, right_hbm, *operands[2:], sems.at[1])
-        late = late + later[0] + later[1]
-    if masks:
-        rows, cols = psi_ref.shape
-        step = 128
-        col = lax.broadcasted_iota(jnp.int32, (step, cols), 1) < info_ref[5]
-        row = lax.broadcasted_iota(jnp.int32, (step, cols), 0)
-        for start in range(0, rows, step):
-            span = pl.ds(start, step)
-            inside = jnp.logical_and(row < info_ref[4] - start, col)
-            values = jnp.where(inside, psi_ref[span, :].astype(jnp.float32), 0.0)
-            live_ref[span, :] = values.astype(live_ref.dtype)
-    for copy in own:
-        copy.wait()
-    for copy in late:
-        copy.start()
-    out_ref[...] = multiply(operands[0][: out_ref.shape[0], :], live_ref[...], operands[1][...])
-    for copy in late:
-        copy.wait()
-
-
-def operand_shapes(width, cols):
-    return [
-        jax.ShapeDtypeStruct((width, width), jnp.bfloat16),
-        jax.ShapeDtypeStruct((cols, cols), jnp.bfloat16),
-    ]
-
-
-def opening_rows(info, live, envs, slot, count, *tokens, masks=False):
-    width, cols = live.shape
-    out_shape = [jax.ShapeDtypeStruct((count, cols), jnp.float32), TOKEN]
-    if masks:
-        out_shape.append(jax.ShapeDtypeStruct(live.shape, live.dtype))
-    out_shape += operand_shapes(width, cols) * 2
-    return pl.pallas_call(
-        functools.partial(opening_kernel, slot, masks, len(tokens)),
-        out_shape=out_shape,
-        in_specs=[SMEM, WHOLE, HBM, HBM] + [ANY] * len(tokens),
-        out_specs=[WHOLE, ANY] + [WHOLE] * (len(out_shape) - 2),
-        scratch_shapes=[pltpu.SemaphoreType.DMA((2, LEFT_PIECES + RIGHT_PIECES))],
-        compiler_params=params(FIRST_MIB if masks else BRING_MIB),
-        cost_estimate=SMALL,
-        name="opening_rows",
-    )(info, live, *envs, *tokens)
-
-
-def term_kernel(first, adds, slot, tokens, info_ref, live_ref, left_ref, right_ref, *refs):
+def term_kernel(adds, brings, tokens, info_ref, live_ref, left_ref, right_ref, *refs):
     refs = list(refs)
     add_refs = [refs.pop(0), refs.pop(0)] if adds else None
     copies = []
-    if slot is not None:
+    if brings:
         left_hbm, right_hbm = refs[:2]
-        sems = refs[-1]
-        out_ref, _, left_next, right_next = refs[2 + tokens : -1]
-        copies = sum(fetch(info_ref, slot, 0, left_hbm, right_hbm, left_next, right_next, sems), [])
+        refs = refs[2:]
+        sems = refs.pop()
+    out_ref = refs[tokens]
+    if brings:
+        copies = fetch_all(info_ref, brings, left_hbm, right_hbm, refs[tokens + 2 :], sems)
         for copy in copies:
             copy.start()
-    else:
-        out_ref, _ = refs[tokens:]
-    count = out_ref.shape[0]
-    block = count
-    for i in range(count // block):
-        span = pl.ds(i * block, block)
-        value = multiply(left_ref[pl.ds(first + i * block, block), :], live_ref[...], right_ref[...])
-        if adds:
-            odd = info_ref[7] == 1
-            value = value + jnp.where(odd, add_refs[1][span, :], add_refs[0][span, :])
-        out_ref[span, :] = value
+    value = multiply(left_ref[...], live_ref[...], right_ref[...])
+    if adds:
+        odd = info_ref[7] == 1
+        value = value + jnp.where(odd, add_refs[1][...], add_refs[0][...])
+    out_ref[...] = value
     for copy in copies:
         copy.wait()
 
 
-def term_rows(info, live, operands, first, count, *tokens, added=None, bring=None):
+def term_rows(info, live, envs, left, right, *tokens, added=None, brings=()):
     width, cols = live.shape
     in_specs = [SMEM, WHOLE, WHOLE, WHOLE]
-    args = [info, live, *operands]
-    out_shape = [jax.ShapeDtypeStruct((count, cols), jnp.float32), TOKEN]
-    out_specs = [WHOLE, ANY]
+    args = [info, live, left, right]
+    out_shape = [jax.ShapeDtypeStruct((left.shape[0], cols), jnp.float32), TOKEN]
     scratch = []
-    slot = None
     if added is not None:
         in_specs += [WHOLE, WHOLE]
         args += added
-    if bring is not None:
-        slot = bring[0]
+    if brings:
         in_specs += [HBM, HBM]
-        args += bring[1:]
-        out_shape += operand_shapes(width, cols)
-        out_specs += [WHOLE, WHOLE]
-        scratch.append(pltpu.SemaphoreType.DMA((LEFT_PIECES + RIGHT_PIECES,)))
-    return pl.pallas_call(
-        functools.partial(term_kernel, first, added is not None, slot, len(tokens)),
+        args += envs
+        out_shape += operand_shapes(width, cols, brings)
+        scratch.append(pltpu.SemaphoreType.DMA((len(brings), 16)))
+    return pl.pallas_call(
+        functools.partial(term_kernel, added is not None, brings, len(tokens)),
         out_shape=out_shape,
         in_specs=in_specs + [ANY] * len(tokens),
-        out_specs=out_specs,
+        out_specs=[WHOLE, ANY] + [WHOLE] * (len(out_shape) - 2),
         scratch_shapes=scratch,
-        compiler_params=params(12 if slot is None else BRING_MIB),
+        compiler_params=params(BRING_MIB if brings else 12),
         cost_estimate=SMALL,
         name="term_rows",
     )(*args, *tokens)
@@ -229,7 +224,7 @@
     sigma_hbm, energy_ref, sigma_buf, sems = refs[-4:]
     count, cols = own_ref.shape
     step = 64
-    piece = 64
+    piece = PIECE
     col = lax.broadcasted_iota(jnp.int32, (step, cols), 1) < info_ref[5]
     row = lax.broadcasted_iota(jnp.int32, (step, cols), 0)
 
@@ -280,7 +275,7 @@
         ),
         in_specs=in_specs,
         out_specs=(ANY, WHOLE),
-        scratch_shapes=[pltpu.VMEM((count, cols), jnp.bfloat16), pltpu.SemaphoreType.DMA((count // 64,))],
+        scratch_shapes=[pltpu.VMEM((count, cols), jnp.bfloat16), pltpu.SemaphoreType.DMA((count // PIECE,))],
         input_output_aliases=aliases,
         compiler_params=params(),
         cost_estimate=SMALL,
@@ -346,19 +341,26 @@
         return send(value, (0, 4))
 
     envs = (left_env, right_env)
-    first0, token, live, *ops = opening_rows(info, psi[0], envs, 0, part, masks=True)
-    ops0, ops1 = ops[:2], ops[2:]
+
+    def term(left, right, *tokens, **more):
+        return term_rows(info, live, envs, left, right, *tokens, **more)
+
+    first0, token, live, right0, left, right1 = first_rows(
+        info, psi[0], envs, part, ((1, 0, part, True),)
+    )
     swapped0 = swap(first0)
-    second0, token, *ops2 = term_rows(info, live, ops1, 0, part, token, bring=(2, *envs))
+    second0, token, left, right2 = term(left, right1, token, brings=((2, 0, part, True),))
     both0, token = add(info, second0, swapped0, token, odd_only=True)
     raised0 = raise_one(both0)
-    third0, token, *ops3 = term_rows(info, live, ops2, 0, part, token, bring=(3, *envs))
+    third0, token, left, left1 = term(
+        left, right2, token, brings=((2, part, rest, False), (1, part, rest, False))
+    )
     moved0 = along(third0)
-    third1, token = term_rows(info, live, ops2, part, rest, token)
+    third1, token, left = term(left, right2, token, brings=((0, part, rest, False),))
     moved1 = along(third1)
-    first1, token = term_rows(info, live, ops0, part, rest, token)
+    first1, token, left3, right3 = term(left, right0, token, brings=((3, 0, part, True),))
     swapped1 = swap(first1)
-    second1, token = term_rows(info, live, ops1, part, rest, token)
+    second1, token, left = term(left1, right1, token, brings=((3, part, rest, False),))
     both1, token = add(info, second1, swapped1, token, odd_only=True)
     raised1 = raise_one(both1)
     raised0, token = hold(raised0, token)
@@ -369,11 +371,12 @@
     relayed1 = relay(raised1)
     summed1, token = add(info, third1, moved1, token)
     crossed1 = across(summed1)
-    own0, token = term_rows(info, live, ops3, 0, part, token, added=(swapped0, raised0))
+    token = touch(relayed0, token)
+    own0, token = term(left3, right3, token, added=(swapped0, raised0))
+
     energy = jnp.zeros((sectors, 128), jnp.float32)
     sigma, energy = finish(info, live, own0, (raised0, relayed0, crossed0), energy, None, 0)
-    token = energy
-    own1, token = term_rows(info, live, ops3, part, rest, token, added=(swapped1, raised1))
+    own1, token = term(left, right3, token, energy, added=(swapped1, raised1))
     sigma, energy = finish(info, live, own1, (raised1, relayed1, crossed1), energy, sigma, part)
     return sigma, sum_over_sectors(energy)
 

time: 79 us -> 78.4 us (level)
  starting transfers between devices: 19.3 us -> 24.3 us
  waiting for transfers between devices: 15.2 us -> 10.6 us
  blocking collectives: 16.6 us -> 15.1 us
    ppermute x8, starting transfers between devices: 14.9 us -> 19.9 us  [send(): return lax.ppermute(value, 'sec', pairs)]
    ppermute x8, waiting for transfers between devices: 10.1 us -> 7.55 us  [send(): return lax.ppermute(value, 'sec', pairs)]
    ppermute x2, waiting for transfers between devices: 5.11 us -> 3 us  [raise_one(): return lax.ppermute(value, 'sec', up)]
    all_to_all x1, blocking collectives: 16.6 us -> 15.1 us  [sum_over_sectors(): arrived = lax.all_to_all(value, 'sec', 0, 0, tiled=True)]
    pallas_call x8 -> x9, Pallas kernels: 17.4 us -> 18.2 us  [the longest x7 14.4 us: term_rows(): pl.pallas_call(functools.partial(term_kernel, added is not None, brings,...]
  transfers between devices with their start and end apart: 10 -> 10, of which waited for: 5 -> 5; matrix products, arithmetic and copies ran while one was open for 0% -> 0% of each run, Pallas kernels for 21% -> 23%
where the time goes in v13:
time: 78.4 us; the launch traced here: 77.9 us
  Pallas kernels  24.6 us (31%)
  starting transfers between devices  24.3 us (31%)
  blocking collectives  15.1 us (19%)
  waiting for transfers between devices  10.6 us (14%)
  between operations  2.17 us (3%)
  local copies, waits for them, and re-layouts  1.32 us (2%)
    ppermute x8, starting transfers between devices, send(): return lax.ppermute(value, 'sec', pairs)  19.9 us
    all_to_all x1, blocking collectives, sum_over_sectors(): arrived = lax.all_to_all(value, 'sec', 0, 0, tiled=True)  15.1 us
    pallas_call x7, Pallas kernels, term_rows(): pl.pallas_call(functools.partial(term_kernel, added is not None, brings,...  14.4 us
    ppermute x8, waiting for transfers between devices, send(): return lax.ppermute(value, 'sec', pairs)  7.55 us
    ppermute x2, starting transfers between devices, raise_one(): return lax.ppermute(value, 'sec', up)  4.31 us
    pallas_call x1, Pallas kernels, first_rows(): pl.pallas_call(functools.partial(first_kernel, count, brings), out_shape=...  3.77 us
    pallas_call x2, Pallas kernels, finish(): pl.pallas_call(functools.partial(finish_kernel, first), out_shape=(jax.Sh...  3.07 us
    ppermute x2, waiting for transfers between devices, raise_one(): return lax.ppermute(value, 'sec', up)  3 us
  transfers between devices with their start and end apart: 10, of which 5 were waited for; matrix products, arithmetic and copies ran while one was open for 0% of the time, Pallas kernels for 23%

profile of v13, /device:TPU:0, one launch (start us, length us, event | category | flops | bytes accessed | tf_op | source)
XLA Modules:
  0.0 77.9 jit_solution(3343465659479930934)
XLA Ops:
  2.0 1.2 %copy-done.1 = bf16[1,1024,512]{2,1,0:T(8,128)(2,1)S(1)} copy-done((bf16[1,1024,512]{2,1,0:T(8,128)(2,1)S(1)}, bf16[1,1024,512]{2,1,0:T(8,128)(2,1)}, u32[]{:S(2)}) %copy-start.1) | copy-done | bytes 1048600
  3.3 3.8 %first_rows.1 = (f32[640,512]{1,0:T(8,128)S(1)}, f32[8,128]{1,0:T(8,128)S(1)}, bf16[1024,512]{1,0:T(8,128)(2,1)S(1)}, bf16[512,512]{1,0:T(8,128)(2,1)S(1)}, bf16...) custom-call(s32[8]{0:T(128)S(1)} %stack.19.info_ref, bf16[1024,512]{1,0:T(8,128)(2,1)S(1)} %bitcast.9, ...), custom_call_target="tpu_custom_call" | custom-call | flops 200000000 | bytes 1000000 | tf_op jit(solution)/shard_map/first_rows/pallas_call | solution.py:94
  7.6 2.0 %term_rows.7 = (f32[640,512]{1,0:T(8,128)S(1)}, f32[8,128]{1,0:T(8,128)S(1)}, bf16[640,1024]{1,0:T(8,128)(2,1)S(1)}, bf16[512,512]{1,0:T(8,128)(2,1)S(1)}) custom-call(s32[8]{0:T(128)S(1)} %stack.19.info_ref, bf16[1024,512]{1,0:T(8,128)(2,1)S(1)} %get-tuple-element.45.live_ref, bf16[640,1024]{1,0:T(8,128)(2,1)S(1)} %get-tuple-element.46.left_ref, ...), custom_call_target="tpu_custom_call" | custom-call | flops 200000000 | bytes 1000000 | tf_op jit(solution)/shard_map/term_rows/pallas_call | solution.py:151
  10.9 2.3 %collective-permute-start.4 = (f32[640,512]{1,0:T(8,128)S(1)}, f32[640,512]{1,0:T(8,128)S(1)}, u32[]{:S(2)}, u32[]{:S(2)}) collective-permute-start(f32[640,512]{1,0:T(8,128)S(1)} %get-tuple-element.69), channel_id=1, source_target_pairs={{1,2},{5,6},{9,10},{13,14},{3,0},{7,4},{11,8},{0,1},{2,3},{4,5},{6... | collective-permute-start | bytes 3932168 | tf_op jit(solution)/shard_map/ppermute | solution.py:332
  13.2 2.9 %term_rows.8 = (f32[640,512]{1,0:T(8,128)S(1)}, f32[8,128]{1,0:T(8,128)S(1)}, bf16[384,1024]{1,0:T(8,128)(2,1)S(1)}, bf16[384,1024]{1,0:T(8,128)(2,1)S(1)}) custom-call(s32[8]{0:T(128)S(1)} %stack.19.info_ref, bf16[1024,512]{1,0:T(8,128)(2,1)S(1)} %get-tuple-element.45.live_ref, bf16[640,1024]{1,0:T(8,128)(2,1)S(1)} %get-tuple-element.49.left_ref, ...), custom_call_target="tpu_custom_call" | custom-call | flops 200000000 | bytes 1000000 | tf_op jit(solution)/shard_map/term_rows/pallas_call | solution.py:151
  16.1 0.7 collective-permute-start.3
  16.9 2.3 %term_rows.9 = (f32[384,512]{1,0:T(8,128)S(1)}, f32[8,128]{1,0:T(8,128)S(1)}, bf16[384,1024]{1,0:T(8,128)(2,1)S(1)}) custom-call(s32[8]{0:T(128)S(1)} %stack.19.info_ref, bf16[1024,512]{1,0:T(8,128)(2,1)S(1)} %get-tuple-element.45.live_ref, bf16[384,1024]{1,0:T(8,128)(2,1)S(1)} %get-tuple-element.56.left_ref, ...), custom_call_target="tpu_custom_call" | custom-call | flops 200000000 | bytes 1000000 | tf_op jit(solution)/shard_map/term_rows/pallas_call | solution.py:151
  19.1 2.0 %term_rows.10 = (f32[384,512]{1,0:T(8,128)S(1)}, f32[8,128]{1,0:T(8,128)S(1)}, bf16[640,1024]{1,0:T(8,128)(2,1)S(1)}, bf16[512,512]{1,0:T(8,128)(2,1)S(1)}) custom-call(s32[8]{0:T(128)S(1)} %stack.19.info_ref, bf16[1024,512]{1,0:T(8,128)(2,1)S(1)} %get-tuple-element.45.live_ref, bf16[384,1024]{1,0:T(8,128)(2,1)S(1)} %get-tuple-element.58.left_ref, ...), custom_call_target="tpu_custom_call" | custom-call | flops 200000000 | bytes 1000000 | tf_op jit(solution)/shard_map/term_rows/pallas_call | solution.py:151
  21.1 3.2 %collective-permute-start.1 = (f32[384,512]{1,0:T(8,128)S(1)}, f32[384,512]{1,0:T(8,128)S(1)}, u32[]{:S(2)}, u32[]{:S(2)}) collective-permute-start(f32[384,512]{1,0:T(8,128)S(1)} %get-tuple-element.64), channel_id=1, source_target_pairs={{0,1},{4,5},{8,9},{12,13},{1,0},{5,4},{9,8},{13,12},{2,3},{6,7},{1... | collective-permute-start | bytes 2359304 | tf_op jit(solution)/shard_map/ppermute | solution.py:316
  24.3 2.2 %term_rows.11 = (f32[384,512]{1,0:T(8,128)S(1)}, f32[8,128]{1,0:T(8,128)S(1)}, bf16[384,1024]{1,0:T(8,128)(2,1)S(1)}) custom-call(s32[8]{0:T(128)S(1)} %stack.19.info_ref, bf16[1024,512]{1,0:T(8,128)(2,1)S(1)} %get-tuple-element.45.live_ref, bf16[384,1024]{1,0:T(8,128)(2,1)S(1)} %get-tuple-element.55.left_ref, ...), custom_call_target="tpu_custom_call" | custom-call | flops 200000000 | bytes 1000000 | tf_op jit(solution)/shard_map/term_rows/pallas_call | solution.py:151
  27.2 2.0 %collective-permute-start.2 = (f32[384,512]{1,0:T(8,128)S(1)}, f32[384,512]{1,0:T(8,128)S(1)}, u32[]{:S(2)}, u32[]{:S(2)}) collective-permute-start(f32[384,512]{1,0:T(8,128)S(1)} %get-tuple-element.67), channel_id=1, source_target_pairs={{1,2},{5,6},{9,10},{13,14},{3,0},{7,4},{11,8},{0,1},{2,3},{4,5},{6... | collective-permute-start | bytes 2359304 | tf_op jit(solution)/shard_map/ppermute | solution.py:332
  29.9 0.9 %collective-permute-done.4.refs_0_ = f32[640,512]{1,0:T(8,128)S(1)} collective-permute-done((f32[640,512]{1,0:T(8,128)S(1)}, f32[640,512]{1,0:T(8,128)S(1)}, u32[]{:S(2)}, u32[]{:S(2)}) %collective-permute-start.4) | collective-permute-done | bytes 1310752 | tf_op jit(solution)/shard_map/ppermute | solution.py:332
  30.8 6.5 %collective-permute-start.5 = (f32[640,512]{1,0:T(8,128)S(1)}, f32[640,512]{1,0:T(8,128)S(1)}, u32[]{:S(2)}, u32[]{:S(2)}) collective-permute-start(f32[640,512]{1,0:T(8,128)S(1)} %get-tuple-element.75.refs_1_.a_ref), channel_id=1, source_target_pairs={{0,4},{4,8},{8,12},{16,20},{20,24},{24,28}} | collective-permute-start | bytes 3932168 | tf_op jit(solution)/shard_map/ppermute | solution.py:316
  37.3 0.7 add_blocks.6
  38.0 0.7 collective-permute-start.7
  38.8 2.1 %collective-permute-done.2.refs_0_ = f32[384,512]{1,0:T(8,128)S(1)} collective-permute-done((f32[384,512]{1,0:T(8,128)S(1)}, f32[384,512]{1,0:T(8,128)S(1)}, u32[]{:S(2)}, u32[]{:S(2)}) %collective-permute-start.2) | collective-permute-done | bytes 786464 | tf_op jit(solution)/shard_map/ppermute | solution.py:332
  42.3 6.8 %collective-permute-start.8 = (f32[384,512]{1,0:T(8,128)S(1)}, f32[384,512]{1,0:T(8,128)S(1)}, u32[]{:S(2)}, u32[]{:S(2)}) collective-permute-start(f32[384,512]{1,0:T(8,128)S(1)} %get-tuple-element.73.refs_1_.a_ref), channel_id=1, source_target_pairs={{0,4},{4,8},{8,12},{16,20},{20,24},{24,28}} | collective-permute-start | bytes 2359304 | tf_op jit(solution)/shard_map/ppermute | solution.py:316
  49.1 3.2 %collective-permute-done.5.refs_0_.b_ref = f32[640,512]{1,0:T(8,128)S(1)} collective-permute-done((f32[640,512]{1,0:T(8,128)S(1)}, f32[640,512]{1,0:T(8,128)S(1)}, u32[]{:S(2)}, u32[]{:S(2)}) %collective-permute-start.5) | collective-permute-done | bytes 1310752 | tf_op jit(solution)/shard_map/ppermute | solution.py:316
  52.3 1.8 %term_rows.12 = (f32[640,512]{1,0:T(8,128)S(1)}, f32[8,128]{1,0:T(8,128)S(1)}) custom-call(s32[8]{0:T(128)S(1)} %stack.19.info_ref, bf16[1024,512]{1,0:T(8,128)(2,1)S(1)} %get-tuple-element.45.live_ref, bf16[640,1024]{1,0:T(8,128)(2,1)S(1)} %get-tuple-element.74.left_ref, bf16[512,512]{1,0:T(8,128)(2,1)S(1)} %get-tuple-element.63.right_ref, ...), custom_call_target="tpu_custom_call" | custom-call | flops 200000000 | bytes 1000000 | tf_op jit(solution)/shard_map/term_rows/pallas_call | solution.py:151
  54.1 1.6 %finish_rows.2 = (bf16[1,1024,512]{2,1,0:T(8,128)(2,1)}, f32[16,128]{1,0:T(8,128)S(1)}) custom-call(s32[8]{0:T(128)S(1)} %stack.19.info_ref, bf16[1024,512]{1,0:T(8,128)(2,1)S(1)} %get-tuple-element.45.live_ref, f32[640,512]{1,0:T(8,128)S(1)} %get-tuple-element.80.own_ref, f32[640,512]{1,0:T(8,128)S(1)} %get-tuple-element.75.refs_1_.a_ref, ...), custom_call_target="tpu_custom_call" | custom-call | flops 200000000 | bytes 1000000 | tf_op jit(solution)/shard_map/finish_rows/pallas_call | solution.py:270
  55.7 1.4 %term_rows.13 = (f32[384,512]{1,0:T(8,128)S(1)}, f32[8,128]{1,0:T(8,128)}) custom-call(s32[8]{0:T(128)S(1)} %stack.19.info_ref, bf16[1024,512]{1,0:T(8,128)(2,1)S(1)} %get-tuple-element.45.live_ref, bf16[384,1024]{1,0:T(8,128)(2,1)S(1)} %get-tuple-element.62.left_ref, bf16[512,512]{1,0:T(8,128)(2,1)S(1)} %get-tuple-element.63.right_ref, ...), custom_call_target="tpu_custom_call" | custom-call | flops 200000000 | bytes 1000000 | tf_op jit(solution)/shard_map/term_rows/pallas_call | solution.py:151
  57.1 3.6 %collective-permute-done.8.b_ref = f32[384,512]{1,0:T(8,128)S(1)} collective-permute-done((f32[384,512]{1,0:T(8,128)S(1)}, f32[384,512]{1,0:T(8,128)S(1)}, u32[]{:S(2)}, u32[]{:S(2)}) %collective-permute-start.8) | collective-permute-done | bytes 786464 | tf_op jit(solution)/shard_map/ppermute | solution.py:316
  60.7 1.5 %finish_rows.3 = (bf16[1,1024,512]{2,1,0:T(8,128)(2,1)}, f32[16,128]{1,0:T(8,128)S(1)}) custom-call(s32[8]{0:T(128)S(1)} %stack.19.info_ref, bf16[1024,512]{1,0:T(8,128)(2,1)S(1)} %get-tuple-element.45.live_ref, f32[384,512]{1,0:T(8,128)S(1)} %get-tuple-element.83.own_ref, ...), custom_call_target="tpu_custom_call", output_to_operand_aliasing={{0}: (7, {})} | custom-call | flops 200000000 | bytes 1000000 | tf_op jit(solution)/shard_map/finish_rows/pallas_call | solution.py:270
  62.2 15.1 %all_to_all.11 = f32[16,1,128]{2,1,0:T(1,128)S(1)} all-to-all(f32[16,1,128]{2,1,0:T(1,128)S(1)} %bitcast.10), channel_id=1, replica_groups=mesh['grp'=2,'sec'=16] {'sec'}, dimensions={0} | all-to-all | bytes 16384 | tf_op jit(solution)/shard_map/all_to_all | solution.py:291
  (21 shorter events, 5.3 us)
Async XLA Ops:
  2.0 1.2 %copy-start.1 = (bf16[1,1024,512]{2,1,0:T(8,128)(2,1)S(1)}, bf16[1,1024,512]{2,1,0:T(8,128)(2,1)}, u32[]{:S(2)}) copy-start(bf16[1,1024,512]{2,1,0:T(8,128)(2,1)} %param.5) | copy-start | bytes 3145732
  3.3 4.3 %copy-start = (bf16[1,4,512,512]{3,2,1,0:T(8,128)(2,1)S(1)}, bf16[1,4,512,512]{3,2,1,0:T(8,128)(2,1)}, u32[]{:S(2)}) copy-start(bf16[1,4,512,512]{3,2,1,0:T(8,128)(2,1)} %refs_1_.9) | copy-start | bytes 6291460
  7.0 3.2 %collective-permute-start = (f32[640,512]{1,0:T(8,128)S(1)}, f32[640,512]{1,0:T(8,128)S(1)}, u32[]{:S(2)}, u32[]{:S(2)}) collective-permute-start(f32[640,512]{1,0:T(8,128)S(1)} %get-tuple-element.52), channel_id=1, source_target_pairs={{0,1},{4,5},{8,9},{12,13},{1,0},{5,4},{9,8},{13,12},{2,3},{6,7},{1... | collective-permute-start | bytes 3932168 | tf_op jit(solution)/shard_map/ppermute | solution.py:316
  10.9 19.9 %collective-permute-start.4 = (f32[640,512]{1,0:T(8,128)S(1)}, f32[640,512]{1,0:T(8,128)S(1)}, u32[]{:S(2)}, u32[]{:S(2)}) collective-permute-start(f32[640,512]{1,0:T(8,128)S(1)} %get-tuple-element.69), channel_id=1, source_target_pairs={{1,2},{5,6},{9,10},{13,14},{3,0},{7,4},{11,8},{0,1},{2,3},{4,5},{6... | collective-permute-start | bytes 3932168 | tf_op jit(solution)/shard_map/ppermute | solution.py:332
  16.1 21.2 %collective-permute-start.3 = (f32[640,512]{1,0:T(8,128)S(1)}, f32[640,512]{1,0:T(8,128)S(1)}, u32[]{:S(2)}, u32[]{:S(2)}) collective-permute-start(f32[640,512]{1,0:T(8,128)S(1)} %get-tuple-element.68.a_ref), channel_id=1, source_target_pairs={{3,6},{7,10},{11,14},{4,1},{8,5},{12,9},{19,22},{23,26},{27,30},{2... | collective-permute-start | bytes 3932168 | tf_op jit(solution)/shard_map/ppermute | solution.py:316
  21.1 5.4 %collective-permute-start.1 = (f32[384,512]{1,0:T(8,128)S(1)}, f32[384,512]{1,0:T(8,128)S(1)}, u32[]{:S(2)}, u32[]{:S(2)}) collective-permute-start(f32[384,512]{1,0:T(8,128)S(1)} %get-tuple-element.64), channel_id=1, source_target_pairs={{0,1},{4,5},{8,9},{12,13},{1,0},{5,4},{9,8},{13,12},{2,3},{6,7},{1... | collective-permute-start | bytes 2359304 | tf_op jit(solution)/shard_map/ppermute | solution.py:316
  27.2 13.7 %collective-permute-start.2 = (f32[384,512]{1,0:T(8,128)S(1)}, f32[384,512]{1,0:T(8,128)S(1)}, u32[]{:S(2)}, u32[]{:S(2)}) collective-permute-start(f32[384,512]{1,0:T(8,128)S(1)} %get-tuple-element.67), channel_id=1, source_target_pairs={{1,2},{5,6},{9,10},{13,14},{3,0},{7,4},{11,8},{0,1},{2,3},{4,5},{6... | collective-permute-start | bytes 2359304 | tf_op jit(solution)/shard_map/ppermute | solution.py:332
  29.1 11.7 %collective-permute-start.6 = (f32[384,512]{1,0:T(8,128)S(1)}, f32[384,512]{1,0:T(8,128)S(1)}, u32[]{:S(2)}, u32[]{:S(2)}) collective-permute-start(f32[384,512]{1,0:T(8,128)S(1)} %get-tuple-element.76.a_ref), channel_id=1, source_target_pairs={{3,6},{7,10},{11,14},{4,1},{8,5},{12,9},{19,22},{23,26},{27,30},{2... | collective-permute-start | bytes 2359304 | tf_op jit(solution)/shard_map/ppermute | solution.py:316
  30.8 21.5 %collective-permute-start.5 = (f32[640,512]{1,0:T(8,128)S(1)}, f32[640,512]{1,0:T(8,128)S(1)}, u32[]{:S(2)}, u32[]{:S(2)}) collective-permute-start(f32[640,512]{1,0:T(8,128)S(1)} %get-tuple-element.75.refs_1_.a_ref), channel_id=1, source_target_pairs={{0,4},{4,8},{8,12},{16,20},{20,24},{24,28}} | collective-permute-start | bytes 3932168 | tf_op jit(solution)/shard_map/ppermute | solution.py:316
  38.0 16.0 %collective-permute-start.7 = (f32[640,512]{1,0:T(8,128)S(1)}, f32[640,512]{1,0:T(8,128)S(1)}, u32[]{:S(2)}, u32[]{:S(2)}) collective-permute-start(f32[640,512]{1,0:T(8,128)S(1)} %get-tuple-element.81), channel_id=1, source_target_pairs={{1,3},{5,7},{9,11},{13,15},{2,1},{6,5},{10,9},{14,13},{17,19},{21,... | collective-permute-start | bytes 3932168 | tf_op jit(solution)/shard_map/ppermute | solution.py:316
  41.5 15.6 %collective-permute-start.9 = (f32[384,512]{1,0:T(8,128)S(1)}, f32[384,512]{1,0:T(8,128)S(1)}, u32[]{:S(2)}, u32[]{:S(2)}) collective-permute-start(f32[384,512]{1,0:T(8,128)S(1)} %get-tuple-element.84), channel_id=1, source_target_pairs={{1,3},{5,7},{9,11},{13,15},{2,1},{6,5},{10,9},{14,13},{17,19},{21,... | collective-permute-start | bytes 2359304 | tf_op jit(solution)/shard_map/ppermute | solution.py:316
  42.3 18.5 %collective-permute-start.8 = (f32[384,512]{1,0:T(8,128)S(1)}, f32[384,512]{1,0:T(8,128)S(1)}, u32[]{:S(2)}, u32[]{:S(2)}) collective-permute-start(f32[384,512]{1,0:T(8,128)S(1)} %get-tuple-element.73.refs_1_.a_ref), channel_id=1, source_target_pairs={{0,4},{4,8},{8,12},{16,20},{20,24},{24,28}} | collective-permute-start | bytes 2359304 | tf_op jit(solution)/shard_map/ppermute | solution.py:316

commit v14 on v9

--- a/solution.py
+++ b/solution.py
@@ -60,7 +60,7 @@
     if masks:
         live_ref = operands.pop(0)
     own, late = fetch(info_ref, slot, left_hbm, right_hbm, *operands, sems)
-    for copy in own + late:
+    for copy in own:
         copy.start()
     if masks:
         rows, cols = psi_ref.shape
@@ -74,6 +74,8 @@
             live_ref[span, :] = values.astype(live_ref.dtype)
     for copy in own:
         copy.wait()
+    for copy in late:
+        copy.start()
     out_ref[...] = multiply(operands[0][: out_ref.shape[0], :], live_ref[...], operands[1][...])
     for copy in late:
         copy.wait()
@@ -316,9 +318,6 @@
     def raise_one(value):
         return lax.ppermute(value, "sec", pairs_up)
 
-    def up_chip(value):
-        return send(value, (0, 1), (2, 1))
-
     def along(value):
         return send(value, (3, 3), (0, -3))
 
@@ -333,9 +332,9 @@
 
     envs = (left_env, right_env)
     first0, token, live, *ops0 = opening_rows(info, psi[0], envs, 0, part, masks=True)
-    paired0 = up_chip(first0)
+    paired0 = swap(first0)
     first1, token = term_rows(info, live, ops0, part, part, token)
-    paired1 = up_chip(first1)
+    paired1 = swap(first1)
     both0, token = add(first0, paired0, token)
     raised0 = raise_one(both0)
     second0, token, *ops1 = opening_rows(info, live, envs, 1, part, token)

time: 76.6 us -> 74.8 us (0.977)
  starting transfers between devices: 21.8 us -> 19.8 us
    ppermute x10, starting transfers between devices: 19.3 us -> 17.2 us  [send(): return lax.ppermute(value, 'sec', pairs)]
  transfers between devices with their start and end apart: 12 -> 12, of which waited for: 3 -> 4; matrix products, arithmetic and copies ran while one was open for 0% -> 0% of each run, Pallas kernels for 20% -> 21%
where the time goes in v14:
time: 74.8 us; the launch traced here: 74.3 us
  Pallas kernels  20.9 us (28%)
  starting transfers between devices  19.8 us (26%)
  blocking collectives  18.2 us (24%)
  waiting for transfers between devices  11.9 us (16%)
  between operations  2.18 us (3%)
  local copies, waits for them, and re-layouts  1.32 us (2%)
    all_to_all x1, blocking collectives, sum_over_sectors(): arrived = lax.all_to_all(value, 'sec', 0, 0, tiled=True)  18.2 us
    ppermute x10, starting transfers between devices, send(): return lax.ppermute(value, 'sec', pairs)  17.2 us
    pallas_call x6, Pallas kernels, term_rows(): pl.pallas_call(functools.partial(term_kernel, first, added is not None, s...  10.4 us
    ppermute x10, waiting for transfers between devices, send(): return lax.ppermute(value, 'sec', pairs)  7.36 us
    pallas_call x2, Pallas kernels, opening_rows(): pl.pallas_call(functools.partial(opening_kernel, slot, masks, len(tokens)...  6.17 us
    ppermute x2, waiting for transfers between devices, raise_one(): return lax.ppermute(value, 'sec', pairs_up)  4.55 us
    pallas_call x2, Pallas kernels, finish(): pl.pallas_call(functools.partial(finish_kernel, first), out_shape=(jax.Sh...  3.07 us
    ppermute x2, starting transfers between devices, raise_one(): return lax.ppermute(value, 'sec', pairs_up)  2.58 us
  transfers between devices with their start and end apart: 12, of which 4 were waited for; matrix products, arithmetic and copies ran while one was open for 0% of the time, Pallas kernels for 21%

profile of v14, /device:TPU:0, one launch (start us, length us, event | category | flops | bytes accessed | tf_op | source)
XLA Modules:
  0.0 74.3 jit_solution(17634731225590306037)
XLA Ops:
  2.0 1.2 %copy-done.1 = bf16[1,1024,512]{2,1,0:T(8,128)(2,1)S(1)} copy-done((bf16[1,1024,512]{2,1,0:T(8,128)(2,1)S(1)}, bf16[1,1024,512]{2,1,0:T(8,128)(2,1)}, u32[]{:S(2)}) %copy-start.1) | copy-done | bytes 1048600
  3.3 3.2 %opening_rows.2 = (f32[512,512]{1,0:T(8,128)S(1)}, f32[8,128]{1,0:T(8,128)S(1)}, bf16[1024,512]{1,0:T(8,128)(2,1)S(1)}, bf16[1024,1024]{1,0:T(8,128)(2,1)S(1)}, bf16[512,512]{1,0:T(8,128)(2,1)S(1)}) custom-call(s32[7]{0:T(128)S(1)} %stack.19.info_ref, bf16[1024,512]{1,0:T(8,128)(2,1)S(1)} %bitcast.9, bf16[1,4,1024,1024]{3,2,1,0:T(8,128)(2,1)} %refs_0_.3, ...), custom_call_target="tpu_custom_call" | custom-call | flops 200000000 | bytes 1000000 | tf_op jit(solution)/shard_map/opening_rows/pallas_call | solution.py:97
  7.0 1.5 %term_rows.6 = (f32[512,512]{1,0:T(8,128)S(1)}, f32[8,128]{1,0:T(8,128)S(1)}) custom-call(s32[7]{0:T(128)S(1)} %stack.19.info_ref, bf16[1024,512]{1,0:T(8,128)(2,1)S(1)} %get-tuple-element.42.live_ref, bf16[1024,1024]{1,0:T(8,128)(2,1)S(1)} %get-tuple-element.44.left_ref, bf16[512,512]{1,0:T(8,128)(2,1)S(1)} %get-tuple-element.45.right_ref, ...), custom_call_target="tpu_custom_call" | custom-call | flops 200000000 | bytes 1000000 | tf_op jit(solution)/shard_map/term_rows/pallas_call | solution.py:152
  9.4 1.3 %collective-permute-start.2 = (f32[512,512]{1,0:T(8,128)S(1)}, f32[512,512]{1,0:T(8,128)S(1)}, u32[]{:S(2)}, u32[]{:S(2)}) collective-permute-start(f32[512,512]{1,0:T(8,128)S(1)} %get-tuple-element.59), channel_id=1, source_target_pairs={{1,2},{5,6},{9,10},{13,14},{3,0},{7,4},{11,8},{17,18},{21,22},{25,... | collective-permute-start | bytes 3145736 | tf_op jit(solution)/shard_map/ppermute | solution.py:319
  10.7 3.0 %opening_rows.3 = (f32[512,512]{1,0:T(8,128)S(1)}, f32[8,128]{1,0:T(8,128)S(1)}, bf16[1024,1024]{1,0:T(8,128)(2,1)S(1)}, bf16[512,512]{1,0:T(8,128)(2,1)S(1)}) custom-call(s32[7]{0:T(128)S(1)} %stack.19.info_ref, bf16[1024,512]{1,0:T(8,128)(2,1)S(1)} %get-tuple-element.42.live_ref, bf16[1,4,1024,1024]{3,2,1,0:T(8,128)(2,1)} %refs_0_.3, ...), custom_call_target="tpu_custom_call" | custom-call | flops 200000000 | bytes 1000000 | tf_op jit(solution)/shard_map/opening_rows/pallas_call | solution.py:97
  13.7 0.7 collective-permute-start.8
  14.6 1.3 %collective-permute-start.7 = (f32[512,512]{1,0:T(8,128)S(1)}, f32[512,512]{1,0:T(8,128)S(1)}, u32[]{:S(2)}, u32[]{:S(2)}) collective-permute-start(f32[512,512]{1,0:T(8,128)S(1)} %get-tuple-element.66), channel_id=1, source_target_pairs={{1,2},{5,6},{9,10},{13,14},{3,0},{7,4},{11,8},{17,18},{21,22},{25,... | collective-permute-start | bytes 3145736 | tf_op jit(solution)/shard_map/ppermute | solution.py:319
  15.9 2.2 %term_rows.7 = (f32[512,512]{1,0:T(8,128)S(1)}, f32[8,128]{1,0:T(8,128)S(1)}, bf16[1024,1024]{1,0:T(8,128)(2,1)S(1)}, bf16[512,512]{1,0:T(8,128)(2,1)S(1)}) custom-call(s32[7]{0:T(128)S(1)} %stack.19.info_ref, bf16[1024,512]{1,0:T(8,128)(2,1)S(1)} %get-tuple-element.42.live_ref, bf16[1024,1024]{1,0:T(8,128)(2,1)S(1)} %get-tuple-element.49.left_ref, ...), custom_call_target="tpu_custom_call" | custom-call | flops 200000000 | bytes 1000000 | tf_op jit(solution)/shard_map/term_rows/pallas_call | solution.py:152
  18.1 2.2 %term_rows.8 = (f32[512,512]{1,0:T(8,128)S(1)}, f32[8,128]{1,0:T(8,128)S(1)}, bf16[1024,1024]{1,0:T(8,128)(2,1)S(1)}, bf16[512,512]{1,0:T(8,128)(2,1)S(1)}) custom-call(s32[7]{0:T(128)S(1)} %stack.19.info_ref, bf16[1024,512]{1,0:T(8,128)(2,1)S(1)} %get-tuple-element.42.live_ref, bf16[1024,1024]{1,0:T(8,128)(2,1)S(1)} %get-tuple-element.54.left_ref, ...), custom_call_target="tpu_custom_call" | custom-call | flops 200000000 | bytes 1000000 | tf_op jit(solution)/shard_map/term_rows/pallas_call | solution.py:152
  20.3 4.4 %collective-permute-start.6 = (f32[512,512]{1,0:T(8,128)S(1)}, f32[512,512]{1,0:T(8,128)S(1)}, u32[]{:S(2)}, u32[]{:S(2)}) collective-permute-start(f32[512,512]{1,0:T(8,128)S(1)} %get-tuple-element.65), channel_id=1, source_target_pairs={{0,1},{4,5},{8,9},{12,13},{1,0},{5,4},{9,8},{13,12},{2,3},{6,7},{1... | collective-permute-start | bytes 3145736 | tf_op jit(solution)/shard_map/ppermute | solution.py:307
  24.7 1.1 %collective-permute-done.2.refs_0_ = f32[512,512]{1,0:T(8,128)S(1)} collective-permute-done((f32[512,512]{1,0:T(8,128)S(1)}, f32[512,512]{1,0:T(8,128)S(1)}, u32[]{:S(2)}, u32[]{:S(2)}) %collective-permute-start.2) | collective-permute-done | bytes 1048608 | tf_op jit(solution)/shard_map/ppermute | solution.py:319
  25.8 4.6 %collective-permute-start.5 = (f32[512,512]{1,0:T(8,128)S(1)}, f32[512,512]{1,0:T(8,128)S(1)}, u32[]{:S(2)}, u32[]{:S(2)}) collective-permute-start(f32[512,512]{1,0:T(8,128)S(1)} %get-tuple-element.64.a_ref), channel_id=1, source_target_pairs={{0,4},{4,8},{8,12},{16,20},{20,24},{24,28}} | collective-permute-start | bytes 3145736 | tf_op jit(solution)/shard_map/ppermute | solution.py:307
  30.4 0.7 collective-permute-start.4
  31.1 1.5 %term_rows.9 = (f32[512,512]{1,0:T(8,128)S(1)}, f32[8,128]{1,0:T(8,128)S(1)}) custom-call(s32[7]{0:T(128)S(1)} %stack.19.info_ref, bf16[1024,512]{1,0:T(8,128)(2,1)S(1)} %get-tuple-element.42.live_ref, bf16[1024,1024]{1,0:T(8,128)(2,1)S(1)} %get-tuple-element.54.left_ref, bf16[512,512]{1,0:T(8,128)(2,1)S(1)} %get-tuple-element.55.right_ref, ...), custom_call_target="tpu_custom_call" | custom-call | flops 200000000 | bytes 1000000 | tf_op jit(solution)/shard_map/term_rows/pallas_call | solution.py:152
  32.8 0.7 collective-permute-start.9
  33.6 3.4 %collective-permute-done.7.refs_0_ = f32[512,512]{1,0:T(8,128)S(1)} collective-permute-done((f32[512,512]{1,0:T(8,128)S(1)}, f32[512,512]{1,0:T(8,128)S(1)}, u32[]{:S(2)}, u32[]{:S(2)}) %collective-permute-start.7) | collective-permute-done | bytes 1048608 | tf_op jit(solution)/shard_map/ppermute | solution.py:319
  37.3 4.4 %collective-permute-start.10 = (f32[512,512]{1,0:T(8,128)S(1)}, f32[512,512]{1,0:T(8,128)S(1)}, u32[]{:S(2)}, u32[]{:S(2)}) collective-permute-start(f32[512,512]{1,0:T(8,128)S(1)} %get-tuple-element.77.a_ref), channel_id=1, source_target_pairs={{0,4},{4,8},{8,12},{16,20},{20,24},{24,28}} | collective-permute-start | bytes 3145736 | tf_op jit(solution)/shard_map/ppermute | solution.py:307
  41.7 1.5 %term_rows.10 = (f32[512,512]{1,0:T(8,128)S(1)}, f32[8,128]{1,0:T(8,128)S(1)}) custom-call(s32[7]{0:T(128)S(1)} %stack.19.info_ref, bf16[1024,512]{1,0:T(8,128)(2,1)S(1)} %get-tuple-element.42.live_ref, bf16[1024,1024]{1,0:T(8,128)(2,1)S(1)} %get-tuple-element.57.left_ref, bf16[512,512]{1,0:T(8,128)(2,1)S(1)} %get-tuple-element.58.right_ref, ...), custom_call_target="tpu_custom_call" | custom-call | flops 200000000 | bytes 1000000 | tf_op jit(solution)/shard_map/term_rows/pallas_call | solution.py:152
  43.4 0.7 collective-permute-start.11
  44.1 1.5 %finish_rows.2 = (bf16[1,1024,512]{2,1,0:T(8,128)(2,1)}, f32[16,128]{1,0:T(8,128)S(1)}) custom-call(s32[7]{0:T(128)S(1)} %stack.19.info_ref, bf16[1024,512]{1,0:T(8,128)(2,1)S(1)} %get-tuple-element.42.live_ref, f32[512,512]{1,0:T(8,128)S(1)} %get-tuple-element.73.own_ref, f32[512,512]{1,0:T(8,128)S(1)} %get-tuple-element.64.a_ref, ...), custom_call_target="tpu_custom_call" | custom-call | flops 200000000 | bytes 1000000 | tf_op jit(solution)/shard_map/finish_rows/pallas_call | solution.py:261
  45.7 1.5 %term_rows.11 = (f32[512,512]{1,0:T(8,128)S(1)}, f32[8,128]{1,0:T(8,128)}) custom-call(s32[7]{0:T(128)S(1)} %stack.19.info_ref, bf16[1024,512]{1,0:T(8,128)(2,1)S(1)} %get-tuple-element.42.live_ref, bf16[1024,1024]{1,0:T(8,128)(2,1)S(1)} %get-tuple-element.57.left_ref, bf16[512,512]{1,0:T(8,128)(2,1)S(1)} %get-tuple-element.58.right_ref, ...), custom_call_target="tpu_custom_call" | custom-call | flops 200000000 | bytes 1000000 | tf_op jit(solution)/shard_map/term_rows/pallas_call | solution.py:152
  47.2 6.7 %collective-permute-done.10.b_ref = f32[512,512]{1,0:T(8,128)S(1)} collective-permute-done((f32[512,512]{1,0:T(8,128)S(1)}, f32[512,512]{1,0:T(8,128)S(1)}, u32[]{:S(2)}, u32[]{:S(2)}) %collective-permute-start.10) | collective-permute-done | bytes 1048608 | tf_op jit(solution)/shard_map/ppermute | solution.py:307
  53.9 1.5 %finish_rows.3 = (bf16[1,1024,512]{2,1,0:T(8,128)(2,1)}, f32[16,128]{1,0:T(8,128)S(1)}) custom-call(s32[7]{0:T(128)S(1)} %stack.19.info_ref, bf16[1024,512]{1,0:T(8,128)(2,1)S(1)} %get-tuple-element.42.live_ref, f32[512,512]{1,0:T(8,128)S(1)} %get-tuple-element.76.own_ref, f32[512,512]{1,0:T(8,128)S(1)} %get-tuple-element.77.a_ref, ...), custom_call_target="tpu_custom_call", output_to_operand_aliasing={{0}: (7, {})} | custom-call | flops 200000000 | bytes 1000000 | tf_op jit(solution)/shard_map/finish_rows/pallas_call | solution.py:261
  55.4 18.2 %all_to_all.11 = f32[16,1,128]{2,1,0:T(1,128)S(1)} all-to-all(f32[16,1,128]{2,1,0:T(1,128)S(1)} %bitcast.10), channel_id=1, replica_groups=mesh['grp'=2,'sec'=16] {'sec'}, dimensions={0} | all-to-all | bytes 16384 | tf_op jit(solution)/shard_map/all_to_all | solution.py:282
  (25 shorter events, 2.9 us)
Async XLA Ops:
  2.0 1.2 %copy-start.1 = (bf16[1,1024,512]{2,1,0:T(8,128)(2,1)S(1)}, bf16[1,1024,512]{2,1,0:T(8,128)(2,1)}, u32[]{:S(2)}) copy-start(bf16[1,1024,512]{2,1,0:T(8,128)(2,1)} %param.5) | copy-start | bytes 3145732
  6.4 2.8 %collective-permute-start = (f32[512,512]{1,0:T(8,128)S(1)}, f32[512,512]{1,0:T(8,128)S(1)}, u32[]{:S(2)}, u32[]{:S(2)}) collective-permute-start(f32[512,512]{1,0:T(8,128)S(1)} %get-tuple-element.43.a_ref), channel_id=1, source_target_pairs={{0,1},{4,5},{8,9},{12,13},{1,0},{5,4},{9,8},{13,12},{2,3},{6,7},{1... | collective-permute-start | bytes 3145736 | tf_op jit(solution)/shard_map/ppermute | solution.py:307
  7.0 3.7 %copy-start = (bf16[1,4,512,512]{3,2,1,0:T(8,128)(2,1)S(1)}, bf16[1,4,512,512]{3,2,1,0:T(8,128)(2,1)}, u32[]{:S(2)}) copy-start(bf16[1,4,512,512]{3,2,1,0:T(8,128)(2,1)} %refs_1_.3) | copy-start | bytes 6291460
  8.5 6.0 %collective-permute-start.1 = (f32[512,512]{1,0:T(8,128)S(1)}, f32[512,512]{1,0:T(8,128)S(1)}, u32[]{:S(2)}, u32[]{:S(2)}) collective-permute-start(f32[512,512]{1,0:T(8,128)S(1)} %get-tuple-element.51.a_ref), channel_id=1, source_target_pairs={{0,1},{4,5},{8,9},{12,13},{1,0},{5,4},{9,8},{13,12},{2,3},{6,7},{1... | collective-permute-start | bytes 3145736 | tf_op jit(solution)/shard_map/ppermute | solution.py:307
  9.4 16.4 %collective-permute-start.2 = (f32[512,512]{1,0:T(8,128)S(1)}, f32[512,512]{1,0:T(8,128)S(1)}, u32[]{:S(2)}, u32[]{:S(2)}) collective-permute-start(f32[512,512]{1,0:T(8,128)S(1)} %get-tuple-element.59), channel_id=1, source_target_pairs={{1,2},{5,6},{9,10},{13,14},{3,0},{7,4},{11,8},{17,18},{21,22},{25,... | collective-permute-start | bytes 3145736 | tf_op jit(solution)/shard_map/ppermute | solution.py:319
  13.7 19.0 %collective-permute-start.8 = (f32[512,512]{1,0:T(8,128)S(1)}, f32[512,512]{1,0:T(8,128)S(1)}, u32[]{:S(2)}, u32[]{:S(2)}) collective-permute-start(f32[512,512]{1,0:T(8,128)S(1)} %get-tuple-element.67.a_ref), channel_id=1, source_target_pairs={{3,6},{7,10},{11,14},{4,1},{8,5},{12,9},{19,22},{23,26},{27,30},{2... | collective-permute-start | bytes 3145736 | tf_op jit(solution)/shard_map/ppermute | solution.py:307
  14.6 22.4 %collective-permute-start.7 = (f32[512,512]{1,0:T(8,128)S(1)}, f32[512,512]{1,0:T(8,128)S(1)}, u32[]{:S(2)}, u32[]{:S(2)}) collective-permute-start(f32[512,512]{1,0:T(8,128)S(1)} %get-tuple-element.66), channel_id=1, source_target_pairs={{1,2},{5,6},{9,10},{13,14},{3,0},{7,4},{11,8},{17,18},{21,22},{25,... | collective-permute-start | bytes 3145736 | tf_op jit(solution)/shard_map/ppermute | solution.py:319
  20.3 17.0 %collective-permute-start.6 = (f32[512,512]{1,0:T(8,128)S(1)}, f32[512,512]{1,0:T(8,128)S(1)}, u32[]{:S(2)}, u32[]{:S(2)}) collective-permute-start(f32[512,512]{1,0:T(8,128)S(1)} %get-tuple-element.65), channel_id=1, source_target_pairs={{0,1},{4,5},{8,9},{12,13},{1,0},{5,4},{9,8},{13,12},{2,3},{6,7},{1... | collective-permute-start | bytes 3145736 | tf_op jit(solution)/shard_map/ppermute | solution.py:307
  25.8 17.4 %collective-permute-start.5 = (f32[512,512]{1,0:T(8,128)S(1)}, f32[512,512]{1,0:T(8,128)S(1)}, u32[]{:S(2)}, u32[]{:S(2)}) collective-permute-start(f32[512,512]{1,0:T(8,128)S(1)} %get-tuple-element.64.a_ref), channel_id=1, source_target_pairs={{0,4},{4,8},{8,12},{16,20},{20,24},{24,28}} | collective-permute-start | bytes 3145736 | tf_op jit(solution)/shard_map/ppermute | solution.py:307
  30.4 12.8 %collective-permute-start.4 = (f32[512,512]{1,0:T(8,128)S(1)}, f32[512,512]{1,0:T(8,128)S(1)}, u32[]{:S(2)}, u32[]{:S(2)}) collective-permute-start(f32[512,512]{1,0:T(8,128)S(1)} %get-tuple-element.63.a_ref), channel_id=1, source_target_pairs={{3,6},{7,10},{11,14},{4,1},{8,5},{12,9},{19,22},{23,26},{27,30},{2... | collective-permute-start | bytes 3145736 | tf_op jit(solution)/shard_map/ppermute | solution.py:307
  32.8 11.3 %collective-permute-start.9 = (f32[512,512]{1,0:T(8,128)S(1)}, f32[512,512]{1,0:T(8,128)S(1)}, u32[]{:S(2)}, u32[]{:S(2)}) collective-permute-start(f32[512,512]{1,0:T(8,128)S(1)} %get-tuple-element.74), channel_id=1, source_target_pairs={{1,3},{5,7},{9,11},{13,15},{2,1},{6,5},{10,9},{14,13},{17,19},{21,... | collective-permute-start | bytes 3145736 | tf_op jit(solution)/shard_map/ppermute | solution.py:307
  37.0 8.7 %collective-permute-start.3 = (f32[512,512]{1,0:T(8,128)S(1)}, f32[512,512]{1,0:T(8,128)S(1)}, u32[]{:S(2)}, u32[]{:S(2)}) collective-permute-start(f32[512,512]{1,0:T(8,128)S(1)} %get-tuple-element.62), channel_id=1, source_target_pairs={{0,1},{4,5},{8,9},{12,13},{1,0},{5,4},{9,8},{13,12},{2,3},{6,7},{1... | collective-permute-start | bytes 3145736 | tf_op jit(solution)/shard_map/ppermute | solution.py:307
  37.3 16.6 %collective-permute-start.10 = (f32[512,512]{1,0:T(8,128)S(1)}, f32[512,512]{1,0:T(8,128)S(1)}, u32[]{:S(2)}, u32[]{:S(2)}) collective-permute-start(f32[512,512]{1,0:T(8,128)S(1)} %get-tuple-element.77.a_ref), channel_id=1, source_target_pairs={{0,4},{4,8},{8,12},{16,20},{20,24},{24,28}} | collective-permute-start | bytes 3145736 | tf_op jit(solution)/shard_map/ppermute | solution.py:307
  43.4 10.5 %collective-permute-start.11 = (f32[512,512]{1,0:T(8,128)S(1)}, f32[512,512]{1,0:T(8,128)S(1)}, u32[]{:S(2)}, u32[]{:S(2)}) collective-permute-start(f32[512,512]{1,0:T(8,128)S(1)} %get-tuple-element.78), channel_id=1, source_target_pairs={{1,3},{5,7},{9,11},{13,15},{2,1},{6,5},{10,9},{14,13},{17,19},{21,... | collective-permute-start | bytes 3145736 | tf_op jit(solution)/shard_map/ppermute | solution.py:307

commit v15 on v14

--- a/solution.py
+++ b/solution.py
@@ -60,7 +60,7 @@
     if masks:
         live_ref = operands.pop(0)
     own, late = fetch(info_ref, slot, left_hbm, right_hbm, *operands, sems)
-    for copy in own:
+    for copy in own + late:
         copy.start()
     if masks:
         rows, cols = psi_ref.shape
@@ -74,8 +74,6 @@
             live_ref[span, :] = values.astype(live_ref.dtype)
     for copy in own:
         copy.wait()
-    for copy in late:
-        copy.start()
     out_ref[...] = multiply(operands[0][: out_ref.shape[0], :], live_ref[...], operands[1][...])
     for copy in late:
         copy.wait()
@@ -274,12 +272,27 @@
     )(*operands)
 
 
+def pair_kernel(a_ref, b_ref, out_ref):
+    out_ref[...] = a_ref[...] + b_ref[...]
+
+
 def sum_kernel(in_ref, out_ref):
     out_ref[0] = jnp.sum(in_ref[:, :1])
 
 
-def sum_over_sectors(value):
-    arrived = lax.all_to_all(value, "sec", 0, 0, tiled=True)
+def sum_over_sectors(value, sectors):
+    other = lax.ppermute(value, "sec", [(s, s ^ 1) for s in range(sectors)])
+    value = pl.pallas_call(
+        pair_kernel,
+        out_shape=jax.ShapeDtypeStruct(value.shape, value.dtype),
+        in_specs=[WHOLE, WHOLE],
+        out_specs=WHOLE,
+        compiler_params=params(),
+        cost_estimate=SMALL,
+        name="pair_energy",
+    )(value, other)
+    groups = [list(range(core, sectors, 2)) for core in range(2)]
+    arrived = lax.all_to_all(value, "sec", 0, 0, axis_index_groups=groups, tiled=True)
     return pl.pallas_call(
         sum_kernel,
         out_shape=jax.ShapeDtypeStruct((1,), jnp.float32),
@@ -358,11 +371,11 @@
     summed1, token = add(second1, moved1, token)
     crossed1 = across(summed1)
 
-    energy = jnp.zeros((sectors, 128), jnp.float32)
+    energy = jnp.zeros((sectors // 2, 128), jnp.float32)
     sigma, energy = finish(info, live, own0, (raised0, relayed0, crossed0), energy, None, 0)
     own1, token = term_rows(info, live, ops3, part, part, token, energy, added=swapped1)
     sigma, energy = finish(info, live, own1, (raised1, relayed1, crossed1), energy, sigma, part)
-    return sigma, sum_over_sectors(energy)
+    return sigma, sum_over_sectors(energy, sectors)
 
 
 def solution(mesh):

time: 74.8 us -> 75.8 us (1.013)
  starting transfers between devices: 19.8 us -> 28 us
  blocking collectives: 18.2 us -> 10.4 us
  waiting for transfers between devices: 11.9 us -> 12.9 us
    ppermute x0 -> x1, starting transfers between devices: none -> 8.23 us  [sum_over_sectors(): other = lax.ppermute(value, 'sec', [(s, s ^ 1) for s in range(sectors)])]
    all_to_all x1, blocking collectives: 18.2 us -> 10.4 us  [sum_over_sectors(): lax.all_to_all(value, 'sec', 0, 0, axis_index_groups=groups, tiled=True)]
    ppermute x0 -> x1, waiting for transfers between devices: none -> 0.82 us  [sum_over_sectors(): other = lax.ppermute(value, 'sec', [(s, s ^ 1) for s in range(sectors)])]
  transfers between devices with their start and end apart: 12 -> 13, of which waited for: 4 -> 5; matrix products, arithmetic and copies ran while one was open for 0% -> 0% of each run, Pallas kernels for 21% -> 20%
where the time goes in v15:
time: 75.8 us; the launch traced here: 75.4 us
  starting transfers between devices  28 us (37%)
  Pallas kernels  20.5 us (27%)
  waiting for transfers between devices  12.9 us (17%)
  blocking collectives  10.4 us (14%)
  between operations  2.19 us (3%)
  local copies, waits for them, and re-layouts  1.32 us (2%)
    ppermute x10, starting transfers between devices, send(): return lax.ppermute(value, 'sec', pairs)  17.2 us
    pallas_call x6, Pallas kernels, term_rows(): pl.pallas_call(functools.partial(term_kernel, first, added is not None, s...  10.4 us
    all_to_all x1, blocking collectives, sum_over_sectors(): lax.all_to_all(value, 'sec', 0, 0, axis_index_groups=groups, tiled=True)  10.4 us
    ppermute x1, starting transfers between devices, sum_over_sectors(): other = lax.ppermute(value, 'sec', [(s, s ^ 1) for s in range(sectors)])  8.23 us
    ppermute x10, waiting for transfers between devices, send(): return lax.ppermute(value, 'sec', pairs)  7.37 us
    pallas_call x2, Pallas kernels, opening_rows(): pl.pallas_call(functools.partial(opening_kernel, slot, masks, len(tokens)...  5.77 us
    ppermute x2, waiting for transfers between devices, raise_one(): return lax.ppermute(value, 'sec', pairs_up)  4.74 us
    pallas_call x2, Pallas kernels, finish(): pl.pallas_call(functools.partial(finish_kernel, first), out_shape=(jax.Sh...  3.07 us
  transfers between devices with their start and end apart: 13, of which 5 were waited for; matrix products, arithmetic and copies ran while one was open for 0% of the time, Pallas kernels for 20%

profile of v15, /device:TPU:0, one launch (start us, length us, event | category | flops | bytes accessed | tf_op | source)
XLA Modules:
  0.0 75.4 jit_solution(11814842204013579319)
XLA Ops:
  2.0 1.2 %copy-done.1 = bf16[1,1024,512]{2,1,0:T(8,128)(2,1)S(1)} copy-done((bf16[1,1024,512]{2,1,0:T(8,128)(2,1)S(1)}, bf16[1,1024,512]{2,1,0:T(8,128)(2,1)}, u32[]{:S(2)}) %copy-start.1) | copy-done | bytes 1048600
  3.3 3.0 %opening_rows.2 = (f32[512,512]{1,0:T(8,128)S(1)}, f32[8,128]{1,0:T(8,128)S(1)}, bf16[1024,512]{1,0:T(8,128)(2,1)S(1)}, bf16[1024,1024]{1,0:T(8,128)(2,1)S(1)}, bf16[512,512]{1,0:T(8,128)(2,1)S(1)}) custom-call(s32[7]{0:T(128)S(1)} %stack.19.info_ref, bf16[1024,512]{1,0:T(8,128)(2,1)S(1)} %bitcast.9, bf16[1,4,1024,1024]{3,2,1,0:T(8,128)(2,1)} %refs_0_.3, ...), custom_call_target="tpu_custom_call" | custom-call | flops 200000000 | bytes 1000000 | tf_op jit(solution)/shard_map/opening_rows/pallas_call | solution.py:95
  6.8 1.5 %term_rows.6 = (f32[512,512]{1,0:T(8,128)S(1)}, f32[8,128]{1,0:T(8,128)S(1)}) custom-call(s32[7]{0:T(128)S(1)} %stack.19.info_ref, bf16[1024,512]{1,0:T(8,128)(2,1)S(1)} %get-tuple-element.42.live_ref, bf16[1024,1024]{1,0:T(8,128)(2,1)S(1)} %get-tuple-element.44.left_ref, bf16[512,512]{1,0:T(8,128)(2,1)S(1)} %get-tuple-element.45.right_ref, ...), custom_call_target="tpu_custom_call" | custom-call | flops 200000000 | bytes 1000000 | tf_op jit(solution)/shard_map/term_rows/pallas_call | solution.py:150
  9.2 1.3 %collective-permute-start.2 = (f32[512,512]{1,0:T(8,128)S(1)}, f32[512,512]{1,0:T(8,128)S(1)}, u32[]{:S(2)}, u32[]{:S(2)}) collective-permute-start(f32[512,512]{1,0:T(8,128)S(1)} %get-tuple-element.59), channel_id=1, source_target_pairs={{1,2},{5,6},{9,10},{13,14},{3,0},{7,4},{11,8},{17,18},{21,22},{25,... | collective-permute-start | bytes 3145736 | tf_op jit(solution)/shard_map/ppermute | solution.py:332
  10.5 2.8 %opening_rows.3 = (f32[512,512]{1,0:T(8,128)S(1)}, f32[8,128]{1,0:T(8,128)S(1)}, bf16[1024,1024]{1,0:T(8,128)(2,1)S(1)}, bf16[512,512]{1,0:T(8,128)(2,1)S(1)}) custom-call(s32[7]{0:T(128)S(1)} %stack.19.info_ref, bf16[1024,512]{1,0:T(8,128)(2,1)S(1)} %get-tuple-element.42.live_ref, bf16[1,4,1024,1024]{3,2,1,0:T(8,128)(2,1)} %refs_0_.3, ...), custom_call_target="tpu_custom_call" | custom-call | flops 200000000 | bytes 1000000 | tf_op jit(solution)/shard_map/opening_rows/pallas_call | solution.py:95
  13.3 0.7 collective-permute-start.8
  14.2 1.3 %collective-permute-start.7 = (f32[512,512]{1,0:T(8,128)S(1)}, f32[512,512]{1,0:T(8,128)S(1)}, u32[]{:S(2)}, u32[]{:S(2)}) collective-permute-start(f32[512,512]{1,0:T(8,128)S(1)} %get-tuple-element.66), channel_id=1, source_target_pairs={{1,2},{5,6},{9,10},{13,14},{3,0},{7,4},{11,8},{17,18},{21,22},{25,... | collective-permute-start | bytes 3145736 | tf_op jit(solution)/shard_map/ppermute | solution.py:332
  15.5 2.2 %term_rows.7 = (f32[512,512]{1,0:T(8,128)S(1)}, f32[8,128]{1,0:T(8,128)S(1)}, bf16[1024,1024]{1,0:T(8,128)(2,1)S(1)}, bf16[512,512]{1,0:T(8,128)(2,1)S(1)}) custom-call(s32[7]{0:T(128)S(1)} %stack.19.info_ref, bf16[1024,512]{1,0:T(8,128)(2,1)S(1)} %get-tuple-element.42.live_ref, bf16[1024,1024]{1,0:T(8,128)(2,1)S(1)} %get-tuple-element.49.left_ref, ...), custom_call_target="tpu_custom_call" | custom-call | flops 200000000 | bytes 1000000 | tf_op jit(solution)/shard_map/term_rows/pallas_call | solution.py:150
  17.7 2.2 %term_rows.8 = (f32[512,512]{1,0:T(8,128)S(1)}, f32[8,128]{1,0:T(8,128)S(1)}, bf16[1024,1024]{1,0:T(8,128)(2,1)S(1)}, bf16[512,512]{1,0:T(8,128)(2,1)S(1)}) custom-call(s32[7]{0:T(128)S(1)} %stack.19.info_ref, bf16[1024,512]{1,0:T(8,128)(2,1)S(1)} %get-tuple-element.42.live_ref, bf16[1024,1024]{1,0:T(8,128)(2,1)S(1)} %get-tuple-element.54.left_ref, ...), custom_call_target="tpu_custom_call" | custom-call | flops 200000000 | bytes 1000000 | tf_op jit(solution)/shard_map/term_rows/pallas_call | solution.py:150
  19.9 4.4 %collective-permute-start.6 = (f32[512,512]{1,0:T(8,128)S(1)}, f32[512,512]{1,0:T(8,128)S(1)}, u32[]{:S(2)}, u32[]{:S(2)}) collective-permute-start(f32[512,512]{1,0:T(8,128)S(1)} %get-tuple-element.65), channel_id=1, source_target_pairs={{0,1},{4,5},{8,9},{12,13},{1,0},{5,4},{9,8},{13,12},{2,3},{6,7},{1... | collective-permute-start | bytes 3145736 | tf_op jit(solution)/shard_map/ppermute | solution.py:320
  24.3 1.3 %collective-permute-done.2.refs_0_ = f32[512,512]{1,0:T(8,128)S(1)} collective-permute-done((f32[512,512]{1,0:T(8,128)S(1)}, f32[512,512]{1,0:T(8,128)S(1)}, u32[]{:S(2)}, u32[]{:S(2)}) %collective-permute-start.2) | collective-permute-done | bytes 1048608 | tf_op jit(solution)/shard_map/ppermute | solution.py:332
  25.6 4.6 %collective-permute-start.5 = (f32[512,512]{1,0:T(8,128)S(1)}, f32[512,512]{1,0:T(8,128)S(1)}, u32[]{:S(2)}, u32[]{:S(2)}) collective-permute-start(f32[512,512]{1,0:T(8,128)S(1)} %get-tuple-element.64.a_ref), channel_id=1, source_target_pairs={{0,4},{4,8},{8,12},{16,20},{20,24},{24,28}} | collective-permute-start | bytes 3145736 | tf_op jit(solution)/shard_map/ppermute | solution.py:320
  30.2 0.7 collective-permute-start.4
  30.9 1.5 %term_rows.9 = (f32[512,512]{1,0:T(8,128)S(1)}, f32[8,128]{1,0:T(8,128)S(1)}) custom-call(s32[7]{0:T(128)S(1)} %stack.19.info_ref, bf16[1024,512]{1,0:T(8,128)(2,1)S(1)} %get-tuple-element.42.live_ref, bf16[1024,1024]{1,0:T(8,128)(2,1)S(1)} %get-tuple-element.54.left_ref, bf16[512,512]{1,0:T(8,128)(2,1)S(1)} %get-tuple-element.55.right_ref, ...), custom_call_target="tpu_custom_call" | custom-call | flops 200000000 | bytes 1000000 | tf_op jit(solution)/shard_map/term_rows/pallas_call | solution.py:150
  33.4 3.4 %collective-permute-done.7.refs_0_ = f32[512,512]{1,0:T(8,128)S(1)} collective-permute-done((f32[512,512]{1,0:T(8,128)S(1)}, f32[512,512]{1,0:T(8,128)S(1)}, u32[]{:S(2)}, u32[]{:S(2)}) %collective-permute-start.7) | collective-permute-done | bytes 1048608 | tf_op jit(solution)/shard_map/ppermute | solution.py:332
  37.1 4.4 %collective-permute-start.10 = (f32[512,512]{1,0:T(8,128)S(1)}, f32[512,512]{1,0:T(8,128)S(1)}, u32[]{:S(2)}, u32[]{:S(2)}) collective-permute-start(f32[512,512]{1,0:T(8,128)S(1)} %get-tuple-element.77.a_ref), channel_id=1, source_target_pairs={{0,4},{4,8},{8,12},{16,20},{20,24},{24,28}} | collective-permute-start | bytes 3145736 | tf_op jit(solution)/shard_map/ppermute | solution.py:320
  41.5 1.5 %term_rows.10 = (f32[512,512]{1,0:T(8,128)S(1)}, f32[8,128]{1,0:T(8,128)S(1)}) custom-call(s32[7]{0:T(128)S(1)} %stack.19.info_ref, bf16[1024,512]{1,0:T(8,128)(2,1)S(1)} %get-tuple-element.42.live_ref, bf16[1024,1024]{1,0:T(8,128)(2,1)S(1)} %get-tuple-element.57.left_ref, bf16[512,512]{1,0:T(8,128)(2,1)S(1)} %get-tuple-element.58.right_ref, ...), custom_call_target="tpu_custom_call" | custom-call | flops 200000000 | bytes 1000000 | tf_op jit(solution)/shard_map/term_rows/pallas_call | solution.py:150
  43.9 1.5 %finish_rows.2 = (bf16[1,1024,512]{2,1,0:T(8,128)(2,1)}, f32[8,128]{1,0:T(8,128)S(1)}) custom-call(s32[7]{0:T(128)S(1)} %stack.19.info_ref, bf16[1024,512]{1,0:T(8,128)(2,1)S(1)} %get-tuple-element.42.live_ref, f32[512,512]{1,0:T(8,128)S(1)} %get-tuple-element.73.own_ref, f32[512,512]{1,0:T(8,128)S(1)} %get-tuple-element.64.a_ref, ...), custom_call_target="tpu_custom_call" | custom-call | flops 200000000 | bytes 1000000 | tf_op jit(solution)/shard_map/finish_rows/pallas_call | solution.py:259
  45.5 1.5 %term_rows.11 = (f32[512,512]{1,0:T(8,128)S(1)}, f32[8,128]{1,0:T(8,128)}) custom-call(s32[7]{0:T(128)S(1)} %stack.19.info_ref, bf16[1024,512]{1,0:T(8,128)(2,1)S(1)} %get-tuple-element.42.live_ref, bf16[1024,1024]{1,0:T(8,128)(2,1)S(1)} %get-tuple-element.57.left_ref, bf16[512,512]{1,0:T(8,128)(2,1)S(1)} %get-tuple-element.58.right_ref, ...), custom_call_target="tpu_custom_call" | custom-call | flops 200000000 | bytes 1000000 | tf_op jit(solution)/shard_map/term_rows/pallas_call | solution.py:150
  47.0 6.7 %collective-permute-done.10.b_ref = f32[512,512]{1,0:T(8,128)S(1)} collective-permute-done((f32[512,512]{1,0:T(8,128)S(1)}, f32[512,512]{1,0:T(8,128)S(1)}, u32[]{:S(2)}, u32[]{:S(2)}) %collective-permute-start.10) | collective-permute-done | bytes 1048608 | tf_op jit(solution)/shard_map/ppermute | solution.py:320
  53.7 1.5 %finish_rows.3 = (bf16[1,1024,512]{2,1,0:T(8,128)(2,1)}, f32[8,128]{1,0:T(8,128)S(1)}) custom-call(s32[7]{0:T(128)S(1)} %stack.19.info_ref, bf16[1024,512]{1,0:T(8,128)(2,1)S(1)} %get-tuple-element.42.live_ref, f32[512,512]{1,0:T(8,128)S(1)} %get-tuple-element.76.own_ref, f32[512,512]{1,0:T(8,128)S(1)} %get-tuple-element.77.a_ref, ...), custom_call_target="tpu_custom_call", output_to_operand_aliasing={{0}: (7, {})} | custom-call | flops 200000000 | bytes 1000000 | tf_op jit(solution)/shard_map/finish_rows/pallas_call | solution.py:259
  55.2 8.2 %collective-permute-start.12 = (f32[8,128]{1,0:T(8,128)S(1)}, f32[8,128]{1,0:T(8,128)S(1)}, u32[]{:S(2)}, u32[]{:S(2)}) collective-permute-start(f32[8,128]{1,0:T(8,128)S(1)} %get-tuple-element.81.a_ref), channel_id=1, source_target_pairs={{0,1},{1,0},{2,3},{3,2},{4,5},{5,4},{6,7},{7,6},{8,9},{9,8},{10,11... | collective-permute-start | bytes 12296 | tf_op jit(solution)/shard_map/ppermute | solution.py:284
  63.5 0.8 %collective-permute-done.12.b_ref = f32[8,128]{1,0:T(8,128)S(1)} collective-permute-done((f32[8,128]{1,0:T(8,128)S(1)}, f32[8,128]{1,0:T(8,128)S(1)}, u32[]{:S(2)}, u32[]{:S(2)}) %collective-permute-start.12) | collective-permute-done | bytes 4128 | tf_op jit(solution)/shard_map/ppermute | solution.py:284
  64.3 10.4 %all_to_all.11 = f32[8,1,128]{2,1,0:T(1,128)S(1)} all-to-all(f32[8,1,128]{2,1,0:T(1,128)S(1)} %bitcast.10), channel_id=1, replica_groups={{0,2,4,6,8,10,12,14},{1,3,5,7,9,11,13,15},{16,18,20,22,24,26,28,30},{17..., dimensions={0} | all-to-all | bytes 8192 | tf_op jit(solution)/shard_map/all_to_all | solution.py:295
  (28 shorter events, 4.3 us)
Async XLA Ops:
  2.0 1.2 %copy-start.1 = (bf16[1,1024,512]{2,1,0:T(8,128)(2,1)S(1)}, bf16[1,1024,512]{2,1,0:T(8,128)(2,1)}, u32[]{:S(2)}) copy-start(bf16[1,1024,512]{2,1,0:T(8,128)(2,1)} %param.5) | copy-start | bytes 3145732
  6.2 2.8 %collective-permute-start = (f32[512,512]{1,0:T(8,128)S(1)}, f32[512,512]{1,0:T(8,128)S(1)}, u32[]{:S(2)}, u32[]{:S(2)}) collective-permute-start(f32[512,512]{1,0:T(8,128)S(1)} %get-tuple-element.43.a_ref), channel_id=1, source_target_pairs={{0,1},{4,5},{8,9},{12,13},{1,0},{5,4},{9,8},{13,12},{2,3},{6,7},{1... | collective-permute-start | bytes 3145736 | tf_op jit(solution)/shard_map/ppermute | solution.py:320
  6.8 3.7 %copy-start = (bf16[1,4,512,512]{3,2,1,0:T(8,128)(2,1)S(1)}, bf16[1,4,512,512]{3,2,1,0:T(8,128)(2,1)}, u32[]{:S(2)}) copy-start(bf16[1,4,512,512]{3,2,1,0:T(8,128)(2,1)} %refs_1_.3) | copy-start | bytes 6291460
  8.3 5.8 %collective-permute-start.1 = (f32[512,512]{1,0:T(8,128)S(1)}, f32[512,512]{1,0:T(8,128)S(1)}, u32[]{:S(2)}, u32[]{:S(2)}) collective-permute-start(f32[512,512]{1,0:T(8,128)S(1)} %get-tuple-element.51.a_ref), channel_id=1, source_target_pairs={{0,1},{4,5},{8,9},{12,13},{1,0},{5,4},{9,8},{13,12},{2,3},{6,7},{1... | collective-permute-start | bytes 3145736 | tf_op jit(solution)/shard_map/ppermute | solution.py:320
  9.2 16.4 %collective-permute-start.2 = (f32[512,512]{1,0:T(8,128)S(1)}, f32[512,512]{1,0:T(8,128)S(1)}, u32[]{:S(2)}, u32[]{:S(2)}) collective-permute-start(f32[512,512]{1,0:T(8,128)S(1)} %get-tuple-element.59), channel_id=1, source_target_pairs={{1,2},{5,6},{9,10},{13,14},{3,0},{7,4},{11,8},{17,18},{21,22},{25,... | collective-permute-start | bytes 3145736 | tf_op jit(solution)/shard_map/ppermute | solution.py:332
  13.3 19.2 %collective-permute-start.8 = (f32[512,512]{1,0:T(8,128)S(1)}, f32[512,512]{1,0:T(8,128)S(1)}, u32[]{:S(2)}, u32[]{:S(2)}) collective-permute-start(f32[512,512]{1,0:T(8,128)S(1)} %get-tuple-element.67.a_ref), channel_id=1, source_target_pairs={{3,6},{7,10},{11,14},{4,1},{8,5},{12,9},{19,22},{23,26},{27,30},{2... | collective-permute-start | bytes 3145736 | tf_op jit(solution)/shard_map/ppermute | solution.py:320
  14.2 22.6 %collective-permute-start.7 = (f32[512,512]{1,0:T(8,128)S(1)}, f32[512,512]{1,0:T(8,128)S(1)}, u32[]{:S(2)}, u32[]{:S(2)}) collective-permute-start(f32[512,512]{1,0:T(8,128)S(1)} %get-tuple-element.66), channel_id=1, source_target_pairs={{1,2},{5,6},{9,10},{13,14},{3,0},{7,4},{11,8},{17,18},{21,22},{25,... | collective-permute-start | bytes 3145736 | tf_op jit(solution)/shard_map/ppermute | solution.py:332
  19.9 17.2 %collective-permute-start.6 = (f32[512,512]{1,0:T(8,128)S(1)}, f32[512,512]{1,0:T(8,128)S(1)}, u32[]{:S(2)}, u32[]{:S(2)}) collective-permute-start(f32[512,512]{1,0:T(8,128)S(1)} %get-tuple-element.65), channel_id=1, source_target_pairs={{0,1},{4,5},{8,9},{12,13},{1,0},{5,4},{9,8},{13,12},{2,3},{6,7},{1... | collective-permute-start | bytes 3145736 | tf_op jit(solution)/shard_map/ppermute | solution.py:320
  25.6 17.4 %collective-permute-start.5 = (f32[512,512]{1,0:T(8,128)S(1)}, f32[512,512]{1,0:T(8,128)S(1)}, u32[]{:S(2)}, u32[]{:S(2)}) collective-permute-start(f32[512,512]{1,0:T(8,128)S(1)} %get-tuple-element.64.a_ref), channel_id=1, source_target_pairs={{0,4},{4,8},{8,12},{16,20},{20,24},{24,28}} | collective-permute-start | bytes 3145736 | tf_op jit(solution)/shard_map/ppermute | solution.py:320
  30.2 12.8 %collective-permute-start.4 = (f32[512,512]{1,0:T(8,128)S(1)}, f32[512,512]{1,0:T(8,128)S(1)}, u32[]{:S(2)}, u32[]{:S(2)}) collective-permute-start(f32[512,512]{1,0:T(8,128)S(1)} %get-tuple-element.63.a_ref), channel_id=1, source_target_pairs={{3,6},{7,10},{11,14},{4,1},{8,5},{12,9},{19,22},{23,26},{27,30},{2... | collective-permute-start | bytes 3145736 | tf_op jit(solution)/shard_map/ppermute | solution.py:320
  32.6 11.3 %collective-permute-start.9 = (f32[512,512]{1,0:T(8,128)S(1)}, f32[512,512]{1,0:T(8,128)S(1)}, u32[]{:S(2)}, u32[]{:S(2)}) collective-permute-start(f32[512,512]{1,0:T(8,128)S(1)} %get-tuple-element.74), channel_id=1, source_target_pairs={{1,3},{5,7},{9,11},{13,15},{2,1},{6,5},{10,9},{14,13},{17,19},{21,... | collective-permute-start | bytes 3145736 | tf_op jit(solution)/shard_map/ppermute | solution.py:320
  36.8 8.7 %collective-permute-start.3 = (f32[512,512]{1,0:T(8,128)S(1)}, f32[512,512]{1,0:T(8,128)S(1)}, u32[]{:S(2)}, u32[]{:S(2)}) collective-permute-start(f32[512,512]{1,0:T(8,128)S(1)} %get-tuple-element.62), channel_id=1, source_target_pairs={{0,1},{4,5},{8,9},{12,13},{1,0},{5,4},{9,8},{13,12},{2,3},{6,7},{1... | collective-permute-start | bytes 3145736 | tf_op jit(solution)/shard_map/ppermute | solution.py:320
  37.1 16.6 %collective-permute-start.10 = (f32[512,512]{1,0:T(8,128)S(1)}, f32[512,512]{1,0:T(8,128)S(1)}, u32[]{:S(2)}, u32[]{:S(2)}) collective-permute-start(f32[512,512]{1,0:T(8,128)S(1)} %get-tuple-element.77.a_ref), channel_id=1, source_target_pairs={{0,4},{4,8},{8,12},{16,20},{20,24},{24,28}} | collective-permute-start | bytes 3145736 | tf_op jit(solution)/shard_map/ppermute | solution.py:320
  43.2 10.5 %collective-permute-start.11 = (f32[512,512]{1,0:T(8,128)S(1)}, f32[512,512]{1,0:T(8,128)S(1)}, u32[]{:S(2)}, u32[]{:S(2)}) collective-permute-start(f32[512,512]{1,0:T(8,128)S(1)} %get-tuple-element.78), channel_id=1, source_target_pairs={{1,3},{5,7},{9,11},{13,15},{2,1},{6,5},{10,9},{14,13},{17,19},{21,... | collective-permute-start | bytes 3145736 | tf_op jit(solution)/shard_map/ppermute | solution.py:320
  55.2 9.1 %collective-permute-start.12 = (f32[8,128]{1,0:T(8,128)S(1)}, f32[8,128]{1,0:T(8,128)S(1)}, u32[]{:S(2)}, u32[]{:S(2)}) collective-permute-start(f32[8,128]{1,0:T(8,128)S(1)} %get-tuple-element.81.a_ref), channel_id=1, source_target_pairs={{0,1},{1,0},{2,3},{3,2},{4,5},{5,4},{6,7},{7,6},{8,9},{9,8},{10,11... | collective-permute-start | bytes 12296 | tf_op jit(solution)/shard_map/ppermute | solution.py:284

commit v16 on v14

--- a/solution.py
+++ b/solution.py
@@ -60,7 +60,7 @@
     if masks:
         live_ref = operands.pop(0)
     own, late = fetch(info_ref, slot, left_hbm, right_hbm, *operands, sems)
-    for copy in own:
+    for copy in own + late:
         copy.start()
     if masks:
         rows, cols = psi_ref.shape
@@ -74,8 +74,6 @@
             live_ref[span, :] = values.astype(live_ref.dtype)
     for copy in own:
         copy.wait()
-    for copy in late:
-        copy.start()
     out_ref[...] = multiply(operands[0][: out_ref.shape[0], :], live_ref[...], operands[1][...])
     for copy in late:
         copy.wait()
@@ -274,21 +272,9 @@
     )(*operands)
 
 
-def sum_kernel(in_ref, out_ref):
-    out_ref[0] = jnp.sum(in_ref[:, :1])
-
-
 def sum_over_sectors(value):
     arrived = lax.all_to_all(value, "sec", 0, 0, tiled=True)
-    return pl.pallas_call(
-        sum_kernel,
-        out_shape=jax.ShapeDtypeStruct((1,), jnp.float32),
-        in_specs=[WHOLE],
-        out_specs=SMEM,
-        compiler_params=params(),
-        cost_estimate=SMALL,
-        name="sum_energy",
-    )(arrived)
+    return jnp.reshape(jnp.sum(arrived[:, 0]), (1,))
 
 
 def on_device(psi, left_env, right_env, row_sizes, col_sizes):

time: 74.8 us -> 74.5 us (level)
  Pallas kernels: 20.9 us -> 19.8 us
where the time goes in v16:
time: 74.5 us; the launch traced here: 74.1 us
  Pallas kernels  19.8 us (27%)
  starting transfers between devices  19.8 us (27%)
  blocking collectives  18.2 us (24%)
  waiting for transfers between devices  12.1 us (16%)
  between operations  2.18 us (3%)
  local copies, waits for them, and re-layouts  1.32 us (2%)
    all_to_all x1, blocking collectives, sum_over_sectors(): arrived = lax.all_to_all(value, 'sec', 0, 0, tiled=True)  18.2 us
    ppermute x10, starting transfers between devices, send(): return lax.ppermute(value, 'sec', pairs)  17.2 us
    pallas_call x6, Pallas kernels, term_rows(): pl.pallas_call(functools.partial(term_kernel, first, added is not None, s...  10.4 us
    ppermute x10, waiting for transfers between devices, send(): return lax.ppermute(value, 'sec', pairs)  7.36 us
    pallas_call x2, Pallas kernels, opening_rows(): pl.pallas_call(functools.partial(opening_kernel, slot, masks, len(tokens)...  5.77 us
    ppermute x2, waiting for transfers between devices, raise_one(): return lax.ppermute(value, 'sec', pairs_up)  4.75 us
    pallas_call x2, Pallas kernels, finish(): pl.pallas_call(functools.partial(finish_kernel, first), out_shape=(jax.Sh...  3.07 us
    ppermute x2, starting transfers between devices, raise_one(): return lax.ppermute(value, 'sec', pairs_up)  2.58 us
  transfers between devices with their start and end apart: 12, of which 4 were waited for; matrix products, arithmetic and copies ran while one was open for 0% of the time, Pallas kernels for 21%

profile of v16, /device:TPU:0, one launch (start us, length us, event | category | flops | bytes accessed | tf_op | source)
XLA Modules:
  0.0 74.1 jit_solution(13189868702450662355)
XLA Ops:
  2.0 1.2 %copy-done.1 = bf16[1,1024,512]{2,1,0:T(8,128)(2,1)S(1)} copy-done((bf16[1,1024,512]{2,1,0:T(8,128)(2,1)S(1)}, bf16[1,1024,512]{2,1,0:T(8,128)(2,1)}, u32[]{:S(2)}) %copy-start.1) | copy-done | bytes 1048600
  3.3 3.0 %opening_rows.2 = (f32[512,512]{1,0:T(8,128)S(1)}, f32[8,128]{1,0:T(8,128)S(1)}, bf16[1024,512]{1,0:T(8,128)(2,1)S(1)}, bf16[1024,1024]{1,0:T(8,128)(2,1)S(1)}, bf16[512,512]{1,0:T(8,128)(2,1)S(1)}) custom-call(s32[7]{0:T(128)S(1)} %stack.19.info_ref, bf16[1024,512]{1,0:T(8,128)(2,1)S(1)} %bitcast.10, bf16[1,4,1024,1024]{3,2,1,0:T(8,128)(2,1)} %refs_0_.3, ...), custom_call_target="tpu_custom_call" | custom-call | flops 200000000 | bytes 1000000 | tf_op jit(solution)/shard_map/opening_rows/pallas_call | solution.py:95
  6.8 1.5 %term_rows.6 = (f32[512,512]{1,0:T(8,128)S(1)}, f32[8,128]{1,0:T(8,128)S(1)}) custom-call(s32[7]{0:T(128)S(1)} %stack.19.info_ref, bf16[1024,512]{1,0:T(8,128)(2,1)S(1)} %get-tuple-element.42.live_ref, bf16[1024,1024]{1,0:T(8,128)(2,1)S(1)} %get-tuple-element.44.left_ref, bf16[512,512]{1,0:T(8,128)(2,1)S(1)} %get-tuple-element.45.right_ref, ...), custom_call_target="tpu_custom_call" | custom-call | flops 200000000 | bytes 1000000 | tf_op jit(solution)/shard_map/term_rows/pallas_call | solution.py:150
  9.2 1.3 %collective-permute-start.2 = (f32[512,512]{1,0:T(8,128)S(1)}, f32[512,512]{1,0:T(8,128)S(1)}, u32[]{:S(2)}, u32[]{:S(2)}) collective-permute-start(f32[512,512]{1,0:T(8,128)S(1)} %get-tuple-element.59), channel_id=1, source_target_pairs={{1,2},{5,6},{9,10},{13,14},{3,0},{7,4},{11,8},{17,18},{21,22},{25,... | collective-permute-start | bytes 3145736 | tf_op jit(solution)/shard_map/ppermute | solution.py:305
  10.5 2.8 %opening_rows.3 = (f32[512,512]{1,0:T(8,128)S(1)}, f32[8,128]{1,0:T(8,128)S(1)}, bf16[1024,1024]{1,0:T(8,128)(2,1)S(1)}, bf16[512,512]{1,0:T(8,128)(2,1)S(1)}) custom-call(s32[7]{0:T(128)S(1)} %stack.19.info_ref, bf16[1024,512]{1,0:T(8,128)(2,1)S(1)} %get-tuple-element.42.live_ref, bf16[1,4,1024,1024]{3,2,1,0:T(8,128)(2,1)} %refs_0_.3, ...), custom_call_target="tpu_custom_call" | custom-call | flops 200000000 | bytes 1000000 | tf_op jit(solution)/shard_map/opening_rows/pallas_call | solution.py:95
  13.3 0.7 collective-permute-start.8
  14.2 1.3 %collective-permute-start.7 = (f32[512,512]{1,0:T(8,128)S(1)}, f32[512,512]{1,0:T(8,128)S(1)}, u32[]{:S(2)}, u32[]{:S(2)}) collective-permute-start(f32[512,512]{1,0:T(8,128)S(1)} %get-tuple-element.66), channel_id=1, source_target_pairs={{1,2},{5,6},{9,10},{13,14},{3,0},{7,4},{11,8},{17,18},{21,22},{25,... | collective-permute-start | bytes 3145736 | tf_op jit(solution)/shard_map/ppermute | solution.py:305
  15.5 2.2 %term_rows.7 = (f32[512,512]{1,0:T(8,128)S(1)}, f32[8,128]{1,0:T(8,128)S(1)}, bf16[1024,1024]{1,0:T(8,128)(2,1)S(1)}, bf16[512,512]{1,0:T(8,128)(2,1)S(1)}) custom-call(s32[7]{0:T(128)S(1)} %stack.19.info_ref, bf16[1024,512]{1,0:T(8,128)(2,1)S(1)} %get-tuple-element.42.live_ref, bf16[1024,1024]{1,0:T(8,128)(2,1)S(1)} %get-tuple-element.49.left_ref, ...), custom_call_target="tpu_custom_call" | custom-call | flops 200000000 | bytes 1000000 | tf_op jit(solution)/shard_map/term_rows/pallas_call | solution.py:150
  17.7 2.2 %term_rows.8 = (f32[512,512]{1,0:T(8,128)S(1)}, f32[8,128]{1,0:T(8,128)S(1)}, bf16[1024,1024]{1,0:T(8,128)(2,1)S(1)}, bf16[512,512]{1,0:T(8,128)(2,1)S(1)}) custom-call(s32[7]{0:T(128)S(1)} %stack.19.info_ref, bf16[1024,512]{1,0:T(8,128)(2,1)S(1)} %get-tuple-element.42.live_ref, bf16[1024,1024]{1,0:T(8,128)(2,1)S(1)} %get-tuple-element.54.left_ref, ...), custom_call_target="tpu_custom_call" | custom-call | flops 200000000 | bytes 1000000 | tf_op jit(solution)/shard_map/term_rows/pallas_call | solution.py:150
  19.9 4.4 %collective-permute-start.6 = (f32[512,512]{1,0:T(8,128)S(1)}, f32[512,512]{1,0:T(8,128)S(1)}, u32[]{:S(2)}, u32[]{:S(2)}) collective-permute-start(f32[512,512]{1,0:T(8,128)S(1)} %get-tuple-element.65), channel_id=1, source_target_pairs={{0,1},{4,5},{8,9},{12,13},{1,0},{5,4},{9,8},{13,12},{2,3},{6,7},{1... | collective-permute-start | bytes 3145736 | tf_op jit(solution)/shard_map/ppermute | solution.py:293
  24.3 1.3 %collective-permute-done.2.refs_0_ = f32[512,512]{1,0:T(8,128)S(1)} collective-permute-done((f32[512,512]{1,0:T(8,128)S(1)}, f32[512,512]{1,0:T(8,128)S(1)}, u32[]{:S(2)}, u32[]{:S(2)}) %collective-permute-start.2) | collective-permute-done | bytes 1048608 | tf_op jit(solution)/shard_map/ppermute | solution.py:305
  25.6 4.6 %collective-permute-start.5 = (f32[512,512]{1,0:T(8,128)S(1)}, f32[512,512]{1,0:T(8,128)S(1)}, u32[]{:S(2)}, u32[]{:S(2)}) collective-permute-start(f32[512,512]{1,0:T(8,128)S(1)} %get-tuple-element.64.a_ref), channel_id=1, source_target_pairs={{0,4},{4,8},{8,12},{16,20},{20,24},{24,28}} | collective-permute-start | bytes 3145736 | tf_op jit(solution)/shard_map/ppermute | solution.py:293
  30.2 0.7 collective-permute-start.4
  30.9 1.5 %term_rows.9 = (f32[512,512]{1,0:T(8,128)S(1)}, f32[8,128]{1,0:T(8,128)S(1)}) custom-call(s32[7]{0:T(128)S(1)} %stack.19.info_ref, bf16[1024,512]{1,0:T(8,128)(2,1)S(1)} %get-tuple-element.42.live_ref, bf16[1024,1024]{1,0:T(8,128)(2,1)S(1)} %get-tuple-element.54.left_ref, bf16[512,512]{1,0:T(8,128)(2,1)S(1)} %get-tuple-element.55.right_ref, ...), custom_call_target="tpu_custom_call" | custom-call | flops 200000000 | bytes 1000000 | tf_op jit(solution)/shard_map/term_rows/pallas_call | solution.py:150
  32.6 0.7 collective-permute-start.9
  33.4 3.4 %collective-permute-done.7.refs_0_ = f32[512,512]{1,0:T(8,128)S(1)} collective-permute-done((f32[512,512]{1,0:T(8,128)S(1)}, f32[512,512]{1,0:T(8,128)S(1)}, u32[]{:S(2)}, u32[]{:S(2)}) %collective-permute-start.7) | collective-permute-done | bytes 1048608 | tf_op jit(solution)/shard_map/ppermute | solution.py:305
  37.1 4.4 %collective-permute-start.10 = (f32[512,512]{1,0:T(8,128)S(1)}, f32[512,512]{1,0:T(8,128)S(1)}, u32[]{:S(2)}, u32[]{:S(2)}) collective-permute-start(f32[512,512]{1,0:T(8,128)S(1)} %get-tuple-element.77.a_ref), channel_id=1, source_target_pairs={{0,4},{4,8},{8,12},{16,20},{20,24},{24,28}} | collective-permute-start | bytes 3145736 | tf_op jit(solution)/shard_map/ppermute | solution.py:293
  41.5 1.5 %term_rows.10 = (f32[512,512]{1,0:T(8,128)S(1)}, f32[8,128]{1,0:T(8,128)S(1)}) custom-call(s32[7]{0:T(128)S(1)} %stack.19.info_ref, bf16[1024,512]{1,0:T(8,128)(2,1)S(1)} %get-tuple-element.42.live_ref, bf16[1024,1024]{1,0:T(8,128)(2,1)S(1)} %get-tuple-element.57.left_ref, bf16[512,512]{1,0:T(8,128)(2,1)S(1)} %get-tuple-element.58.right_ref, ...), custom_call_target="tpu_custom_call" | custom-call | flops 200000000 | bytes 1000000 | tf_op jit(solution)/shard_map/term_rows/pallas_call | solution.py:150
  43.2 0.7 collective-permute-start.11
  43.9 1.5 %finish_rows.2 = (bf16[1,1024,512]{2,1,0:T(8,128)(2,1)}, f32[16,128]{1,0:T(8,128)S(1)}) custom-call(s32[7]{0:T(128)S(1)} %stack.19.info_ref, bf16[1024,512]{1,0:T(8,128)(2,1)S(1)} %get-tuple-element.42.live_ref, f32[512,512]{1,0:T(8,128)S(1)} %get-tuple-element.73.own_ref, f32[512,512]{1,0:T(8,128)S(1)} %get-tuple-element.64.a_ref, ...), custom_call_target="tpu_custom_call" | custom-call | flops 200000000 | bytes 1000000 | tf_op jit(solution)/shard_map/finish_rows/pallas_call | solution.py:259
  45.5 1.5 %term_rows.11 = (f32[512,512]{1,0:T(8,128)S(1)}, f32[8,128]{1,0:T(8,128)}) custom-call(s32[7]{0:T(128)S(1)} %stack.19.info_ref, bf16[1024,512]{1,0:T(8,128)(2,1)S(1)} %get-tuple-element.42.live_ref, bf16[1024,1024]{1,0:T(8,128)(2,1)S(1)} %get-tuple-element.57.left_ref, bf16[512,512]{1,0:T(8,128)(2,1)S(1)} %get-tuple-element.58.right_ref, ...), custom_call_target="tpu_custom_call" | custom-call | flops 200000000 | bytes 1000000 | tf_op jit(solution)/shard_map/term_rows/pallas_call | solution.py:150
  47.0 6.7 %collective-permute-done.10.b_ref = f32[512,512]{1,0:T(8,128)S(1)} collective-permute-done((f32[512,512]{1,0:T(8,128)S(1)}, f32[512,512]{1,0:T(8,128)S(1)}, u32[]{:S(2)}, u32[]{:S(2)}) %collective-permute-start.10) | collective-permute-done | bytes 1048608 | tf_op jit(solution)/shard_map/ppermute | solution.py:293
  53.7 1.5 %finish_rows.3 = (bf16[1,1024,512]{2,1,0:T(8,128)(2,1)}, f32[16,128]{1,0:T(8,128)S(1)}) custom-call(s32[7]{0:T(128)S(1)} %stack.19.info_ref, bf16[1024,512]{1,0:T(8,128)(2,1)S(1)} %get-tuple-element.42.live_ref, f32[512,512]{1,0:T(8,128)S(1)} %get-tuple-element.76.own_ref, f32[512,512]{1,0:T(8,128)S(1)} %get-tuple-element.77.a_ref, ...), custom_call_target="tpu_custom_call", output_to_operand_aliasing={{0}: (7, {})} | custom-call | flops 200000000 | bytes 1000000 | tf_op jit(solution)/shard_map/finish_rows/pallas_call | solution.py:259
  55.2 18.2 %all_to_all.12 = f32[16,1,128]{2,1,0:T(1,128)S(1)} all-to-all(f32[16,1,128]{2,1,0:T(1,128)S(1)} %bitcast.11), channel_id=1, replica_groups=mesh['grp'=2,'sec'=16] {'sec'}, dimensions={0} | all-to-all | bytes 16384 | tf_op jit(solution)/shard_map/all_to_all | solution.py:276
  (25 shorter events, 2.8 us)
Async XLA Ops:
  2.0 1.2 %copy-start.1 = (bf16[1,1024,512]{2,1,0:T(8,128)(2,1)S(1)}, bf16[1,1024,512]{2,1,0:T(8,128)(2,1)}, u32[]{:S(2)}) copy-start(bf16[1,1024,512]{2,1,0:T(8,128)(2,1)} %param.5) | copy-start | bytes 3145732
  6.2 2.8 %collective-permute-start = (f32[512,512]{1,0:T(8,128)S(1)}, f32[512,512]{1,0:T(8,128)S(1)}, u32[]{:S(2)}, u32[]{:S(2)}) collective-permute-start(f32[512,512]{1,0:T(8,128)S(1)} %get-tuple-element.43.a_ref), channel_id=1, source_target_pairs={{0,1},{4,5},{8,9},{12,13},{1,0},{5,4},{9,8},{13,12},{2,3},{6,7},{1... | collective-permute-start | bytes 3145736 | tf_op jit(solution)/shard_map/ppermute | solution.py:293
  6.8 3.7 %copy-start = (bf16[1,4,512,512]{3,2,1,0:T(8,128)(2,1)S(1)}, bf16[1,4,512,512]{3,2,1,0:T(8,128)(2,1)}, u32[]{:S(2)}) copy-start(bf16[1,4,512,512]{3,2,1,0:T(8,128)(2,1)} %refs_1_.3) | copy-start | bytes 6291460
  8.3 5.8 %collective-permute-start.1 = (f32[512,512]{1,0:T(8,128)S(1)}, f32[512,512]{1,0:T(8,128)S(1)}, u32[]{:S(2)}, u32[]{:S(2)}) collective-permute-start(f32[512,512]{1,0:T(8,128)S(1)} %get-tuple-element.51.a_ref), channel_id=1, source_target_pairs={{0,1},{4,5},{8,9},{12,13},{1,0},{5,4},{9,8},{13,12},{2,3},{6,7},{1... | collective-permute-start | bytes 3145736 | tf_op jit(solution)/shard_map/ppermute | solution.py:293
  9.2 16.4 %collective-permute-start.2 = (f32[512,512]{1,0:T(8,128)S(1)}, f32[512,512]{1,0:T(8,128)S(1)}, u32[]{:S(2)}, u32[]{:S(2)}) collective-permute-start(f32[512,512]{1,0:T(8,128)S(1)} %get-tuple-element.59), channel_id=1, source_target_pairs={{1,2},{5,6},{9,10},{13,14},{3,0},{7,4},{11,8},{17,18},{21,22},{25,... | collective-permute-start | bytes 3145736 | tf_op jit(solution)/shard_map/ppermute | solution.py:305
  13.3 19.2 %collective-permute-start.8 = (f32[512,512]{1,0:T(8,128)S(1)}, f32[512,512]{1,0:T(8,128)S(1)}, u32[]{:S(2)}, u32[]{:S(2)}) collective-permute-start(f32[512,512]{1,0:T(8,128)S(1)} %get-tuple-element.67.a_ref), channel_id=1, source_target_pairs={{3,6},{7,10},{11,14},{4,1},{8,5},{12,9},{19,22},{23,26},{27,30},{2... | collective-permute-start | bytes 3145736 | tf_op jit(solution)/shard_map/ppermute | solution.py:293
  14.2 22.6 %collective-permute-start.7 = (f32[512,512]{1,0:T(8,128)S(1)}, f32[512,512]{1,0:T(8,128)S(1)}, u32[]{:S(2)}, u32[]{:S(2)}) collective-permute-start(f32[512,512]{1,0:T(8,128)S(1)} %get-tuple-element.66), channel_id=1, source_target_pairs={{1,2},{5,6},{9,10},{13,14},{3,0},{7,4},{11,8},{17,18},{21,22},{25,... | collective-permute-start | bytes 3145736 | tf_op jit(solution)/shard_map/ppermute | solution.py:305
  19.9 17.2 %collective-permute-start.6 = (f32[512,512]{1,0:T(8,128)S(1)}, f32[512,512]{1,0:T(8,128)S(1)}, u32[]{:S(2)}, u32[]{:S(2)}) collective-permute-start(f32[512,512]{1,0:T(8,128)S(1)} %get-tuple-element.65), channel_id=1, source_target_pairs={{0,1},{4,5},{8,9},{12,13},{1,0},{5,4},{9,8},{13,12},{2,3},{6,7},{1... | collective-permute-start | bytes 3145736 | tf_op jit(solution)/shard_map/ppermute | solution.py:293
  25.6 17.4 %collective-permute-start.5 = (f32[512,512]{1,0:T(8,128)S(1)}, f32[512,512]{1,0:T(8,128)S(1)}, u32[]{:S(2)}, u32[]{:S(2)}) collective-permute-start(f32[512,512]{1,0:T(8,128)S(1)} %get-tuple-element.64.a_ref), channel_id=1, source_target_pairs={{0,4},{4,8},{8,12},{16,20},{20,24},{24,28}} | collective-permute-start | bytes 3145736 | tf_op jit(solution)/shard_map/ppermute | solution.py:293
  30.2 12.8 %collective-permute-start.4 = (f32[512,512]{1,0:T(8,128)S(1)}, f32[512,512]{1,0:T(8,128)S(1)}, u32[]{:S(2)}, u32[]{:S(2)}) collective-permute-start(f32[512,512]{1,0:T(8,128)S(1)} %get-tuple-element.63.a_ref), channel_id=1, source_target_pairs={{3,6},{7,10},{11,14},{4,1},{8,5},{12,9},{19,22},{23,26},{27,30},{2... | collective-permute-start | bytes 3145736 | tf_op jit(solution)/shard_map/ppermute | solution.py:293
  32.6 11.3 %collective-permute-start.9 = (f32[512,512]{1,0:T(8,128)S(1)}, f32[512,512]{1,0:T(8,128)S(1)}, u32[]{:S(2)}, u32[]{:S(2)}) collective-permute-start(f32[512,512]{1,0:T(8,128)S(1)} %get-tuple-element.74), channel_id=1, source_target_pairs={{1,3},{5,7},{9,11},{13,15},{2,1},{6,5},{10,9},{14,13},{17,19},{21,... | collective-permute-start | bytes 3145736 | tf_op jit(solution)/shard_map/ppermute | solution.py:293
  36.8 8.7 %collective-permute-start.3 = (f32[512,512]{1,0:T(8,128)S(1)}, f32[512,512]{1,0:T(8,128)S(1)}, u32[]{:S(2)}, u32[]{:S(2)}) collective-permute-start(f32[512,512]{1,0:T(8,128)S(1)} %get-tuple-element.62), channel_id=1, source_target_pairs={{0,1},{4,5},{8,9},{12,13},{1,0},{5,4},{9,8},{13,12},{2,3},{6,7},{1... | collective-permute-start | bytes 3145736 | tf_op jit(solution)/shard_map/ppermute | solution.py:293
  37.1 16.6 %collective-permute-start.10 = (f32[512,512]{1,0:T(8,128)S(1)}, f32[512,512]{1,0:T(8,128)S(1)}, u32[]{:S(2)}, u32[]{:S(2)}) collective-permute-start(f32[512,512]{1,0:T(8,128)S(1)} %get-tuple-element.77.a_ref), channel_id=1, source_target_pairs={{0,4},{4,8},{8,12},{16,20},{20,24},{24,28}} | collective-permute-start | bytes 3145736 | tf_op jit(solution)/shard_map/ppermute | solution.py:293
  43.2 10.5 %collective-permute-start.11 = (f32[512,512]{1,0:T(8,128)S(1)}, f32[512,512]{1,0:T(8,128)S(1)}, u32[]{:S(2)}, u32[]{:S(2)}) collective-permute-start(f32[512,512]{1,0:T(8,128)S(1)} %get-tuple-element.78), channel_id=1, source_target_pairs={{1,3},{5,7},{9,11},{13,15},{2,1},{6,5},{10,9},{14,13},{17,19},{21,... | collective-permute-start | bytes 3145736 | tf_op jit(solution)/shard_map/ppermute | solution.py:293

commit v17 on v16

--- a/solution.py
+++ b/solution.py
@@ -43,7 +43,7 @@
             )
         )
     half = LEFT_PIECES // 2
-    return left[:half] + right, left[half:]
+    return left[:half], right, left[half:]
 
 
 def multiply(left, live, right):
@@ -59,8 +59,8 @@
     psi_ref = live_ref
     if masks:
         live_ref = operands.pop(0)
-    own, late = fetch(info_ref, slot, left_hbm, right_hbm, *operands, sems)
-    for copy in own + late:
+    left, right, late = fetch(info_ref, slot, left_hbm, right_hbm, *operands, sems)
+    for copy in left + right + late:
         copy.start()
     if masks:
         rows, cols = psi_ref.shape
@@ -72,9 +72,16 @@
             inside = jnp.logical_and(row < info_ref[4] - start, col)
             values = jnp.where(inside, psi_ref[span, :].astype(jnp.float32), 0.0)
             live_ref[span, :] = values.astype(live_ref.dtype)
-    for copy in own:
+    for copy in left:
         copy.wait()
-    out_ref[...] = multiply(operands[0][: out_ref.shape[0], :], live_ref[...], operands[1][...])
+    value = jnp.dot(
+        operands[0][: out_ref.shape[0], :], live_ref[...], preferred_element_type=jnp.float32
+    )
+    for copy in right:
+        copy.wait()
+    out_ref[...] = jnp.dot(
+        value.astype(jnp.bfloat16), operands[1][...], preferred_element_type=jnp.float32
+    )
     for copy in late:
         copy.wait()
 

time: 74.5 us -> 74.5 us (level)
  no operation moved by 1% of the time
where the time goes in v17:
time: 74.5 us; the launch traced here: 74.1 us
  Pallas kernels  20 us (27%)
  starting transfers between devices  19.8 us (27%)
  blocking collectives  18.2 us (24%)
  waiting for transfers between devices  11.9 us (16%)
  between operations  2.18 us (3%)
  local copies, waits for them, and re-layouts  1.32 us (2%)
    all_to_all x1, blocking collectives, sum_over_sectors(): arrived = lax.all_to_all(value, 'sec', 0, 0, tiled=True)  18.2 us
    ppermute x10, starting transfers between devices, send(): return lax.ppermute(value, 'sec', pairs)  17.2 us
    pallas_call x6, Pallas kernels, term_rows(): pl.pallas_call(functools.partial(term_kernel, first, added is not None, s...  10.4 us
    ppermute x10, waiting for transfers between devices, send(): return lax.ppermute(value, 'sec', pairs)  7.36 us
    pallas_call x2, Pallas kernels, opening_rows(): pl.pallas_call(functools.partial(opening_kernel, slot, masks, len(tokens)...  5.95 us
    ppermute x2, waiting for transfers between devices, raise_one(): return lax.ppermute(value, 'sec', pairs_up)  4.58 us
    pallas_call x2, Pallas kernels, finish(): pl.pallas_call(functools.partial(finish_kernel, first), out_shape=(jax.Sh...  3.07 us
    ppermute x2, starting transfers between devices, raise_one(): return lax.ppermute(value, 'sec', pairs_up)  2.58 us
  transfers between devices with their start and end apart: 12, of which 4 were waited for; matrix products, arithmetic and copies ran while one was open for 0% of the time, Pallas kernels for 21%

profile of v17, /device:TPU:0, one launch (start us, length us, event | category | flops | bytes accessed | tf_op | source)
XLA Modules:
  0.0 74.1 jit_solution(8294594865275858312)
XLA Ops:
  2.0 1.2 %copy-done.1 = bf16[1,1024,512]{2,1,0:T(8,128)(2,1)S(1)} copy-done((bf16[1,1024,512]{2,1,0:T(8,128)(2,1)S(1)}, bf16[1,1024,512]{2,1,0:T(8,128)(2,1)}, u32[]{:S(2)}) %copy-start.1) | copy-done | bytes 1048600
  3.3 3.0 %opening_rows.2 = (f32[512,512]{1,0:T(8,128)S(1)}, f32[8,128]{1,0:T(8,128)S(1)}, bf16[1024,512]{1,0:T(8,128)(2,1)S(1)}, bf16[1024,1024]{1,0:T(8,128)(2,1)S(1)}, bf16[512,512]{1,0:T(8,128)(2,1)S(1)}) custom-call(s32[7]{0:T(128)S(1)} %stack.19.info_ref, bf16[1024,512]{1,0:T(8,128)(2,1)S(1)} %bitcast.10, bf16[1,4,1024,1024]{3,2,1,0:T(8,128)(2,1)} %refs_0_.3, ...), custom_call_target="tpu_custom_call" | custom-call | flops 200000000 | bytes 1000000 | tf_op jit(solution)/shard_map/opening_rows/pallas_call | solution.py:102
  6.8 1.5 %term_rows.6 = (f32[512,512]{1,0:T(8,128)S(1)}, f32[8,128]{1,0:T(8,128)S(1)}) custom-call(s32[7]{0:T(128)S(1)} %stack.19.info_ref, bf16[1024,512]{1,0:T(8,128)(2,1)S(1)} %get-tuple-element.42.live_ref, bf16[1024,1024]{1,0:T(8,128)(2,1)S(1)} %get-tuple-element.44.left_ref, bf16[512,512]{1,0:T(8,128)(2,1)S(1)} %get-tuple-element.45.right_ref, ...), custom_call_target="tpu_custom_call" | custom-call | flops 200000000 | bytes 1000000 | tf_op jit(solution)/shard_map/term_rows/pallas_call | solution.py:157
  9.2 1.3 %collective-permute-start.2 = (f32[512,512]{1,0:T(8,128)S(1)}, f32[512,512]{1,0:T(8,128)S(1)}, u32[]{:S(2)}, u32[]{:S(2)}) collective-permute-start(f32[512,512]{1,0:T(8,128)S(1)} %get-tuple-element.59), channel_id=1, source_target_pairs={{1,2},{5,6},{9,10},{13,14},{3,0},{7,4},{11,8},{17,18},{21,22},{25,... | collective-permute-start | bytes 3145736 | tf_op jit(solution)/shard_map/ppermute | solution.py:312
  10.5 3.0 %opening_rows.3 = (f32[512,512]{1,0:T(8,128)S(1)}, f32[8,128]{1,0:T(8,128)S(1)}, bf16[1024,1024]{1,0:T(8,128)(2,1)S(1)}, bf16[512,512]{1,0:T(8,128)(2,1)S(1)}) custom-call(s32[7]{0:T(128)S(1)} %stack.19.info_ref, bf16[1024,512]{1,0:T(8,128)(2,1)S(1)} %get-tuple-element.42.live_ref, bf16[1,4,1024,1024]{3,2,1,0:T(8,128)(2,1)} %refs_0_.3, ...), custom_call_target="tpu_custom_call" | custom-call | flops 200000000 | bytes 1000000 | tf_op jit(solution)/shard_map/opening_rows/pallas_call | solution.py:102
  13.5 0.7 collective-permute-start.8
  14.4 1.3 %collective-permute-start.7 = (f32[512,512]{1,0:T(8,128)S(1)}, f32[512,512]{1,0:T(8,128)S(1)}, u32[]{:S(2)}, u32[]{:S(2)}) collective-permute-start(f32[512,512]{1,0:T(8,128)S(1)} %get-tuple-element.66), channel_id=1, source_target_pairs={{1,2},{5,6},{9,10},{13,14},{3,0},{7,4},{11,8},{17,18},{21,22},{25,... | collective-permute-start | bytes 3145736 | tf_op jit(solution)/shard_map/ppermute | solution.py:312
  15.7 2.2 %term_rows.7 = (f32[512,512]{1,0:T(8,128)S(1)}, f32[8,128]{1,0:T(8,128)S(1)}, bf16[1024,1024]{1,0:T(8,128)(2,1)S(1)}, bf16[512,512]{1,0:T(8,128)(2,1)S(1)}) custom-call(s32[7]{0:T(128)S(1)} %stack.19.info_ref, bf16[1024,512]{1,0:T(8,128)(2,1)S(1)} %get-tuple-element.42.live_ref, bf16[1024,1024]{1,0:T(8,128)(2,1)S(1)} %get-tuple-element.49.left_ref, ...), custom_call_target="tpu_custom_call" | custom-call | flops 200000000 | bytes 1000000 | tf_op jit(solution)/shard_map/term_rows/pallas_call | solution.py:157
  17.9 2.2 %term_rows.8 = (f32[512,512]{1,0:T(8,128)S(1)}, f32[8,128]{1,0:T(8,128)S(1)}, bf16[1024,1024]{1,0:T(8,128)(2,1)S(1)}, bf16[512,512]{1,0:T(8,128)(2,1)S(1)}) custom-call(s32[7]{0:T(128)S(1)} %stack.19.info_ref, bf16[1024,512]{1,0:T(8,128)(2,1)S(1)} %get-tuple-element.42.live_ref, bf16[1024,1024]{1,0:T(8,128)(2,1)S(1)} %get-tuple-element.54.left_ref, ...), custom_call_target="tpu_custom_call" | custom-call | flops 200000000 | bytes 1000000 | tf_op jit(solution)/shard_map/term_rows/pallas_call | solution.py:157
  20.1 4.4 %collective-permute-start.6 = (f32[512,512]{1,0:T(8,128)S(1)}, f32[512,512]{1,0:T(8,128)S(1)}, u32[]{:S(2)}, u32[]{:S(2)}) collective-permute-start(f32[512,512]{1,0:T(8,128)S(1)} %get-tuple-element.65), channel_id=1, source_target_pairs={{0,1},{4,5},{8,9},{12,13},{1,0},{5,4},{9,8},{13,12},{2,3},{6,7},{1... | collective-permute-start | bytes 3145736 | tf_op jit(solution)/shard_map/ppermute | solution.py:300
  24.4 1.1 %collective-permute-done.2.refs_0_ = f32[512,512]{1,0:T(8,128)S(1)} collective-permute-done((f32[512,512]{1,0:T(8,128)S(1)}, f32[512,512]{1,0:T(8,128)S(1)}, u32[]{:S(2)}, u32[]{:S(2)}) %collective-permute-start.2) | collective-permute-done | bytes 1048608 | tf_op jit(solution)/shard_map/ppermute | solution.py:312
  25.6 4.6 %collective-permute-start.5 = (f32[512,512]{1,0:T(8,128)S(1)}, f32[512,512]{1,0:T(8,128)S(1)}, u32[]{:S(2)}, u32[]{:S(2)}) collective-permute-start(f32[512,512]{1,0:T(8,128)S(1)} %get-tuple-element.64.a_ref), channel_id=1, source_target_pairs={{0,4},{4,8},{8,12},{16,20},{20,24},{24,28}} | collective-permute-start | bytes 3145736 | tf_op jit(solution)/shard_map/ppermute | solution.py:300
  30.2 0.7 collective-permute-start.4
  31.0 1.5 %term_rows.9 = (f32[512,512]{1,0:T(8,128)S(1)}, f32[8,128]{1,0:T(8,128)S(1)}) custom-call(s32[7]{0:T(128)S(1)} %stack.19.info_ref, bf16[1024,512]{1,0:T(8,128)(2,1)S(1)} %get-tuple-element.42.live_ref, bf16[1024,1024]{1,0:T(8,128)(2,1)S(1)} %get-tuple-element.54.left_ref, bf16[512,512]{1,0:T(8,128)(2,1)S(1)} %get-tuple-element.55.right_ref, ...), custom_call_target="tpu_custom_call" | custom-call | flops 200000000 | bytes 1000000 | tf_op jit(solution)/shard_map/term_rows/pallas_call | solution.py:157
  32.6 0.7 collective-permute-start.9
  33.4 3.4 %collective-permute-done.7.refs_0_ = f32[512,512]{1,0:T(8,128)S(1)} collective-permute-done((f32[512,512]{1,0:T(8,128)S(1)}, f32[512,512]{1,0:T(8,128)S(1)}, u32[]{:S(2)}, u32[]{:S(2)}) %collective-permute-start.7) | collective-permute-done | bytes 1048608 | tf_op jit(solution)/shard_map/ppermute | solution.py:312
  37.1 4.4 %collective-permute-start.10 = (f32[512,512]{1,0:T(8,128)S(1)}, f32[512,512]{1,0:T(8,128)S(1)}, u32[]{:S(2)}, u32[]{:S(2)}) collective-permute-start(f32[512,512]{1,0:T(8,128)S(1)} %get-tuple-element.77.a_ref), channel_id=1, source_target_pairs={{0,4},{4,8},{8,12},{16,20},{20,24},{24,28}} | collective-permute-start | bytes 3145736 | tf_op jit(solution)/shard_map/ppermute | solution.py:300
  41.5 1.5 %term_rows.10 = (f32[512,512]{1,0:T(8,128)S(1)}, f32[8,128]{1,0:T(8,128)S(1)}) custom-call(s32[7]{0:T(128)S(1)} %stack.19.info_ref, bf16[1024,512]{1,0:T(8,128)(2,1)S(1)} %get-tuple-element.42.live_ref, bf16[1024,1024]{1,0:T(8,128)(2,1)S(1)} %get-tuple-element.57.left_ref, bf16[512,512]{1,0:T(8,128)(2,1)S(1)} %get-tuple-element.58.right_ref, ...), custom_call_target="tpu_custom_call" | custom-call | flops 200000000 | bytes 1000000 | tf_op jit(solution)/shard_map/term_rows/pallas_call | solution.py:157
  43.2 0.7 collective-permute-start.11
  43.9 1.5 %finish_rows.2 = (bf16[1,1024,512]{2,1,0:T(8,128)(2,1)}, f32[16,128]{1,0:T(8,128)S(1)}) custom-call(s32[7]{0:T(128)S(1)} %stack.19.info_ref, bf16[1024,512]{1,0:T(8,128)(2,1)S(1)} %get-tuple-element.42.live_ref, f32[512,512]{1,0:T(8,128)S(1)} %get-tuple-element.73.own_ref, f32[512,512]{1,0:T(8,128)S(1)} %get-tuple-element.64.a_ref, ...), custom_call_target="tpu_custom_call" | custom-call | flops 200000000 | bytes 1000000 | tf_op jit(solution)/shard_map/finish_rows/pallas_call | solution.py:266
  45.5 1.5 %term_rows.11 = (f32[512,512]{1,0:T(8,128)S(1)}, f32[8,128]{1,0:T(8,128)}) custom-call(s32[7]{0:T(128)S(1)} %stack.19.info_ref, bf16[1024,512]{1,0:T(8,128)(2,1)S(1)} %get-tuple-element.42.live_ref, bf16[1024,1024]{1,0:T(8,128)(2,1)S(1)} %get-tuple-element.57.left_ref, bf16[512,512]{1,0:T(8,128)(2,1)S(1)} %get-tuple-element.58.right_ref, ...), custom_call_target="tpu_custom_call" | custom-call | flops 200000000 | bytes 1000000 | tf_op jit(solution)/shard_map/term_rows/pallas_call | solution.py:157
  47.0 6.7 %collective-permute-done.10.b_ref = f32[512,512]{1,0:T(8,128)S(1)} collective-permute-done((f32[512,512]{1,0:T(8,128)S(1)}, f32[512,512]{1,0:T(8,128)S(1)}, u32[]{:S(2)}, u32[]{:S(2)}) %collective-permute-start.10) | collective-permute-done | bytes 1048608 | tf_op jit(solution)/shard_map/ppermute | solution.py:300
  53.7 1.5 %finish_rows.3 = (bf16[1,1024,512]{2,1,0:T(8,128)(2,1)}, f32[16,128]{1,0:T(8,128)S(1)}) custom-call(s32[7]{0:T(128)S(1)} %stack.19.info_ref, bf16[1024,512]{1,0:T(8,128)(2,1)S(1)} %get-tuple-element.42.live_ref, f32[512,512]{1,0:T(8,128)S(1)} %get-tuple-element.76.own_ref, f32[512,512]{1,0:T(8,128)S(1)} %get-tuple-element.77.a_ref, ...), custom_call_target="tpu_custom_call", output_to_operand_aliasing={{0}: (7, {})} | custom-call | flops 200000000 | bytes 1000000 | tf_op jit(solution)/shard_map/finish_rows/pallas_call | solution.py:266
  55.3 18.2 %all_to_all.12 = f32[16,1,128]{2,1,0:T(1,128)S(1)} all-to-all(f32[16,1,128]{2,1,0:T(1,128)S(1)} %bitcast.11), channel_id=1, replica_groups=mesh['grp'=2,'sec'=16] {'sec'}, dimensions={0} | all-to-all | bytes 16384 | tf_op jit(solution)/shard_map/all_to_all | solution.py:283
  (25 shorter events, 2.8 us)
Async XLA Ops:
  2.0 1.2 %copy-start.1 = (bf16[1,1024,512]{2,1,0:T(8,128)(2,1)S(1)}, bf16[1,1024,512]{2,1,0:T(8,128)(2,1)}, u32[]{:S(2)}) copy-start(bf16[1,1024,512]{2,1,0:T(8,128)(2,1)} %param.5) | copy-start | bytes 3145732
  6.2 2.8 %collective-permute-start = (f32[512,512]{1,0:T(8,128)S(1)}, f32[512,512]{1,0:T(8,128)S(1)}, u32[]{:S(2)}, u32[]{:S(2)}) collective-permute-start(f32[512,512]{1,0:T(8,128)S(1)} %get-tuple-element.43.a_ref), channel_id=1, source_target_pairs={{0,1},{4,5},{8,9},{12,13},{1,0},{5,4},{9,8},{13,12},{2,3},{6,7},{1... | collective-permute-start | bytes 3145736 | tf_op jit(solution)/shard_map/ppermute | solution.py:300
  6.8 3.7 %copy-start = (bf16[1,4,512,512]{3,2,1,0:T(8,128)(2,1)S(1)}, bf16[1,4,512,512]{3,2,1,0:T(8,128)(2,1)}, u32[]{:S(2)}) copy-start(bf16[1,4,512,512]{3,2,1,0:T(8,128)(2,1)} %refs_1_.3) | copy-start | bytes 6291460
  8.3 5.9 %collective-permute-start.1 = (f32[512,512]{1,0:T(8,128)S(1)}, f32[512,512]{1,0:T(8,128)S(1)}, u32[]{:S(2)}, u32[]{:S(2)}) collective-permute-start(f32[512,512]{1,0:T(8,128)S(1)} %get-tuple-element.51.a_ref), channel_id=1, source_target_pairs={{0,1},{4,5},{8,9},{12,13},{1,0},{5,4},{9,8},{13,12},{2,3},{6,7},{1... | collective-permute-start | bytes 3145736 | tf_op jit(solution)/shard_map/ppermute | solution.py:300
  9.2 16.4 %collective-permute-start.2 = (f32[512,512]{1,0:T(8,128)S(1)}, f32[512,512]{1,0:T(8,128)S(1)}, u32[]{:S(2)}, u32[]{:S(2)}) collective-permute-start(f32[512,512]{1,0:T(8,128)S(1)} %get-tuple-element.59), channel_id=1, source_target_pairs={{1,2},{5,6},{9,10},{13,14},{3,0},{7,4},{11,8},{17,18},{21,22},{25,... | collective-permute-start | bytes 3145736 | tf_op jit(solution)/shard_map/ppermute | solution.py:312
  13.5 19.0 %collective-permute-start.8 = (f32[512,512]{1,0:T(8,128)S(1)}, f32[512,512]{1,0:T(8,128)S(1)}, u32[]{:S(2)}, u32[]{:S(2)}) collective-permute-start(f32[512,512]{1,0:T(8,128)S(1)} %get-tuple-element.67.a_ref), channel_id=1, source_target_pairs={{3,6},{7,10},{11,14},{4,1},{8,5},{12,9},{19,22},{23,26},{27,30},{2... | collective-permute-start | bytes 3145736 | tf_op jit(solution)/shard_map/ppermute | solution.py:300
  14.4 22.4 %collective-permute-start.7 = (f32[512,512]{1,0:T(8,128)S(1)}, f32[512,512]{1,0:T(8,128)S(1)}, u32[]{:S(2)}, u32[]{:S(2)}) collective-permute-start(f32[512,512]{1,0:T(8,128)S(1)} %get-tuple-element.66), channel_id=1, source_target_pairs={{1,2},{5,6},{9,10},{13,14},{3,0},{7,4},{11,8},{17,18},{21,22},{25,... | collective-permute-start | bytes 3145736 | tf_op jit(solution)/shard_map/ppermute | solution.py:312
  20.1 17.0 %collective-permute-start.6 = (f32[512,512]{1,0:T(8,128)S(1)}, f32[512,512]{1,0:T(8,128)S(1)}, u32[]{:S(2)}, u32[]{:S(2)}) collective-permute-start(f32[512,512]{1,0:T(8,128)S(1)} %get-tuple-element.65), channel_id=1, source_target_pairs={{0,1},{4,5},{8,9},{12,13},{1,0},{5,4},{9,8},{13,12},{2,3},{6,7},{1... | collective-permute-start | bytes 3145736 | tf_op jit(solution)/shard_map/ppermute | solution.py:300
  25.6 17.4 %collective-permute-start.5 = (f32[512,512]{1,0:T(8,128)S(1)}, f32[512,512]{1,0:T(8,128)S(1)}, u32[]{:S(2)}, u32[]{:S(2)}) collective-permute-start(f32[512,512]{1,0:T(8,128)S(1)} %get-tuple-element.64.a_ref), channel_id=1, source_target_pairs={{0,4},{4,8},{8,12},{16,20},{20,24},{24,28}} | collective-permute-start | bytes 3145736 | tf_op jit(solution)/shard_map/ppermute | solution.py:300
  30.2 12.8 %collective-permute-start.4 = (f32[512,512]{1,0:T(8,128)S(1)}, f32[512,512]{1,0:T(8,128)S(1)}, u32[]{:S(2)}, u32[]{:S(2)}) collective-permute-start(f32[512,512]{1,0:T(8,128)S(1)} %get-tuple-element.63.a_ref), channel_id=1, source_target_pairs={{3,6},{7,10},{11,14},{4,1},{8,5},{12,9},{19,22},{23,26},{27,30},{2... | collective-permute-start | bytes 3145736 | tf_op jit(solution)/shard_map/ppermute | solution.py:300
  32.6 11.3 %collective-permute-start.9 = (f32[512,512]{1,0:T(8,128)S(1)}, f32[512,512]{1,0:T(8,128)S(1)}, u32[]{:S(2)}, u32[]{:S(2)}) collective-permute-start(f32[512,512]{1,0:T(8,128)S(1)} %get-tuple-element.74), channel_id=1, source_target_pairs={{1,3},{5,7},{9,11},{13,15},{2,1},{6,5},{10,9},{14,13},{17,19},{21,... | collective-permute-start | bytes 3145736 | tf_op jit(solution)/shard_map/ppermute | solution.py:300
  36.8 8.7 %collective-permute-start.3 = (f32[512,512]{1,0:T(8,128)S(1)}, f32[512,512]{1,0:T(8,128)S(1)}, u32[]{:S(2)}, u32[]{:S(2)}) collective-permute-start(f32[512,512]{1,0:T(8,128)S(1)} %get-tuple-element.62), channel_id=1, source_target_pairs={{0,1},{4,5},{8,9},{12,13},{1,0},{5,4},{9,8},{13,12},{2,3},{6,7},{1... | collective-permute-start | bytes 3145736 | tf_op jit(solution)/shard_map/ppermute | solution.py:300
  37.1 16.6 %collective-permute-start.10 = (f32[512,512]{1,0:T(8,128)S(1)}, f32[512,512]{1,0:T(8,128)S(1)}, u32[]{:S(2)}, u32[]{:S(2)}) collective-permute-start(f32[512,512]{1,0:T(8,128)S(1)} %get-tuple-element.77.a_ref), channel_id=1, source_target_pairs={{0,4},{4,8},{8,12},{16,20},{20,24},{24,28}} | collective-permute-start | bytes 3145736 | tf_op jit(solution)/shard_map/ppermute | solution.py:300
  43.2 10.5 %collective-permute-start.11 = (f32[512,512]{1,0:T(8,128)S(1)}, f32[512,512]{1,0:T(8,128)S(1)}, u32[]{:S(2)}, u32[]{:S(2)}) collective-permute-start(f32[512,512]{1,0:T(8,128)S(1)} %get-tuple-element.78), channel_id=1, source_target_pairs={{1,3},{5,7},{9,11},{13,15},{2,1},{6,5},{10,9},{14,13},{17,19},{21,... | collective-permute-start | bytes 3145736 | tf_op jit(solution)/shard_map/ppermute | solution.py:300

commit v18 on v16

--- a/solution.py
+++ b/solution.py
@@ -43,7 +43,7 @@
             )
         )
     half = LEFT_PIECES // 2
-    return left[:half] + right, left[half:]
+    return left[:half], right, left[half:]
 
 
 def multiply(left, live, right):
@@ -59,8 +59,8 @@
     psi_ref = live_ref
     if masks:
         live_ref = operands.pop(0)
-    own, late = fetch(info_ref, slot, left_hbm, right_hbm, *operands, sems)
-    for copy in own + late:
+    left, right, late = fetch(info_ref, slot, left_hbm, right_hbm, *operands, sems)
+    for copy in left + right + late:
         copy.start()
     if masks:
         rows, cols = psi_ref.shape
@@ -72,9 +72,18 @@
             inside = jnp.logical_and(row < info_ref[4] - start, col)
             values = jnp.where(inside, psi_ref[span, :].astype(jnp.float32), 0.0)
             live_ref[span, :] = values.astype(live_ref.dtype)
-    for copy in own:
-        copy.wait()
-    out_ref[...] = multiply(operands[0][: out_ref.shape[0], :], live_ref[...], operands[1][...])
+    block = out_ref.shape[0] // 2
+    for i in range(2):
+        span = pl.ds(i * block, block)
+        for copy in left[i * len(left) // 2 : (i + 1) * len(left) // 2]:
+            copy.wait()
+        value = jnp.dot(operands[0][span, :], live_ref[...], preferred_element_type=jnp.float32)
+        if i == 0:
+            for copy in right:
+                copy.wait()
+        out_ref[span, :] = jnp.dot(
+            value.astype(jnp.bfloat16), operands[1][...], preferred_element_type=jnp.float32
+        )
     for copy in late:
         copy.wait()
 

time: 74.5 us -> 74.6 us (level)
  no operation moved by 1% of the time
where the time goes in v18:
time: 74.6 us; the launch traced here: 74.2 us
  Pallas kernels  20.2 us (27%)
  starting transfers between devices  19.8 us (27%)
  blocking collectives  18.2 us (24%)
  waiting for transfers between devices  11.8 us (16%)
  between operations  2.18 us (3%)
  local copies, waits for them, and re-layouts  1.32 us (2%)
    all_to_all x1, blocking collectives, sum_over_sectors(): arrived = lax.all_to_all(value, 'sec', 0, 0, tiled=True)  18.2 us
    ppermute x10, starting transfers between devices, send(): return lax.ppermute(value, 'sec', pairs)  17.2 us
    pallas_call x6, Pallas kernels, term_rows(): pl.pallas_call(functools.partial(term_kernel, first, added is not None, s...  10.4 us
    ppermute x10, waiting for transfers between devices, send(): return lax.ppermute(value, 'sec', pairs)  7.36 us
    pallas_call x2, Pallas kernels, opening_rows(): pl.pallas_call(functools.partial(opening_kernel, slot, masks, len(tokens)...  6.12 us
    ppermute x2, waiting for transfers between devices, raise_one(): return lax.ppermute(value, 'sec', pairs_up)  4.49 us
    pallas_call x2, Pallas kernels, finish(): pl.pallas_call(functools.partial(finish_kernel, first), out_shape=(jax.Sh...  3.07 us
    ppermute x2, starting transfers between devices, raise_one(): return lax.ppermute(value, 'sec', pairs_up)  2.58 us
  transfers between devices with their start and end apart: 12, of which 4 were waited for; matrix products, arithmetic and copies ran while one was open for 0% of the time, Pallas kernels for 21%

profile of v18, /device:TPU:0, one launch (start us, length us, event | category | flops | bytes accessed | tf_op | source)
XLA Modules:
  0.0 74.2 jit_solution(4796133230549365277)
XLA Ops:
  2.0 1.2 %copy-done.1 = bf16[1,1024,512]{2,1,0:T(8,128)(2,1)S(1)} copy-done((bf16[1,1024,512]{2,1,0:T(8,128)(2,1)S(1)}, bf16[1,1024,512]{2,1,0:T(8,128)(2,1)}, u32[]{:S(2)}) %copy-start.1) | copy-done | bytes 1048600
  3.3 3.1 %opening_rows.2 = (f32[512,512]{1,0:T(8,128)S(1)}, f32[8,128]{1,0:T(8,128)S(1)}, bf16[1024,512]{1,0:T(8,128)(2,1)S(1)}, bf16[1024,1024]{1,0:T(8,128)(2,1)S(1)}, bf16[512,512]{1,0:T(8,128)(2,1)S(1)}) custom-call(s32[7]{0:T(128)S(1)} %stack.19.info_ref, bf16[1024,512]{1,0:T(8,128)(2,1)S(1)} %bitcast.10, bf16[1,4,1024,1024]{3,2,1,0:T(8,128)(2,1)} %refs_0_.3, ...), custom_call_target="tpu_custom_call" | custom-call | flops 200000000 | bytes 1000000 | tf_op jit(solution)/shard_map/opening_rows/pallas_call | solution.py:104
  6.9 1.5 %term_rows.6 = (f32[512,512]{1,0:T(8,128)S(1)}, f32[8,128]{1,0:T(8,128)S(1)}) custom-call(s32[7]{0:T(128)S(1)} %stack.19.info_ref, bf16[1024,512]{1,0:T(8,128)(2,1)S(1)} %get-tuple-element.42.live_ref, bf16[1024,1024]{1,0:T(8,128)(2,1)S(1)} %get-tuple-element.44.left_ref, bf16[512,512]{1,0:T(8,128)(2,1)S(1)} %get-tuple-element.45.right_ref, ...), custom_call_target="tpu_custom_call" | custom-call | flops 200000000 | bytes 1000000 | tf_op jit(solution)/shard_map/term_rows/pallas_call | solution.py:159
  9.3 1.3 %collective-permute-start.2 = (f32[512,512]{1,0:T(8,128)S(1)}, f32[512,512]{1,0:T(8,128)S(1)}, u32[]{:S(2)}, u32[]{:S(2)}) collective-permute-start(f32[512,512]{1,0:T(8,128)S(1)} %get-tuple-element.59), channel_id=1, source_target_pairs={{1,2},{5,6},{9,10},{13,14},{3,0},{7,4},{11,8},{17,18},{21,22},{25,... | collective-permute-start | bytes 3145736 | tf_op jit(solution)/shard_map/ppermute | solution.py:314
  10.6 3.1 %opening_rows.3 = (f32[512,512]{1,0:T(8,128)S(1)}, f32[8,128]{1,0:T(8,128)S(1)}, bf16[1024,1024]{1,0:T(8,128)(2,1)S(1)}, bf16[512,512]{1,0:T(8,128)(2,1)S(1)}) custom-call(s32[7]{0:T(128)S(1)} %stack.19.info_ref, bf16[1024,512]{1,0:T(8,128)(2,1)S(1)} %get-tuple-element.42.live_ref, bf16[1,4,1024,1024]{3,2,1,0:T(8,128)(2,1)} %refs_0_.3, ...), custom_call_target="tpu_custom_call" | custom-call | flops 200000000 | bytes 1000000 | tf_op jit(solution)/shard_map/opening_rows/pallas_call | solution.py:104
  13.7 0.7 collective-permute-start.8
  14.6 1.3 %collective-permute-start.7 = (f32[512,512]{1,0:T(8,128)S(1)}, f32[512,512]{1,0:T(8,128)S(1)}, u32[]{:S(2)}, u32[]{:S(2)}) collective-permute-start(f32[512,512]{1,0:T(8,128)S(1)} %get-tuple-element.66), channel_id=1, source_target_pairs={{1,2},{5,6},{9,10},{13,14},{3,0},{7,4},{11,8},{17,18},{21,22},{25,... | collective-permute-start | bytes 3145736 | tf_op jit(solution)/shard_map/ppermute | solution.py:314
  15.9 2.2 %term_rows.7 = (f32[512,512]{1,0:T(8,128)S(1)}, f32[8,128]{1,0:T(8,128)S(1)}, bf16[1024,1024]{1,0:T(8,128)(2,1)S(1)}, bf16[512,512]{1,0:T(8,128)(2,1)S(1)}) custom-call(s32[7]{0:T(128)S(1)} %stack.19.info_ref, bf16[1024,512]{1,0:T(8,128)(2,1)S(1)} %get-tuple-element.42.live_ref, bf16[1024,1024]{1,0:T(8,128)(2,1)S(1)} %get-tuple-element.49.left_ref, ...), custom_call_target="tpu_custom_call" | custom-call | flops 200000000 | bytes 1000000 | tf_op jit(solution)/shard_map/term_rows/pallas_call | solution.py:159
  18.0 2.2 %term_rows.8 = (f32[512,512]{1,0:T(8,128)S(1)}, f32[8,128]{1,0:T(8,128)S(1)}, bf16[1024,1024]{1,0:T(8,128)(2,1)S(1)}, bf16[512,512]{1,0:T(8,128)(2,1)S(1)}) custom-call(s32[7]{0:T(128)S(1)} %stack.19.info_ref, bf16[1024,512]{1,0:T(8,128)(2,1)S(1)} %get-tuple-element.42.live_ref, bf16[1024,1024]{1,0:T(8,128)(2,1)S(1)} %get-tuple-element.54.left_ref, ...), custom_call_target="tpu_custom_call" | custom-call | flops 200000000 | bytes 1000000 | tf_op jit(solution)/shard_map/term_rows/pallas_call | solution.py:159
  20.2 4.4 %collective-permute-start.6 = (f32[512,512]{1,0:T(8,128)S(1)}, f32[512,512]{1,0:T(8,128)S(1)}, u32[]{:S(2)}, u32[]{:S(2)}) collective-permute-start(f32[512,512]{1,0:T(8,128)S(1)} %get-tuple-element.65), channel_id=1, source_target_pairs={{0,1},{4,5},{8,9},{12,13},{1,0},{5,4},{9,8},{13,12},{2,3},{6,7},{1... | collective-permute-start | bytes 3145736 | tf_op jit(solution)/shard_map/ppermute | solution.py:302
  24.6 1.1 %collective-permute-done.2.refs_0_ = f32[512,512]{1,0:T(8,128)S(1)} collective-permute-done((f32[512,512]{1,0:T(8,128)S(1)}, f32[512,512]{1,0:T(8,128)S(1)}, u32[]{:S(2)}, u32[]{:S(2)}) %collective-permute-start.2) | collective-permute-done | bytes 1048608 | tf_op jit(solution)/shard_map/ppermute | solution.py:314
  25.7 4.6 %collective-permute-start.5 = (f32[512,512]{1,0:T(8,128)S(1)}, f32[512,512]{1,0:T(8,128)S(1)}, u32[]{:S(2)}, u32[]{:S(2)}) collective-permute-start(f32[512,512]{1,0:T(8,128)S(1)} %get-tuple-element.64.a_ref), channel_id=1, source_target_pairs={{0,4},{4,8},{8,12},{16,20},{20,24},{24,28}} | collective-permute-start | bytes 3145736 | tf_op jit(solution)/shard_map/ppermute | solution.py:302
  30.3 0.7 collective-permute-start.4
  31.0 1.5 %term_rows.9 = (f32[512,512]{1,0:T(8,128)S(1)}, f32[8,128]{1,0:T(8,128)S(1)}) custom-call(s32[7]{0:T(128)S(1)} %stack.19.info_ref, bf16[1024,512]{1,0:T(8,128)(2,1)S(1)} %get-tuple-element.42.live_ref, bf16[1024,1024]{1,0:T(8,128)(2,1)S(1)} %get-tuple-element.54.left_ref, bf16[512,512]{1,0:T(8,128)(2,1)S(1)} %get-tuple-element.55.right_ref, ...), custom_call_target="tpu_custom_call" | custom-call | flops 200000000 | bytes 1000000 | tf_op jit(solution)/shard_map/term_rows/pallas_call | solution.py:159
  32.7 0.7 collective-permute-start.9
  33.5 3.4 %collective-permute-done.7.refs_0_ = f32[512,512]{1,0:T(8,128)S(1)} collective-permute-done((f32[512,512]{1,0:T(8,128)S(1)}, f32[512,512]{1,0:T(8,128)S(1)}, u32[]{:S(2)}, u32[]{:S(2)}) %collective-permute-start.7) | collective-permute-done | bytes 1048608 | tf_op jit(solution)/shard_map/ppermute | solution.py:314
  37.2 4.4 %collective-permute-start.10 = (f32[512,512]{1,0:T(8,128)S(1)}, f32[512,512]{1,0:T(8,128)S(1)}, u32[]{:S(2)}, u32[]{:S(2)}) collective-permute-start(f32[512,512]{1,0:T(8,128)S(1)} %get-tuple-element.77.a_ref), channel_id=1, source_target_pairs={{0,4},{4,8},{8,12},{16,20},{20,24},{24,28}} | collective-permute-start | bytes 3145736 | tf_op jit(solution)/shard_map/ppermute | solution.py:302
  41.6 1.5 %term_rows.10 = (f32[512,512]{1,0:T(8,128)S(1)}, f32[8,128]{1,0:T(8,128)S(1)}) custom-call(s32[7]{0:T(128)S(1)} %stack.19.info_ref, bf16[1024,512]{1,0:T(8,128)(2,1)S(1)} %get-tuple-element.42.live_ref, bf16[1024,1024]{1,0:T(8,128)(2,1)S(1)} %get-tuple-element.57.left_ref, bf16[512,512]{1,0:T(8,128)(2,1)S(1)} %get-tuple-element.58.right_ref, ...), custom_call_target="tpu_custom_call" | custom-call | flops 200000000 | bytes 1000000 | tf_op jit(solution)/shard_map/term_rows/pallas_call | solution.py:159
  43.3 0.7 collective-permute-start.11
  44.0 1.5 %finish_rows.2 = (bf16[1,1024,512]{2,1,0:T(8,128)(2,1)}, f32[16,128]{1,0:T(8,128)S(1)}) custom-call(s32[7]{0:T(128)S(1)} %stack.19.info_ref, bf16[1024,512]{1,0:T(8,128)(2,1)S(1)} %get-tuple-element.42.live_ref, f32[512,512]{1,0:T(8,128)S(1)} %get-tuple-element.73.own_ref, f32[512,512]{1,0:T(8,128)S(1)} %get-tuple-element.64.a_ref, ...), custom_call_target="tpu_custom_call" | custom-call | flops 200000000 | bytes 1000000 | tf_op jit(solution)/shard_map/finish_rows/pallas_call | solution.py:268
  45.6 1.5 %term_rows.11 = (f32[512,512]{1,0:T(8,128)S(1)}, f32[8,128]{1,0:T(8,128)}) custom-call(s32[7]{0:T(128)S(1)} %stack.19.info_ref, bf16[1024,512]{1,0:T(8,128)(2,1)S(1)} %get-tuple-element.42.live_ref, bf16[1024,1024]{1,0:T(8,128)(2,1)S(1)} %get-tuple-element.57.left_ref, bf16[512,512]{1,0:T(8,128)(2,1)S(1)} %get-tuple-element.58.right_ref, ...), custom_call_target="tpu_custom_call" | custom-call | flops 200000000 | bytes 1000000 | tf_op jit(solution)/shard_map/term_rows/pallas_call | solution.py:159
  47.1 6.7 %collective-permute-done.10.b_ref = f32[512,512]{1,0:T(8,128)S(1)} collective-permute-done((f32[512,512]{1,0:T(8,128)S(1)}, f32[512,512]{1,0:T(8,128)S(1)}, u32[]{:S(2)}, u32[]{:S(2)}) %collective-permute-start.10) | collective-permute-done | bytes 1048608 | tf_op jit(solution)/shard_map/ppermute | solution.py:302
  53.8 1.5 %finish_rows.3 = (bf16[1,1024,512]{2,1,0:T(8,128)(2,1)}, f32[16,128]{1,0:T(8,128)S(1)}) custom-call(s32[7]{0:T(128)S(1)} %stack.19.info_ref, bf16[1024,512]{1,0:T(8,128)(2,1)S(1)} %get-tuple-element.42.live_ref, f32[512,512]{1,0:T(8,128)S(1)} %get-tuple-element.76.own_ref, f32[512,512]{1,0:T(8,128)S(1)} %get-tuple-element.77.a_ref, ...), custom_call_target="tpu_custom_call", output_to_operand_aliasing={{0}: (7, {})} | custom-call | flops 200000000 | bytes 1000000 | tf_op jit(solution)/shard_map/finish_rows/pallas_call | solution.py:268
  55.3 18.2 %all_to_all.12 = f32[16,1,128]{2,1,0:T(1,128)S(1)} all-to-all(f32[16,1,128]{2,1,0:T(1,128)S(1)} %bitcast.11), channel_id=1, replica_groups=mesh['grp'=2,'sec'=16] {'sec'}, dimensions={0} | all-to-all | bytes 16384 | tf_op jit(solution)/shard_map/all_to_all | solution.py:285
  (25 shorter events, 2.8 us)
Async XLA Ops:
  2.0 1.2 %copy-start.1 = (bf16[1,1024,512]{2,1,0:T(8,128)(2,1)S(1)}, bf16[1,1024,512]{2,1,0:T(8,128)(2,1)}, u32[]{:S(2)}) copy-start(bf16[1,1024,512]{2,1,0:T(8,128)(2,1)} %param.5) | copy-start | bytes 3145732
  6.3 2.8 %collective-permute-start = (f32[512,512]{1,0:T(8,128)S(1)}, f32[512,512]{1,0:T(8,128)S(1)}, u32[]{:S(2)}, u32[]{:S(2)}) collective-permute-start(f32[512,512]{1,0:T(8,128)S(1)} %get-tuple-element.43.a_ref), channel_id=1, source_target_pairs={{0,1},{4,5},{8,9},{12,13},{1,0},{5,4},{9,8},{13,12},{2,3},{6,7},{1... | collective-permute-start | bytes 3145736 | tf_op jit(solution)/shard_map/ppermute | solution.py:302
  6.9 3.7 %copy-start = (bf16[1,4,512,512]{3,2,1,0:T(8,128)(2,1)S(1)}, bf16[1,4,512,512]{3,2,1,0:T(8,128)(2,1)}, u32[]{:S(2)}) copy-start(bf16[1,4,512,512]{3,2,1,0:T(8,128)(2,1)} %refs_1_.3) | copy-start | bytes 6291460
  8.4 6.0 %collective-permute-start.1 = (f32[512,512]{1,0:T(8,128)S(1)}, f32[512,512]{1,0:T(8,128)S(1)}, u32[]{:S(2)}, u32[]{:S(2)}) collective-permute-start(f32[512,512]{1,0:T(8,128)S(1)} %get-tuple-element.51.a_ref), channel_id=1, source_target_pairs={{0,1},{4,5},{8,9},{12,13},{1,0},{5,4},{9,8},{13,12},{2,3},{6,7},{1... | collective-permute-start | bytes 3145736 | tf_op jit(solution)/shard_map/ppermute | solution.py:302
  9.3 16.4 %collective-permute-start.2 = (f32[512,512]{1,0:T(8,128)S(1)}, f32[512,512]{1,0:T(8,128)S(1)}, u32[]{:S(2)}, u32[]{:S(2)}) collective-permute-start(f32[512,512]{1,0:T(8,128)S(1)} %get-tuple-element.59), channel_id=1, source_target_pairs={{1,2},{5,6},{9,10},{13,14},{3,0},{7,4},{11,8},{17,18},{21,22},{25,... | collective-permute-start | bytes 3145736 | tf_op jit(solution)/shard_map/ppermute | solution.py:314
  13.7 18.9 %collective-permute-start.8 = (f32[512,512]{1,0:T(8,128)S(1)}, f32[512,512]{1,0:T(8,128)S(1)}, u32[]{:S(2)}, u32[]{:S(2)}) collective-permute-start(f32[512,512]{1,0:T(8,128)S(1)} %get-tuple-element.67.a_ref), channel_id=1, source_target_pairs={{3,6},{7,10},{11,14},{4,1},{8,5},{12,9},{19,22},{23,26},{27,30},{2... | collective-permute-start | bytes 3145736 | tf_op jit(solution)/shard_map/ppermute | solution.py:302
  14.6 22.3 %collective-permute-start.7 = (f32[512,512]{1,0:T(8,128)S(1)}, f32[512,512]{1,0:T(8,128)S(1)}, u32[]{:S(2)}, u32[]{:S(2)}) collective-permute-start(f32[512,512]{1,0:T(8,128)S(1)} %get-tuple-element.66), channel_id=1, source_target_pairs={{1,2},{5,6},{9,10},{13,14},{3,0},{7,4},{11,8},{17,18},{21,22},{25,... | collective-permute-start | bytes 3145736 | tf_op jit(solution)/shard_map/ppermute | solution.py:314
  20.2 16.9 %collective-permute-start.6 = (f32[512,512]{1,0:T(8,128)S(1)}, f32[512,512]{1,0:T(8,128)S(1)}, u32[]{:S(2)}, u32[]{:S(2)}) collective-permute-start(f32[512,512]{1,0:T(8,128)S(1)} %get-tuple-element.65), channel_id=1, source_target_pairs={{0,1},{4,5},{8,9},{12,13},{1,0},{5,4},{9,8},{13,12},{2,3},{6,7},{1... | collective-permute-start | bytes 3145736 | tf_op jit(solution)/shard_map/ppermute | solution.py:302
  25.7 17.4 %collective-permute-start.5 = (f32[512,512]{1,0:T(8,128)S(1)}, f32[512,512]{1,0:T(8,128)S(1)}, u32[]{:S(2)}, u32[]{:S(2)}) collective-permute-start(f32[512,512]{1,0:T(8,128)S(1)} %get-tuple-element.64.a_ref), channel_id=1, source_target_pairs={{0,4},{4,8},{8,12},{16,20},{20,24},{24,28}} | collective-permute-start | bytes 3145736 | tf_op jit(solution)/shard_map/ppermute | solution.py:302
  30.3 12.8 %collective-permute-start.4 = (f32[512,512]{1,0:T(8,128)S(1)}, f32[512,512]{1,0:T(8,128)S(1)}, u32[]{:S(2)}, u32[]{:S(2)}) collective-permute-start(f32[512,512]{1,0:T(8,128)S(1)} %get-tuple-element.63.a_ref), channel_id=1, source_target_pairs={{3,6},{7,10},{11,14},{4,1},{8,5},{12,9},{19,22},{23,26},{27,30},{2... | collective-permute-start | bytes 3145736 | tf_op jit(solution)/shard_map/ppermute | solution.py:302
  32.7 11.3 %collective-permute-start.9 = (f32[512,512]{1,0:T(8,128)S(1)}, f32[512,512]{1,0:T(8,128)S(1)}, u32[]{:S(2)}, u32[]{:S(2)}) collective-permute-start(f32[512,512]{1,0:T(8,128)S(1)} %get-tuple-element.74), channel_id=1, source_target_pairs={{1,3},{5,7},{9,11},{13,15},{2,1},{6,5},{10,9},{14,13},{17,19},{21,... | collective-permute-start | bytes 3145736 | tf_op jit(solution)/shard_map/ppermute | solution.py:302
  36.9 8.7 %collective-permute-start.3 = (f32[512,512]{1,0:T(8,128)S(1)}, f32[512,512]{1,0:T(8,128)S(1)}, u32[]{:S(2)}, u32[]{:S(2)}) collective-permute-start(f32[512,512]{1,0:T(8,128)S(1)} %get-tuple-element.62), channel_id=1, source_target_pairs={{0,1},{4,5},{8,9},{12,13},{1,0},{5,4},{9,8},{13,12},{2,3},{6,7},{1... | collective-permute-start | bytes 3145736 | tf_op jit(solution)/shard_map/ppermute | solution.py:302
  37.2 16.6 %collective-permute-start.10 = (f32[512,512]{1,0:T(8,128)S(1)}, f32[512,512]{1,0:T(8,128)S(1)}, u32[]{:S(2)}, u32[]{:S(2)}) collective-permute-start(f32[512,512]{1,0:T(8,128)S(1)} %get-tuple-element.77.a_ref), channel_id=1, source_target_pairs={{0,4},{4,8},{8,12},{16,20},{20,24},{24,28}} | collective-permute-start | bytes 3145736 | tf_op jit(solution)/shard_map/ppermute | solution.py:302
  43.3 10.5 %collective-permute-start.11 = (f32[512,512]{1,0:T(8,128)S(1)}, f32[512,512]{1,0:T(8,128)S(1)}, u32[]{:S(2)}, u32[]{:S(2)}) collective-permute-start(f32[512,512]{1,0:T(8,128)S(1)} %get-tuple-element.78), channel_id=1, source_target_pairs={{1,3},{5,7},{9,11},{13,15},{2,1},{6,5},{10,9},{14,13},{17,19},{21,... | collective-permute-start | bytes 3145736 | tf_op jit(solution)/shard_map/ppermute | solution.py:302

commit v19 on v17

--- a/solution.py
+++ b/solution.py
@@ -58,12 +58,14 @@
     operands = refs[2:-1]
     psi_ref = live_ref
     if masks:
-        live_ref = operands.pop(0)
+        live_ref, sizes_ref = operands.pop(0), operands.pop(0)
     left, right, late = fetch(info_ref, slot, left_hbm, right_hbm, *operands, sems)
     for copy in left + right + late:
         copy.start()
     if masks:
         rows, cols = psi_ref.shape
+        sizes_ref[:8, :] = jnp.full((8, cols), info_ref[4], jnp.int32)
+        sizes_ref[8:, :] = jnp.full((8, cols), info_ref[5], jnp.int32)
         step = 128
         col = lax.broadcasted_iota(jnp.int32, (step, cols), 1) < info_ref[5]
         row = lax.broadcasted_iota(jnp.int32, (step, cols), 0)
@@ -98,6 +100,7 @@
     out_shape = [jax.ShapeDtypeStruct((count, cols), jnp.float32), TOKEN]
     if masks:
         out_shape.append(jax.ShapeDtypeStruct(live.shape, live.dtype))
+        out_shape.append(jax.ShapeDtypeStruct((16, cols), jnp.int32))
     out_shape += operand_shapes(width, cols)
     return pl.pallas_call(
         functools.partial(opening_kernel, slot, masks, len(tokens)),
@@ -216,12 +219,14 @@
     )(value, token)
 
 
-def finish_kernel(first, info_ref, live_ref, own_ref, a_ref, b_ref, c_ref, before_ref, *refs):
+def finish_kernel(first, sizes_ref, live_ref, own_ref, a_ref, b_ref, c_ref, before_ref, *refs):
+    place = lax.axis_index("sec") % 4
+    which = jnp.where(place == 0, 1, jnp.where(place == 2, 0, 2))
     sigma_hbm, energy_ref, sigma_buf, sems = refs[-4:]
     count, cols = own_ref.shape
     step = 64
     piece = count // sems.shape[0]
-    col = lax.broadcasted_iota(jnp.int32, (step, cols), 1) < info_ref[5]
+    col = lax.broadcasted_iota(jnp.int32, (step, cols), 1) < sizes_ref[8:9, :]
     row = lax.broadcasted_iota(jnp.int32, (step, cols), 0)
 
     def copy(i):
@@ -237,7 +242,7 @@
             def body(n, energy):
                 start = pl.multiple_of(i * piece + n * step, step)
                 span = pl.ds(start, step)
-                inside = jnp.logical_and(row < info_ref[4] - first - start, col)
+                inside = jnp.logical_and(row < sizes_ref[0:1, :] - (first + start), col)
                 total = jnp.where(inside, own_ref[span, :] + arrival[span, :], 0.0)
                 sigma_buf[span, :] = total.astype(sigma_buf.dtype)
                 here = pl.ds(pl.multiple_of(first + start, step), step)
@@ -249,15 +254,15 @@
         energy_ref[...] = before_ref[...] + jnp.sum(energy)
 
     for n, arrival in enumerate((a_ref, b_ref, c_ref)):
-        pl.when(info_ref[6] == n)(functools.partial(work, arrival))
+        pl.when(which == n)(functools.partial(work, arrival))
     for i in range(count // piece):
         copy(i).wait()
 
 
-def finish(info, live, own, arrivals, before, sigma, first):
+def finish(sizes, live, own, arrivals, before, sigma, first):
     count, cols = own.shape
-    in_specs = [SMEM] + [WHOLE] * 6
-    operands = [info, live, own, *arrivals, before]
+    in_specs = [WHOLE] * 7
+    operands = [sizes, live, own, *arrivals, before]
     aliases = {}
     if sigma is not None:
         in_specs.append(ANY)
@@ -324,7 +329,7 @@
         return send(value, (0, 4))
 
     envs = (left_env, right_env)
-    first0, token, live, *ops0 = opening_rows(info, psi[0], envs, 0, part, masks=True)
+    first0, token, live, sizes, *ops0 = opening_rows(info, psi[0], envs, 0, part, masks=True)
     paired0 = swap(first0)
     first1, token = term_rows(info, live, ops0, part, part, token)
     paired1 = swap(first1)
@@ -352,9 +357,9 @@
     crossed1 = across(summed1)
 
     energy = jnp.zeros((sectors, 128), jnp.float32)
-    sigma, energy = finish(info, live, own0, (raised0, relayed0, crossed0), energy, None, 0)
+    sigma, energy = finish(sizes, live, own0, (raised0, relayed0, crossed0), energy, None, 0)
     own1, token = term_rows(info, live, ops3, part, part, token, energy, added=swapped1)
-    sigma, energy = finish(info, live, own1, (raised1, relayed1, crossed1), energy, sigma, part)
+    sigma, energy = finish(sizes, live, own1, (raised1, relayed1, crossed1), energy, sigma, part)
     return sigma, sum_over_sectors(energy)
 
 

time: 74.5 us -> 74 us (level)
  Pallas kernels: 20 us -> 19 us
    pallas_call x2, Pallas kernels: 3.07 us -> 2.06 us  [finish(): pl.pallas_call(functools.partial(finish_kernel, first), out_shape=(jax.Sh...]
  transfers between devices with their start and end apart: 12 -> 12, of which waited for: 4 -> 4; matrix products, arithmetic and copies ran while one was open for 0% -> 0% of each run, Pallas kernels for 21% -> 20%
where the time goes in v19:
time: 74 us; the launch traced here: 73.6 us
  starting transfers between devices  19.8 us (27%)
  Pallas kernels  19 us (26%)
  blocking collectives  18.2 us (25%)
  waiting for transfers between devices  12.4 us (17%)
  between operations  2.19 us (3%)
  local copies, waits for them, and re-layouts  1.32 us (2%)
    all_to_all x1, blocking collectives, sum_over_sectors(): arrived = lax.all_to_all(value, 'sec', 0, 0, tiled=True)  18.2 us
    ppermute x10, starting transfers between devices, send(): return lax.ppermute(value, 'sec', pairs)  17.2 us
    pallas_call x6, Pallas kernels, term_rows(): pl.pallas_call(functools.partial(term_kernel, first, added is not None, s...  10.4 us
    ppermute x10, waiting for transfers between devices, send(): return lax.ppermute(value, 'sec', pairs)  7.84 us
    pallas_call x2, Pallas kernels, opening_rows(): pl.pallas_call(functools.partial(opening_kernel, slot, masks, len(tokens)...  5.96 us
    ppermute x2, waiting for transfers between devices, raise_one(): return lax.ppermute(value, 'sec', pairs_up)  4.6 us
    ppermute x2, starting transfers between devices, raise_one(): return lax.ppermute(value, 'sec', pairs_up)  2.58 us
    pallas_call x2, Pallas kernels, finish(): pl.pallas_call(functools.partial(finish_kernel, first), out_shape=(jax.Sh...  2.06 us
  transfers between devices with their start and end apart: 12, of which 4 were waited for; matrix products, arithmetic and copies ran while one was open for 0% of the time, Pallas kernels for 20%

profile of v19, /device:TPU:0, one launch (start us, length us, event | category | flops | bytes accessed | tf_op | source)
XLA Modules:
  0.0 73.6 jit_solution(16269627104380747503)
XLA Ops:
  2.0 1.2 %copy-done.1 = bf16[1,1024,512]{2,1,0:T(8,128)(2,1)S(1)} copy-done((bf16[1,1024,512]{2,1,0:T(8,128)(2,1)S(1)}, bf16[1,1024,512]{2,1,0:T(8,128)(2,1)}, u32[]{:S(2)}) %copy-start.1) | copy-done | bytes 1048600
  3.3 3.0 %opening_rows.2 = (f32[512,512]{1,0:T(8,128)S(1)}, f32[8,128]{1,0:T(8,128)S(1)}, bf16[1024,512]{1,0:T(8,128)(2,1)S(1)}, s32[16,512]{1,0:T(8,128)S(1)}, bf16[1024...) custom-call(s32[7]{0:T(128)S(1)} %stack.19.info_ref, bf16[1024,512]{1,0:T(8,128)(2,1)S(1)} %bitcast.10, ...), custom_call_target="tpu_custom_call" | custom-call | flops 200000000 | bytes 1000000 | tf_op jit(solution)/shard_map/opening_rows/pallas_call | solution.py:105
  6.8 1.5 %term_rows.6 = (f32[512,512]{1,0:T(8,128)S(1)}, f32[8,128]{1,0:T(8,128)S(1)}) custom-call(s32[7]{0:T(128)S(1)} %stack.19.info_ref, bf16[1024,512]{1,0:T(8,128)(2,1)S(1)} %get-tuple-element.44.live_ref, bf16[1024,1024]{1,0:T(8,128)(2,1)S(1)} %get-tuple-element.46.left_ref, bf16[512,512]{1,0:T(8,128)(2,1)S(1)} %get-tuple-element.47.right_ref, ...), custom_call_target="tpu_custom_call" | custom-call | flops 200000000 | bytes 1000000 | tf_op jit(solution)/shard_map/term_rows/pallas_call | solution.py:160
  9.2 1.3 %collective-permute-start.2 = (f32[512,512]{1,0:T(8,128)S(1)}, f32[512,512]{1,0:T(8,128)S(1)}, u32[]{:S(2)}, u32[]{:S(2)}) collective-permute-start(f32[512,512]{1,0:T(8,128)S(1)} %get-tuple-element.61), channel_id=1, source_target_pairs={{1,2},{5,6},{9,10},{13,14},{3,0},{7,4},{11,8},{17,18},{21,22},{25,... | collective-permute-start | bytes 3145736 | tf_op jit(solution)/shard_map/ppermute | solution.py:317
  10.5 3.0 %opening_rows.3 = (f32[512,512]{1,0:T(8,128)S(1)}, f32[8,128]{1,0:T(8,128)S(1)}, bf16[1024,1024]{1,0:T(8,128)(2,1)S(1)}, bf16[512,512]{1,0:T(8,128)(2,1)S(1)}) custom-call(s32[7]{0:T(128)S(1)} %stack.19.info_ref, bf16[1024,512]{1,0:T(8,128)(2,1)S(1)} %get-tuple-element.44.live_ref, bf16[1,4,1024,1024]{3,2,1,0:T(8,128)(2,1)} %refs_0_.3, ...), custom_call_target="tpu_custom_call" | custom-call | flops 200000000 | bytes 1000000 | tf_op jit(solution)/shard_map/opening_rows/pallas_call | solution.py:105
  13.5 0.7 collective-permute-start.8
  14.4 1.3 %collective-permute-start.7 = (f32[512,512]{1,0:T(8,128)S(1)}, f32[512,512]{1,0:T(8,128)S(1)}, u32[]{:S(2)}, u32[]{:S(2)}) collective-permute-start(f32[512,512]{1,0:T(8,128)S(1)} %get-tuple-element.68), channel_id=1, source_target_pairs={{1,2},{5,6},{9,10},{13,14},{3,0},{7,4},{11,8},{17,18},{21,22},{25,... | collective-permute-start | bytes 3145736 | tf_op jit(solution)/shard_map/ppermute | solution.py:317
  15.7 2.2 %term_rows.7 = (f32[512,512]{1,0:T(8,128)S(1)}, f32[8,128]{1,0:T(8,128)S(1)}, bf16[1024,1024]{1,0:T(8,128)(2,1)S(1)}, bf16[512,512]{1,0:T(8,128)(2,1)S(1)}) custom-call(s32[7]{0:T(128)S(1)} %stack.19.info_ref, bf16[1024,512]{1,0:T(8,128)(2,1)S(1)} %get-tuple-element.44.live_ref, bf16[1024,1024]{1,0:T(8,128)(2,1)S(1)} %get-tuple-element.51.left_ref, ...), custom_call_target="tpu_custom_call" | custom-call | flops 200000000 | bytes 1000000 | tf_op jit(solution)/shard_map/term_rows/pallas_call | solution.py:160
  17.9 2.2 %term_rows.8 = (f32[512,512]{1,0:T(8,128)S(1)}, f32[8,128]{1,0:T(8,128)S(1)}, bf16[1024,1024]{1,0:T(8,128)(2,1)S(1)}, bf16[512,512]{1,0:T(8,128)(2,1)S(1)}) custom-call(s32[7]{0:T(128)S(1)} %stack.19.info_ref, bf16[1024,512]{1,0:T(8,128)(2,1)S(1)} %get-tuple-element.44.live_ref, bf16[1024,1024]{1,0:T(8,128)(2,1)S(1)} %get-tuple-element.56.left_ref, ...), custom_call_target="tpu_custom_call" | custom-call | flops 200000000 | bytes 1000000 | tf_op jit(solution)/shard_map/term_rows/pallas_call | solution.py:160
  20.1 4.4 %collective-permute-start.6 = (f32[512,512]{1,0:T(8,128)S(1)}, f32[512,512]{1,0:T(8,128)S(1)}, u32[]{:S(2)}, u32[]{:S(2)}) collective-permute-start(f32[512,512]{1,0:T(8,128)S(1)} %get-tuple-element.67), channel_id=1, source_target_pairs={{0,1},{4,5},{8,9},{12,13},{1,0},{5,4},{9,8},{13,12},{2,3},{6,7},{1... | collective-permute-start | bytes 3145736 | tf_op jit(solution)/shard_map/ppermute | solution.py:305
  24.4 1.2 %collective-permute-done.2.refs_0_ = f32[512,512]{1,0:T(8,128)S(1)} collective-permute-done((f32[512,512]{1,0:T(8,128)S(1)}, f32[512,512]{1,0:T(8,128)S(1)}, u32[]{:S(2)}, u32[]{:S(2)}) %collective-permute-start.2) | collective-permute-done | bytes 1048608 | tf_op jit(solution)/shard_map/ppermute | solution.py:317
  25.6 4.6 %collective-permute-start.5 = (f32[512,512]{1,0:T(8,128)S(1)}, f32[512,512]{1,0:T(8,128)S(1)}, u32[]{:S(2)}, u32[]{:S(2)}) collective-permute-start(f32[512,512]{1,0:T(8,128)S(1)} %get-tuple-element.66.a_ref), channel_id=1, source_target_pairs={{0,4},{4,8},{8,12},{16,20},{20,24},{24,28}} | collective-permute-start | bytes 3145736 | tf_op jit(solution)/shard_map/ppermute | solution.py:305
  30.2 0.7 collective-permute-start.4
  31.0 1.5 %term_rows.9 = (f32[512,512]{1,0:T(8,128)S(1)}, f32[8,128]{1,0:T(8,128)S(1)}) custom-call(s32[7]{0:T(128)S(1)} %stack.19.info_ref, bf16[1024,512]{1,0:T(8,128)(2,1)S(1)} %get-tuple-element.44.live_ref, bf16[1024,1024]{1,0:T(8,128)(2,1)S(1)} %get-tuple-element.56.left_ref, bf16[512,512]{1,0:T(8,128)(2,1)S(1)} %get-tuple-element.57.right_ref, ...), custom_call_target="tpu_custom_call" | custom-call | flops 200000000 | bytes 1000000 | tf_op jit(solution)/shard_map/term_rows/pallas_call | solution.py:160
  32.7 0.7 collective-permute-start.9
  33.4 3.4 %collective-permute-done.7.refs_0_ = f32[512,512]{1,0:T(8,128)S(1)} collective-permute-done((f32[512,512]{1,0:T(8,128)S(1)}, f32[512,512]{1,0:T(8,128)S(1)}, u32[]{:S(2)}, u32[]{:S(2)}) %collective-permute-start.7) | collective-permute-done | bytes 1048608 | tf_op jit(solution)/shard_map/ppermute | solution.py:317
  37.1 4.4 %collective-permute-start.10 = (f32[512,512]{1,0:T(8,128)S(1)}, f32[512,512]{1,0:T(8,128)S(1)}, u32[]{:S(2)}, u32[]{:S(2)}) collective-permute-start(f32[512,512]{1,0:T(8,128)S(1)} %get-tuple-element.79.a_ref), channel_id=1, source_target_pairs={{0,4},{4,8},{8,12},{16,20},{20,24},{24,28}} | collective-permute-start | bytes 3145736 | tf_op jit(solution)/shard_map/ppermute | solution.py:305
  41.5 1.5 %term_rows.10 = (f32[512,512]{1,0:T(8,128)S(1)}, f32[8,128]{1,0:T(8,128)S(1)}) custom-call(s32[7]{0:T(128)S(1)} %stack.19.info_ref, bf16[1024,512]{1,0:T(8,128)(2,1)S(1)} %get-tuple-element.44.live_ref, bf16[1024,1024]{1,0:T(8,128)(2,1)S(1)} %get-tuple-element.59.left_ref, bf16[512,512]{1,0:T(8,128)(2,1)S(1)} %get-tuple-element.60.right_ref, ...), custom_call_target="tpu_custom_call" | custom-call | flops 200000000 | bytes 1000000 | tf_op jit(solution)/shard_map/term_rows/pallas_call | solution.py:160
  43.2 0.7 collective-permute-start.11
  44.0 1.0 %finish_rows.2 = (bf16[1,1024,512]{2,1,0:T(8,128)(2,1)}, f32[16,128]{1,0:T(8,128)S(1)}) custom-call(s32[16,512]{1,0:T(8,128)S(1)} %get-tuple-element.43.sizes_ref, bf16[1024,512]{1,0:T(8,128)(2,1)S(1)} %get-tuple-element.44.live_ref, f32[512,512]{1,0:T(8,128)S(1)} %get-tuple-element.75.own_ref, f32[512,512]{1,0:T(8,128)S(1)} %get-tuple-element.66.a_ref, ...), custom_call_target="tpu_custom_call" | custom-call | flops 200000000 | bytes 1000000 | tf_op jit(solution)/shard_map/finish_rows/pallas_call | solution.py:271
  45.0 1.5 %term_rows.11 = (f32[512,512]{1,0:T(8,128)S(1)}, f32[8,128]{1,0:T(8,128)}) custom-call(s32[7]{0:T(128)S(1)} %stack.19.info_ref, bf16[1024,512]{1,0:T(8,128)(2,1)S(1)} %get-tuple-element.44.live_ref, bf16[1024,1024]{1,0:T(8,128)(2,1)S(1)} %get-tuple-element.59.left_ref, bf16[512,512]{1,0:T(8,128)(2,1)S(1)} %get-tuple-element.60.right_ref, ...), custom_call_target="tpu_custom_call" | custom-call | flops 200000000 | bytes 1000000 | tf_op jit(solution)/shard_map/term_rows/pallas_call | solution.py:160
  46.5 7.2 %collective-permute-done.10.b_ref = f32[512,512]{1,0:T(8,128)S(1)} collective-permute-done((f32[512,512]{1,0:T(8,128)S(1)}, f32[512,512]{1,0:T(8,128)S(1)}, u32[]{:S(2)}, u32[]{:S(2)}) %collective-permute-start.10) | collective-permute-done | bytes 1048608 | tf_op jit(solution)/shard_map/ppermute | solution.py:305
  53.7 1.0 %finish_rows.3 = (bf16[1,1024,512]{2,1,0:T(8,128)(2,1)}, f32[16,128]{1,0:T(8,128)S(1)}) custom-call(s32[16,512]{1,0:T(8,128)S(1)} %get-tuple-element.43.sizes_ref, bf16[1024,512]{1,0:T(8,128)(2,1)S(1)} %get-tuple-element.44.live_ref, f32[512,512]{1,0:T(8,128)S(1)} %get-tuple-element.78.own_ref, ...), custom_call_target="tpu_custom_call", output_to_operand_aliasing={{0}: (7, {})} | custom-call | flops 200000000 | bytes 1000000 | tf_op jit(solution)/shard_map/finish_rows/pallas_call | solution.py:271
  54.7 18.2 %all_to_all.12 = f32[16,1,128]{2,1,0:T(1,128)S(1)} all-to-all(f32[16,1,128]{2,1,0:T(1,128)S(1)} %bitcast.11), channel_id=1, replica_groups=mesh['grp'=2,'sec'=16] {'sec'}, dimensions={0} | all-to-all | bytes 16384 | tf_op jit(solution)/shard_map/all_to_all | solution.py:288
  (25 shorter events, 2.8 us)
Async XLA Ops:
  2.0 1.2 %copy-start.1 = (bf16[1,1024,512]{2,1,0:T(8,128)(2,1)S(1)}, bf16[1,1024,512]{2,1,0:T(8,128)(2,1)}, u32[]{:S(2)}) copy-start(bf16[1,1024,512]{2,1,0:T(8,128)(2,1)} %param.5) | copy-start | bytes 3145732
  6.2 2.8 %collective-permute-start = (f32[512,512]{1,0:T(8,128)S(1)}, f32[512,512]{1,0:T(8,128)S(1)}, u32[]{:S(2)}, u32[]{:S(2)}) collective-permute-start(f32[512,512]{1,0:T(8,128)S(1)} %get-tuple-element.45.a_ref), channel_id=1, source_target_pairs={{0,1},{4,5},{8,9},{12,13},{1,0},{5,4},{9,8},{13,12},{2,3},{6,7},{1... | collective-permute-start | bytes 3145736 | tf_op jit(solution)/shard_map/ppermute | solution.py:305
  6.8 3.7 %copy-start = (bf16[1,4,512,512]{3,2,1,0:T(8,128)(2,1)S(1)}, bf16[1,4,512,512]{3,2,1,0:T(8,128)(2,1)}, u32[]{:S(2)}) copy-start(bf16[1,4,512,512]{3,2,1,0:T(8,128)(2,1)} %refs_1_.3) | copy-start | bytes 6291460
  8.3 6.0 %collective-permute-start.1 = (f32[512,512]{1,0:T(8,128)S(1)}, f32[512,512]{1,0:T(8,128)S(1)}, u32[]{:S(2)}, u32[]{:S(2)}) collective-permute-start(f32[512,512]{1,0:T(8,128)S(1)} %get-tuple-element.53.a_ref), channel_id=1, source_target_pairs={{0,1},{4,5},{8,9},{12,13},{1,0},{5,4},{9,8},{13,12},{2,3},{6,7},{1... | collective-permute-start | bytes 3145736 | tf_op jit(solution)/shard_map/ppermute | solution.py:305
  9.2 16.4 %collective-permute-start.2 = (f32[512,512]{1,0:T(8,128)S(1)}, f32[512,512]{1,0:T(8,128)S(1)}, u32[]{:S(2)}, u32[]{:S(2)}) collective-permute-start(f32[512,512]{1,0:T(8,128)S(1)} %get-tuple-element.61), channel_id=1, source_target_pairs={{1,2},{5,6},{9,10},{13,14},{3,0},{7,4},{11,8},{17,18},{21,22},{25,... | collective-permute-start | bytes 3145736 | tf_op jit(solution)/shard_map/ppermute | solution.py:317
  13.5 19.0 %collective-permute-start.8 = (f32[512,512]{1,0:T(8,128)S(1)}, f32[512,512]{1,0:T(8,128)S(1)}, u32[]{:S(2)}, u32[]{:S(2)}) collective-permute-start(f32[512,512]{1,0:T(8,128)S(1)} %get-tuple-element.69.a_ref), channel_id=1, source_target_pairs={{3,6},{7,10},{11,14},{4,1},{8,5},{12,9},{19,22},{23,26},{27,30},{2... | collective-permute-start | bytes 3145736 | tf_op jit(solution)/shard_map/ppermute | solution.py:305
  14.4 22.4 %collective-permute-start.7 = (f32[512,512]{1,0:T(8,128)S(1)}, f32[512,512]{1,0:T(8,128)S(1)}, u32[]{:S(2)}, u32[]{:S(2)}) collective-permute-start(f32[512,512]{1,0:T(8,128)S(1)} %get-tuple-element.68), channel_id=1, source_target_pairs={{1,2},{5,6},{9,10},{13,14},{3,0},{7,4},{11,8},{17,18},{21,22},{25,... | collective-permute-start | bytes 3145736 | tf_op jit(solution)/shard_map/ppermute | solution.py:317
  20.1 17.0 %collective-permute-start.6 = (f32[512,512]{1,0:T(8,128)S(1)}, f32[512,512]{1,0:T(8,128)S(1)}, u32[]{:S(2)}, u32[]{:S(2)}) collective-permute-start(f32[512,512]{1,0:T(8,128)S(1)} %get-tuple-element.67), channel_id=1, source_target_pairs={{0,1},{4,5},{8,9},{12,13},{1,0},{5,4},{9,8},{13,12},{2,3},{6,7},{1... | collective-permute-start | bytes 3145736 | tf_op jit(solution)/shard_map/ppermute | solution.py:305
  25.6 17.4 %collective-permute-start.5 = (f32[512,512]{1,0:T(8,128)S(1)}, f32[512,512]{1,0:T(8,128)S(1)}, u32[]{:S(2)}, u32[]{:S(2)}) collective-permute-start(f32[512,512]{1,0:T(8,128)S(1)} %get-tuple-element.66.a_ref), channel_id=1, source_target_pairs={{0,4},{4,8},{8,12},{16,20},{20,24},{24,28}} | collective-permute-start | bytes 3145736 | tf_op jit(solution)/shard_map/ppermute | solution.py:305
  30.2 12.8 %collective-permute-start.4 = (f32[512,512]{1,0:T(8,128)S(1)}, f32[512,512]{1,0:T(8,128)S(1)}, u32[]{:S(2)}, u32[]{:S(2)}) collective-permute-start(f32[512,512]{1,0:T(8,128)S(1)} %get-tuple-element.65.a_ref), channel_id=1, source_target_pairs={{3,6},{7,10},{11,14},{4,1},{8,5},{12,9},{19,22},{23,26},{27,30},{2... | collective-permute-start | bytes 3145736 | tf_op jit(solution)/shard_map/ppermute | solution.py:305
  32.7 11.3 %collective-permute-start.9 = (f32[512,512]{1,0:T(8,128)S(1)}, f32[512,512]{1,0:T(8,128)S(1)}, u32[]{:S(2)}, u32[]{:S(2)}) collective-permute-start(f32[512,512]{1,0:T(8,128)S(1)} %get-tuple-element.76), channel_id=1, source_target_pairs={{1,3},{5,7},{9,11},{13,15},{2,1},{6,5},{10,9},{14,13},{17,19},{21,... | collective-permute-start | bytes 3145736 | tf_op jit(solution)/shard_map/ppermute | solution.py:305
  36.8 8.2 %collective-permute-start.3 = (f32[512,512]{1,0:T(8,128)S(1)}, f32[512,512]{1,0:T(8,128)S(1)}, u32[]{:S(2)}, u32[]{:S(2)}) collective-permute-start(f32[512,512]{1,0:T(8,128)S(1)} %get-tuple-element.64), channel_id=1, source_target_pairs={{0,1},{4,5},{8,9},{12,13},{1,0},{5,4},{9,8},{13,12},{2,3},{6,7},{1... | collective-permute-start | bytes 3145736 | tf_op jit(solution)/shard_map/ppermute | solution.py:305
  37.1 16.6 %collective-permute-start.10 = (f32[512,512]{1,0:T(8,128)S(1)}, f32[512,512]{1,0:T(8,128)S(1)}, u32[]{:S(2)}, u32[]{:S(2)}) collective-permute-start(f32[512,512]{1,0:T(8,128)S(1)} %get-tuple-element.79.a_ref), channel_id=1, source_target_pairs={{0,4},{4,8},{8,12},{16,20},{20,24},{24,28}} | collective-permute-start | bytes 3145736 | tf_op jit(solution)/shard_map/ppermute | solution.py:305
  43.2 10.5 %collective-permute-start.11 = (f32[512,512]{1,0:T(8,128)S(1)}, f32[512,512]{1,0:T(8,128)S(1)}, u32[]{:S(2)}, u32[]{:S(2)}) collective-permute-start(f32[512,512]{1,0:T(8,128)S(1)} %get-tuple-element.80), channel_id=1, source_target_pairs={{1,3},{5,7},{9,11},{13,15},{2,1},{6,5},{10,9},{14,13},{17,19},{21,... | collective-permute-start | bytes 3145736 | tf_op jit(solution)/shard_map/ppermute | solution.py:305

commit v20 on v19

--- a/solution.py
+++ b/solution.py
@@ -54,15 +54,23 @@
 def opening_kernel(slot, masks, tokens, info_ref, live_ref, left_hbm, right_hbm, *refs):
     refs = list(refs[tokens:])
     out_ref, _ = refs[:2]
-    sems = refs[-1]
-    operands = refs[2:-1]
+    sems = refs.pop()
+    if masks:
+        info_copy = pltpu.make_async_copy(info_ref, refs[-1], sems.at[sems.shape[0] - 1])
+        info_copy.start()
+        info_ref = refs.pop()
+        terms = [jnp.where(lax.axis_index("sec") % 2 == 0, 2, 1)]
+    else:
+        terms = info_ref
+    operands = refs[2:]
     psi_ref = live_ref
     if masks:
         live_ref, sizes_ref = operands.pop(0), operands.pop(0)
-    left, right, late = fetch(info_ref, slot, left_hbm, right_hbm, *operands, sems)
+    left, right, late = fetch(terms, slot, left_hbm, right_hbm, *operands, sems)
     for copy in left + right + late:
         copy.start()
     if masks:
+        info_copy.wait()
         rows, cols = psi_ref.shape
         sizes_ref[:8, :] = jnp.full((8, cols), info_ref[4], jnp.int32)
         sizes_ref[8:, :] = jnp.full((8, cols), info_ref[5], jnp.int32)
@@ -105,9 +113,10 @@
     return pl.pallas_call(
         functools.partial(opening_kernel, slot, masks, len(tokens)),
         out_shape=out_shape,
-        in_specs=[SMEM, WHOLE, HBM, HBM] + [ANY] * len(tokens),
+        in_specs=[ANY if masks else SMEM, WHOLE, HBM, HBM] + [ANY] * len(tokens),
         out_specs=[WHOLE, ANY] + [WHOLE] * (len(out_shape) - 2),
-        scratch_shapes=[pltpu.SemaphoreType.DMA((LEFT_PIECES + RIGHT_PIECES,))],
+        scratch_shapes=([pltpu.SMEM(info.shape, info.dtype)] if masks else [])
+        + [pltpu.SemaphoreType.DMA((LEFT_PIECES + RIGHT_PIECES + 1,))],
         compiler_params=params(FIRST_MIB if masks else BRING_MIB),
         cost_estimate=SMALL,
         name="opening_rows",
@@ -141,7 +150,7 @@
 
 def term_rows(info, live, operands, first, count, *tokens, added=None, bring=None):
     width, cols = live.shape
-    in_specs = [SMEM, WHOLE, WHOLE, WHOLE]
+    in_specs = [ANY if bring is None else SMEM, WHOLE, WHOLE, WHOLE]
     args = [info, live, *operands]
     out_shape = [jax.ShapeDtypeStruct((count, cols), jnp.float32), TOKEN]
     out_specs = [WHOLE, ANY]

time: 74 us -> 73.5 us (level)
  Pallas kernels: 19 us -> 16.3 us
  waiting for transfers between devices: 12.4 us -> 14.6 us
    pallas_call x6, Pallas kernels: 10.4 us -> 8.28 us  [term_rows(): pl.pallas_call(functools.partial(term_kernel, first, added is not None, s...]
    ppermute x10, waiting for transfers between devices: 7.84 us -> 9.47 us  [send(): return lax.ppermute(value, 'sec', pairs)]
  transfers between devices with their start and end apart: 12 -> 12, of which waited for: 4 -> 4; matrix products, arithmetic and copies ran while one was open for 0% -> 0% of each run, Pallas kernels for 20% -> 18%
where the time goes in v20:
time: 73.5 us; the launch traced here: 73.1 us
  starting transfers between devices  19.8 us (27%)
  blocking collectives  18.2 us (25%)
  Pallas kernels  16.3 us (22%)
  waiting for transfers between devices  14.6 us (20%)
  between operations  2.19 us (3%)
  local copies, waits for them, and re-layouts  1.32 us (2%)
    all_to_all x1, blocking collectives, sum_over_sectors(): arrived = lax.all_to_all(value, 'sec', 0, 0, tiled=True)  18.2 us
    ppermute x10, starting transfers between devices, send(): return lax.ppermute(value, 'sec', pairs)  17.2 us
    ppermute x10, waiting for transfers between devices, send(): return lax.ppermute(value, 'sec', pairs)  9.47 us
    pallas_call x6, Pallas kernels, term_rows(): pl.pallas_call(functools.partial(term_kernel, first, added is not None, s...  8.28 us
    pallas_call x2, Pallas kernels, opening_rows(): pl.pallas_call(functools.partial(opening_kernel, slot, masks, len(tokens)...  5.42 us
    ppermute x2, waiting for transfers between devices, raise_one(): return lax.ppermute(value, 'sec', pairs_up)  5.12 us
    ppermute x2, starting transfers between devices, raise_one(): return lax.ppermute(value, 'sec', pairs_up)  2.58 us
    pallas_call x2, Pallas kernels, finish(): pl.pallas_call(functools.partial(finish_kernel, first), out_shape=(jax.Sh...  2.06 us
  transfers between devices with their start and end apart: 12, of which 4 were waited for; matrix products, arithmetic and copies ran while one was open for 0% of the time, Pallas kernels for 18%

profile of v20, /device:TPU:0, one launch (start us, length us, event | category | flops | bytes accessed | tf_op | source)
XLA Modules:
  0.0 73.1 jit_solution(4847395257916116712)
XLA Ops:
  2.0 1.2 %copy-done.1 = bf16[1,1024,512]{2,1,0:T(8,128)(2,1)S(1)} copy-done((bf16[1,1024,512]{2,1,0:T(8,128)(2,1)S(1)}, bf16[1,1024,512]{2,1,0:T(8,128)(2,1)}, u32[]{:S(2)}) %copy-start.1) | copy-done | bytes 1048600
  3.3 2.4 %opening_rows.2 = (f32[512,512]{1,0:T(8,128)S(1)}, f32[8,128]{1,0:T(8,128)S(1)}, bf16[1024,512]{1,0:T(8,128)(2,1)S(1)}, s32[16,512]{1,0:T(8,128)S(1)}, bf16[1024...) custom-call(s32[7]{0:T(128)S(1)} %stack.19.info_ref, bf16[1024,512]{1,0:T(8,128)(2,1)S(1)} %bitcast.10, ...), custom_call_target="tpu_custom_call" | custom-call | flops 200000000 | bytes 1000000 | tf_op jit(solution)/shard_map/opening_rows/pallas_call | solution.py:113
  6.2 1.0 %term_rows.6 = (f32[512,512]{1,0:T(8,128)S(1)}, f32[8,128]{1,0:T(8,128)S(1)}) custom-call(s32[7]{0:T(128)S(1)} %stack.19.info_ref, bf16[1024,512]{1,0:T(8,128)(2,1)S(1)} %get-tuple-element.44.live_ref, bf16[1024,1024]{1,0:T(8,128)(2,1)S(1)} %get-tuple-element.46.left_ref, bf16[512,512]{1,0:T(8,128)(2,1)S(1)} %get-tuple-element.47.right_ref, ...), custom_call_target="tpu_custom_call" | custom-call | flops 200000000 | bytes 1000000 | tf_op jit(solution)/shard_map/term_rows/pallas_call | solution.py:169
  7.3 1.2 %collective-permute-done.b_ref = f32[512,512]{1,0:T(8,128)S(1)} collective-permute-done((f32[512,512]{1,0:T(8,128)S(1)}, f32[512,512]{1,0:T(8,128)S(1)}, u32[]{:S(2)}, u32[]{:S(2)}) %collective-permute-start) | collective-permute-done | bytes 1048608 | tf_op jit(solution)/shard_map/ppermute | solution.py:314
  8.7 1.3 %collective-permute-start.2 = (f32[512,512]{1,0:T(8,128)S(1)}, f32[512,512]{1,0:T(8,128)S(1)}, u32[]{:S(2)}, u32[]{:S(2)}) collective-permute-start(f32[512,512]{1,0:T(8,128)S(1)} %get-tuple-element.61), channel_id=1, source_target_pairs={{1,2},{5,6},{9,10},{13,14},{3,0},{7,4},{11,8},{17,18},{21,22},{25,... | collective-permute-start | bytes 3145736 | tf_op jit(solution)/shard_map/ppermute | solution.py:326
  10.0 3.0 %opening_rows.3 = (f32[512,512]{1,0:T(8,128)S(1)}, f32[8,128]{1,0:T(8,128)S(1)}, bf16[1024,1024]{1,0:T(8,128)(2,1)S(1)}, bf16[512,512]{1,0:T(8,128)(2,1)S(1)}) custom-call(s32[7]{0:T(128)S(1)} %stack.19.info_ref, bf16[1024,512]{1,0:T(8,128)(2,1)S(1)} %get-tuple-element.44.live_ref, bf16[1,4,1024,1024]{3,2,1,0:T(8,128)(2,1)} %refs_0_.3, ...), custom_call_target="tpu_custom_call" | custom-call | flops 200000000 | bytes 1000000 | tf_op jit(solution)/shard_map/opening_rows/pallas_call | solution.py:113
  13.0 0.7 collective-permute-start.8
  13.9 1.3 %collective-permute-start.7 = (f32[512,512]{1,0:T(8,128)S(1)}, f32[512,512]{1,0:T(8,128)S(1)}, u32[]{:S(2)}, u32[]{:S(2)}) collective-permute-start(f32[512,512]{1,0:T(8,128)S(1)} %get-tuple-element.68), channel_id=1, source_target_pairs={{1,2},{5,6},{9,10},{13,14},{3,0},{7,4},{11,8},{17,18},{21,22},{25,... | collective-permute-start | bytes 3145736 | tf_op jit(solution)/shard_map/ppermute | solution.py:326
  15.2 2.2 %term_rows.7 = (f32[512,512]{1,0:T(8,128)S(1)}, f32[8,128]{1,0:T(8,128)S(1)}, bf16[1024,1024]{1,0:T(8,128)(2,1)S(1)}, bf16[512,512]{1,0:T(8,128)(2,1)S(1)}) custom-call(s32[7]{0:T(128)S(1)} %stack.19.info_ref, bf16[1024,512]{1,0:T(8,128)(2,1)S(1)} %get-tuple-element.44.live_ref, bf16[1024,1024]{1,0:T(8,128)(2,1)S(1)} %get-tuple-element.51.left_ref, ...), custom_call_target="tpu_custom_call" | custom-call | flops 200000000 | bytes 1000000 | tf_op jit(solution)/shard_map/term_rows/pallas_call | solution.py:169
  17.4 2.2 %term_rows.8 = (f32[512,512]{1,0:T(8,128)S(1)}, f32[8,128]{1,0:T(8,128)S(1)}, bf16[1024,1024]{1,0:T(8,128)(2,1)S(1)}, bf16[512,512]{1,0:T(8,128)(2,1)S(1)}) custom-call(s32[7]{0:T(128)S(1)} %stack.19.info_ref, bf16[1024,512]{1,0:T(8,128)(2,1)S(1)} %get-tuple-element.44.live_ref, bf16[1024,1024]{1,0:T(8,128)(2,1)S(1)} %get-tuple-element.56.left_ref, ...), custom_call_target="tpu_custom_call" | custom-call | flops 200000000 | bytes 1000000 | tf_op jit(solution)/shard_map/term_rows/pallas_call | solution.py:169
  19.5 4.4 %collective-permute-start.6 = (f32[512,512]{1,0:T(8,128)S(1)}, f32[512,512]{1,0:T(8,128)S(1)}, u32[]{:S(2)}, u32[]{:S(2)}) collective-permute-start(f32[512,512]{1,0:T(8,128)S(1)} %get-tuple-element.67), channel_id=1, source_target_pairs={{0,1},{4,5},{8,9},{12,13},{1,0},{5,4},{9,8},{13,12},{2,3},{6,7},{1... | collective-permute-start | bytes 3145736 | tf_op jit(solution)/shard_map/ppermute | solution.py:314
  23.9 1.1 %collective-permute-done.2.refs_0_ = f32[512,512]{1,0:T(8,128)S(1)} collective-permute-done((f32[512,512]{1,0:T(8,128)S(1)}, f32[512,512]{1,0:T(8,128)S(1)}, u32[]{:S(2)}, u32[]{:S(2)}) %collective-permute-start.2) | collective-permute-done | bytes 1048608 | tf_op jit(solution)/shard_map/ppermute | solution.py:326
  25.1 4.6 %collective-permute-start.5 = (f32[512,512]{1,0:T(8,128)S(1)}, f32[512,512]{1,0:T(8,128)S(1)}, u32[]{:S(2)}, u32[]{:S(2)}) collective-permute-start(f32[512,512]{1,0:T(8,128)S(1)} %get-tuple-element.66.a_ref), channel_id=1, source_target_pairs={{0,4},{4,8},{8,12},{16,20},{20,24},{24,28}} | collective-permute-start | bytes 3145736 | tf_op jit(solution)/shard_map/ppermute | solution.py:314
  30.4 1.0 %term_rows.9 = (f32[512,512]{1,0:T(8,128)S(1)}, f32[8,128]{1,0:T(8,128)S(1)}) custom-call(s32[7]{0:T(128)S(1)} %stack.19.info_ref, bf16[1024,512]{1,0:T(8,128)(2,1)S(1)} %get-tuple-element.44.live_ref, bf16[1024,1024]{1,0:T(8,128)(2,1)S(1)} %get-tuple-element.56.left_ref, bf16[512,512]{1,0:T(8,128)(2,1)S(1)} %get-tuple-element.57.right_ref, ...), custom_call_target="tpu_custom_call" | custom-call | flops 200000000 | bytes 1000000 | tf_op jit(solution)/shard_map/term_rows/pallas_call | solution.py:169
  31.6 0.7 collective-permute-start.9
  32.3 4.0 %collective-permute-done.7.refs_0_ = f32[512,512]{1,0:T(8,128)S(1)} collective-permute-done((f32[512,512]{1,0:T(8,128)S(1)}, f32[512,512]{1,0:T(8,128)S(1)}, u32[]{:S(2)}, u32[]{:S(2)}) %collective-permute-start.7) | collective-permute-done | bytes 1048608 | tf_op jit(solution)/shard_map/ppermute | solution.py:326
  36.6 4.4 %collective-permute-start.10 = (f32[512,512]{1,0:T(8,128)S(1)}, f32[512,512]{1,0:T(8,128)S(1)}, u32[]{:S(2)}, u32[]{:S(2)}) collective-permute-start(f32[512,512]{1,0:T(8,128)S(1)} %get-tuple-element.79.a_ref), channel_id=1, source_target_pairs={{0,4},{4,8},{8,12},{16,20},{20,24},{24,28}} | collective-permute-start | bytes 3145736 | tf_op jit(solution)/shard_map/ppermute | solution.py:314
  41.0 1.0 %term_rows.10 = (f32[512,512]{1,0:T(8,128)S(1)}, f32[8,128]{1,0:T(8,128)S(1)}) custom-call(s32[7]{0:T(128)S(1)} %stack.19.info_ref, bf16[1024,512]{1,0:T(8,128)(2,1)S(1)} %get-tuple-element.44.live_ref, bf16[1024,1024]{1,0:T(8,128)(2,1)S(1)} %get-tuple-element.59.left_ref, bf16[512,512]{1,0:T(8,128)(2,1)S(1)} %get-tuple-element.60.right_ref, ...), custom_call_target="tpu_custom_call" | custom-call | flops 200000000 | bytes 1000000 | tf_op jit(solution)/shard_map/term_rows/pallas_call | solution.py:169
  42.1 0.7 collective-permute-start.11
  42.9 1.0 %finish_rows.2 = (bf16[1,1024,512]{2,1,0:T(8,128)(2,1)}, f32[16,128]{1,0:T(8,128)S(1)}) custom-call(s32[16,512]{1,0:T(8,128)S(1)} %get-tuple-element.43.sizes_ref, bf16[1024,512]{1,0:T(8,128)(2,1)S(1)} %get-tuple-element.44.live_ref, f32[512,512]{1,0:T(8,128)S(1)} %get-tuple-element.75.own_ref, f32[512,512]{1,0:T(8,128)S(1)} %get-tuple-element.66.a_ref, ...), custom_call_target="tpu_custom_call" | custom-call | flops 200000000 | bytes 1000000 | tf_op jit(solution)/shard_map/finish_rows/pallas_call | solution.py:280
  43.9 1.0 %term_rows.11 = (f32[512,512]{1,0:T(8,128)S(1)}, f32[8,128]{1,0:T(8,128)}) custom-call(s32[7]{0:T(128)S(1)} %stack.19.info_ref, bf16[1024,512]{1,0:T(8,128)(2,1)S(1)} %get-tuple-element.44.live_ref, bf16[1024,1024]{1,0:T(8,128)(2,1)S(1)} %get-tuple-element.59.left_ref, bf16[512,512]{1,0:T(8,128)(2,1)S(1)} %get-tuple-element.60.right_ref, ...), custom_call_target="tpu_custom_call" | custom-call | flops 200000000 | bytes 1000000 | tf_op jit(solution)/shard_map/term_rows/pallas_call | solution.py:169
  44.9 8.3 %collective-permute-done.10.b_ref = f32[512,512]{1,0:T(8,128)S(1)} collective-permute-done((f32[512,512]{1,0:T(8,128)S(1)}, f32[512,512]{1,0:T(8,128)S(1)}, u32[]{:S(2)}, u32[]{:S(2)}) %collective-permute-start.10) | collective-permute-done | bytes 1048608 | tf_op jit(solution)/shard_map/ppermute | solution.py:314
  53.2 1.0 %finish_rows.3 = (bf16[1,1024,512]{2,1,0:T(8,128)(2,1)}, f32[16,128]{1,0:T(8,128)S(1)}) custom-call(s32[16,512]{1,0:T(8,128)S(1)} %get-tuple-element.43.sizes_ref, bf16[1024,512]{1,0:T(8,128)(2,1)S(1)} %get-tuple-element.44.live_ref, f32[512,512]{1,0:T(8,128)S(1)} %get-tuple-element.78.own_ref, ...), custom_call_target="tpu_custom_call", output_to_operand_aliasing={{0}: (7, {})} | custom-call | flops 200000000 | bytes 1000000 | tf_op jit(solution)/shard_map/finish_rows/pallas_call | solution.py:280
  54.2 18.2 %all_to_all.12 = f32[16,1,128]{2,1,0:T(1,128)S(1)} all-to-all(f32[16,1,128]{2,1,0:T(1,128)S(1)} %bitcast.11), channel_id=1, replica_groups=mesh['grp'=2,'sec'=16] {'sec'}, dimensions={0} | all-to-all | bytes 16384 | tf_op jit(solution)/shard_map/all_to_all | solution.py:297
  (25 shorter events, 2.9 us)
Async XLA Ops:
  2.0 1.2 %copy-start.1 = (bf16[1,1024,512]{2,1,0:T(8,128)(2,1)S(1)}, bf16[1,1024,512]{2,1,0:T(8,128)(2,1)}, u32[]{:S(2)}) copy-start(bf16[1,1024,512]{2,1,0:T(8,128)(2,1)} %param.5) | copy-start | bytes 3145732
  5.7 2.8 %collective-permute-start = (f32[512,512]{1,0:T(8,128)S(1)}, f32[512,512]{1,0:T(8,128)S(1)}, u32[]{:S(2)}, u32[]{:S(2)}) collective-permute-start(f32[512,512]{1,0:T(8,128)S(1)} %get-tuple-element.45.a_ref), channel_id=1, source_target_pairs={{0,1},{4,5},{8,9},{12,13},{1,0},{5,4},{9,8},{13,12},{2,3},{6,7},{1... | collective-permute-start | bytes 3145736 | tf_op jit(solution)/shard_map/ppermute | solution.py:314
  6.2 3.7 %copy-start = (bf16[1,4,512,512]{3,2,1,0:T(8,128)(2,1)S(1)}, bf16[1,4,512,512]{3,2,1,0:T(8,128)(2,1)}, u32[]{:S(2)}) copy-start(bf16[1,4,512,512]{3,2,1,0:T(8,128)(2,1)} %refs_1_.3) | copy-start | bytes 6291460
  7.2 6.5 %collective-permute-start.1 = (f32[512,512]{1,0:T(8,128)S(1)}, f32[512,512]{1,0:T(8,128)S(1)}, u32[]{:S(2)}, u32[]{:S(2)}) collective-permute-start(f32[512,512]{1,0:T(8,128)S(1)} %get-tuple-element.53.a_ref), channel_id=1, source_target_pairs={{0,1},{4,5},{8,9},{12,13},{1,0},{5,4},{9,8},{13,12},{2,3},{6,7},{1... | collective-permute-start | bytes 3145736 | tf_op jit(solution)/shard_map/ppermute | solution.py:314
  8.7 16.4 %collective-permute-start.2 = (f32[512,512]{1,0:T(8,128)S(1)}, f32[512,512]{1,0:T(8,128)S(1)}, u32[]{:S(2)}, u32[]{:S(2)}) collective-permute-start(f32[512,512]{1,0:T(8,128)S(1)} %get-tuple-element.61), channel_id=1, source_target_pairs={{1,2},{5,6},{9,10},{13,14},{3,0},{7,4},{11,8},{17,18},{21,22},{25,... | collective-permute-start | bytes 3145736 | tf_op jit(solution)/shard_map/ppermute | solution.py:326
  13.0 18.5 %collective-permute-start.8 = (f32[512,512]{1,0:T(8,128)S(1)}, f32[512,512]{1,0:T(8,128)S(1)}, u32[]{:S(2)}, u32[]{:S(2)}) collective-permute-start(f32[512,512]{1,0:T(8,128)S(1)} %get-tuple-element.69.a_ref), channel_id=1, source_target_pairs={{3,6},{7,10},{11,14},{4,1},{8,5},{12,9},{19,22},{23,26},{27,30},{2... | collective-permute-start | bytes 3145736 | tf_op jit(solution)/shard_map/ppermute | solution.py:314
  13.9 22.4 %collective-permute-start.7 = (f32[512,512]{1,0:T(8,128)S(1)}, f32[512,512]{1,0:T(8,128)S(1)}, u32[]{:S(2)}, u32[]{:S(2)}) collective-permute-start(f32[512,512]{1,0:T(8,128)S(1)} %get-tuple-element.68), channel_id=1, source_target_pairs={{1,2},{5,6},{9,10},{13,14},{3,0},{7,4},{11,8},{17,18},{21,22},{25,... | collective-permute-start | bytes 3145736 | tf_op jit(solution)/shard_map/ppermute | solution.py:326
  19.5 17.0 %collective-permute-start.6 = (f32[512,512]{1,0:T(8,128)S(1)}, f32[512,512]{1,0:T(8,128)S(1)}, u32[]{:S(2)}, u32[]{:S(2)}) collective-permute-start(f32[512,512]{1,0:T(8,128)S(1)} %get-tuple-element.67), channel_id=1, source_target_pairs={{0,1},{4,5},{8,9},{12,13},{1,0},{5,4},{9,8},{13,12},{2,3},{6,7},{1... | collective-permute-start | bytes 3145736 | tf_op jit(solution)/shard_map/ppermute | solution.py:314
  25.1 16.9 %collective-permute-start.5 = (f32[512,512]{1,0:T(8,128)S(1)}, f32[512,512]{1,0:T(8,128)S(1)}, u32[]{:S(2)}, u32[]{:S(2)}) collective-permute-start(f32[512,512]{1,0:T(8,128)S(1)} %get-tuple-element.66.a_ref), channel_id=1, source_target_pairs={{0,4},{4,8},{8,12},{16,20},{20,24},{24,28}} | collective-permute-start | bytes 3145736 | tf_op jit(solution)/shard_map/ppermute | solution.py:314
  29.7 12.3 %collective-permute-start.4 = (f32[512,512]{1,0:T(8,128)S(1)}, f32[512,512]{1,0:T(8,128)S(1)}, u32[]{:S(2)}, u32[]{:S(2)}) collective-permute-start(f32[512,512]{1,0:T(8,128)S(1)} %get-tuple-element.65.a_ref), channel_id=1, source_target_pairs={{3,6},{7,10},{11,14},{4,1},{8,5},{12,9},{19,22},{23,26},{27,30},{2... | collective-permute-start | bytes 3145736 | tf_op jit(solution)/shard_map/ppermute | solution.py:314
  31.6 11.3 %collective-permute-start.9 = (f32[512,512]{1,0:T(8,128)S(1)}, f32[512,512]{1,0:T(8,128)S(1)}, u32[]{:S(2)}, u32[]{:S(2)}) collective-permute-start(f32[512,512]{1,0:T(8,128)S(1)} %get-tuple-element.76), channel_id=1, source_target_pairs={{1,3},{5,7},{9,11},{13,15},{2,1},{6,5},{10,9},{14,13},{17,19},{21,... | collective-permute-start | bytes 3145736 | tf_op jit(solution)/shard_map/ppermute | solution.py:314
  36.3 7.6 %collective-permute-start.3 = (f32[512,512]{1,0:T(8,128)S(1)}, f32[512,512]{1,0:T(8,128)S(1)}, u32[]{:S(2)}, u32[]{:S(2)}) collective-permute-start(f32[512,512]{1,0:T(8,128)S(1)} %get-tuple-element.64), channel_id=1, source_target_pairs={{0,1},{4,5},{8,9},{12,13},{1,0},{5,4},{9,8},{13,12},{2,3},{6,7},{1... | collective-permute-start | bytes 3145736 | tf_op jit(solution)/shard_map/ppermute | solution.py:314
  36.6 16.6 %collective-permute-start.10 = (f32[512,512]{1,0:T(8,128)S(1)}, f32[512,512]{1,0:T(8,128)S(1)}, u32[]{:S(2)}, u32[]{:S(2)}) collective-permute-start(f32[512,512]{1,0:T(8,128)S(1)} %get-tuple-element.79.a_ref), channel_id=1, source_target_pairs={{0,4},{4,8},{8,12},{16,20},{20,24},{24,28}} | collective-permute-start | bytes 3145736 | tf_op jit(solution)/shard_map/ppermute | solution.py:314
  42.1 11.1 %collective-permute-start.11 = (f32[512,512]{1,0:T(8,128)S(1)}, f32[512,512]{1,0:T(8,128)S(1)}, u32[]{:S(2)}, u32[]{:S(2)}) collective-permute-start(f32[512,512]{1,0:T(8,128)S(1)} %get-tuple-element.80), channel_id=1, source_target_pairs={{1,3},{5,7},{9,11},{13,15},{2,1},{6,5},{10,9},{14,13},{17,19},{21,... | collective-permute-start | bytes 3145736 | tf_op jit(solution)/shard_map/ppermute | solution.py:314
